TPU v7x, 32 devices: a whole 2x2x4 slice. The times are simulated.
32 devices in a mesh: dp: 8 (over z, y), mp: 4 (over x, core).
Axes of the slice: x: 2, y: 2, z: 4, core: 2. Of those that a mesh axis runs over, the one named last changes fastest.
Arguments:
- tokens: bfloat16 [7168, 2304], P('dp'), may hold values from -6 to 6
- segments: int32 [7168], P('dp'), may hold values from -1 to 3, as said below
- cotangent: bfloat16 [7168, 2304], P('dp'), may hold values from -6 to 6
- query_weight: float32 [2304, 2048], P('dp', 'mp'), may hold values from -0.21875 to 0.21875
- keyval_weight: float32 [2, 2304, 1024], P(None, 'dp', 'mp'), may hold values from -0.21875 to 0.21875
- output_weight: float32 [2048, 2304], P('mp', 'dp'), may hold values from -0.125 to 0.125
- gateup_weight: float32 [2, 2304, 9216], P(None, 'dp', 'mp'), may hold values from -0.125 to 0.125
- down_weight: float32 [9216, 2304], P('mp', 'dp'), may hold values from -0.0625 to 0.0625
- norm_gains: float32 [4, 2304], P(None, 'dp'), may hold values from -0.5 to 0.5
- moment_query: float32 [2304, 2048], P('dp', 'mp'), may hold values from -18 to 18
- moment_keyval: float32 [2, 2304, 1024], P(None, 'dp', 'mp'), may hold values from -18 to 18
- moment_output: float32 [2048, 2304], P('mp', 'dp'), may hold values from -18 to 18
- moment_gateup: float32 [2, 2304, 9216], P(None, 'dp', 'mp'), may hold values from -18 to 18
- moment_down: float32 [9216, 2304], P('mp', 'dp'), may hold values from -18 to 18
- moment_gains: float32 [4, 2304], P(None, 'dp'), may hold values from -18 to 18
- square_query: float32 [2304, 2048], P('dp', 'mp'), may hold values from 10 to 3000
- square_keyval: float32 [2, 2304, 1024], P(None, 'dp', 'mp'), may hold values from 10 to 3000
- square_output: float32 [2048, 2304], P('mp', 'dp'), may hold values from 10 to 3000
- square_gateup: float32 [2, 2304, 9216], P(None, 'dp', 'mp'), may hold values from 10 to 3000
- square_down: float32 [9216, 2304], P('mp', 'dp'), may hold values from 10 to 3000
- square_gains: float32 [4, 2304], P(None, 'dp'), may hold values from 10 to 3000
Outputs:
- block_out: bfloat16 [7168, 2304], P('dp')
- input_grad: float32 [7168, 2304], P('dp')
- grad_query: float32 [2304, 2048], P('dp', 'mp')
- grad_keyval: float32 [2, 2304, 1024], P(None, 'dp', 'mp')
- grad_output: float32 [2048, 2304], P('mp', 'dp')
- grad_gateup: float32 [2, 2304, 9216], P(None, 'dp', 'mp')
- grad_down: float32 [9216, 2304], P('mp', 'dp')
- grad_gains: float32 [4, 2304], P(None, 'dp')
- change_query: float32 [2304, 2048], P('dp', 'mp')
- change_keyval: float32 [2, 2304, 1024], P(None, 'dp', 'mp')
- change_output: float32 [2048, 2304], P('mp', 'dp')
- change_gateup: float32 [2, 2304, 9216], P(None, 'dp', 'mp')
- change_down: float32 [9216, 2304], P('mp', 'dp')
- change_gains: float32 [4, 2304], P(None, 'dp')
- momenta_query: float32 [2304, 2048], P('dp', 'mp')
- momenta_keyval: float32 [2, 2304, 1024], P(None, 'dp', 'mp')
- momenta_output: float32 [2048, 2304], P('mp', 'dp')
- momenta_gateup: float32 [2, 2304, 9216], P(None, 'dp', 'mp')
- momenta_down: float32 [9216, 2304], P('mp', 'dp')
- momenta_gains: float32 [4, 2304], P(None, 'dp')
- squares_query: float32 [2304, 2048], P('dp', 'mp')
- squares_keyval: float32 [2, 2304, 1024], P(None, 'dp', 'mp')
- squares_output: float32 [2048, 2304], P('mp', 'dp')
- squares_gateup: float32 [2, 2304, 9216], P(None, 'dp', 'mp')
- squares_down: float32 [9216, 2304], P('mp', 'dp')
- squares_gains: float32 [4, 2304], P(None, 'dp')
Inputs may be any that keep to these rules, and one draw needn't show every extreme that they name: `segments`: within each block of 896 slots of one index of dp, ids are non-decreasing from 0 over the leading slots and -1 on the padding slots at the block's end; in some block one sequence of 896 tokens fills it, some block is half padding, and in some block ids reach 3.
All inputs are finite; a program needn't handle non-finite values.
Results may differ from a plain program's by a relative error of at most 0.035.
The roundings to bfloat16 on the way count: a program that leaves them out, or rounds other values in their place, can miss the bound.
Values may be sent and summed in bfloat16 or wider, within the bound.
No kernel may reach another device: no remote copies, remote signals or barrier semaphores. Data moves between devices by JAX's collectives and lax.ppermute only.
A program may use at most 320 MiB of HBM per device.

v0:
```python
import jax
import jax.numpy as jnp
from jax import lax
from jax.sharding import PartitionSpec as P

HEADS = 8
KV_HEADS = 4
HEAD_DIM = 256
WINDOW = 4096
ADAM_STEP = 5


norm_eps = 1e-06
cap_value = 50.0
rope_base = 10000.0
learn_rate = 0.1
beta_one = 0.9
beta_two = 0.95
adam_eps = 1e-08
decay_rate = 0.1


def rms_norm(tensor, gain_vec):
    factor = lax.rsqrt(jnp.mean(tensor * tensor, axis=-1, keepdims=True) + norm_eps)
    return tensor * factor * (1.0 + gain_vec)


def rotate(tensor, cosine, sine):
    half_dim = tensor.shape[-1] // 2
    first = tensor[..., :half_dim]
    second = tensor[..., half_dim:]
    return jnp.concatenate(
        [first * cosine - second * sine, second * cosine + first * sine], axis=-1
    )


def layout(labels):
    length = labels.shape[0]
    places = jnp.arange(length, dtype=jnp.int32)
    same_seq = labels[:, None] == labels[None, :]
    earlier = places[None, :] < places[:, None]
    position = jnp.sum((same_seq & earlier).astype(jnp.int32), axis=1)
    allowed = (
        same_seq
        & (places[None, :] <= places[:, None])
        & (places[:, None] - places[None, :] < WINDOW)
    )
    half_dim = HEAD_DIM // 2
    freq = rope_base ** (-2.0 * jnp.arange(half_dim, dtype=jnp.float32) / HEAD_DIM)
    angle = position.astype(jnp.float32)[:, None] * freq[None, :]
    return (allowed, jnp.cos(angle)[:, None, :], jnp.sin(angle)[:, None, :])


def scores(queries, key_rows, allowed):
    raw_scores = jnp.einsum("qkgd,skd->kgqs", queries, key_rows, preferred_element_type=jnp.float32)
    squashed = jnp.tanh(raw_scores / cap_value)
    capped = jnp.where(allowed[None, None], cap_value * squashed, -1e30)
    return (squashed, capped)


def norm_back(tensor, gain_vec, grad_in):
    unused, pull = jax.vjp(rms_norm, tensor, gain_vec)
    return pull(grad_in)


def rotate_back(grad_in, cosine, sine, shape_like):
    unused, pull = jax.vjp(lambda tensor: rotate(tensor, cosine, sine), shape_like)
    return pull(grad_in)[0]


def adam_step(master, gradient, moment, square, steps_done):
    new_moment = beta_one * moment + (1.0 - beta_one) * gradient
    new_square = beta_two * square + (1.0 - beta_two) * gradient * gradient
    fix_one = 1.0 - beta_one**steps_done
    fix_two = 1.0 - beta_two**steps_done
    stride = new_moment / fix_one / (jnp.sqrt(new_square / fix_two) + adam_eps)
    return (-learn_rate * (stride + decay_rate * master), new_moment, new_square)


def shards(
    tokens,
    segments,
    cotangent,
    query_weight,
    keyval_weight,
    output_weight,
    gateup_weight,
    down_weight,
    norm_gains,
    moment_query,
    moment_keyval,
    moment_output,
    moment_gateup,
    moment_down,
    moment_gains,
    square_query,
    square_keyval,
    square_output,
    square_gateup,
    square_down,
    square_gains,
):
    masters = (query_weight, keyval_weight, output_weight, gateup_weight, down_weight, norm_gains)
    low_query, low_keyval, low_output, low_gateup, low_down, low_gains = tuple(
        (master.astype(jnp.bfloat16) for master in masters)
    )
    wq_local, wkv_local, wo_local, wgu_local, wdn_local, gain_low = (
        lax.all_gather(low_query, "dp", axis=0, tiled=True),
        lax.all_gather(low_keyval, "dp", axis=1, tiled=True),
        lax.all_gather(low_output, "dp", axis=1, tiled=True),
        lax.all_gather(low_gateup, "dp", axis=1, tiled=True),
        lax.all_gather(low_down, "dp", axis=1, tiled=True),
        lax.all_gather(low_gains, "dp", axis=1, tiled=True),
    )
    gain_all = gain_low.astype(jnp.float32)
    length = tokens.shape[0]
    group = HEADS // KV_HEADS
    kv_local = wkv_local.shape[2] // HEAD_DIM
    heads_local = kv_local * group
    qscale = HEAD_DIM ** (-0.5)
    allowed, cosine, sine = layout(segments)
    valid = (segments >= 0).astype(jnp.float32)[:, None]
    inputs = tokens.astype(jnp.float32)
    normed = rms_norm(inputs, gain_all[0])
    normed_low = normed.astype(jnp.bfloat16)
    qraw = jnp.dot(normed_low, wq_local, preferred_element_type=jnp.float32).reshape(
        length, heads_local, HEAD_DIM
    )
    queries = (
        (rotate(qraw, cosine, sine) * qscale)
        .astype(jnp.bfloat16)
        .reshape(length, kv_local, group, HEAD_DIM)
    )
    kraw = jnp.dot(normed_low, wkv_local[0], preferred_element_type=jnp.float32).reshape(
        length, kv_local, HEAD_DIM
    )
    key_rows = rotate(kraw, cosine, sine).astype(jnp.bfloat16)
    value_rows = (
        jnp.dot(normed_low, wkv_local[1], preferred_element_type=jnp.float32)
        .astype(jnp.bfloat16)
        .reshape(length, kv_local, HEAD_DIM)
    )
    squashed, capped = scores(queries, key_rows, allowed)
    row_top = jnp.max(capped, axis=-1, keepdims=True)
    log_total = row_top + jnp.log(jnp.sum(jnp.exp(capped - row_top), axis=-1, keepdims=True))
    probs_low = jnp.exp(capped - log_total).astype(jnp.bfloat16)
    mixed_low = jnp.einsum(
        "kgqs,skd->qkgd", probs_low, value_rows, preferred_element_type=jnp.float32
    ).astype(jnp.bfloat16)
    mixed_low = mixed_low.reshape(length, heads_local * HEAD_DIM)
    attn_part = jnp.dot(mixed_low, wo_local, preferred_element_type=jnp.float32)
    attn_sum = lax.psum(attn_part, "mp")
    residual = inputs + rms_norm(attn_sum, gain_all[1])
    hidden_in = rms_norm(residual, gain_all[2]).astype(jnp.bfloat16)
    gate_out = jnp.dot(hidden_in, wgu_local[0], preferred_element_type=jnp.float32)
    up_out = jnp.dot(hidden_in, wgu_local[1], preferred_element_type=jnp.float32)
    act_low = (jax.nn.gelu(gate_out, approximate=True) * up_out).astype(jnp.bfloat16)
    ffn_part = jnp.dot(act_low, wdn_local, preferred_element_type=jnp.float32)
    ffn_sum = lax.psum(ffn_part, "mp")
    block_out = (residual + rms_norm(ffn_sum, gain_all[3])).astype(jnp.bfloat16)
    grad_out = cotangent.astype(jnp.float32) * valid
    grad_ffn, grad_gain3 = norm_back(ffn_sum, gain_all[3], grad_out)
    grad_ffn_low = grad_ffn.astype(jnp.bfloat16)
    grad_wdn = jnp.einsum("tf,td->fd", act_low, grad_ffn_low, preferred_element_type=jnp.float32)
    grad_act = jnp.einsum("td,fd->tf", grad_ffn_low, wdn_local, preferred_element_type=jnp.float32)
    unused, pull_act = jax.vjp(
        lambda gate_in, up_in: jax.nn.gelu(gate_in, approximate=True) * up_in, gate_out, up_out
    )
    grad_gate, grad_up = pull_act(grad_act)
    grad_gate = grad_gate.astype(jnp.bfloat16)
    grad_up = grad_up.astype(jnp.bfloat16)
    grad_wgu = jnp.stack(
        [
            jnp.einsum("td,tf->df", hidden_in, grad_gate, preferred_element_type=jnp.float32),
            jnp.einsum("td,tf->df", hidden_in, grad_up, preferred_element_type=jnp.float32),
        ]
    )
    hidden_part = jnp.einsum(
        "tf,df->td", grad_gate, wgu_local[0], preferred_element_type=jnp.float32
    )
    hidden_part = hidden_part + jnp.einsum(
        "tf,df->td", grad_up, wgu_local[1], preferred_element_type=jnp.float32
    )
    grad_hidden = lax.psum(hidden_part, "mp")
    grad_resid_n, grad_gain2 = norm_back(residual, gain_all[2], grad_hidden)
    grad_resid = grad_out + grad_resid_n
    grad_attn, grad_gain1 = norm_back(attn_sum, gain_all[1], grad_resid)
    grad_attn_low = grad_attn.astype(jnp.bfloat16)
    grad_wo = jnp.einsum("te,td->ed", mixed_low, grad_attn_low, preferred_element_type=jnp.float32)
    grad_mixed = jnp.einsum(
        "td,ed->te", grad_attn_low, wo_local, preferred_element_type=jnp.float32
    )
    grad_mixed = grad_mixed.astype(jnp.bfloat16).reshape(length, kv_local, group, HEAD_DIM)
    squashed, capped = scores(queries, key_rows, allowed)
    probs = jnp.exp(capped - log_total)
    probs_low = probs.astype(jnp.bfloat16)
    grad_probs = jnp.einsum(
        "qkgd,skd->kgqs", grad_mixed, value_rows, preferred_element_type=jnp.float32
    )
    grad_value = jnp.einsum(
        "kgqs,qkgd->skd", probs_low, grad_mixed, preferred_element_type=jnp.float32
    )
    grad_value = grad_value.astype(jnp.bfloat16).reshape(length, kv_local * HEAD_DIM)
    grad_capped = probs * (grad_probs - jnp.sum(probs * grad_probs, axis=-1, keepdims=True))
    grad_scores = (grad_capped * (1.0 - squashed * squashed)).astype(jnp.bfloat16)
    grad_query = jnp.einsum(
        "kgqs,skd->qkgd", grad_scores, key_rows, preferred_element_type=jnp.float32
    )
    grad_query = grad_query.reshape(length, heads_local, HEAD_DIM) * qscale
    grad_qraw = (
        rotate_back(grad_query, cosine, sine, qraw)
        .astype(jnp.bfloat16)
        .reshape(length, heads_local * HEAD_DIM)
    )
    grad_key = jnp.einsum(
        "kgqs,qkgd->skd", grad_scores, queries, preferred_element_type=jnp.float32
    )
    grad_kraw = (
        rotate_back(grad_key, cosine, sine, kraw)
        .astype(jnp.bfloat16)
        .reshape(length, kv_local * HEAD_DIM)
    )
    grad_wq = jnp.einsum("td,te->de", normed_low, grad_qraw, preferred_element_type=jnp.float32)
    grad_wkv = jnp.stack(
        [
            jnp.einsum("td,te->de", normed_low, grad_kraw, preferred_element_type=jnp.float32),
            jnp.einsum("td,te->de", normed_low, grad_value, preferred_element_type=jnp.float32),
        ]
    )
    normed_part = jnp.einsum("te,de->td", grad_qraw, wq_local, preferred_element_type=jnp.float32)
    normed_part = normed_part + jnp.einsum(
        "te,de->td", grad_kraw, wkv_local[0], preferred_element_type=jnp.float32
    )
    normed_part = normed_part + jnp.einsum(
        "te,de->td", grad_value, wkv_local[1], preferred_element_type=jnp.float32
    )
    grad_normed = lax.psum(normed_part.astype(jnp.bfloat16), "mp").astype(jnp.float32)
    grad_inputs_n, grad_gain0 = norm_back(inputs, gain_all[0], grad_normed)
    input_grad = grad_resid + grad_inputs_n
    grad_gains = jnp.stack([grad_gain0, grad_gain1, grad_gain2, grad_gain3])
    sum_wq, sum_wkv, sum_wo, sum_wgu, sum_wdn, sum_gains = (
        lax.psum_scatter(grad_wq, "dp", scatter_dimension=0, tiled=True),
        lax.psum_scatter(grad_wkv, "dp", scatter_dimension=1, tiled=True),
        lax.psum_scatter(grad_wo, "dp", scatter_dimension=1, tiled=True),
        lax.psum_scatter(grad_wgu, "dp", scatter_dimension=1, tiled=True),
        lax.psum_scatter(grad_wdn, "dp", scatter_dimension=1, tiled=True),
        lax.psum_scatter(grad_gains, "dp", scatter_dimension=1, tiled=True),
    )
    totals = (sum_wq, sum_wkv, sum_wo, sum_wgu, sum_wdn, sum_gains)
    moments = (moment_query, moment_keyval, moment_output, moment_gateup, moment_down, moment_gains)
    squares = (square_query, square_keyval, square_output, square_gateup, square_down, square_gains)
    steps_done = float(ADAM_STEP)
    updates = [
        adam_step(master, total, moment, square, steps_done)
        for master, total, moment, square in zip(masters, totals, moments, squares)
    ]
    return (
        block_out,
        input_grad,
        totals[0],
        totals[1],
        totals[2],
        totals[3],
        totals[4],
        totals[5],
        updates[0][0],
        updates[1][0],
        updates[2][0],
        updates[3][0],
        updates[4][0],
        updates[5][0],
        updates[0][1],
        updates[1][1],
        updates[2][1],
        updates[3][1],
        updates[4][1],
        updates[5][1],
        updates[0][2],
        updates[1][2],
        updates[2][2],
        updates[3][2],
        updates[4][2],
        updates[5][2],
    )


def solution(mesh):
    return jax.shard_map(
        shards,
        mesh=mesh,
        in_specs=(
            P("dp", None),
            P("dp"),
            P("dp", None),
            P("dp", "mp"),
            P(None, "dp", "mp"),
            P("mp", "dp"),
            P(None, "dp", "mp"),
            P("mp", "dp"),
            P(None, "dp"),
            P("dp", "mp"),
            P(None, "dp", "mp"),
            P("mp", "dp"),
            P(None, "dp", "mp"),
            P("mp", "dp"),
            P(None, "dp"),
            P("dp", "mp"),
            P(None, "dp", "mp"),
            P("mp", "dp"),
            P(None, "dp", "mp"),
            P("mp", "dp"),
            P(None, "dp"),
        ),
        out_specs=(
            P("dp", None),
            P("dp", None),
            P("dp", "mp"),
            P(None, "dp", "mp"),
            P("mp", "dp"),
            P(None, "dp", "mp"),
            P("mp", "dp"),
            P(None, "dp"),
            P("dp", "mp"),
            P(None, "dp", "mp"),
            P("mp", "dp"),
            P(None, "dp", "mp"),
            P("mp", "dp"),
            P(None, "dp"),
            P("dp", "mp"),
            P(None, "dp", "mp"),
            P("mp", "dp"),
            P(None, "dp", "mp"),
            P("mp", "dp"),
            P(None, "dp"),
            P("dp", "mp"),
            P(None, "dp", "mp"),
            P("mp", "dp"),
            P(None, "dp", "mp"),
            P("mp", "dp"),
            P(None, "dp"),
        ),
        check_vma=False,
    )
```

profile of v0, /device:TPU:0, one launch (start us, length us, event | category | flops | bytes accessed | tf_op | source)
XLA Modules:
  0.0 2841.1 jit_solution(11559682314894944507)
XLA Ops:
  19.7 32.3 %all-gather = bf16[8,288,4]{1,2,0:T(4,128)(2,1)S(1)} all-gather(bf16[1,288,4]{1,2,0:T(4,128)(2,1)S(1)} %convert_bitcast_fusion), channel_id=1, replica_groups=mesh['dp'=8,'mp'=4] {'dp'}, dimensions={0}, use_global_device_ids=true | all-gather | bytes 20736 | tf_op jit(solution)/shard_map/all_gather | solution.py:113
  54.4 5.5 fusion.6
  59.9 5.8 all-gather.9.cloned.1.call-done
  65.7 5.6 fusion.98
  73.0 46.2 %all-gather.7.cloned.1.call-done = bf16[2,2304,256]{2,1,0:T(8,128)(2,1)} async-done(((bf16[2,288,256]{2,1,0:T(8,128)(2,1)}), bf16[2,2304,256]{2,1,0:T(8,128)(2,1)}) %all-gather.7.cloned.1.call-update) | async-done | bytes 2359312 | tf_op jit(solution)/shard_map/all_gather | solution.py:109
  119.2 4.0 convolution_bitcast_fusion.5
  138.7 33.9 %all-gather.11.cloned.1.call-done = bf16[512,2304]{0,1:T(8,128)(2,1)} async-done(((bf16[512,288]{0,1:T(8,128)(2,1)}), bf16[512,2304]{0,1:T(8,128)(2,1)}) %all-gather.11.cloned.1.call-update) | async-done | bytes 2359312 | tf_op jit(solution)/shard_map/all_gather | solution.py:110
  172.6 7.4 fusion.99
  180.1 4.5 convert_element_type.134
  186.3 143.1 %all-reduce.9.cloned.1.call-done = f32[896,2304]{1,0:T(8,128)} async-done(((f32[896,2304]{1,0:T(8,128)}), f32[896,2304]{1,0:T(8,128)}) %all-reduce.9.cloned.1.call-update) | async-done | bytes 8257552 | tf_op jit(solution)/shard_map/psum | solution.py:152
  329.4 4.1 multiply_reduce_fusion.8
  334.1 5.1 multiply_reduce_fusion.7
  339.3 3.2 copy-done
  345.2 393.1 %all-gather.13.cloned.1.call-done = bf16[2,2304,2304]{2,1,0:T(8,128)(2,1)} async-done(((bf16[2,288,2304]{2,1,0:T(8,128)(2,1)}), bf16[2,2304,2304]{2,1,0:T(8,128)(2,1)}) %all-gather.13.cloned.1.call-update) | async-done | bytes 21233680 | tf_op jit(solution)/shard_map/all_gather | solution.py:111
  738.4 15.9 fusion.3
  754.2 18.8 multiply_convert_fusion.1
  773.0 120.7 %all-gather.15.cloned.1.call-done = bf16[2304,2304]{0,1:T(8,128)(2,1)} async-done(((bf16[2304,288]{0,1:T(8,128)(2,1)}), bf16[2304,2304]{0,1:T(8,128)(2,1)}) %all-gather.15.cloned.1.call-update) | async-done | bytes 10616848 | tf_op jit(solution)/shard_map/all_gather | solution.py:112
  893.7 15.1 fusion.100
  909.4 148.4 %all-reduce.11.cloned.1.call-done = f32[896,2304]{1,0:T(8,128)} async-done(((f32[896,2304]{1,0:T(8,128)}), f32[896,2304]{1,0:T(8,128)}) %all-reduce.11.cloned.1.call-update) | async-done | bytes 8257552 | tf_op jit(solution)/shard_map/psum | solution.py:159
  1057.9 4.1 multiply_reduce_fusion.6
  1062.0 7.2 multiply_reduce_fusion
  1070.9 5.9 fusion.15
  1076.8 24.2 multiply_convert_fusion
  1101.0 15.2 fusion.2
  1116.3 18.3 fusion.25
  1134.6 151.0 %all-reduce.13.cloned.1.call-done = f32[896,2304]{1,0:T(8,128)} async-done(((f32[896,2304]{1,0:T(8,128)}), f32[896,2304]{1,0:T(8,128)}) %all-reduce.13.cloned.1.call-update) | async-done | bytes 8257552 | tf_op jit(solution)/shard_map/psum | solution.py:184
  1285.6 6.9 multiply_reduce_fusion.1
  1292.6 11.7 multiply_reduce_fusion.2
  1326.5 4.2 fusion.101
  1332.1 3.4 add_convert_fusion
  1335.6 84.6 %all-reduce.15.cloned.1.call-done = bf16[896,2304]{1,0:T(8,128)(2,1)} async-done(((bf16[896,2304]{1,0:T(8,128)(2,1)}), bf16[896,2304]{1,0:T(8,128)(2,1)}) %all-reduce.15.cloned.1.call-update) | async-done | bytes 4128784 | tf_op jit(solution)/shard_map/psum | solution.py:237
  1420.2 5.8 fusion.7
  1427.6 7.3 fusion.103
  1434.9 6.5 fusion.102
  1441.5 3.8 convolution_bitcast_fusion.3
  1449.3 18.2 fusion.104
  1467.7 14.6 convolution_bitcast_fusion
  1482.3 16.9 convolution_bitcast_fusion.1
  1499.2 23.1 pad_maximum_fusion
  1523.0 10.1 fusion.18
  1535.0 55.9 %reduce-scatter.13.cloned.1.call-done = f32[512,288]{0,1:T(8,128)} async-done(((f32[512,2304]{0,1:T(8,128)}), f32[512,288]{0,1:T(8,128)}) %reduce-scatter.13.cloned.1.call-update) | async-done | bytes 589840 | tf_op jit(solution)/shard_map/reduce_scatter | solution.py:244
  1593.8 96.8 %reduce-scatter.9.cloned.1.call-done = f32[288,512]{1,0:T(8,128)} async-done(((f32[2304,512]{1,0:T(8,128)}), f32[288,512]{1,0:T(8,128)}) %reduce-scatter.9.cloned.1.call-update) | async-done | bytes 589840 | tf_op jit(solution)/shard_map/reduce_scatter | solution.py:242
  1690.6 3.1 add_multiply_fusion.4
  1693.7 96.9 %reduce-scatter.11.cloned.1.call-done = f32[2,288,256]{2,1,0:T(8,128)} async-done(((f32[2,2304,256]{2,1,0:T(8,128)}), f32[2,288,256]{2,1,0:T(8,128)}) %reduce-scatter.11.cloned.1.call-update) | async-done | bytes 589840 | tf_op jit(solution)/shard_map/reduce_scatter | solution.py:243
  1793.6 348.4 %reduce-scatter.17.cloned.1.call-done = f32[2304,288]{0,1:T(8,128)} async-done(((f32[2304,2304]{0,1:T(8,128)}), f32[2304,288]{0,1:T(8,128)}) %reduce-scatter.17.cloned.1.call-update) | async-done | bytes 2654224 | tf_op jit(solution)/shard_map/reduce_scatter | solution.py:246
  2142.0 7.7 add_multiply_fusion.1
  2149.8 670.2 %reduce-scatter.15.cloned.1.call-done = f32[2,288,2304]{2,1,0:T(8,128)} async-done(((f32[2,2304,2304]{2,1,0:T(8,128)}), f32[2,288,2304]{2,1,0:T(8,128)}) %reduce-scatter.15.cloned.1.call-update) | async-done | bytes 5308432 | tf_op jit(solution)/shard_map/reduce_scatter | solution.py:245
  2820.0 14.4 add_multiply_fusion
  (241 shorter events, 77.0 us)
Async XLA Ops:
  7.2 58.5 %all-gather.9.cloned.1.call-start = ((), (), s32[]{:S(2)}) async-start(), calls=%async_computation.7 | async-start | bytes 2654208 | tf_op jit(solution)/shard_map/all_gather | solution.py:108
  9.1 110.1 %all-gather.7.cloned.1.call-start = ((), (), s32[]{:S(2)}) async-start(), calls=%async_computation.6 | async-start | bytes 2654208 | tf_op jit(solution)/shard_map/all_gather | solution.py:109
  11.0 161.6 %all-gather.11.cloned.1.call-start = ((), (), s32[]{:S(2)}) async-start(), calls=%async_computation.8 | async-start | bytes 2654208 | tf_op jit(solution)/shard_map/all_gather | solution.py:110
  12.9 316.6 %all-reduce.9.cloned.1.call-start = ((), (), s32[]{:S(2)}) async-start(), calls=%async_computation.9 | async-start | bytes 16515072 | tf_op jit(solution)/shard_map/psum | solution.py:152
  12.9 47.0 %copy-start.61 = (f32[128]{0:T(128)}, f32[128]{0:T(128)S(1)}, u32[]{:S(2)}) copy-start(f32[128]{0:T(128)S(1)} %multiply_power_fusion) | copy-start | bytes 1540
  15.3 120.2 %copy-start.8 = (pred[896,896]{0,1:T(8,128)(4,1)}, pred[896,896]{0,1:T(8,128)(4,1)S(1)}, u32[]{:S(2)}) copy-start(pred[896,896]{0,1:T(8,128)(4,1)S(1)} %fusion.34) | copy-start | bytes 2408452
  19.1 52.2 %copy-start.38 = (f32[896]{0:T(1024)}, f32[896]{0:T(1024)S(1)}, u32[]{:S(2)}) copy-start(f32[896]{0:T(1024)S(1)} %fusion.76) | copy-start | bytes 10756
  19.7 51.6 %copy-start.40 = (f32[896]{0:T(1024)}, f32[896]{0:T(1024)S(1)}, u32[]{:S(2)}) copy-start(f32[896]{0:T(1024)S(1)} %convert_element_type.125) | copy-start | bytes 10756
  54.4 70.9 %copy-start.10 = (f32[896,128]{1,0:T(8,128)}, f32[896,128]{1,0:T(8,128)S(1)}, u32[]{:S(2)}) copy-start(f32[896,128]{1,0:T(8,128)S(1)} %get-tuple-element.73) | copy-start | bytes 1376260
  54.4 70.9 %copy-start.12 = (f32[896,128]{1,0:T(8,128)}, f32[896,128]{1,0:T(8,128)S(1)}, u32[]{:S(2)}) copy-start(f32[896,128]{1,0:T(8,128)S(1)} %get-tuple-element.74) | copy-start | bytes 1376260
  73.0 52.4 %copy-start.19 = (f32[896,2,128]{2,0,1:T(8,128)S(1)}, f32[896,2,128]{2,0,1:T(8,128)}, u32[]{:S(2)}) copy-start(f32[896,2,128]{2,0,1:T(8,128)} %copy.111) | copy-start | bytes 2752516
  138.7 41.3 %copy-start.65 = (bf16[256,2,896]{2,0,1:T(8,128)(2,1)}, bf16[256,2,896]{2,0,1:T(8,128)(2,1)S(1)}, u32[]{:S(2)}) copy-start(bf16[256,2,896]{2,0,1:T(8,128)(2,1)S(1)} %convolution_convert_fusion) | copy-start | bytes 2752516
  180.0 558.3 %all-gather.13.cloned.1.call-start = ((), (), s32[]{:S(2)}) async-start(), calls=%async_computation.10 | async-start | bytes 23887872 | tf_op jit(solution)/shard_map/all_gather | solution.py:111
  184.6 149.5 %copy-start.31 = (f32[2304]{0:T(1024)S(1)}, f32[2304]{0:T(1024)}, u32[]{:S(2)}) copy-start(f32[2304]{0:T(1024)} %get-tuple-element.36) | copy-start | bytes 27652
  184.6 709.0 %all-gather.15.cloned.1.call-start = ((), (), s32[]{:S(2)}) async-start(), calls=%async_computation.11 | async-start | bytes 11943936 | tf_op jit(solution)/shard_map/all_gather | solution.py:112
  185.9 872.0 %all-reduce.11.cloned.1.call-start = ((), (), s32[]{:S(2)}) async-start(), calls=%async_computation.12 | async-start | bytes 16515072 | tf_op jit(solution)/shard_map/psum | solution.py:159
  339.3 414.9 %copy-start.53 = (f32[896]{0:T(1024)}, f32[896]{0:T(1024)S(1)}, u32[]{:S(2)}) copy-start(f32[896]{0:T(1024)S(1)} %get-tuple-element.57) | copy-start | bytes 10756
  738.4 15.9 copy-start.14
  908.7 153.2 %copy-start.37 = (f32[2304]{0:T(1024)S(1)}, f32[2304]{0:T(1024)}, u32[]{:S(2)}) copy-start(f32[2304]{0:T(1024)} %get-tuple-element.34) | copy-start | bytes 27652
  908.8 376.8 %all-reduce.13.cloned.1.call-start = ((), (), s32[]{:S(2)}) async-start(), calls=%async_computation.13 | async-start | bytes 16515072 | tf_op jit(solution)/shard_map/psum | solution.py:184
  1057.9 11.3 slice-start
  1057.9 11.3 copy-start.4
  1062.0 9.0 slice-start.1
  1101.0 15.3 copy-start.68
  1134.5 151.1 %copy-start.34 = (f32[2304]{0:T(1024)S(1)}, f32[2304]{0:T(1024)}, u32[]{:S(2)}) copy-start(f32[2304]{0:T(1024)} %get-tuple-element.35) | copy-start | bytes 27652
  1134.5 151.1 %copy-start.46 = (f32[896]{0:T(1024)S(1)}, f32[896]{0:T(1024)}, u32[]{:S(2)}) copy-start(f32[896]{0:T(1024)} %copy-done.45) | copy-start | bytes 10756
  1134.5 157.9 %copy-start.54 = (f32[896]{0:T(1024)S(1)}, f32[896]{0:T(1024)}, u32[]{:S(2)}) copy-start(f32[896]{0:T(1024)} %copy-done.53) | copy-start | bytes 10756
  1134.6 158.0 %copy-start.32 = (f32[2304]{0:T(1024)S(1)}, f32[2304]{0:T(1024)}, u32[]{:S(2)}) copy-start(f32[2304]{0:T(1024)} %get-tuple-element.36) | copy-start | bytes 27652
  1134.6 158.0 %copy-start.44 = (f32[896]{0:T(1024)S(1)}, f32[896]{0:T(1024)}, u32[]{:S(2)}) copy-start(f32[896]{0:T(1024)} %copy-done.43) | copy-start | bytes 10756
  1134.6 285.6 %all-reduce.15.cloned.1.call-start = ((), (), s32[]{:S(2)}) async-start(), calls=%async_computation.14 | async-start | bytes 8257536 | tf_op jit(solution)/shard_map/psum | solution.py:237
  1285.6 18.8 slice-start.2
  1292.5 11.8 copy-start.49
  1292.5 11.8 slice-start.3
  1332.0 88.2 %copy-start.36 = (f32[2304]{0:T(1024)S(1)}, f32[2304]{0:T(1024)}, u32[]{:S(2)}) copy-start(f32[2304]{0:T(1024)} %copy-done.35) | copy-start | bytes 27652
  1332.0 88.2 %copy-start.39 = (f32[896]{0:T(1024)S(1)}, f32[896]{0:T(1024)}, u32[]{:S(2)}) copy-start(f32[896]{0:T(1024)} %copy-done.38) | copy-start | bytes 10756
  1335.5 197.6 %reduce-scatter.19.cloned.1.call-start = ((), (), s32[]{:S(2)}) async-start(), calls=%async_computation.20 | async-start | bytes 1327104
  1427.5 163.4 %reduce-scatter.13.cloned.1.call-start = ((), (), s32[]{:S(2)}) async-start(), calls=%async_computation.17 | async-start | bytes 5308416 | tf_op jit(solution)/shard_map/reduce_scatter | solution.py:244
  1434.9 255.7 %reduce-scatter.9.cloned.1.call-start = ((), (), s32[]{:S(2)}) async-start(), calls=%async_computation.15 | async-start | bytes 5308416 | tf_op jit(solution)/shard_map/reduce_scatter | solution.py:242
  1441.4 349.1 %reduce-scatter.11.cloned.1.call-start = ((), (), s32[]{:S(2)}) async-start(), calls=%async_computation.16 | async-start | bytes 5308416 | tf_op jit(solution)/shard_map/reduce_scatter | solution.py:243
  1449.3 692.8 %reduce-scatter.17.cloned.1.call-start = ((), (), s32[]{:S(2)}) async-start(), calls=%async_computation.19 | async-start | bytes 23887872 | tf_op jit(solution)/shard_map/reduce_scatter | solution.py:246
  1467.6 1352.4 %reduce-scatter.15.cloned.1.call-start = ((), (), s32[]{:S(2)}) async-start(), calls=%async_computation.18 | async-start | bytes 47775744 | tf_op jit(solution)/shard_map/reduce_scatter | solution.py:245
  1467.7 14.6 copy-start.15
  1523.0 11.3 copy-start.58
  1523.0 11.3 copy-start.59
  1523.0 11.3 copy-start.60
  1523.0 67.9 %copy-start.20 = (f32[512,288]{0,1:T(8,128)S(1)}, f32[512,288]{0,1:T(8,128)}, u32[]{:S(2)}) copy-start(f32[512,288]{0,1:T(8,128)} %param.26) | copy-start | bytes 1769476
  1533.1 609.0 %copy-start.7 = (f32[2304,288]{0,1:T(8,128)S(1)}, f32[2304,288]{0,1:T(8,128)}, u32[]{:S(2)}) copy-start(f32[2304,288]{0,1:T(8,128)} %param.28) | copy-start | bytes 7962628
  1534.3 615.4 %copy-start.57 = (f32[4,288]{1,0:T(4,128)}, f32[4,288]{1,0:T(4,128)S(1)}, u32[]{:S(2)}) copy-start(f32[4,288]{1,0:T(4,128)S(1)} %copy.109) | copy-start | bytes 13828
  (42 other events, 135.6 us)
Sparse Core Ops, SparseCore 0:
  10.8 54.8 all-gather.8
  68.5 50.6 all-gather.6
  121.9 50.5 all-gather.10
  180.1 149.2 all-reduce.8
  331.5 406.8 all-gather.12
  741.2 152.4 all-gather.14
  908.9 148.9 all-reduce.10
  1134.7 150.8 all-reduce.12
  1335.6 84.5 all-reduce.14
  1427.6 64.1 reduce-scatter.18
  1496.6 94.2 reduce-scatter.12
  1595.5 94.9 reduce-scatter.8
  1695.4 95.1 reduce-scatter.10
  1794.9 347.1 reduce-scatter.16
  2146.8 673.1 reduce-scatter.14
where the time goes:
time: 2850 us; the launch traced here: 2840 us
  waiting for transfers between devices  2400 us (84%)
  matrix products  218 us (8%)
  other arithmetic  158 us (6%)
  blocking collectives  32.3 us (1%)
    reduce_scatter x1, waiting for transfers between devices, shards(): lax.psum_scatter(grad_wgu, 'dp', scatter_dimension=1, tiled=True)  670 us
    all_gather x1, waiting for transfers between devices, shards(): lax.all_gather(low_gateup, 'dp', axis=1, tiled=True)  393 us
    reduce_scatter x1, waiting for transfers between devices, shards(): lax.psum_scatter(grad_wdn, 'dp', scatter_dimension=1, tiled=True)  348 us
    psum x1, waiting for transfers between devices, shards(): grad_hidden = lax.psum(hidden_part, 'mp')  151 us
    psum x1, waiting for transfers between devices, shards(): ffn_sum = lax.psum(ffn_part, 'mp')  148 us
    psum x1, waiting for transfers between devices, shards(): attn_sum = lax.psum(attn_part, 'mp')  143 us
    all_gather x1, waiting for transfers between devices, shards(): lax.all_gather(low_down, 'dp', axis=1, tiled=True)  121 us
    reduce_scatter x1, waiting for transfers between devices, shards(): lax.psum_scatter(grad_wkv, 'dp', scatter_dimension=1, tiled=True)  96.9 us
  transfers between devices with their start and end apart: 15, of which 14 were waited for; matrix products, arithmetic and copies ran while one was open for 8% of the time, Pallas kernels for 0%

commit v1 on v0

--- a/solution.py
+++ b/solution.py
@@ -75,6 +75,81 @@
     fix_two = 1.0 - beta_two**steps_done
     stride = new_moment / fix_one / (jnp.sqrt(new_square / fix_two) + adam_eps)
     return (-learn_rate * (stride + decay_rate * master), new_moment, new_square)
+
+
+def ring_pairs(extent):
+    outer = extent // 2
+    return [
+        (2 * place + side, 2 * ((place + 1) % outer) + side)
+        for place in range(outer)
+        for side in range(2)
+    ]
+
+
+def swap_pairs(extent, stride):
+    return [(place, place ^ stride) for place in range(extent)]
+
+
+def rows_at(tensor, index, count):
+    return lax.dynamic_slice_in_dim(tensor, index * count, count, 0)
+
+
+def gather_rows(own, extent):
+    if extent % 2:
+        return lax.all_gather(own, "dp", axis=0, tiled=True)
+    outer = extent // 2
+    index = lax.axis_index("dp")
+    place, side = index // 2, index % 2
+    count = own.shape[0]
+    ring, swap = ring_pairs(extent), swap_pairs(extent, 1)
+    full = jnp.zeros((extent * count,) + own.shape[1:], own.dtype)
+    held = own
+    for step in range(outer):
+        if step:
+            held = lax.ppermute(held, "dp", ring)
+        other = lax.ppermute(held, "dp", swap)
+        source = 2 * lax.rem(place - step + outer, outer)
+        full = lax.dynamic_update_slice_in_dim(full, held, (source + side) * count, 0)
+        full = lax.dynamic_update_slice_in_dim(full, other, (source + 1 - side) * count, 0)
+    return full
+
+
+def scatter_rows(partial, extent):
+    if extent % 2:
+        return lax.psum_scatter(
+            partial.astype(jnp.float32), "dp", scatter_dimension=0, tiled=True
+        )
+    outer = extent // 2
+    index = lax.axis_index("dp")
+    place, side = index // 2, index % 2
+    count = partial.shape[0] // extent
+    ring, swap = ring_pairs(extent), swap_pairs(extent, 1)
+    total = None
+    for hops in range(outer - 1, -1, -1):
+        target = 2 * lax.rem(place + hops, outer)
+        other = lax.ppermute(rows_at(partial, target + 1 - side, count), "dp", swap)
+        both = rows_at(partial, target + side, count).astype(jnp.float32) + other.astype(jnp.float32)
+        if total is not None:
+            both = both + lax.ppermute(total, "dp", ring).astype(jnp.float32)
+        total = both.astype(partial.dtype) if hops else both
+    return total
+
+
+def sum_heads(partial, extent):
+    if extent != 4:
+        return lax.psum(partial, "mp")
+    half = partial.shape[0] // 2
+    side = lax.rem(lax.axis_index("mp"), 2)
+    given = rows_at(partial, 1 - side, half).astype(jnp.bfloat16)
+    kept = rows_at(partial, side, half)
+    kept = kept + lax.ppermute(given, "mp", swap_pairs(4, 1)).astype(jnp.float32)
+    kept = kept.astype(jnp.bfloat16)
+    far = lax.ppermute(kept, "mp", swap_pairs(4, 2))
+    mine = (kept.astype(jnp.float32) + far.astype(jnp.float32)).astype(jnp.bfloat16)
+    theirs = lax.ppermute(mine, "mp", swap_pairs(4, 1))
+    first = jnp.where(side == 0, mine, theirs)
+    second = jnp.where(side == 0, theirs, mine)
+    return jnp.concatenate([first, second], axis=0).astype(jnp.float32)
 
 
 def shards(
@@ -101,21 +176,29 @@
     square_gains,
 ):
     masters = (query_weight, keyval_weight, output_weight, gateup_weight, down_weight, norm_gains)
-    low_query, low_keyval, low_output, low_gateup, low_down, low_gains = tuple(
-        (master.astype(jnp.bfloat16) for master in masters)
-    )
-    wq_local, wkv_local, wo_local, wgu_local, wdn_local, gain_low = (
-        lax.all_gather(low_query, "dp", axis=0, tiled=True),
-        lax.all_gather(low_keyval, "dp", axis=1, tiled=True),
-        lax.all_gather(low_output, "dp", axis=1, tiled=True),
-        lax.all_gather(low_gateup, "dp", axis=1, tiled=True),
-        lax.all_gather(low_down, "dp", axis=1, tiled=True),
-        lax.all_gather(low_gains, "dp", axis=1, tiled=True),
-    )
+    low = jnp.bfloat16
+    groups, parts = lax.axis_size("dp"), lax.axis_size("mp")
+    gain_low = gather_rows(norm_gains.astype(low).T, groups).T
+    mixer = jnp.concatenate(
+        [
+            query_weight.astype(low),
+            keyval_weight[0].astype(low),
+            keyval_weight[1].astype(low),
+            output_weight.astype(low).T,
+        ],
+        axis=1,
+    )
+    mixer = gather_rows(mixer, groups)
+    width_q, width_kv = query_weight.shape[1], keyval_weight.shape[2]
+    wqkv_local = mixer[:, : width_q + 2 * width_kv]
+    wo_turned = mixer[:, width_q + 2 * width_kv :]
+    wg_local = gather_rows(gateup_weight[0].astype(low), groups)
+    wu_local = gather_rows(gateup_weight[1].astype(low), groups)
+    wdn_turned = gather_rows(down_weight.astype(low).T, groups)
     gain_all = gain_low.astype(jnp.float32)
     length = tokens.shape[0]
     group = HEADS // KV_HEADS
-    kv_local = wkv_local.shape[2] // HEAD_DIM
+    kv_local = width_kv // HEAD_DIM
     heads_local = kv_local * group
     qscale = HEAD_DIM ** (-0.5)
     allowed, cosine, sine = layout(segments)
@@ -123,20 +206,17 @@
     inputs = tokens.astype(jnp.float32)
     normed = rms_norm(inputs, gain_all[0])
     normed_low = normed.astype(jnp.bfloat16)
-    qraw = jnp.dot(normed_low, wq_local, preferred_element_type=jnp.float32).reshape(
-        length, heads_local, HEAD_DIM
-    )
+    mixer_raw = jnp.dot(normed_low, wqkv_local, preferred_element_type=jnp.float32)
+    qraw = mixer_raw[:, :width_q].reshape(length, heads_local, HEAD_DIM)
     queries = (
         (rotate(qraw, cosine, sine) * qscale)
         .astype(jnp.bfloat16)
         .reshape(length, kv_local, group, HEAD_DIM)
     )
-    kraw = jnp.dot(normed_low, wkv_local[0], preferred_element_type=jnp.float32).reshape(
-        length, kv_local, HEAD_DIM
-    )
+    kraw = mixer_raw[:, width_q : width_q + width_kv].reshape(length, kv_local, HEAD_DIM)
     key_rows = rotate(kraw, cosine, sine).astype(jnp.bfloat16)
     value_rows = (
-        jnp.dot(normed_low, wkv_local[1], preferred_element_type=jnp.float32)
+        mixer_raw[:, width_q + width_kv :]
         .astype(jnp.bfloat16)
         .reshape(length, kv_local, HEAD_DIM)
     )
@@ -148,47 +228,43 @@
         "kgqs,skd->qkgd", probs_low, value_rows, preferred_element_type=jnp.float32
     ).astype(jnp.bfloat16)
     mixed_low = mixed_low.reshape(length, heads_local * HEAD_DIM)
-    attn_part = jnp.dot(mixed_low, wo_local, preferred_element_type=jnp.float32)
-    attn_sum = lax.psum(attn_part, "mp")
+    attn_part = jnp.einsum("te,de->td", mixed_low, wo_turned, preferred_element_type=jnp.float32)
+    attn_sum = sum_heads(attn_part, parts)
     residual = inputs + rms_norm(attn_sum, gain_all[1])
     hidden_in = rms_norm(residual, gain_all[2]).astype(jnp.bfloat16)
-    gate_out = jnp.dot(hidden_in, wgu_local[0], preferred_element_type=jnp.float32)
-    up_out = jnp.dot(hidden_in, wgu_local[1], preferred_element_type=jnp.float32)
+    gate_out = jnp.dot(hidden_in, wg_local, preferred_element_type=jnp.float32)
+    up_out = jnp.dot(hidden_in, wu_local, preferred_element_type=jnp.float32)
     act_low = (jax.nn.gelu(gate_out, approximate=True) * up_out).astype(jnp.bfloat16)
-    ffn_part = jnp.dot(act_low, wdn_local, preferred_element_type=jnp.float32)
-    ffn_sum = lax.psum(ffn_part, "mp")
+    ffn_part = jnp.einsum("tf,df->td", act_low, wdn_turned, preferred_element_type=jnp.float32)
+    ffn_sum = sum_heads(ffn_part, parts)
     block_out = (residual + rms_norm(ffn_sum, gain_all[3])).astype(jnp.bfloat16)
     grad_out = cotangent.astype(jnp.float32) * valid
     grad_ffn, grad_gain3 = norm_back(ffn_sum, gain_all[3], grad_out)
     grad_ffn_low = grad_ffn.astype(jnp.bfloat16)
-    grad_wdn = jnp.einsum("tf,td->fd", act_low, grad_ffn_low, preferred_element_type=jnp.float32)
-    grad_act = jnp.einsum("td,fd->tf", grad_ffn_low, wdn_local, preferred_element_type=jnp.float32)
+    grad_wdn = jnp.einsum("td,tf->df", grad_ffn_low, act_low, preferred_element_type=jnp.float32).astype(low)
+    grad_act = jnp.einsum("td,df->tf", grad_ffn_low, wdn_turned, preferred_element_type=jnp.float32)
     unused, pull_act = jax.vjp(
         lambda gate_in, up_in: jax.nn.gelu(gate_in, approximate=True) * up_in, gate_out, up_out
     )
     grad_gate, grad_up = pull_act(grad_act)
     grad_gate = grad_gate.astype(jnp.bfloat16)
     grad_up = grad_up.astype(jnp.bfloat16)
-    grad_wgu = jnp.stack(
-        [
-            jnp.einsum("td,tf->df", hidden_in, grad_gate, preferred_element_type=jnp.float32),
-            jnp.einsum("td,tf->df", hidden_in, grad_up, preferred_element_type=jnp.float32),
-        ]
-    )
+    grad_wg = jnp.einsum("td,tf->df", hidden_in, grad_gate, preferred_element_type=jnp.float32).astype(low)
+    grad_wu = jnp.einsum("td,tf->df", hidden_in, grad_up, preferred_element_type=jnp.float32).astype(low)
     hidden_part = jnp.einsum(
-        "tf,df->td", grad_gate, wgu_local[0], preferred_element_type=jnp.float32
+        "tf,df->td", grad_gate, wg_local, preferred_element_type=jnp.float32
     )
     hidden_part = hidden_part + jnp.einsum(
-        "tf,df->td", grad_up, wgu_local[1], preferred_element_type=jnp.float32
-    )
-    grad_hidden = lax.psum(hidden_part, "mp")
+        "tf,df->td", grad_up, wu_local, preferred_element_type=jnp.float32
+    )
+    grad_hidden = sum_heads(hidden_part, parts)
     grad_resid_n, grad_gain2 = norm_back(residual, gain_all[2], grad_hidden)
     grad_resid = grad_out + grad_resid_n
     grad_attn, grad_gain1 = norm_back(attn_sum, gain_all[1], grad_resid)
     grad_attn_low = grad_attn.astype(jnp.bfloat16)
-    grad_wo = jnp.einsum("te,td->ed", mixed_low, grad_attn_low, preferred_element_type=jnp.float32)
+    grad_wo = jnp.einsum("td,te->de", grad_attn_low, mixed_low, preferred_element_type=jnp.float32).astype(low)
     grad_mixed = jnp.einsum(
-        "td,ed->te", grad_attn_low, wo_local, preferred_element_type=jnp.float32
+        "td,de->te", grad_attn_low, wo_turned, preferred_element_type=jnp.float32
     )
     grad_mixed = grad_mixed.astype(jnp.bfloat16).reshape(length, kv_local, group, HEAD_DIM)
     squashed, capped = scores(queries, key_rows, allowed)
@@ -220,32 +296,22 @@
         .astype(jnp.bfloat16)
         .reshape(length, kv_local * HEAD_DIM)
     )
-    grad_wq = jnp.einsum("td,te->de", normed_low, grad_qraw, preferred_element_type=jnp.float32)
-    grad_wkv = jnp.stack(
-        [
-            jnp.einsum("td,te->de", normed_low, grad_kraw, preferred_element_type=jnp.float32),
-            jnp.einsum("td,te->de", normed_low, grad_value, preferred_element_type=jnp.float32),
-        ]
-    )
-    normed_part = jnp.einsum("te,de->td", grad_qraw, wq_local, preferred_element_type=jnp.float32)
-    normed_part = normed_part + jnp.einsum(
-        "te,de->td", grad_kraw, wkv_local[0], preferred_element_type=jnp.float32
-    )
-    normed_part = normed_part + jnp.einsum(
-        "te,de->td", grad_value, wkv_local[1], preferred_element_type=jnp.float32
-    )
-    grad_normed = lax.psum(normed_part.astype(jnp.bfloat16), "mp").astype(jnp.float32)
+    grad_mixer_raw = jnp.concatenate([grad_qraw, grad_kraw, grad_value], axis=1)
+    grad_wqkv = jnp.einsum("td,te->de", normed_low, grad_mixer_raw, preferred_element_type=jnp.float32).astype(low)
+    normed_part = jnp.einsum(
+        "te,de->td", grad_mixer_raw, wqkv_local, preferred_element_type=jnp.float32
+    )
+    grad_normed = sum_heads(normed_part, parts)
     grad_inputs_n, grad_gain0 = norm_back(inputs, gain_all[0], grad_normed)
     input_grad = grad_resid + grad_inputs_n
     grad_gains = jnp.stack([grad_gain0, grad_gain1, grad_gain2, grad_gain3])
-    sum_wq, sum_wkv, sum_wo, sum_wgu, sum_wdn, sum_gains = (
-        lax.psum_scatter(grad_wq, "dp", scatter_dimension=0, tiled=True),
-        lax.psum_scatter(grad_wkv, "dp", scatter_dimension=1, tiled=True),
-        lax.psum_scatter(grad_wo, "dp", scatter_dimension=1, tiled=True),
-        lax.psum_scatter(grad_wgu, "dp", scatter_dimension=1, tiled=True),
-        lax.psum_scatter(grad_wdn, "dp", scatter_dimension=1, tiled=True),
-        lax.psum_scatter(grad_gains, "dp", scatter_dimension=1, tiled=True),
-    )
+    sum_wdn = scatter_rows(grad_wdn, groups).T
+    sum_wgu = jnp.stack([scatter_rows(grad_wg, groups), scatter_rows(grad_wu, groups)])
+    sum_wo = scatter_rows(grad_wo, groups).T
+    sum_wqkv = scatter_rows(grad_wqkv, groups)
+    sum_wq = sum_wqkv[:, :width_q]
+    sum_wkv = jnp.stack([sum_wqkv[:, width_q : width_q + width_kv], sum_wqkv[:, width_q + width_kv :]])
+    sum_gains = scatter_rows(grad_gains.T, groups).T
     totals = (sum_wq, sum_wkv, sum_wo, sum_wgu, sum_wdn, sum_gains)
     moments = (moment_query, moment_keyval, moment_output, moment_gateup, moment_down, moment_gains)
     squares = (square_query, square_keyval, square_output, square_gateup, square_down, square_gains)

time: 2850 us -> 1230 us (0.43)
  waiting for transfers between devices: 2400 us -> 708 us
  starting transfers between devices: 1.21 us -> 85.9 us
  local copies, waits for them, and re-layouts: 21.1 us -> 89.8 us
  blocking collectives: 32.3 us -> 0 us
  matrix products: 218 us -> 189 us
    reduce_scatter x5 -> x0, waiting for transfers between devices: 1270 us -> none  [the longest x1 670 us: shards(): lax.psum_scatter(grad_wgu, 'dp', scatter_dimension=1, tiled=True)]
    ppermute x0 -> x89, waiting for transfers between devices: none -> 708 us  [the longest x18 171 us: scatter_rows(): both = both + lax.ppermute(total, 'dp', ring).astype(jnp.float32)]
    all_gather x5 -> x0, waiting for transfers between devices: 600 us -> none  [the longest x1 393 us: shards(): lax.all_gather(low_gateup, 'dp', axis=1, tiled=True)]
    psum x4 -> x0, waiting for transfers between devices: 527 us -> none  [the longest x1 151 us: shards(): grad_hidden = lax.psum(hidden_part, 'mp')]
    ppermute x0 -> x89, starting transfers between devices: none -> 85.9 us  [the longest x24 25.8 us: scatter_rows(): other = lax.ppermute(rows_at(partial, target + 1 - side, count), 'dp', swap)]
    dynamic_update_slice x0 -> x38, local copies, waits for them, and re-layouts: none -> 34.4 us  [the longest x18 17.2 us: gather_rows(): lax.dynamic_update_slice_in_dim(full, held, (source + side) * count, 0)]
    all_gather x1 -> x0, blocking collectives: 32.3 us -> none  [shards(): lax.all_gather(low_gains, 'dp', axis=1, tiled=True)]
    dot_general x19 -> x13, matrix products: 174 us -> 147 us  [the longest x1 25.5 us: shards(): jnp.einsum('td,df->tf', grad_ffn_low, wdn_turned, preferred_element_type=...]
  transfers between devices with their start and end apart: 15 -> 89, of which waited for: 14 -> 40; matrix products, arithmetic and copies ran while one was open for 8% -> 19% of each run, Pallas kernels for 0% -> 0%
where the time goes in v1:
time: 1230 us; the launch traced here: 1220 us
  waiting for transfers between devices  708 us (58%)
  matrix products  189 us (15%)
  other arithmetic  142 us (12%)
  local copies, waits for them, and re-layouts  89.8 us (7%)
  starting transfers between devices  85.9 us (7%)
    ppermute x18, waiting for transfers between devices, scatter_rows(): both = both + lax.ppermute(total, 'dp', ring).astype(jnp.float32)  171 us
    ppermute x20, waiting for transfers between devices, gather_rows(): other = lax.ppermute(held, 'dp', swap)  157 us
    ppermute x15, waiting for transfers between devices, gather_rows(): held = lax.ppermute(held, 'dp', ring)  155 us
    ppermute x24, waiting for transfers between devices, scatter_rows(): other = lax.ppermute(rows_at(partial, target + 1 - side, count), 'dp', swap)  150 us
    ppermute x4, waiting for transfers between devices, sum_heads(): far = lax.ppermute(kept, 'mp', swap_pairs(4, 2))  67.8 us
    mul x6, other arithmetic, adam_step(): -learn_rate * (stride + decay_rate * master)  26.6 us
    convert_element_type x15, other arithmetic, scatter_rows(): total = both.astype(partial.dtype) if hops else both  25.8 us
    ppermute x24, starting transfers between devices, scatter_rows(): other = lax.ppermute(rows_at(partial, target + 1 - side, count), 'dp', swap)  25.8 us
  transfers between devices with their start and end apart: 89, of which 40 were waited for; matrix products, arithmetic and copies ran while one was open for 19% of the time, Pallas kernels for 0%

profile of v1, /device:TPU:0, one launch (start us, length us, event | category | flops | bytes accessed | tf_op | source)
XLA Modules:
  0.0 1218.1 jit_solution(8868364203838945953)
XLA Ops:
  18.0 5.0 broadcast.322.clone
  41.3 19.1 %collective-permute-done.2 = bf16[288,4]{0,1:T(4,128)(2,1)S(1)} collective-permute-done((bf16[288,4]{0,1:T(4,128)(2,1)S(1)}, bf16[288,4]{0,1:T(4,128)(2,1)S(1)}, u32[]{:S(2)}, u32[]{:S(2)}) %collective-permute-start.2) | collective-permute-done | bytes 2336 | tf_op jit(solution)/shard_map/ppermute | solution.py:110
  74.9 42.2 %collective-permute-done.10 = bf16[288,1536]{1,0:T(8,128)(2,1)S(1)} collective-permute-done((bf16[288,1536]{1,0:T(8,128)(2,1)}, bf16[288,1536]{1,0:T(8,128)(2,1)S(1)}, u32[]{:S(2)}, u32[]{:S(2)}) %collective-permute-start.10) | collective-permute-done | bytes 884768 | tf_op jit(solution)/shard_map/ppermute | solution.py:109
  126.6 37.8 %collective-permute-done.12 = bf16[288,1536]{1,0:T(8,128)(2,1)S(1)} collective-permute-done((bf16[288,1536]{1,0:T(8,128)(2,1)S(1)}, bf16[288,1536]{1,0:T(8,128)(2,1)S(1)}, u32[]{:S(2)}, u32[]{:S(2)}) %collective-permute-start.12) | collective-permute-done | bytes 884768 | tf_op jit(solution)/shard_map/ppermute | solution.py:109
  168.2 15.7 %collective-permute-done.13 = bf16[288,1536]{1,0:T(8,128)(2,1)S(1)} collective-permute-done((bf16[288,1536]{1,0:T(8,128)(2,1)S(1)}, bf16[288,1536]{1,0:T(8,128)(2,1)S(1)}, u32[]{:S(2)}, u32[]{:S(2)}) %collective-permute-start.13) | collective-permute-done | bytes 884768 | tf_op jit(solution)/shard_map/ppermute | solution.py:110
  225.6 20.8 %collective-permute-done.19 = bf16[288,2304]{1,0:T(8,128)(2,1)S(1)} collective-permute-done((bf16[288,2304]{1,0:T(8,128)(2,1)}, bf16[288,2304]{1,0:T(8,128)(2,1)S(1)}, u32[]{:S(2)}, u32[]{:S(2)}) %collective-permute-start.19) | collective-permute-done | bytes 1327136 | tf_op jit(solution)/shard_map/ppermute | solution.py:110
  246.4 9.1 collective-permute-start.29
  261.1 18.5 %collective-permute-done.34 = bf16[288,2304]{1,0:T(8,128)(2,1)S(1)} collective-permute-done((bf16[288,2304]{1,0:T(8,128)(2,1)}, bf16[288,2304]{1,0:T(8,128)(2,1)S(1)}, u32[]{:S(2)}, u32[]{:S(2)}) %collective-permute-start.34) | collective-permute-done | bytes 1327136 | tf_op jit(solution)/shard_map/ppermute | solution.py:109
  280.5 22.8 %collective-permute-done.28 = bf16[288,2304]{1,0:T(8,128)(2,1)S(1)} collective-permute-done((bf16[288,2304]{1,0:T(8,128)(2,1)}, bf16[288,2304]{1,0:T(8,128)(2,1)S(1)}, u32[]{:S(2)}, u32[]{:S(2)}) %collective-permute-start.28) | collective-permute-done | bytes 1327136 | tf_op jit(solution)/shard_map/ppermute | solution.py:110
  309.8 26.7 %collective-permute-done.22 = bf16[288,2304]{1,0:T(8,128)(2,1)S(1)} collective-permute-done((bf16[288,2304]{1,0:T(8,128)(2,1)S(1)}, bf16[288,2304]{1,0:T(8,128)(2,1)S(1)}, u32[]{:S(2)}, u32[]{:S(2)}) %collective-permute-start.22) | collective-permute-done | bytes 1327136 | tf_op jit(solution)/shard_map/ppermute | solution.py:109
  341.4 23.1 %collective-permute-done.36 = bf16[288,2304]{1,0:T(8,128)(2,1)S(1)} collective-permute-done((bf16[288,2304]{1,0:T(8,128)(2,1)S(1)}, bf16[288,2304]{1,0:T(8,128)(2,1)S(1)}, u32[]{:S(2)}, u32[]{:S(2)}) %collective-permute-start.36) | collective-permute-done | bytes 1327136 | tf_op jit(solution)/shard_map/ppermute | solution.py:109
  365.3 23.3 %collective-permute-done.30 = bf16[288,2304]{1,0:T(8,128)(2,1)S(1)} collective-permute-done((bf16[288,2304]{1,0:T(8,128)(2,1)S(1)}, bf16[288,2304]{1,0:T(8,128)(2,1)S(1)}, u32[]{:S(2)}, u32[]{:S(2)}) %collective-permute-start.30) | collective-permute-done | bytes 1327136 | tf_op jit(solution)/shard_map/ppermute | solution.py:110
  389.8 27.2 %collective-permute-done.23 = bf16[288,2304]{1,0:T(8,128)(2,1)S(1)} collective-permute-done((bf16[288,2304]{1,0:T(8,128)(2,1)S(1)}, bf16[288,2304]{1,0:T(8,128)(2,1)S(1)}, u32[]{:S(2)}, u32[]{:S(2)}) %collective-permute-start.23) | collective-permute-done | bytes 1327136 | tf_op jit(solution)/shard_map/ppermute | solution.py:110
  418.2 26.9 %collective-permute-done.37 = bf16[288,2304]{1,0:T(8,128)(2,1)S(1)} collective-permute-done((bf16[288,2304]{1,0:T(8,128)(2,1)S(1)}, bf16[288,2304]{1,0:T(8,128)(2,1)S(1)}, u32[]{:S(2)}, u32[]{:S(2)}) %collective-permute-start.37) | collective-permute-done | bytes 1327136 | tf_op jit(solution)/shard_map/ppermute | solution.py:110
  453.1 5.8 multiply_convert_fusion.2
  458.9 15.2 %fusion.142 = f32[896,2304]{1,0:T(8,128)} fusion(bf16[896,2304]{1,0:T(8,128)(2,1)S(1)} %multiply_convert_fusion.2, bf16[2304,2304]{1,0:T(8,128)(2,1)} %constant_dynamic-update-slice_fusion.16), kind=kOutput, calls=%fused_computation.335 | convolution fusion | flops 9512681472 | bytes 23003136 | tf_op jit(solution)/shard_map/dot_general | solution.py:235
  474.1 17.1 %multiply_convert_fusion.1 = (bf16[896,2304]{1,0:T(8,128)(2,1)}, f32[896,2304]{1,0:T(8,128)}) fusion(f32[896,2304]{1,0:T(8,128)} %fusion.142, bf16[896,2304]{1,0:T(8,128)(2,1)S(1)} %multiply_convert_fusion.2, bf16[2304,2304]{1,0:T(8,128)(2,1)} %constant_dynamic-update-slice_fusion.8), kind=kOutput, calls=%fused_computation.62 | convolution fusion | flops 9533325312 | bytes 35389440 | tf_op jit(solution)/shard_map/dot_general | solution.py:236
  491.2 11.8 fusion.143
  509.4 45.5 %collective-permute-done.39 = bf16[448,2304]{1,0:T(8,128)(2,1)S(1)} collective-permute-done((bf16[448,2304]{1,0:T(8,128)(2,1)S(1)}, bf16[448,2304]{1,0:T(8,128)(2,1)S(1)}, u32[]{:S(2)}, u32[]{:S(2)}) %collective-permute-start.39) | collective-permute-done | bytes 2064416 | tf_op jit(solution)/shard_map/ppermute | solution.py:147
  568.4 14.8 %convolution_convert_fusion = bf16[2304,2304]{1,0:T(8,128)(2,1)} fusion(bf16[896,2304]{1,0:T(8,128)(2,1)S(1)} %copy-done.90, bf16[896,2304]{1,0:T(8,128)(2,1)S(1)} %copy-done.13, f32[896]{0:T(1024)S(1)} %multiply_multiply_fusion.12, f32[896]{0:T(1024)S(1)} %compare_convert_fusion, f32[2304]{0:T(1024)S(1)} %get-tuple-element.35, f32[896]{0:T(1024)S(1)} %fusion.119, ...), kind=kOutput, calls=%fused_computation | convolution fusion | flops 9542762496 | bytes 23023104 | tf_op jit(solution)/shard_map/td,tf->df/dot_general | solution.py:244
  583.2 25.5 %fusion.22 = (bf16[896,2304]{1,0:T(8,128)(2,1)}, bf16[896,2304]{1,0:T(8,128)(2,1)}) fusion(f32[896,2304]{1,0:T(8,128)} %fusion.142, f32[896,2304]{1,0:T(8,128)} %get-tuple-element.123, bf16[2304,2304]{1,0:T(8,128)(2,1)} %copy-done.16, bf16[896,2304]{1,0:T(8,128)(2,1)} %param.23, f32[896]{0:T(1024)S(1)} %multiply_multiply_fusion.12, ...), kind=kOutput, calls=%fused_computation.48 | convolution fusion | flops 9586999296 | bytes 43666944 | tf_op jit(solution)/shard_map/td,df->tf/dot_general | solution.py:245
  608.7 15.1 %fusion.144 = f32[896,2304]{1,0:T(8,128)} fusion(bf16[896,2304]{1,0:T(8,128)(2,1)} %get-tuple-element.66, bf16[2304,2304]{1,0:T(8,128)(2,1)} %constant_dynamic-update-slice_fusion.8), kind=kOutput, calls=%fused_computation.337 | convolution fusion | flops 9512681472 | bytes 23003136 | tf_op jit(solution)/shard_map/tf,df->td/dot_general | solution.py:257
  623.8 13.7 %convolution_convert_fusion.1 = bf16[2304,2304]{1,0:T(8,128)(2,1)} fusion(bf16[896,2304]{1,0:T(8,128)(2,1)S(1)} %copy-done.32, bf16[896,2304]{1,0:T(8,128)(2,1)S(1)} %copy-done.91), kind=kOutput, calls=%fused_computation.1 | convolution fusion | flops 9517989888 | bytes 18874368 | tf_op jit(solution)/shard_map/td,tf->df/dot_general | solution.py:253
  637.5 13.7 %convolution_convert_fusion.2 = bf16[2304,2304]{1,0:T(8,128)(2,1)} fusion(bf16[896,2304]{1,0:T(8,128)(2,1)S(1)} %copy-done.32, bf16[896,2304]{1,0:T(8,128)(2,1)S(1)} %copy-done.92), kind=kOutput, calls=%fused_computation.2 | convolution fusion | flops 9517989888 | bytes 18874368 | tf_op jit(solution)/shard_map/td,tf->df/dot_general | solution.py:252
  651.2 17.8 %convolution_add_fusion = f32[896,2304]{1,0:T(8,128)} fusion(f32[896,2304]{1,0:T(8,128)} %fusion.144, bf16[896,2304]{1,0:T(8,128)(2,1)} %get-tuple-element.65, bf16[2304,2304]{1,0:T(8,128)(2,1)} %constant_dynamic-update-slice_fusion.16), kind=kOutput, calls=%fused_computation.77 | convolution fusion | flops 9514745856 | bytes 31260672 | tf_op jit(solution)/shard_map/tf,df->td/dot_general | solution.py:254
  669.1 5.5 constant_dynamic-slice_fusion.11
  676.0 5.3 constant_dynamic-slice_fusion.15
  686.8 19.9 %collective-permute-done.78 = bf16[288,2304]{1,0:T(8,128)(2,1)S(1)} collective-permute-done((bf16[288,2304]{1,0:T(8,128)(2,1)}, bf16[288,2304]{1,0:T(8,128)(2,1)S(1)}, u32[]{:S(2)}, u32[]{:S(2)}) %collective-permute-start.78) | collective-permute-done | bytes 1327136 | tf_op jit(solution)/shard_map/ppermute | solution.py:130
  710.9 24.3 %collective-permute-done.71 = bf16[288,2304]{1,0:T(8,128)(2,1)S(1)} collective-permute-done((bf16[288,2304]{1,0:T(8,128)(2,1)S(1)}, bf16[288,2304]{1,0:T(8,128)(2,1)S(1)}, u32[]{:S(2)}, u32[]{:S(2)}) %collective-permute-start.71) | collective-permute-done | bytes 1327136 | tf_op jit(solution)/shard_map/ppermute | solution.py:130
  738.3 82.2 %collective-permute-done.64 = bf16[288,2304]{1,0:T(8,128)(2,1)S(1)} collective-permute-done((bf16[288,2304]{1,0:T(8,128)(2,1)}, bf16[288,2304]{1,0:T(8,128)(2,1)S(1)}, u32[]{:S(2)}, u32[]{:S(2)}) %collective-permute-start.64) | collective-permute-done | bytes 1327136 | tf_op jit(solution)/shard_map/ppermute | solution.py:130
  826.5 28.3 %collective-permute-done.79 = bf16[288,2304]{1,0:T(8,128)(2,1)} collective-permute-done((bf16[288,2304]{1,0:T(8,128)(2,1)}, bf16[288,2304]{1,0:T(8,128)(2,1)}, u32[]{:S(2)}, u32[]{:S(2)}) %collective-permute-start.79) | collective-permute-done | bytes 1327136 | tf_op jit(solution)/shard_map/ppermute | solution.py:133
  859.9 23.2 %collective-permute-done.72 = bf16[288,2304]{1,0:T(8,128)(2,1)S(1)} collective-permute-done((bf16[288,2304]{1,0:T(8,128)(2,1)S(1)}, bf16[288,2304]{1,0:T(8,128)(2,1)S(1)}, u32[]{:S(2)}, u32[]{:S(2)}) %collective-permute-start.72) | collective-permute-done | bytes 1327136 | tf_op jit(solution)/shard_map/ppermute | solution.py:133
  887.1 22.2 %collective-permute-done.65 = bf16[288,2304]{1,0:T(8,128)(2,1)S(1)} collective-permute-done((bf16[288,2304]{1,0:T(8,128)(2,1)S(1)}, bf16[288,2304]{1,0:T(8,128)(2,1)S(1)}, u32[]{:S(2)}, u32[]{:S(2)}) %collective-permute-start.65) | collective-permute-done | bytes 1327136 | tf_op jit(solution)/shard_map/ppermute | solution.py:133
  910.9 7.0 collective-permute-done.69
  917.9 25.3 %collective-permute-done.73 = bf16[288,2304]{1,0:T(8,128)(2,1)S(1)} collective-permute-done((bf16[288,2304]{1,0:T(8,128)(2,1)S(1)}, bf16[288,2304]{1,0:T(8,128)(2,1)S(1)}, u32[]{:S(2)}, u32[]{:S(2)}) %collective-permute-start.73) | collective-permute-done | bytes 1327136 | tf_op jit(solution)/shard_map/ppermute | solution.py:133
  947.4 24.2 %collective-permute-done.66 = bf16[288,2304]{1,0:T(8,128)(2,1)S(1)} collective-permute-done((bf16[288,2304]{1,0:T(8,128)(2,1)S(1)}, bf16[288,2304]{1,0:T(8,128)(2,1)S(1)}, u32[]{:S(2)}, u32[]{:S(2)}) %collective-permute-start.66) | collective-permute-done | bytes 1327136 | tf_op jit(solution)/shard_map/ppermute | solution.py:133
  974.5 25.6 %collective-permute-done.80 = bf16[288,2304]{1,0:T(8,128)(2,1)S(1)} collective-permute-done((bf16[288,2304]{1,0:T(8,128)(2,1)S(1)}, bf16[288,2304]{1,0:T(8,128)(2,1)S(1)}, u32[]{:S(2)}, u32[]{:S(2)}) %collective-permute-start.80) | collective-permute-done | bytes 1327136 | tf_op jit(solution)/shard_map/ppermute | solution.py:133
  1011.4 13.3 %fusion.12 = (f32[2304]{0:T(1024)S(1)}, f32[896]{0:T(1024)S(1)}, f32[896,2304]{1,0:T(8,128)S(1)}, bf16[896,2304]{1,0:T(8,128)(2,1)}) fusion(f32[896]{0:T(1024)S(1)} %copy-done.64, bf16[448,2304]{1,0:T(8,128)(2,1)S(1)} %copy-done.8, bf16[448,2304]{1,0:T(8,128)(2,1)S(1)} %copy-done.6, f32[2304]{0:T(1024)S(1)} %copy-done.59, ...), kind=kLoop, calls=%fused_computation.38 | loop fusion | flops 68121472 | bytes 33088512 | tf_op jit(solution)/shard_map/transpose(jvp())/reduce_sum | solution.py:25
  1024.7 5.5 fusion.25
  1062.5 8.1 convolution_convert_fusion.3
  1083.7 10.3 collective-permute-done.50
  1101.0 5.7 collective-permute-done.58
  1113.0 5.1 collective-permute-done.51
  1121.8 12.0 add_multiply_fusion
  1142.2 22.4 %collective-permute-done.45 = bf16[448,2304]{1,0:T(8,128)(2,1)} collective-permute-done((bf16[448,2304]{1,0:T(8,128)(2,1)S(1)}, bf16[448,2304]{1,0:T(8,128)(2,1)}, u32[]{:S(2)}, u32[]{:S(2)}) %collective-permute-start.45) | collective-permute-done | bytes 2064416 | tf_op jit(solution)/shard_map/ppermute | solution.py:147
  1170.2 7.8 add_multiply_fusion.1
  1204.0 4.6 collective-permute-done.87
  1208.8 8.0 fusion.26
  (525 shorter events, 304.8 us)
Async XLA Ops:
  10.8 57.9 %collective-permute-start.7 = (bf16[288,1536]{1,0:T(8,128)(2,1)}, bf16[288,1536]{1,0:T(8,128)(2,1)}, u32[]{:S(2)}, u32[]{:S(2)}) collective-permute-start(bf16[288,1536]{1,0:T(8,128)(2,1)} %get-tuple-element.110), channel_id=1, source_target_pairs={{0,4},{4,0},{8,12},{12,8},{16,20},{20,16},{24,28},{28,24},{1,5},{5... | collective-permute-start | bytes 2654216 | tf_op jit(solution)/shard_map/ppermute | solution.py:110
  11.3 55.5 %collective-permute-start.8 = (bf16[288,1536]{1,0:T(8,128)(2,1)}, bf16[288,1536]{1,0:T(8,128)(2,1)}, u32[]{:S(2)}, u32[]{:S(2)}) collective-permute-start(bf16[288,1536]{1,0:T(8,128)(2,1)} %get-tuple-element.110), channel_id=1, source_target_pairs={{0,8},{4,12},{8,16},{12,20},{16,24},{20,28},{24,0},{28,4},{1,9},{5... | collective-permute-start | bytes 2654216 | tf_op jit(solution)/shard_map/ppermute | solution.py:109
  14.9 59.1 %collective-permute-start.24 = (bf16[288,2304]{1,0:T(8,128)(2,1)}, bf16[288,2304]{1,0:T(8,128)(2,1)}, u32[]{:S(2)}, u32[]{:S(2)}) collective-permute-start(bf16[288,2304]{1,0:T(8,128)(2,1)} %get-tuple-element.97), channel_id=1, source_target_pairs={{0,4},{4,0},{8,12},{12,8},{16,20},{20,16},{24,28},{28,24},{1,5},{5... | collective-permute-start | bytes 3981320 | tf_op jit(solution)/shard_map/ppermute | solution.py:110
  64.0 55.5 %collective-permute-start.25 = (bf16[288,2304]{1,0:T(8,128)(2,1)}, bf16[288,2304]{1,0:T(8,128)(2,1)}, u32[]{:S(2)}, u32[]{:S(2)}) collective-permute-start(bf16[288,2304]{1,0:T(8,128)(2,1)} %get-tuple-element.97), channel_id=1, source_target_pairs={{0,8},{4,12},{8,16},{12,20},{16,24},{20,28},{24,0},{28,4},{1,9},{5... | collective-permute-start | bytes 3981320 | tf_op jit(solution)/shard_map/ppermute | solution.py:109
  66.1 56.4 %collective-permute-start.17 = (bf16[288,2304]{1,0:T(8,128)(2,1)}, bf16[288,2304]{1,0:T(8,128)(2,1)S(1)}, u32[]{:S(2)}, u32[]{:S(2)}) collective-permute-start(bf16[288,2304]{1,0:T(8,128)(2,1)} %get-tuple-element.96), channel_id=1, source_target_pairs={{0,4},{4,0},{8,12},{12,8},{16,20},{20,16},{24,28},{28,24},{1,5},{5... | collective-permute-start | bytes 3981320 | tf_op jit(solution)/shard_map/ppermute | solution.py:110
  66.8 50.2 %collective-permute-start.10 = (bf16[288,1536]{1,0:T(8,128)(2,1)}, bf16[288,1536]{1,0:T(8,128)(2,1)S(1)}, u32[]{:S(2)}, u32[]{:S(2)}) collective-permute-start(bf16[288,1536]{1,0:T(8,128)(2,1)} %collective-permute-done.8), channel_id=1, source_target_pairs={{0,8},{4,12},{8,16},{12,20},{16,24},{20,28},{24,0},{28,4},{1,9},{5... | collective-permute-start | bytes 2654216 | tf_op jit(solution)/shard_map/ppermute | solution.py:109
  68.7 142.9 %collective-permute-start.18 = (bf16[288,2304]{1,0:T(8,128)(2,1)}, bf16[288,2304]{1,0:T(8,128)(2,1)}, u32[]{:S(2)}, u32[]{:S(2)}) collective-permute-start(bf16[288,2304]{1,0:T(8,128)(2,1)} %get-tuple-element.96), channel_id=1, source_target_pairs={{0,8},{4,12},{8,16},{12,20},{16,24},{20,28},{24,0},{28,4},{1,9},{5... | collective-permute-start | bytes 3981320 | tf_op jit(solution)/shard_map/ppermute | solution.py:109
  74.0 51.2 %collective-permute-start.9 = (bf16[288,1536]{1,0:T(8,128)(2,1)}, bf16[288,1536]{1,0:T(8,128)(2,1)S(1)}, u32[]{:S(2)}, u32[]{:S(2)}) collective-permute-start(bf16[288,1536]{1,0:T(8,128)(2,1)} %collective-permute-done.8), channel_id=1, source_target_pairs={{0,4},{4,0},{8,12},{12,8},{16,20},{20,16},{24,28},{28,24},{1,5},{5... | collective-permute-start | bytes 2654216 | tf_op jit(solution)/shard_map/ppermute | solution.py:110
  117.0 47.4 %collective-permute-start.12 = (bf16[288,1536]{1,0:T(8,128)(2,1)S(1)}, bf16[288,1536]{1,0:T(8,128)(2,1)S(1)}, u32[]{:S(2)}, u32[]{:S(2)}) collective-permute-start(bf16[288,1536]{1,0:T(8,128)(2,1)S(1)} %collective-permute-done.10), channel_id=1, source_target_pairs={{0,8},{4,12},{8,16},{12,20},{16,24},{20,28},{24,0},{28,4},{1,9},{5... | collective-permute-start | bytes 2654216 | tf_op jit(solution)/shard_map/ppermute | solution.py:109
  119.5 94.7 %collective-permute-start.31 = (bf16[288,2304]{1,0:T(8,128)(2,1)}, bf16[288,2304]{1,0:T(8,128)(2,1)}, u32[]{:S(2)}, u32[]{:S(2)}) collective-permute-start(bf16[288,2304]{1,0:T(8,128)(2,1)} %get-tuple-element.64), channel_id=1, source_target_pairs={{0,4},{4,0},{8,12},{12,8},{16,20},{20,16},{24,28},{28,24},{1,5},{5... | collective-permute-start | bytes 3981320 | tf_op jit(solution)/shard_map/ppermute | solution.py:110
  122.5 43.1 %collective-permute-start.11 = (bf16[288,1536]{1,0:T(8,128)(2,1)S(1)}, bf16[288,1536]{1,0:T(8,128)(2,1)S(1)}, u32[]{:S(2)}, u32[]{:S(2)}) collective-permute-start(bf16[288,1536]{1,0:T(8,128)(2,1)S(1)} %collective-permute-done.10), channel_id=1, source_target_pairs={{0,4},{4,0},{8,12},{12,8},{16,20},{20,16},{24,28},{28,24},{1,5},{5... | collective-permute-start | bytes 2654216 | tf_op jit(solution)/shard_map/ppermute | solution.py:110
  125.2 91.9 %collective-permute-start.32 = (bf16[288,2304]{1,0:T(8,128)(2,1)}, bf16[288,2304]{1,0:T(8,128)(2,1)}, u32[]{:S(2)}, u32[]{:S(2)}) collective-permute-start(bf16[288,2304]{1,0:T(8,128)(2,1)} %get-tuple-element.64), channel_id=1, source_target_pairs={{0,8},{4,12},{8,16},{12,20},{16,24},{20,28},{24,0},{28,4},{1,9},{5... | collective-permute-start | bytes 3981320 | tf_op jit(solution)/shard_map/ppermute | solution.py:109
  165.7 57.0 %collective-permute-start.27 = (bf16[288,2304]{1,0:T(8,128)(2,1)}, bf16[288,2304]{1,0:T(8,128)(2,1)}, u32[]{:S(2)}, u32[]{:S(2)}) collective-permute-start(bf16[288,2304]{1,0:T(8,128)(2,1)} %collective-permute-done.25), channel_id=1, source_target_pairs={{0,8},{4,12},{8,16},{12,20},{16,24},{20,28},{24,0},{28,4},{1,9},{5... | collective-permute-start | bytes 3981320 | tf_op jit(solution)/shard_map/ppermute | solution.py:109
  211.6 45.0 %collective-permute-start.14 = (bf16[448,2304]{1,0:T(8,128)(2,1)S(1)}, bf16[448,2304]{1,0:T(8,128)(2,1)S(1)}, u32[]{:S(2)}, u32[]{:S(2)}) collective-permute-start(bf16[448,2304]{1,0:T(8,128)(2,1)S(1)} %dynamic-slice_convert_fusion.3), channel_id=1, source_target_pairs={{0,1},{1,0},{2,3},{3,2},{4,5},{5,4},{6,7},{7,6},{8,9},{9,8},{10,11... | collective-permute-start | bytes 6193160 | tf_op jit(solution)/shard_map/ppermute | solution.py:145
  218.7 60.9 %collective-permute-start.34 = (bf16[288,2304]{1,0:T(8,128)(2,1)}, bf16[288,2304]{1,0:T(8,128)(2,1)S(1)}, u32[]{:S(2)}, u32[]{:S(2)}) collective-permute-start(bf16[288,2304]{1,0:T(8,128)(2,1)} %collective-permute-done.32), channel_id=1, source_target_pairs={{0,8},{4,12},{8,16},{12,20},{16,24},{20,28},{24,0},{28,4},{1,9},{5... | collective-permute-start | bytes 3981320 | tf_op jit(solution)/shard_map/ppermute | solution.py:109
  222.6 57.0 %collective-permute-start.33 = (bf16[288,2304]{1,0:T(8,128)(2,1)}, bf16[288,2304]{1,0:T(8,128)(2,1)S(1)}, u32[]{:S(2)}, u32[]{:S(2)}) collective-permute-start(bf16[288,2304]{1,0:T(8,128)(2,1)} %collective-permute-done.32), channel_id=1, source_target_pairs={{0,4},{4,0},{8,12},{12,8},{16,20},{20,16},{24,28},{28,24},{1,5},{5... | collective-permute-start | bytes 3981320 | tf_op jit(solution)/shard_map/ppermute | solution.py:110
  246.4 61.7 %collective-permute-start.29 = (bf16[288,2304]{1,0:T(8,128)(2,1)}, bf16[288,2304]{1,0:T(8,128)(2,1)S(1)}, u32[]{:S(2)}, u32[]{:S(2)}) collective-permute-start(bf16[288,2304]{1,0:T(8,128)(2,1)} %collective-permute-done.27), channel_id=1, source_target_pairs={{0,8},{4,12},{8,16},{12,20},{16,24},{20,28},{24,0},{28,4},{1,9},{5... | collective-permute-start | bytes 3981320 | tf_op jit(solution)/shard_map/ppermute | solution.py:109
  256.6 46.7 %collective-permute-start.28 = (bf16[288,2304]{1,0:T(8,128)(2,1)}, bf16[288,2304]{1,0:T(8,128)(2,1)S(1)}, u32[]{:S(2)}, u32[]{:S(2)}) collective-permute-start(bf16[288,2304]{1,0:T(8,128)(2,1)} %collective-permute-done.27), channel_id=1, source_target_pairs={{0,4},{4,0},{8,12},{12,8},{16,20},{20,16},{24,28},{28,24},{1,5},{5... | collective-permute-start | bytes 3981320 | tf_op jit(solution)/shard_map/ppermute | solution.py:110
  258.4 81.3 %collective-permute-start.15 = (bf16[448,2304]{1,0:T(8,128)(2,1)S(1)}, bf16[448,2304]{1,0:T(8,128)(2,1)S(1)}, u32[]{:S(2)}, u32[]{:S(2)}) collective-permute-start(bf16[448,2304]{1,0:T(8,128)(2,1)S(1)} %add_convert_fusion.7), channel_id=1, source_target_pairs={{0,2},{1,3},{2,0},{3,1},{4,6},{5,7},{6,4},{7,5},{8,10},{9,11},{10,... | collective-permute-start | bytes 6193160 | tf_op jit(solution)/shard_map/ppermute | solution.py:147
  279.6 56.9 %collective-permute-start.22 = (bf16[288,2304]{1,0:T(8,128)(2,1)S(1)}, bf16[288,2304]{1,0:T(8,128)(2,1)S(1)}, u32[]{:S(2)}, u32[]{:S(2)}) collective-permute-start(bf16[288,2304]{1,0:T(8,128)(2,1)S(1)} %collective-permute-done.20), channel_id=1, source_target_pairs={{0,8},{4,12},{8,16},{12,20},{16,24},{20,28},{24,0},{28,4},{1,9},{5... | collective-permute-start | bytes 3981320 | tf_op jit(solution)/shard_map/ppermute | solution.py:109
  279.6 57.5 %collective-permute-start.21 = (bf16[288,2304]{1,0:T(8,128)(2,1)S(1)}, bf16[288,2304]{1,0:T(8,128)(2,1)S(1)}, u32[]{:S(2)}, u32[]{:S(2)}) collective-permute-start(bf16[288,2304]{1,0:T(8,128)(2,1)S(1)} %collective-permute-done.20), channel_id=1, source_target_pairs={{0,4},{4,0},{8,12},{12,8},{16,20},{20,16},{24,28},{28,24},{1,5},{5... | collective-permute-start | bytes 3981320 | tf_op jit(solution)/shard_map/ppermute | solution.py:110
  303.3 61.3 %collective-permute-start.36 = (bf16[288,2304]{1,0:T(8,128)(2,1)S(1)}, bf16[288,2304]{1,0:T(8,128)(2,1)S(1)}, u32[]{:S(2)}, u32[]{:S(2)}) collective-permute-start(bf16[288,2304]{1,0:T(8,128)(2,1)S(1)} %collective-permute-done.34), channel_id=1, source_target_pairs={{0,8},{4,12},{8,16},{12,20},{16,24},{20,28},{24,0},{28,4},{1,9},{5... | collective-permute-start | bytes 3981320 | tf_op jit(solution)/shard_map/ppermute | solution.py:109
  308.1 57.0 %collective-permute-start.35 = (bf16[288,2304]{1,0:T(8,128)(2,1)S(1)}, bf16[288,2304]{1,0:T(8,128)(2,1)S(1)}, u32[]{:S(2)}, u32[]{:S(2)}) collective-permute-start(bf16[288,2304]{1,0:T(8,128)(2,1)S(1)} %collective-permute-done.34), channel_id=1, source_target_pairs={{0,4},{4,0},{8,12},{12,8},{16,20},{20,16},{24,28},{28,24},{1,5},{5... | collective-permute-start | bytes 3981320 | tf_op jit(solution)/shard_map/ppermute | solution.py:110
  336.5 52.1 %collective-permute-start.30 = (bf16[288,2304]{1,0:T(8,128)(2,1)S(1)}, bf16[288,2304]{1,0:T(8,128)(2,1)S(1)}, u32[]{:S(2)}, u32[]{:S(2)}) collective-permute-start(bf16[288,2304]{1,0:T(8,128)(2,1)S(1)} %collective-permute-done.29), channel_id=1, source_target_pairs={{0,4},{4,0},{8,12},{12,8},{16,20},{20,16},{24,28},{28,24},{1,5},{5... | collective-permute-start | bytes 3981320 | tf_op jit(solution)/shard_map/ppermute | solution.py:110
  337.1 79.9 %collective-permute-start.23 = (bf16[288,2304]{1,0:T(8,128)(2,1)S(1)}, bf16[288,2304]{1,0:T(8,128)(2,1)S(1)}, u32[]{:S(2)}, u32[]{:S(2)}) collective-permute-start(bf16[288,2304]{1,0:T(8,128)(2,1)S(1)} %collective-permute-done.22), channel_id=1, source_target_pairs={{0,4},{4,0},{8,12},{12,8},{16,20},{20,16},{24,28},{28,24},{1,5},{5... | collective-permute-start | bytes 3981320 | tf_op jit(solution)/shard_map/ppermute | solution.py:110
  340.2 105.0 %collective-permute-start.16 = (bf16[448,2304]{1,0:T(8,128)(2,1)S(1)}, bf16[448,2304]{1,0:T(8,128)(2,1)S(1)}, u32[]{:S(2)}, u32[]{:S(2)}) collective-permute-start(bf16[448,2304]{1,0:T(8,128)(2,1)S(1)} %add_convert_fusion.6), channel_id=1, source_target_pairs={{0,1},{1,0},{2,3},{3,2},{4,5},{5,4},{6,7},{7,6},{8,9},{9,8},{10,11... | collective-permute-start | bytes 6193160 | tf_op jit(solution)/shard_map/ppermute | solution.py:149
  364.5 80.5 %collective-permute-start.37 = (bf16[288,2304]{1,0:T(8,128)(2,1)S(1)}, bf16[288,2304]{1,0:T(8,128)(2,1)S(1)}, u32[]{:S(2)}, u32[]{:S(2)}) collective-permute-start(bf16[288,2304]{1,0:T(8,128)(2,1)S(1)} %collective-permute-done.36), channel_id=1, source_target_pairs={{0,4},{4,0},{8,12},{12,8},{16,20},{20,16},{24,28},{28,24},{1,5},{5... | collective-permute-start | bytes 3981320 | tf_op jit(solution)/shard_map/ppermute | solution.py:110
  507.9 47.0 %collective-permute-start.39 = (bf16[448,2304]{1,0:T(8,128)(2,1)S(1)}, bf16[448,2304]{1,0:T(8,128)(2,1)S(1)}, u32[]{:S(2)}, u32[]{:S(2)}) collective-permute-start(bf16[448,2304]{1,0:T(8,128)(2,1)S(1)} %add_convert_fusion.5), channel_id=1, source_target_pairs={{0,2},{1,3},{2,0},{3,1},{4,6},{5,7},{6,4},{7,5},{8,10},{9,11},{10,... | collective-permute-start | bytes 6193160 | tf_op jit(solution)/shard_map/ppermute | solution.py:147
  681.3 53.9 %collective-permute-start.71 = (bf16[288,2304]{1,0:T(8,128)(2,1)S(1)}, bf16[288,2304]{1,0:T(8,128)(2,1)S(1)}, u32[]{:S(2)}, u32[]{:S(2)}) collective-permute-start(bf16[288,2304]{1,0:T(8,128)(2,1)S(1)} %get-tuple-element.76), channel_id=1, source_target_pairs={{0,4},{4,0},{8,12},{12,8},{16,20},{20,16},{24,28},{28,24},{1,5},{5... | collective-permute-start | bytes 3981320 | tf_op jit(solution)/shard_map/ppermute | solution.py:130
  682.2 138.8 %collective-permute-start.41 = (bf16[448,2304]{1,0:T(8,128)(2,1)S(1)}, bf16[448,2304]{1,0:T(8,128)(2,1)S(1)}, u32[]{:S(2)}, u32[]{:S(2)}) collective-permute-start(bf16[448,2304]{1,0:T(8,128)(2,1)S(1)} %dynamic-slice_convert_fusion.1), channel_id=1, source_target_pairs={{0,1},{1,0},{2,3},{3,2},{4,5},{5,4},{6,7},{7,6},{8,9},{9,8},{10,11... | collective-permute-start | bytes 6193160 | tf_op jit(solution)/shard_map/ppermute | solution.py:145
  682.3 140.4 %collective-permute-start.77 = (bf16[288,2304]{1,0:T(8,128)(2,1)}, bf16[288,2304]{1,0:T(8,128)(2,1)S(1)}, u32[]{:S(2)}, u32[]{:S(2)}) collective-permute-start(bf16[288,2304]{1,0:T(8,128)(2,1)} %get-tuple-element.69), channel_id=1, source_target_pairs={{0,4},{4,0},{8,12},{12,8},{16,20},{20,16},{24,28},{28,24},{1,5},{5... | collective-permute-start | bytes 3981320 | tf_op jit(solution)/shard_map/ppermute | solution.py:130
  683.7 175.1 %collective-permute-start.70 = (bf16[288,2304]{1,0:T(8,128)(2,1)}, bf16[288,2304]{1,0:T(8,128)(2,1)S(1)}, u32[]{:S(2)}, u32[]{:S(2)}) collective-permute-start(bf16[288,2304]{1,0:T(8,128)(2,1)} %get-tuple-element.77), channel_id=1, source_target_pairs={{0,4},{4,0},{8,12},{12,8},{16,20},{20,16},{24,28},{28,24},{1,5},{5... | collective-permute-start | bytes 3981320 | tf_op jit(solution)/shard_map/ppermute | solution.py:130
  706.7 113.8 %collective-permute-start.64 = (bf16[288,2304]{1,0:T(8,128)(2,1)}, bf16[288,2304]{1,0:T(8,128)(2,1)S(1)}, u32[]{:S(2)}, u32[]{:S(2)}) collective-permute-start(bf16[288,2304]{1,0:T(8,128)(2,1)} %get-tuple-element.72), channel_id=1, source_target_pairs={{0,4},{4,0},{8,12},{12,8},{16,20},{20,16},{24,28},{28,24},{1,5},{5... | collective-permute-start | bytes 3981320 | tf_op jit(solution)/shard_map/ppermute | solution.py:130
  735.2 151.1 %collective-permute-start.63 = (bf16[288,2304]{1,0:T(8,128)(2,1)}, bf16[288,2304]{1,0:T(8,128)(2,1)S(1)}, u32[]{:S(2)}, u32[]{:S(2)}) collective-permute-start(bf16[288,2304]{1,0:T(8,128)(2,1)} %get-tuple-element.73), channel_id=1, source_target_pairs={{0,4},{4,0},{8,12},{12,8},{16,20},{20,16},{24,28},{28,24},{1,5},{5... | collective-permute-start | bytes 3981320 | tf_op jit(solution)/shard_map/ppermute | solution.py:130
  821.0 62.2 %collective-permute-start.72 = (bf16[288,2304]{1,0:T(8,128)(2,1)S(1)}, bf16[288,2304]{1,0:T(8,128)(2,1)S(1)}, u32[]{:S(2)}, u32[]{:S(2)}) collective-permute-start(bf16[288,2304]{1,0:T(8,128)(2,1)S(1)} %add_convert_fusion.13), channel_id=1, source_target_pairs={{0,8},{4,12},{8,16},{12,20},{16,24},{20,28},{24,0},{28,4},{1,9},{5... | collective-permute-start | bytes 3981320 | tf_op jit(solution)/shard_map/ppermute | solution.py:133
  822.6 86.7 %collective-permute-start.65 = (bf16[288,2304]{1,0:T(8,128)(2,1)S(1)}, bf16[288,2304]{1,0:T(8,128)(2,1)S(1)}, u32[]{:S(2)}, u32[]{:S(2)}) collective-permute-start(bf16[288,2304]{1,0:T(8,128)(2,1)S(1)} %add_convert_fusion.16), channel_id=1, source_target_pairs={{0,8},{4,12},{8,16},{12,20},{16,24},{20,28},{24,0},{28,4},{1,9},{5... | collective-permute-start | bytes 3981320 | tf_op jit(solution)/shard_map/ppermute | solution.py:133
  854.8 55.1 %collective-permute-start.42 = (bf16[448,2304]{1,0:T(8,128)(2,1)S(1)}, bf16[448,2304]{1,0:T(8,128)(2,1)S(1)}, u32[]{:S(2)}, u32[]{:S(2)}) collective-permute-start(bf16[448,2304]{1,0:T(8,128)(2,1)S(1)} %add_convert_fusion.3), channel_id=1, source_target_pairs={{0,2},{1,3},{2,0},{3,1},{4,6},{5,7},{6,4},{7,5},{8,10},{9,11},{10,... | collective-permute-start | bytes 6193160 | tf_op jit(solution)/shard_map/ppermute | solution.py:147
  858.8 115.7 %collective-permute-start.76 = (bf16[288,2304]{1,0:T(8,128)(2,1)}, bf16[288,2304]{1,0:T(8,128)(2,1)S(1)}, u32[]{:S(2)}, u32[]{:S(2)}) collective-permute-start(bf16[288,2304]{1,0:T(8,128)(2,1)} %get-tuple-element.70), channel_id=1, source_target_pairs={{0,4},{4,0},{8,12},{12,8},{16,20},{20,16},{24,28},{28,24},{1,5},{5... | collective-permute-start | bytes 3981320 | tf_op jit(solution)/shard_map/ppermute | solution.py:130
  886.3 59.8 %collective-permute-start.62 = (bf16[288,2304]{1,0:T(8,128)(2,1)}, bf16[288,2304]{1,0:T(8,128)(2,1)S(1)}, u32[]{:S(2)}, u32[]{:S(2)}) collective-permute-start(bf16[288,2304]{1,0:T(8,128)(2,1)} %get-tuple-element.74), channel_id=1, source_target_pairs={{0,4},{4,0},{8,12},{12,8},{16,20},{20,16},{24,28},{28,24},{1,5},{5... | collective-permute-start | bytes 3981320 | tf_op jit(solution)/shard_map/ppermute | solution.py:130
  909.9 61.7 %collective-permute-start.66 = (bf16[288,2304]{1,0:T(8,128)(2,1)S(1)}, bf16[288,2304]{1,0:T(8,128)(2,1)S(1)}, u32[]{:S(2)}, u32[]{:S(2)}) collective-permute-start(bf16[288,2304]{1,0:T(8,128)(2,1)S(1)} %add_convert_fusion.15), channel_id=1, source_target_pairs={{0,8},{4,12},{8,16},{12,20},{16,24},{20,28},{24,0},{28,4},{1,9},{5... | collective-permute-start | bytes 3981320 | tf_op jit(solution)/shard_map/ppermute | solution.py:133
  917.9 82.1 %collective-permute-start.80 = (bf16[288,2304]{1,0:T(8,128)(2,1)S(1)}, bf16[288,2304]{1,0:T(8,128)(2,1)S(1)}, u32[]{:S(2)}, u32[]{:S(2)}) collective-permute-start(bf16[288,2304]{1,0:T(8,128)(2,1)S(1)} %add_convert_fusion.9), channel_id=1, source_target_pairs={{0,8},{4,12},{8,16},{12,20},{16,24},{20,28},{24,0},{28,4},{1,9},{5... | collective-permute-start | bytes 3981320 | tf_op jit(solution)/shard_map/ppermute | solution.py:133
  943.2 60.3 %collective-permute-start.43 = (bf16[448,2304]{1,0:T(8,128)(2,1)S(1)}, bf16[448,2304]{1,0:T(8,128)(2,1)S(1)}, u32[]{:S(2)}, u32[]{:S(2)}) collective-permute-start(bf16[448,2304]{1,0:T(8,128)(2,1)S(1)} %add_convert_fusion.2), channel_id=1, source_target_pairs={{0,1},{1,0},{2,3},{3,2},{4,5},{5,4},{6,7},{7,6},{8,9},{9,8},{10,11... | collective-permute-start | bytes 6193160 | tf_op jit(solution)/shard_map/ppermute | solution.py:149
  946.1 131.6 %collective-permute-start.68 = (bf16[288,2304]{1,0:T(8,128)(2,1)}, bf16[288,2304]{1,0:T(8,128)(2,1)}, u32[]{:S(2)}, u32[]{:S(2)}) collective-permute-start(bf16[288,2304]{1,0:T(8,128)(2,1)} %get-tuple-element.75), channel_id=1, source_target_pairs={{0,4},{4,0},{8,12},{12,8},{16,20},{20,16},{24,28},{28,24},{1,5},{5... | collective-permute-start | bytes 3981320 | tf_op jit(solution)/shard_map/ppermute | solution.py:130
  971.6 123.3 %collective-permute-start.61 = (bf16[288,2304]{1,0:T(8,128)(2,1)}, bf16[288,2304]{1,0:T(8,128)(2,1)}, u32[]{:S(2)}, u32[]{:S(2)}) collective-permute-start(bf16[288,2304]{1,0:T(8,128)(2,1)} %get-tuple-element.71), channel_id=1, source_target_pairs={{0,4},{4,0},{8,12},{12,8},{16,20},{20,16},{24,28},{28,24},{1,5},{5... | collective-permute-start | bytes 3981320 | tf_op jit(solution)/shard_map/ppermute | solution.py:130
  974.5 103.3 %collective-permute-start.74 = (bf16[288,2304]{1,0:T(8,128)(2,1)}, bf16[288,2304]{1,0:T(8,128)(2,1)}, u32[]{:S(2)}, u32[]{:S(2)}) collective-permute-start(bf16[288,2304]{1,0:T(8,128)(2,1)} %add_convert_fusion.11), channel_id=1, source_target_pairs={{0,8},{4,12},{8,16},{12,20},{16,24},{20,28},{24,0},{28,4},{1,9},{5... | collective-permute-start | bytes 3981320 | tf_op jit(solution)/shard_map/ppermute | solution.py:133
  1000.1 95.0 %collective-permute-start.67 = (bf16[288,2304]{1,0:T(8,128)(2,1)}, bf16[288,2304]{1,0:T(8,128)(2,1)}, u32[]{:S(2)}, u32[]{:S(2)}) collective-permute-start(bf16[288,2304]{1,0:T(8,128)(2,1)} %add_convert_fusion.14), channel_id=1, source_target_pairs={{0,8},{4,12},{8,16},{12,20},{16,24},{20,28},{24,0},{28,4},{1,9},{5... | collective-permute-start | bytes 3981320 | tf_op jit(solution)/shard_map/ppermute | solution.py:133
  1119.7 44.8 %collective-permute-start.45 = (bf16[448,2304]{1,0:T(8,128)(2,1)S(1)}, bf16[448,2304]{1,0:T(8,128)(2,1)}, u32[]{:S(2)}, u32[]{:S(2)}) collective-permute-start(bf16[448,2304]{1,0:T(8,128)(2,1)S(1)} %add_convert_fusion.1), channel_id=1, source_target_pairs={{0,2},{1,3},{2,0},{3,1},{4,6},{5,7},{6,4},{7,5},{8,10},{9,11},{10,... | collective-permute-start | bytes 6193160 | tf_op jit(solution)/shard_map/ppermute | solution.py:147
  1138.3 43.2 %collective-permute-start.47 = (bf16[288,1024]{1,0:T(8,128)(2,1)}, bf16[288,1024]{1,0:T(8,128)(2,1)}, u32[]{:S(2)}, u32[]{:S(2)}) collective-permute-start(bf16[288,1024]{1,0:T(8,128)(2,1)} %get-tuple-element.80), channel_id=1, source_target_pairs={{0,4},{4,0},{8,12},{12,8},{16,20},{20,16},{24,28},{28,24},{1,5},{5... | collective-permute-start | bytes 1769480 | tf_op jit(solution)/shard_map/ppermute | solution.py:130
  (150 other events, 3623.4 us)

commit v2 on v0

v2 whole, which is shorter than its diff:
```python
from functools import partial

import jax
import jax.numpy as jnp
from jax import lax
from jax.experimental import pallas as pl
from jax.experimental.layout import Layout, with_layout_constraint
from jax.experimental.pallas import tpu as pltpu
from jax.sharding import PartitionSpec as P

HEADS = 8
KV_HEADS = 4
HEAD_DIM = 256
WINDOW = 4096
ADAM_STEP = 5


norm_eps = 1e-06
cap_value = 50.0
rope_base = 10000.0
learn_rate = 0.1
beta_one = 0.9
beta_two = 0.95
adam_eps = 1e-08
decay_rate = 0.1


low = jnp.bfloat16
wide = jnp.float32


def tie(tensor, *others):
    return lax.optimization_barrier((tensor,) + others)[0]


def plain(tensor):
    return with_layout_constraint(tensor, Layout(tuple(range(tensor.ndim))))


def ring_pairs(extent, hops=1):
    outer = extent // 2
    return [
        (2 * place + side, 2 * ((place + hops) % outer) + side)
        for place in range(outer)
        for side in range(2)
    ]


def swap_pairs(extent, stride):
    return [(place, place ^ stride) for place in range(extent)]


def rows_at(tensor, index, count):
    return lax.dynamic_slice_in_dim(tensor, index * count, count, 0)


def add(first, second, kind=low):
    return (first.astype(wide) + second.astype(wide)).astype(kind)


BLOCK = 64


def by_rows(body, side, rows, whole, outs, sums):
    length = rows[0].shape[0]

    def blocked(width):
        return pl.BlockSpec((BLOCK, width), lambda i: (i, 0))

    def kept(shape):
        return pl.BlockSpec(shape, lambda i: (0, 0))

    return pl.pallas_call(
        body,
        grid=(length // BLOCK,),
        in_specs=[pl.BlockSpec(memory_space=pltpu.SMEM)]
        + [blocked(t.shape[1]) for t in rows]
        + [kept(t.shape) for t in whole],
        out_specs=[blocked(width) for width, kind in outs] + [kept((1, width)) for width in sums],
        out_shape=[jax.ShapeDtypeStruct((length, width), kind) for width, kind in outs]
        + [jax.ShapeDtypeStruct((1, width), wide) for width in sums],
        compiler_params=pltpu.CompilerParams(vmem_limit_bytes=48 * 1024 * 1024),
    )(side, *rows, *whole)


def factor_of(value):
    return lax.rsqrt(jnp.mean(value * value, axis=-1, keepdims=True) + norm_eps)


def back_of(value, factor, gain, grad):
    scaled = grad * (1.0 + gain)
    shared = factor * factor * jnp.mean(scaled * value, axis=-1, keepdims=True)
    return factor * (scaled - shared * value), grad * (value * factor)


def add_up(ref, value):
    @pl.when(pl.program_id(0) == 0)
    def start():
        ref[...] = jnp.zeros_like(ref)

    ref[...] += jnp.sum(value, axis=0, keepdims=True)


def pieces_of(value, groups):
    count = value.shape[1] // groups
    return [value[:, k * count : (k + 1) * count] for k in range(groups)]


def turn(value, side, groups):
    cut = pieces_of(value, groups)
    even, odd = jnp.concatenate(cut[0::2], axis=1), jnp.concatenate(cut[1::2], axis=1)
    first, second = jnp.where(side == 0, even, odd), jnp.where(side == 0, odd, even)
    return jnp.concatenate([first, second], axis=1)


def straighten(value, side, groups):
    half = value.shape[1] // 2
    own, peer = value[:, :half], value[:, half:]
    even, odd = jnp.where(side == 0, own, peer), jnp.where(side == 0, peer, own)
    woven = zip(pieces_of(even, groups // 2), pieces_of(odd, groups // 2))
    return jnp.concatenate([cut for pair in woven for cut in pair], axis=1)


def start_body(groups, side, tokens, cotangent, valid, inputs, grad_out):
    inputs[...] = turn(tokens[...].astype(wide), side[0], groups).astype(low)
    grad_out[...] = turn(cotangent[...].astype(wide) * valid[...], side[0], groups).astype(low)


def normed_body(side, inputs, gains, normed):
    value = inputs[...].astype(wide)
    normed[...] = (value * factor_of(value) * (1.0 + gains[0:1])).astype(low)


def residual_of(inputs, attn, gains):
    value, mixed = inputs[...].astype(wide), attn[...].astype(wide)
    factor = factor_of(mixed)
    return value + mixed * factor * (1.0 + gains[1:2]), mixed, factor


def hidden_body(side, inputs, attn, gains, hidden):
    residual = residual_of(inputs, attn, gains)[0]
    hidden[...] = (residual * factor_of(residual) * (1.0 + gains[2:3])).astype(low)


def ffn_of(own, peer):
    return jnp.concatenate([own[...].astype(wide), peer[...].astype(wide)], axis=1)


def ffn_back_body(side, own, peer, grad_out, gains, grad_own, grad_peer, grad_gain):
    ffn = ffn_of(own, peer)
    grad, term = back_of(ffn, factor_of(ffn), gains[3:4], grad_out[...].astype(wide))
    half = ffn.shape[1] // 2
    grad_own[...] = grad[:, :half].astype(low)
    grad_peer[...] = grad[:, half:].astype(low)
    add_up(grad_gain, term)


def out_body(groups, side, inputs, attn, own, peer, gains, out):
    ffn = ffn_of(own, peer)
    value = residual_of(inputs, attn, gains)[0] + ffn * factor_of(ffn) * (1.0 + gains[3:4])
    out[...] = straighten(value, side[0], groups).astype(low)


def attn_back_body(side, inputs, attn, grad_hidden, grad_out, gains, grad_resid, grad_attn, gain1, gain2):
    residual, mixed, factor = residual_of(inputs, attn, gains)
    grad, term2 = back_of(residual, factor_of(residual), gains[2:3], grad_hidden[...].astype(wide))
    grad = grad + grad_out[...].astype(wide)
    grad_resid[...] = grad
    back, term1 = back_of(mixed, factor, gains[1:2], grad)
    grad_attn[...] = back.astype(low)
    add_up(gain1, term1)
    add_up(gain2, term2)


def in_back_body(groups, side, inputs, grad_normed, grad_resid, gains, input_grad, gain0):
    value = inputs[...].astype(wide)
    grad, term = back_of(value, factor_of(value), gains[0:1], grad_normed[...].astype(wide))
    input_grad[...] = straighten(grad_resid[...] + grad, side[0], groups)
    add_up(gain0, term)


def rotate(tensor, cosine, sine):
    half_dim = tensor.shape[-1] // 2
    first = tensor[..., :half_dim]
    second = tensor[..., half_dim:]
    return jnp.concatenate(
        [first * cosine - second * sine, second * cosine + first * sine], axis=-1
    )


def layout(labels):
    length = labels.shape[0]
    places = jnp.arange(length, dtype=jnp.int32)
    same_seq = labels[:, None] == labels[None, :]
    earlier = places[None, :] < places[:, None]
    position = jnp.sum((same_seq & earlier).astype(jnp.int32), axis=1)
    allowed = (
        same_seq
        & (places[None, :] <= places[:, None])
        & (places[:, None] - places[None, :] < WINDOW)
    )
    half_dim = HEAD_DIM // 2
    freq = rope_base ** (-2.0 * jnp.arange(half_dim, dtype=jnp.float32) / HEAD_DIM)
    angle = position.astype(jnp.float32)[:, None] * freq[None, :]
    return (allowed, jnp.cos(angle)[:, None, :], jnp.sin(angle)[:, None, :])


def scores(queries, key_rows, allowed):
    raw_scores = jnp.einsum("qkgd,skd->kgqs", queries, key_rows, preferred_element_type=jnp.float32)
    squashed = jnp.tanh(raw_scores / cap_value)
    capped = jnp.where(allowed[None, None], cap_value * squashed, -1e30)
    return (squashed, capped)


def rotate_back(grad_in, cosine, sine, shape_like):
    unused, pull = jax.vjp(lambda tensor: rotate(tensor, cosine, sine), shape_like)
    return pull(grad_in)[0]


def adam_step(master, gradient, moment, square, steps_done):
    new_moment = beta_one * moment + (1.0 - beta_one) * gradient
    new_square = beta_two * square + (1.0 - beta_two) * gradient * gradient
    fix_one = 1.0 - beta_one**steps_done
    fix_two = 1.0 - beta_two**steps_done
    stride = new_moment / fix_one / (jnp.sqrt(new_square / fix_two) + adam_eps)
    return (-learn_rate * (stride + decay_rate * master), new_moment, new_square)


def shards(
    tokens,
    segments,
    cotangent,
    query_weight,
    keyval_weight,
    output_weight,
    gateup_weight,
    down_weight,
    norm_gains,
    moment_query,
    moment_keyval,
    moment_output,
    moment_gateup,
    moment_down,
    moment_gains,
    square_query,
    square_keyval,
    square_output,
    square_gateup,
    square_down,
    square_gains,
):
    groups, parts = lax.axis_size("dp"), lax.axis_size("mp")
    outer = groups // 2
    index = lax.axis_index("dp")
    place = index // 2
    side = lax.rem(index, 2).astype(jnp.int32).reshape(1)
    length, features = tokens.shape
    half = features // 2
    count = features // groups
    group = HEADS // KV_HEADS
    width_q, width_kv = query_weight.shape[1], keyval_weight.shape[2]
    width_qkv = width_q + 2 * width_kv
    width_mixer = width_qkv + output_weight.shape[0]
    width_ff = down_weight.shape[0]
    kv_local = width_kv // HEAD_DIM
    heads_local = kv_local * group
    qscale = HEAD_DIM ** (-0.5)
    core = lax.rem(lax.axis_index("mp"), 2)
    paired = outer == 4 and parts == 4

    def dot(pattern, first, second):
        return jnp.einsum(pattern, first, second, preferred_element_type=wide)

    def around(tensor):
        return lax.ppermute(tensor, "dp", ring_pairs(groups))

    def swap(tensor):
        return lax.ppermute(tensor, "dp", swap_pairs(groups, 1))

    def near(tensor):
        return lax.ppermute(tensor, "mp", swap_pairs(parts, 1))

    def far(tensor):
        return lax.ppermute(tensor, "mp", swap_pairs(parts, 2))

    def apart(partial_sum):
        rows = length // 2
        return rows_at(partial_sum, 1 - core, rows), rows_at(partial_sum, core, rows)

    def together(mine, theirs):
        first = jnp.where(core == 0, mine, theirs)
        second = jnp.where(core == 0, theirs, mine)
        return jnp.concatenate([first, second], axis=0)

    allowed, cosine, sine = layout(segments)
    valid = (segments >= 0).astype(wide)[:, None]

    def projections(inputs, weights, gains):
        (normed_low,) = by_rows(normed_body, side, [inputs], [gains], [(features, low)], [])
        mixer_raw = dot("td,de->te", normed_low, weights[:, :width_qkv])
        qraw = mixer_raw[:, :width_q].reshape(length, heads_local, HEAD_DIM)
        kraw = mixer_raw[:, width_q : width_q + width_kv].reshape(length, kv_local, HEAD_DIM)
        queries = (
            (rotate(qraw, cosine, sine) * qscale).astype(low).reshape(length, kv_local, group, HEAD_DIM)
        )
        key_rows = rotate(kraw, cosine, sine).astype(low)
        value_rows = mixer_raw[:, width_q + width_kv :].astype(low).reshape(length, kv_local, HEAD_DIM)
        return normed_low, queries, key_rows, value_rows

    def attention(projected, weights):
        unused, queries, key_rows, value_rows = projected
        squashed, capped = scores(queries, key_rows, allowed)
        row_top = jnp.max(capped, axis=-1, keepdims=True)
        log_total = row_top + jnp.log(jnp.sum(jnp.exp(capped - row_top), axis=-1, keepdims=True))
        probs = jnp.exp(capped - log_total)
        probs_low = probs.astype(low)
        mixed_low = dot("kgqs,skd->qkgd", probs_low, value_rows).astype(low)
        mixed_low = mixed_low.reshape(length, heads_local * HEAD_DIM)
        attn_part = dot("te,de->td", mixed_low, weights[:, width_qkv:]).astype(low)
        return attn_part, projected + (squashed, probs, probs_low, mixed_low)

    def attention_back(grad_attn, weights, saved):
        normed_low, queries, key_rows, value_rows, squashed, probs, probs_low, mixed_low = saved
        grad_mixed = dot("td,de->te", grad_attn, weights[:, width_qkv:]).astype(low)
        grad_mixed = grad_mixed.reshape(length, kv_local, group, HEAD_DIM)
        grad_probs = dot("qkgd,skd->kgqs", grad_mixed, value_rows)
        grad_value = dot("kgqs,qkgd->skd", probs_low, grad_mixed)
        grad_value = grad_value.astype(low).reshape(length, kv_local * HEAD_DIM)
        grad_capped = probs * (grad_probs - jnp.sum(probs * grad_probs, axis=-1, keepdims=True))
        grad_scores = (grad_capped * (1.0 - squashed * squashed)).astype(low)
        grad_query = dot("kgqs,skd->qkgd", grad_scores, key_rows)
        grad_query = grad_query.reshape(length, heads_local, HEAD_DIM) * qscale
        shape_q = jnp.zeros((length, heads_local, HEAD_DIM), wide)
        grad_qraw = rotate_back(grad_query, cosine, sine, shape_q).astype(low)
        grad_key = dot("kgqs,qkgd->skd", grad_scores, queries)
        shape_k = jnp.zeros((length, kv_local, HEAD_DIM), wide)
        grad_kraw = rotate_back(grad_key, cosine, sine, shape_k).astype(low)
        flat = [t.reshape(length, -1) for t in (grad_qraw, grad_kraw, grad_value)]
        return plain(jnp.concatenate(flat, axis=1))

    def gated(gate_in, up_in):
        return jax.nn.gelu(gate_in, approximate=True) * up_in

    def weight_grad(first, second):
        return plain(dot("td,te->de", first, second).astype(low))

    def ffn_back(ffn_own, ffn_peer, grad_out, gains):
        return by_rows(
            ffn_back_body, side, [ffn_own, ffn_peer, grad_out], [gains], [(half, low)] * 2, [features]
        )

    def layer_out(inputs, attn_sum, ffn_own, ffn_peer, gains):
        rows = [inputs, attn_sum, ffn_own, ffn_peer]
        return by_rows(partial(out_body, groups), side, rows, [gains], [(features, low)], [])[0]

    def attn_back(inputs, attn_sum, grad_hidden, grad_out, gains):
        rows = [inputs, attn_sum, grad_hidden, grad_out]
        outs = [(features, wide), (features, low)]
        return by_rows(attn_back_body, side, rows, [gains], outs, [features] * 2)

    def in_back(inputs, grad_normed, grad_resid, gains):
        rows = [inputs, grad_normed, grad_resid]
        return by_rows(partial(in_back_body, groups), side, rows, [gains], [(features, wide)], [features])

    steps_done = float(ADAM_STEP)

    def updated(master, total, moment, square):
        return (total,) + adam_step(master, total, moment, square, steps_done)

    def update_gate_up(sums):
        return updated(gateup_weight, jnp.stack(sums), moment_gateup, square_gateup)

    def update_down(total):
        return updated(down_weight.T, total, moment_down.T, square_down.T)

    def update_mixer(total):
        total = plain(total)
        sum_k, sum_v = total[:, width_q : width_q + width_kv], total[:, width_q + width_kv : width_qkv]
        return (
            updated(query_weight, total[:, :width_q], moment_query, square_query),
            updated(keyval_weight, jnp.stack([sum_k, sum_v]), moment_keyval, square_keyval),
            updated(output_weight.T, total[:, width_qkv:], moment_output.T, square_output.T),
        )

    gain_row = norm_gains.astype(low).reshape(1, 4 * count)
    mixer = jnp.concatenate(
        [
            query_weight.astype(low),
            keyval_weight[0].astype(low),
            keyval_weight[1].astype(low),
            output_weight.astype(low).T,
        ],
        axis=1,
    )
    mixer = jnp.concatenate([mixer, jnp.pad(gain_row, ((0, 15), (0, width_mixer - 4 * count)))], axis=0)
    mixer = plain(mixer)

    def source(step):
        return lax.rem(place - step + outer, outer)

    def put(full, piece, step, offset=0):
        return lax.dynamic_update_slice_in_dim(full, piece, source(step) * count + offset, 0)

    def gains_of(held, peer):
        gain_low = jnp.zeros((2, outer, 4, count), low)
        for at, pieces in enumerate((held, peer)):
            for step, piece in enumerate(pieces):
                gain_piece = piece[count, : 4 * count].reshape(1, 1, 4, count)
                gain_low = lax.dynamic_update_slice(gain_low, gain_piece, (at, source(step), 0, 0))
        return jnp.moveaxis(gain_low.reshape(groups, 4, count), 1, 0).reshape(4, features).astype(wide)

    def start(tokens_in, cotangent_in):
        return by_rows(
            partial(start_body, groups), side, [tokens_in, cotangent_in, valid], [], [(features, low)] * 2, []
        )

    clock = [jnp.broadcast_to(valid[:8], (8, 128))]

    def sync(values):
        values, clock[0] = lax.optimization_barrier((values, clock[0]))
        return values

    always = index < groups

    def whole(work, *values):
        shapes = jax.eval_shape(work, *values)

        def blank(*unused):
            return jax.tree.map(lambda t: jnp.zeros(t.shape, t.dtype), shapes)

        return lax.cond(always, work, blank, *values)

    def behind(*values):
        values, clock[0] = lax.optimization_barrier((values, clock[0] * 0.5))
        return values

    gate, up = plain(gateup_weight[0].astype(low)), plain(gateup_weight[1].astype(low))
    down = plain(down_weight.astype(low).T)

    def down_part(act_low, weights):
        return dot("tf,df->td", act_low, weights).astype(low)

    def act_back(grad_own, grad_peer, gate_out, up_out, wd_own, wd_peer):
        grad_act = dot("td,df->tf", grad_own, wd_own) + dot("td,df->tf", grad_peer, wd_peer)
        unused, pull_act = jax.vjp(gated, gate_out, up_out)
        return tuple(grad.astype(low) for grad in pull_act(grad_act))

    def hidden_back(grad_gate, grad_up, wg, wu):
        return (dot("tf,df->td", grad_gate, wg) + dot("tf,df->td", grad_up, wu)).astype(low)

    def results(block_out, input_grad, new_mixer, new_gate_up, new_down, sum_gains):
        new_query, new_keyval, new_output = new_mixer
        new_gains = updated(norm_gains, sum_gains, moment_gains, square_gains)
        turned_back = [tuple(t.T for t in group_of) for group_of in (new_output, new_down)]
        new = (new_query, new_keyval, turned_back[0], new_gate_up, turned_back[1], new_gains)
        return (block_out, input_grad) + tuple(new[at][kind] for kind in range(4) for at in range(6))

    def simple():
        def gathered(own):
            rows = lax.all_gather(own, "dp", axis=0, tiled=True).reshape(outer, 2, -1, own.shape[1])
            return jnp.moveaxis(jnp.where(side == 0, rows, rows[:, ::-1]), 1, 0)

        def whole_rows(own):
            return gathered(own).reshape(features, own.shape[1])

        def scattered(rows):
            rows = rows.astype(wide).reshape(2, outer, count, rows.shape[1])
            rows = jnp.moveaxis(jnp.where(side == 0, rows, rows[::-1]), 0, 1).reshape(features, -1)
            return lax.psum_scatter(rows, "dp", scatter_dimension=0, tiled=True)

        def over_heads(part):
            return lax.psum(part.astype(wide), "mp").astype(low)

        rows = gathered(mixer)
        full = rows[:, :, :count].reshape(features, width_mixer)
        gains = jnp.moveaxis(rows[:, :, count, : 4 * count].reshape(groups, 4, count), 1, 0)
        gains = gains.reshape(4, features).astype(wide)
        wg, wu, wd = whole_rows(gate), whole_rows(up), whole_rows(down)
        inputs, grad_out = start(tokens, cotangent)
        attn_part, saved = attention(projections(inputs, full, gains), full)
        attn_sum = over_heads(attn_part)
        (hidden_in,) = by_rows(hidden_body, side, [inputs, attn_sum], [gains], [(features, low)], [])
        gate_out, up_out = dot("td,df->tf", hidden_in, wg), dot("td,df->tf", hidden_in, wu)
        act_low = gated(gate_out, up_out).astype(low)
        ffn = over_heads(down_part(act_low, wd))
        own, peer = ffn[:, :half], ffn[:, half:]
        block_out = layer_out(inputs, attn_sum, own, peer, gains)
        grad_own, grad_peer, gain3 = ffn_back(own, peer, grad_out, gains)
        grad_gate, grad_up = act_back(grad_own, grad_peer, gate_out, up_out, wd[:half], wd[half:])
        sum_down = scattered(weight_grad(jnp.concatenate([grad_own, grad_peer], axis=1), act_low))
        sums = [scattered(weight_grad(hidden_in, grad)) for grad in (grad_gate, grad_up)]
        grad_hidden = over_heads(hidden_back(grad_gate, grad_up, wg, wu))
        grad_resid, grad_attn, gain1, gain2 = attn_back(inputs, attn_sum, grad_hidden, grad_out, gains)
        grad_raw = attention_back(grad_attn, full, saved)
        grads = weight_grad(saved[0], grad_raw), weight_grad(grad_attn, saved[-1])
        sum_mixer = scattered(jnp.concatenate(grads, axis=1))
        grad_normed = over_heads(dot("te,de->td", grad_raw, full[:, :width_qkv]))
        input_grad, gain0 = in_back(inputs, grad_normed, grad_resid, gains)
        sum_gains = scattered(jnp.concatenate([gain0, gain1, gain2, gain3], axis=0).T).T
        return results(
            block_out, input_grad, update_mixer(sum_mixer), update_gate_up(sums), update_down(sum_down), sum_gains
        )

    if not paired:
        return simple()
    cut = count // 3 * 2

    m1, n0 = around(mixer), swap(mixer)
    inputs, grad_out = start(tokens, cotangent)
    m1, n0, mixer = sync((m1, n0, mixer))
    m2, n1 = around(m1), swap(m1)
    full = put(put(jnp.zeros((features, width_mixer), low), mixer[:count], 0), n0[:count], 0, half)
    wg, wu = jnp.zeros((features, width_ff), low), jnp.zeros((features, width_ff), low)
    m2, n1, m1, full, gate, up, wg, wu = sync((m2, n1, m1, full, gate, up, wg, wu))
    m3, n2 = around(m2), swap(m2)
    full = put(put(full, m1[:count], 1), n1[:count], 1, half)
    m3, n2, m2, full, gate, up, down = sync((m3, n2, m2, full, gate, up, down))
    g1, n3, down_far = around(gate), swap(m3), swap(down[cut:])
    full = put(put(full, m2[:count], 2), n2[:count], 2, half)
    wg = put(wg, gate, 0)
    wu = put(wu, up, 0)
    n3, m3, g1, down_far, full, gate, up, wg, wu, inputs, grad_out = sync(
        (n3, m3, g1, down_far, full, gate, up, wg, wu, inputs, grad_out)
    )
    u1, g2, h0, v0 = around(up), around(g1), swap(gate), swap(up)

    def attend(inputs, full, m3, n3, gains):
        full = put(put(full, m3[:count], 3), n3[:count], 3, half)
        attn_part, saved = attention(projections(inputs, full, gains), full)
        return apart(attn_part) + (saved, full)

    gains = gains_of((mixer, m1, m2, m3), (n0, n1, n2, n3))
    given, kept, saved, full = whole(attend, inputs, full, m3, n3, gains)
    given, kept, u1, g1, g2, v0, h0, saved, gains = sync((given, kept, u1, g1, g2, v0, h0, saved, gains))
    u2, g3, h1, v1 = around(u1), around(g2), swap(g1), swap(u1)
    kept = add(kept, near(given))
    across = far(kept)
    wg, wu, h0, v0, u1, g1 = behind(wg, wu, h0, v0, u1, g1)
    wg = put(put(wg, g1, 1), h0, 0, half)
    wu = put(put(wu, u1, 1), v0, 0, half)
    u2, g2, g3, h1, v1, across, kept, wg, wu, down = sync((u2, g2, g3, h1, v1, across, kept, wg, wu, down))
    u3, d1, h2, v2 = around(u2), around(down), swap(g2), swap(u2)
    mine = add(kept, across)
    attn_sum = together(mine, near(mine))
    (hidden_in,) = by_rows(hidden_body, side, [inputs, attn_sum], [gains], [(features, low)], [])
    wg = put(put(wg, g2, 2), h1, 1, half)
    wu = put(put(wu, u2, 2), v1, 1, half)
    u3, g3, d1, h2, v2, hidden_in, wg, wu = sync((u3, g3, d1, h2, v2, hidden_in, wg, wu))
    d2, h3, v3 = around(d1), swap(g3), swap(u3)
    wg, wu, h2, v2, u3, g3 = behind(wg, wu, h2, v2, u3, g3)
    wg = put(put(wg, g3, 3), h2, 2, half)
    wu = put(put(wu, u3, 3), v2, 2, half)
    wd_own = put(put(jnp.zeros((half, width_ff), low), down, 0), d1, 1)
    wd_peer = put(jnp.zeros((half, width_ff), low), down_far, 0, cut)
    d3 = around(d2)
    down_cut, d1_cut = down[:cut], d1[:cut]
    d2, d3, h3, v3, wg, wu, wd_own, wd_peer, down_cut, d1_cut, down_far = sync(
        (d2, d3, h3, v3, wg, wu, wd_own, wd_peer, down_cut, d1_cut, down_far)
    )
    f1, e0, e1 = around(down_far), swap(down_cut), swap(d1_cut)
    wg, wu, h3, v3 = behind(wg, wu, h3, v3)
    wg = put(wg, h3, 3, half)
    wu = put(wu, v3, 3, half)
    gate_out = dot("td,df->tf", hidden_in, wg)
    up_out = dot("td,df->tf", hidden_in, wu)
    act_low = gated(gate_out, up_out).astype(low)
    wd_own = put(put(wd_own, d2, 2), d3, 3)
    d2_cut, d3_cut = d2[:cut], d3[:cut]
    f1, e0, e1, act_low, wd_own, d2_cut, d3_cut = sync((f1, e0, e1, act_low, wd_own, d2_cut, d3_cut))
    f2, e2, e3 = around(f1), swap(d2_cut), swap(d3_cut)

    given, kept = apart(whole(down_part, act_low, wd_own))
    kept = add(kept, near(given))
    across = far(kept)
    wd_peer, f1, e0, e1, f2 = behind(wd_peer, f1, e0, e1, f2)
    f3 = around(f2)
    wd_peer = put(put(put(put(wd_peer, f1, 1, cut), f2, 2, cut), e0, 0), e1, 1)
    f3, e2, e3, across, kept, wd_peer = sync((f3, e2, e3, across, kept, wd_peer))
    wd_peer = put(put(put(wd_peer, f3, 3, cut), e2, 2), e3, 3)
    given, kept_peer = apart(down_part(act_low, wd_peer))
    mine = add(kept, across)
    kept_peer = add(kept_peer, near(given))
    ffn_own = together(mine, near(mine))
    across = far(kept_peer)
    mine = add(kept_peer, across)
    ffn_peer = together(mine, near(mine))

    def piece(tensor, hops):
        return rows_at(tensor, lax.rem(place + hops, outer), count)

    def plus(own, arrived, total=None, kind=low):
        both = own.astype(wide) + arrived.astype(wide)
        if total is not None:
            both = both + total.astype(wide)
        return both.astype(kind)

    def pieces(tensor):
        return [piece(tensor, hops) for hops in (3, 2, 1, 0)]

    def both(hops, offset, tensors):
        target = lax.rem(place + hops, outer) * count + offset
        cuts = [lax.dynamic_slice_in_dim(t, target, count, 0) for t in tensors]
        return plain(jnp.concatenate(cuts, axis=1))

    grad_ffn_own, grad_ffn_peer, grad_gain3 = ffn_back(ffn_own, ffn_peer, grad_out, gains)
    sent = pieces(weight_grad(grad_ffn_peer, act_low))
    far_parts = [given[cut:] for given in sent]
    sent = [given[:cut] for given in sent]
    sent, far_parts, grad_ffn_own, grad_ffn_peer = sync((sent, far_parts, grad_ffn_own, grad_ffn_peer))
    def grown(arrived):
        return jnp.pad(arrived, ((0, count - cut), (0, 0)))

    d3, d2, f3 = swap(sent[0]), swap(sent[1]), around(far_parts[0])

    def act_step(grad_own, grad_peer, gate_out, up_out, act_low, wd_own, wd_peer):
        back_of_act = act_back(grad_own, grad_peer, gate_out, up_out, wd_own, wd_peer)
        return back_of_act + (weight_grad(grad_own, act_low),)

    grad_gate, grad_up, wd_grad = whole(
        act_step, grad_ffn_own, grad_ffn_peer, gate_out, up_out, act_low, wd_own, wd_peer
    )
    d3, d2, f3, grad_gate, grad_up, wd_grad, sent[2:], far_parts[1:] = sync(
        (d3, d2, f3, grad_gate, grad_up, wd_grad, sent[2:], far_parts[1:])
    )
    d1, d0, f2 = swap(sent[2]), swap(sent[3]), around(add(far_parts[1], f3))
    came = around(plus(piece(wd_grad, 3), grown(d3)))

    def hidden_step(grad_gate, grad_up, hidden_in, wg, wu):
        given_kept = apart(hidden_back(grad_gate, grad_up, wg, wu))
        return given_kept + (pieces(weight_grad(hidden_in[:, half:], grad_gate)),)

    given, kept, gate_sent = whole(hidden_step, grad_gate, grad_up, hidden_in, wg, wu)
    d1, d0, f2, came, given, kept, gate_sent, grad_gate, grad_up = sync(
        (d1, d0, f2, came, given, kept, gate_sent, grad_gate, grad_up)
    )
    h3, theirs = swap(gate_sent[0]), near(given)
    came = around(plus(piece(wd_grad, 2), grown(d2), came))

    def rest_of_grads(grad_gate, grad_up, hidden_in):
        up_sent = pieces(weight_grad(hidden_in[:, half:], grad_up))
        wg_grad = weight_grad(hidden_in[:, :half], grad_gate)
        return up_sent, wg_grad, weight_grad(hidden_in[:, :half], grad_up)

    up_sent, wg_grad, wu_grad = whole(rest_of_grads, grad_gate, grad_up, hidden_in)
    h3, theirs, came, up_sent, wg_grad, wu_grad, gate_sent[1:], kept = sync(
        (h3, theirs, came, up_sent, wg_grad, wu_grad, gate_sent[1:], kept)
    )
    kept = add(kept, theirs)
    across, h2, v3 = far(kept), swap(gate_sent[1]), swap(up_sent[0])
    came = around(plus(piece(wd_grad, 1), grown(d1), came))
    gate_came = around(plus(piece(wg_grad, 3), h3))
    across, h2, v3, came, gate_came, kept, gate_sent[2:], up_sent[1:] = sync(
        (across, h2, v3, came, gate_came, kept, gate_sent[2:], up_sent[1:])
    )
    h1, h0 = swap(gate_sent[2]), swap(gate_sent[3])
    mine = add(kept, across)
    theirs = near(mine)
    gate_came = around(plus(piece(wg_grad, 2), h2, gate_came))
    up_came = around(plus(piece(wu_grad, 3), v3))

    def mixer_back(inputs, attn_sum, mine, theirs, grad_out, gains, full, saved):
        grad_hidden = together(mine, theirs)
        grad_resid, grad_attn, gain1, gain2 = attn_back(inputs, attn_sum, grad_hidden, grad_out, gains)
        grad_raw = attention_back(grad_attn, full, saved)
        given, kept = apart(dot("te,de->td", grad_raw, full[:, :width_qkv]).astype(low))
        return given, kept, grad_resid, grad_attn, gain1, gain2, grad_raw

    given, kept, grad_resid, grad_attn, grad_gain1, grad_gain2, grad_raw = whole(
        mixer_back, inputs, attn_sum, mine, theirs, grad_out, gains, full, saved
    )
    h1, h0, gate_came, up_came, given, kept, grad_resid, grad_attn, grad_raw, up_sent[1:], f2 = sync(
        (h1, h0, gate_came, up_came, given, kept, grad_resid, grad_attn, grad_raw, up_sent[1:], f2)
    )
    v2, v1, theirs = swap(up_sent[1]), swap(up_sent[2]), near(given)
    gate_came = around(plus(piece(wg_grad, 1), h1, gate_came))
    f1 = around(add(far_parts[2], f2))

    def mixer_grads(normed_low, mixed_low, grad_raw, grad_attn):
        grads = weight_grad(normed_low, grad_raw), weight_grad(grad_attn, mixed_low)
        pairs = ((3, 2), (1, 0))
        mixer_sent = [jnp.concatenate([both(hops, half, grads) for hops in pair], axis=0) for pair in pairs]
        return mixer_sent, [both(hops, 0, grads) for hops in (3, 2, 1, 0)]

    mixer_sent, mixer_own = whole(mixer_grads, saved[0], saved[-1], grad_raw, grad_attn)
    v2, v1, f1, theirs, gate_came, mixer_sent, mixer_own, kept, up_sent[3] = sync(
        (v2, v1, f1, theirs, gate_came, mixer_sent, mixer_own, kept, up_sent[3])
    )
    kept = add(kept, theirs)
    across, v0, x32 = far(kept), swap(up_sent[3]), swap(mixer_sent[0])
    up_came = around(plus(piece(wu_grad, 2), v2, up_came))
    up_came = around(plus(piece(wu_grad, 1), v1, up_came))
    v0, x32, up_came, across, kept, mixer_sent[1], inputs, f1 = sync(
        (v0, x32, up_came, across, kept, mixer_sent[1], inputs, f1)
    )
    x10, b_far = swap(mixer_sent[1]), swap(add(far_parts[3], f1))
    mine = add(kept, across)
    theirs = near(mine)
    passed = around(plus(mixer_own[0], x32[:count]))

    def finish(inputs, mine, theirs, grad_resid, attn_sum, ffn_own, ffn_peer, gains):
        block_out = layer_out(inputs, attn_sum, ffn_own, ffn_peer, gains)
        input_grad, gain0 = in_back(inputs, together(mine, theirs), grad_resid, gains)
        return block_out, input_grad, gain0

    block_out, input_grad, grad_gain0 = whole(
        finish, inputs, mine, theirs, grad_resid, attn_sum, ffn_own, ffn_peer, gains
    )
    x10, b_far, passed, block_out, input_grad, grad_gain0, x32 = sync(
        (x10, b_far, passed, block_out, input_grad, grad_gain0, x32)
    )
    passed = around(plus(mixer_own[1], x32[count:], passed))
    grad_gains = jnp.concatenate([grad_gain0, grad_gain1, grad_gain2, grad_gain3], axis=0)
    gain_sum = grad_gains[:, :half] + swap(grad_gains[:, half:])
    gain_sum = gain_sum.reshape(4, outer, count)
    down_total = plus(piece(wd_grad, 0), jnp.concatenate([d0, b_far], axis=0), came, wide)
    new_down = update_down(behind(down_total)[0])
    sum_gate = plus(piece(wg_grad, 0), h0, gate_came, wide)
    sum_up = plus(piece(wu_grad, 0), v0, up_came, wide)
    new_gate_up = update_gate_up([sum_gate, sum_up])
    passed, gain_sum, new_down, new_gate_up = sync((passed, gain_sum, new_down, new_gate_up))
    passed = around(plus(mixer_own[2], x10[:count], passed))
    sum_gains = lax.dynamic_index_in_dim(gain_sum, place, 1, False)
    for hops in (1, 2, 3):
        given = lax.dynamic_index_in_dim(gain_sum, lax.rem(place + hops, outer), 1, False)
        sum_gains = sum_gains + lax.ppermute(given, "dp", ring_pairs(groups, hops))
    new_mixer = update_mixer(plus(mixer_own[3], x10[count:], passed, wide))
    return results(block_out, input_grad, new_mixer, new_gate_up, new_down, sum_gains)


def solution(mesh):
    return jax.shard_map(
        shards,
        mesh=mesh,
        in_specs=(
            P("dp", None),
            P("dp"),
            P("dp", None),
            P("dp", "mp"),
            P(None, "dp", "mp"),
            P("mp", "dp"),
            P(None, "dp", "mp"),
            P("mp", "dp"),
            P(None, "dp"),
            P("dp", "mp"),
            P(None, "dp", "mp"),
            P("mp", "dp"),
            P(None, "dp", "mp"),
            P("mp", "dp"),
            P(None, "dp"),
            P("dp", "mp"),
            P(None, "dp", "mp"),
            P("mp", "dp"),
            P(None, "dp", "mp"),
            P("mp", "dp"),
            P(None, "dp"),
        ),
        out_specs=(
            P("dp", None),
            P("dp", None),
            P("dp", "mp"),
            P(None, "dp", "mp"),
            P("mp", "dp"),
            P(None, "dp", "mp"),
            P("mp", "dp"),
            P(None, "dp"),
            P("dp", "mp"),
            P(None, "dp", "mp"),
            P("mp", "dp"),
            P(None, "dp", "mp"),
            P("mp", "dp"),
            P(None, "dp"),
            P("dp", "mp"),
            P(None, "dp", "mp"),
            P("mp", "dp"),
            P(None, "dp", "mp"),
            P("mp", "dp"),
            P(None, "dp"),
            P("dp", "mp"),
            P(None, "dp", "mp"),
            P("mp", "dp"),
            P(None, "dp", "mp"),
            P("mp", "dp"),
            P(None, "dp"),
        ),
        check_vma=False,
    )
```

time: 2850 us -> 1060 us (0.37)
  waiting for transfers between devices: 2400 us -> 422 us
  local copies, waits for them, and re-layouts: 21.1 us -> 135 us
  Pallas kernels: 0 us -> 75.7 us
  starting transfers between devices: 1.21 us -> 73.7 us
  blocking collectives: 32.3 us -> 0 us
    reduce_scatter x5 -> x0, waiting for transfers between devices: 1270 us -> none  [the longest x1 670 us: shards(): lax.psum_scatter(grad_wgu, 'dp', scatter_dimension=1, tiled=True)]
    all_gather x5 -> x0, waiting for transfers between devices: 600 us -> none  [the longest x1 393 us: shards(): lax.all_gather(low_gateup, 'dp', axis=1, tiled=True)]
    psum x4 -> x0, waiting for transfers between devices: 527 us -> none  [the longest x1 151 us: shards(): grad_hidden = lax.psum(hidden_part, 'mp')]
    ppermute x0 -> x81, waiting for transfers between devices: none -> 422 us  [the longest x30 209 us: around(): return lax.ppermute(tensor, 'dp', ring_pairs(groups))]
    pallas_call x0 -> x7, Pallas kernels: none -> 75.7 us  [by_rows(): pl.pallas_call(body, grid=(length // BLOCK,), in_specs=[pl.BlockSpec(memo...]
    ppermute x0 -> x81, starting transfers between devices: none -> 73.7 us  [the longest x33 34.8 us: swap(): return lax.ppermute(tensor, 'dp', swap_pairs(groups, 1))]
    dynamic_update_slice x0 -> x43, local copies, waits for them, and re-layouts: none -> 52.7 us  [the longest x35 52.1 us: put(): lax.dynamic_update_slice_in_dim(full, piece, source(step) * count + offse...]
    reduce_sum x9 -> x1, other arithmetic: 49.9 us -> 1.47 us  [attention(): jnp.sum(jnp.exp(capped - row_top), axis=-1, keepdims=True)]
  transfers between devices with their start and end apart: 15 -> 81, of which waited for: 14 -> 35; matrix products, arithmetic and copies ran while one was open for 8% -> 37% of each run, Pallas kernels for 0% -> 6%
where the time goes in v2:
time: 1060 us; the launch traced here: 1050 us
  waiting for transfers between devices  422 us (40%)
  matrix products  210 us (20%)
  local copies, waits for them, and re-layouts  135 us (13%)
  other arithmetic  131 us (12%)
  Pallas kernels  75.7 us (7%)
  starting transfers between devices  73.7 us (7%)
    ppermute x30, waiting for transfers between devices, around(): return lax.ppermute(tensor, 'dp', ring_pairs(groups))  209 us
    dot_general x25, matrix products, dot(): return jnp.einsum(pattern, first, second, preferred_element_type=wide)  208 us
    ppermute x33, waiting for transfers between devices, swap(): return lax.ppermute(tensor, 'dp', swap_pairs(groups, 1))  162 us
    pallas_call x7, Pallas kernels, by_rows(): pl.pallas_call(body, grid=(length // BLOCK,), in_specs=[pl.BlockSpec(memo...  75.7 us
    dynamic_update_slice x35, local copies, waits for them, and re-layouts, put(): lax.dynamic_update_slice_in_dim(full, piece, source(step) * count + offse...  52.1 us
    ppermute x33, starting transfers between devices, swap(): return lax.ppermute(tensor, 'dp', swap_pairs(groups, 1))  34.8 us
    convert_element_type x12, other arithmetic, plus(): return both.astype(kind)  31.6 us
    ppermute x30, starting transfers between devices, around(): return lax.ppermute(tensor, 'dp', ring_pairs(groups))  29.2 us
  transfers between devices with their start and end apart: 81, of which 35 were waited for; matrix products, arithmetic and copies ran while one was open for 37% of the time, Pallas kernels for 6%

profile of v2, /device:TPU:0, one launch (start us, length us, event | category | flops | bytes accessed | tf_op | source)
XLA Modules:
  0.0 1050.0 jit_solution(3275405474579884280)
XLA Ops:
  18.3 11.3 %shard_map.404 = (bf16[896,2304]{1,0:T(8,128)(2,1)}, bf16[896,2304]{1,0:T(8,128)(2,1)}) custom-call(s32[1]{0:T(128)} %bitcast.51.side, bf16[896,2304]{1,0:T(8,128)(2,1)S(1)} %copy-done, bf16[896,2304]{1,0:T(8,128)(2,1)} %cotangent.1, f32[896,1]{1,0:T(8,128)S(1)} %broadcast_in_dim.19.valid), custom_call_target="tpu_custom_call" | custom-call | tf_op jit(solution)/shard_map/pallas_call | solution.py:73
  39.9 13.6 %collective-permute-done.3 = bf16[304,1536]{1,0:T(8,128)(2,1)S(1)} collective-permute-done((bf16[304,1536]{1,0:T(8,128)(2,1)}, bf16[304,1536]{1,0:T(8,128)(2,1)S(1)}, u32[]{:S(2)}, u32[]{:S(2)}) %collective-permute-start.3) | collective-permute-done | bytes 933920 | tf_op jit(solution)/shard_map/ppermute | solution.py:278
  61.8 9.8 copy.135
  92.0 15.3 %collective-permute-done.6 = bf16[304,1536]{1,0:T(8,128)(2,1)S(1)} collective-permute-done((bf16[304,1536]{1,0:T(8,128)(2,1)S(1)}, bf16[304,1536]{1,0:T(8,128)(2,1)S(1)}, u32[]{:S(2)}, u32[]{:S(2)}) %collective-permute-start.6) | collective-permute-done | bytes 933920 | tf_op jit(solution)/shard_map/ppermute | solution.py:278
  122.9 45.6 %conditional.8 = (bf16[448,2304]{1,0:T(8,128)(2,1)S(1)}, bf16[448,2304]{1,0:T(8,128)(2,1)S(1)}, bf16[896,2304]{1,0:T(8,128)(2,1)}, bf16[896,1,2,256]{3,0,2,1:T(8...) conditional(s32[]{:T(128)} %convert_element_type.467, ...), branch_computations={%region_1.2_spmd, %region_2.5_spmd} | conditional | flops 8018638848 | bytes 196019904 | solution.py:431
  122.9 8.5 branch_1_fun.5
  191.8 44.8 %collective-permute-done.14 = bf16[288,2304]{1,0:T(8,128)(2,1)S(1)} collective-permute-done((bf16[288,2304]{1,0:T(8,128)(2,1)}, bf16[288,2304]{1,0:T(8,128)(2,1)S(1)}, u32[]{:S(2)}, u32[]{:S(2)}) %collective-permute-start.14) | collective-permute-done | bytes 1327136 | tf_op jit(solution)/shard_map/ppermute | solution.py:275
  255.4 8.1 shard_map.405
  263.5 37.0 %collective-permute-done.21 = bf16[288,2304]{1,0:T(8,128)(2,1)} collective-permute-done((bf16[288,2304]{1,0:T(8,128)(2,1)}, bf16[288,2304]{1,0:T(8,128)(2,1)}, u32[]{:S(2)}, u32[]{:S(2)}) %collective-permute-start.21) | collective-permute-done | bytes 1327136 | tf_op jit(solution)/shard_map/ppermute | solution.py:278
  311.0 25.1 %collective-permute-done.24 = bf16[288,2304]{1,0:T(8,128)(2,1)S(1)} collective-permute-done((bf16[288,2304]{1,0:T(8,128)(2,1)}, bf16[288,2304]{1,0:T(8,128)(2,1)S(1)}, u32[]{:S(2)}, u32[]{:S(2)}) %collective-permute-start.24) | collective-permute-done | bytes 1327136 | tf_op jit(solution)/shard_map/ppermute | solution.py:275
  346.8 19.5 %collective-permute-done.27 = bf16[288,2304]{1,0:T(8,128)(2,1)S(1)} collective-permute-done((bf16[288,2304]{1,0:T(8,128)(2,1)}, bf16[288,2304]{1,0:T(8,128)(2,1)S(1)}, u32[]{:S(2)}, u32[]{:S(2)}) %collective-permute-start.27) | collective-permute-done | bytes 1327136 | tf_op jit(solution)/shard_map/ppermute | solution.py:278
  371.7 13.7 %fusion.94 = f32[896,2304]{1,0:T(8,128)} fusion(bf16[896,2304]{1,0:T(8,128)(2,1)S(1)} %copy-done.31, bf16[2304,2304]{1,0:T(8,128)(2,1)} %constant_dynamic-update-slice_fusion.10), kind=kOutput, calls=%fused_computation.303 | convolution fusion | flops 9512681472 | bytes 23003136 | tf_op jit(solution)/shard_map/td,df->tf/dot_general | solution.py:272
  385.3 16.9 %fusion.67 = (bf16[896,2304]{1,0:T(8,128)(2,1)}, f32[896,2304]{1,0:T(8,128)}) fusion(f32[896,2304]{1,0:T(8,128)} %fusion.94, bf16[896,2304]{1,0:T(8,128)(2,1)S(1)} %copy-done.31, bf16[2304,2304]{1,0:T(8,128)(2,1)} %constant_dynamic-update-slice_fusion.9), kind=kOutput, calls=%fused_computation.144 | convolution fusion | flops 9533325312 | bytes 35389440 | tf_op jit(solution)/shard_map/td,df->tf/dot_general | solution.py:272
  417.7 12.8 %collective-permute-done.31 = bf16[96,2304]{1,0:T(8,128)(2,1)} collective-permute-done((bf16[96,2304]{1,0:T(8,128)(2,1)}, bf16[96,2304]{1,0:T(8,128)(2,1)}, u32[]{:S(2)}, u32[]{:S(2)}) %collective-permute-start.31) | collective-permute-done | bytes 442400 | tf_op jit(solution)/shard_map/ppermute | solution.py:275
  444.9 11.9 %collective-permute-done.34 = bf16[192,2304]{1,0:T(8,128)(2,1)S(1)} collective-permute-done((bf16[192,2304]{1,0:T(8,128)(2,1)}, bf16[192,2304]{1,0:T(8,128)(2,1)S(1)}, u32[]{:S(2)}, u32[]{:S(2)}) %collective-permute-start.34) | collective-permute-done | bytes 884768 | tf_op jit(solution)/shard_map/ppermute | solution.py:278
  460.4 8.3 convolution_convert_fusion.11
  472.5 24.2 %collective-permute-done.39 = bf16[448,1152]{1,0:T(8,128)(2,1)S(1)} collective-permute-done((bf16[448,1152]{1,0:T(8,128)(2,1)S(1)}, bf16[448,1152]{1,0:T(8,128)(2,1)S(1)}, u32[]{:S(2)}, u32[]{:S(2)}) %collective-permute-start.39) | collective-permute-done | bytes 1032224 | tf_op jit(solution)/shard_map/ppermute | solution.py:284
  501.6 7.5 shard_map.406
  509.1 8.4 convolution_convert_fusion.10
  525.2 36.1 %conditional.10 = (bf16[896,2304]{1,0:T(8,128)(2,1)}, bf16[896,2304]{1,0:T(8,128)(2,1)}, bf16[1152,2304]{1,0:T(8,128)(2,1)S(1)}) conditional(s32[]{:T(128)} %convert_element_type.467, () %tuple.130, (bf16[896,1152]{1,0:T(8,128)(2,1)S(1)}, bf16[1152,2304]{1,0:T(8,128)(2,1)S(1)}, bf16[896,1152]{1,0:T(8,128)(2,1)S(1)}, bf16[1152,2304]{1,0:T(8,128)(2,1)}, ...), branch_computations={%region_7.8_spmd, %region_8.9_spmd} | conditional | flops 14323286016 | bytes 113541264 | solution.py:431
  527.2 7.7 fusion.92
  534.9 18.1 %multiply_convert_fusion = (bf16[896,2304]{1,0:T(8,128)(2,1)}, bf16[896,2304]{1,0:T(8,128)(2,1)}) fusion(f32[896,2304]{1,0:T(8,128)} %get-tuple-element.192, f32[896,2304]{1,0:T(8,128)} %get-tuple-element.191, f32[896,2304]{1,0:T(8,128)} %fusion.92, bf16[896,1152]{1,0:T(8,128)(2,1)} %copy-done.92, bf16[1152,2304]{1,0:T(8,128)(2,1)S(1)} %copy-done.30), kind=kOutput, calls=%fused_computation.50 | convolution fusion | flops 4807950336 | bytes 40402944 | tf_op jit(solution)/shard_map/cond/branch_1_fun/td,df->tf/dot_general | solution.py:272
  553.0 8.3 convolution_convert_fusion.2
  572.2 46.0 %conditional.11 = (bf16[448,2304]{1,0:T(8,128)(2,1)}, bf16[448,2304]{1,0:T(8,128)(2,1)S(1)}, bf16[288,2304]{1,0:T(8,128)(2,1)}, bf16[288,2304]{1,0:T(8,128)(2,1)...) conditional(s32[]{:T(128)} %convert_element_type.467, () %tuple.133, (bf16[896,2304]{1,0:T(8,128)(2,1)}, ...), branch_computations={%region_9.10_spmd, %region_10.11_spmd} | conditional | flops 23788486656 | bytes 97026736 | solution.py:431
  572.2 15.0 %fusion.93 = f32[896,2304]{1,0:T(8,128)} fusion(bf16[896,2304]{1,0:T(8,128)(2,1)} %get-tuple-element.194, bf16[2304,2304]{1,0:T(8,128)(2,1)} %get-tuple-element.195), kind=kOutput, calls=%fused_computation.302 | convolution fusion | flops 9512681472 | bytes 23003136 | tf_op jit(solution)/shard_map/cond/branch_1_fun/tf,df->td/dot_general | solution.py:272
  587.2 17.2 %add_convert_fusion.1 = bf16[896,2304]{1,0:T(8,128)(2,1)} fusion(f32[896,2304]{1,0:T(8,128)} %fusion.93, bf16[896,2304]{1,0:T(8,128)(2,1)} %get-tuple-element.196, bf16[2304,2304]{1,0:T(8,128)(2,1)} %get-tuple-element.197), kind=kOutput, calls=%fused_computation.53 | convolution fusion | flops 9516810240 | bytes 27131904 | tf_op jit(solution)/shard_map/cond/branch_1_fun/tf,df->td/dot_general | solution.py:272
  604.3 8.6 convolution_convert_fusion.3
  624.2 30.6 %conditional.12 = (bf16[288,2304]{1,0:T(8,128)(2,1)}, bf16[288,2304]{1,0:T(8,128)(2,1)}, bf16[288,2304]{1,0:T(8,128)(2,1)}, bf16[288,2304]{1,0:T(8,128)(2,1)}, b...) conditional(s32[]{:T(128)} %convert_element_type.467, () %tuple.136, (bf16[896,2304]{1,0:T(8,128)(2,1)}, ...), branch_computations={%region_11.12_spmd, %region_12.13_spmd} | conditional | flops 14276984832 | bytes 61637152 | solution.py:431
  624.2 10.3 convolution_convert_fusion.5
  634.5 9.5 convolution_convert_fusion.4
  644.0 8.3 convolution_convert_fusion.6
  667.3 24.3 %collective-permute-done.55 = bf16[288,2304]{1,0:T(8,128)(2,1)S(1)} collective-permute-done((bf16[288,2304]{1,0:T(8,128)(2,1)S(1)}, bf16[288,2304]{1,0:T(8,128)(2,1)S(1)}, u32[]{:S(2)}, u32[]{:S(2)}) %collective-permute-start.55) | collective-permute-done | bytes 1327136 | tf_op jit(solution)/shard_map/ppermute | solution.py:275
  691.6 26.0 %collective-permute-done.54 = bf16[288,2304]{1,0:T(8,128)(2,1)S(1)} collective-permute-done((bf16[288,2304]{1,0:T(8,128)(2,1)S(1)}, bf16[288,2304]{1,0:T(8,128)(2,1)S(1)}, u32[]{:S(2)}, u32[]{:S(2)}) %collective-permute-start.54) | collective-permute-done | bytes 1327136 | tf_op jit(solution)/shard_map/ppermute | solution.py:275
  734.8 59.2 %conditional.13 = (bf16[448,2304]{1,0:T(8,128)(2,1)}, bf16[448,2304]{1,0:T(8,128)(2,1)}, f32[896,2304]{1,0:T(8,128)}, bf16[896,2304]{1,0:T(8,128)(2,1)}, f32[1,2...) conditional(s32[]{:T(128)} %convert_element_type.467, () %tuple.140, (s32[]{:T(128)}, ...), branch_computations={%region_13.14_spmd, %region_14.16_spmd} | conditional | flops 9665787904 | bytes 197016160 | solution.py:431
  743.0 13.9 %branch_1_fun.6 = (f32[896,2304]{1,0:T(8,128)}, bf16[896,2304]{1,0:T(8,128)(2,1)}, f32[1,2304]{1,0:T(1,128)}, f32[1,2304]{1,0:T(1,128)}) custom-call(s32[1]{0:T(128)} %get-tuple-element.206.side, bf16[896,2304]{1,0:T(8,128)(2,1)S(1)} %copy-done.2, bf16[896,2304]{1,0:T(8,128)(2,1)S(1)} %copy-done.6, bf16[896,2304]{1,0:T(8,128)(2,1)S(1)} %pad_maximum_fusion.1.grad_hidden, ...), custom_call_target="tpu_custom_call" | custom-call | tf_op jit(solution)/shard_map/cond/branch_1_fun/pallas_call | solution.py:73
  769.4 7.7 fusion.37
  784.3 7.4 convolution_convert_fusion.7
  804.5 22.7 %conditional.14 = (bf16[576,1536]{1,0:T(8,128)(2,1)}, bf16[576,1536]{1,0:T(8,128)(2,1)}, bf16[288,1536]{1,0:T(8,128)(2,1)S(1)}, bf16[288,1536]{1,0:T(8,128)(2,1)...) conditional(s32[]{:T(128)} %convert_element_type.467, () %tuple.143, ...), branch_computations={%region_16.17_spmd, %region_17.18_spmd} | conditional | flops 6366560256 | bytes 62915356 | solution.py:431
  827.2 13.6 %collective-permute-done.63 = bf16[96,2304]{1,0:T(8,128)(2,1)} collective-permute-done((bf16[96,2304]{1,0:T(8,128)(2,1)}, bf16[96,2304]{1,0:T(8,128)(2,1)}, u32[]{:S(2)}, u32[]{:S(2)}) %collective-permute-start.63) | collective-permute-done | bytes 442400 | tf_op jit(solution)/shard_map/ppermute | solution.py:275
  840.9 17.8 %collective-permute-done.62 = bf16[288,2304]{1,0:T(8,128)(2,1)} collective-permute-done((bf16[288,2304]{1,0:T(8,128)(2,1)}, bf16[288,2304]{1,0:T(8,128)(2,1)}, u32[]{:S(2)}, u32[]{:S(2)}) %collective-permute-start.62) | collective-permute-done | bytes 1327136 | tf_op jit(solution)/shard_map/ppermute | solution.py:278
  868.7 24.8 %collective-permute-done.68 = bf16[288,2304]{1,0:T(8,128)(2,1)S(1)} collective-permute-done((bf16[288,2304]{1,0:T(8,128)(2,1)S(1)}, bf16[288,2304]{1,0:T(8,128)(2,1)S(1)}, u32[]{:S(2)}, u32[]{:S(2)}) %collective-permute-start.68) | collective-permute-done | bytes 1327136 | tf_op jit(solution)/shard_map/ppermute | solution.py:275
  898.6 32.9 %collective-permute-done.67 = bf16[576,1536]{1,0:T(8,128)(2,1)S(1)} collective-permute-done((bf16[576,1536]{1,0:T(8,128)(2,1)}, bf16[576,1536]{1,0:T(8,128)(2,1)S(1)}, u32[]{:S(2)}, u32[]{:S(2)}) %collective-permute-start.67) | collective-permute-done | bytes 1769504 | tf_op jit(solution)/shard_map/ppermute | solution.py:278
  941.0 12.2 %add_multiply_fusion = (f32[2,288,2304]{2,1,0:T(8,128)}, f32[2,288,2304]{2,1,0:T(8,128)}, f32[2,288,2304]{2,1,0:T(8,128)}, f32[2,288,2304]{2,1,0:T(8,128)}) fusion(f32[2,288,2304]{2,1,0:T(8,128)S(1)} %bitcast.229, f32[1,288,2304]{2,1,0:T(8,128)S(1)} %add_bitcast_fusion, f32[1,288,2304]{2,1,0:T(8,128)S(1)} %add_bitcast_fusion.1, f32[2,288,2304]{2,1,0:T(8,128)} %param.49, ...), kind=kLoop, calls=%fused_computation.148 | loop fusion | flops 19906560 | bytes 42467328 | tf_op jit(solution)/shard_map/mul | solution.py:226
  953.2 31.1 %conditional.15 = (bf16[896,2304]{1,0:T(8,128)(2,1)}, f32[896,2304]{1,0:T(8,128)}, f32[1,2304]{1,0:T(1,128)}) conditional(s32[]{:T(128)} %convert_element_type.467, () %tuple.147, (s32[1]{0:T(128)}, bf16[896,2304]{1,0:T(8,128)(2,1)}, bf16[896,2304]{1,0:T(8,128)(2,1)}, bf16[896,1152]{1,0:T(8,128)(2,1)S(1)}, bf16[896,1152]{1,0:T(8,128)(2,1)}, ...), branch_computations={%region_18.19_spmd, %region_19.20_spmd} | conditional | flops 10321921 | bytes 33030206 | solution.py:431
  953.2 12.7 %branch_1_fun.7 = bf16[896,2304]{1,0:T(8,128)(2,1)} custom-call(s32[1]{0:T(128)} %get-tuple-element.231.side, bf16[896,2304]{1,0:T(8,128)(2,1)} %get-tuple-element.232.inputs, bf16[896,2304]{1,0:T(8,128)(2,1)} %get-tuple-element.233.attn, bf16[896,1152]{1,0:T(8,128)(2,1)S(1)} %get-tuple-element.234.own, bf16[896,1152]{1,0:T(8,128)(2,1)} %get-tuple-element.235.peer, ...), custom_call_target="tpu_custom_call" | custom-call | tf_op jit(solution)/shard_map/cond/branch_1_fun/pallas_call | solution.py:73
  970.6 13.7 %branch_1_fun.8 = (f32[896,2304]{1,0:T(8,128)}, f32[1,2304]{1,0:T(1,128)}) custom-call(s32[1]{0:T(128)} %get-tuple-element.231.side, bf16[896,2304]{1,0:T(8,128)(2,1)S(1)} %copy-done.3, bf16[896,2304]{1,0:T(8,128)(2,1)S(1)} %pad_maximum_fusion.7.grad_normed, f32[896,2304]{1,0:T(8,128)} %get-tuple-element.240.grad_resid, f32[4,2304]{1,0:T(4,128)S(1)} %get-tuple-element.236.gains), custom_call_target="tpu_custom_call" | custom-call | tf_op jit(solution)/shard_map/cond/branch_1_fun/pallas_call | solution.py:73
  998.1 17.9 %collective-permute-done.75 = bf16[288,1536]{1,0:T(8,128)(2,1)} collective-permute-done((bf16[288,1536]{1,0:T(8,128)(2,1)}, bf16[288,1536]{1,0:T(8,128)(2,1)}, u32[]{:S(2)}, u32[]{:S(2)}) %collective-permute-start.75) | collective-permute-done | bytes 884768 | tf_op jit(solution)/shard_map/ppermute | solution.py:275
  1023.3 18.0 %collective-permute-done.78 = f32[4,288]{1,0:T(4,128)S(1)} collective-permute-done((f32[4,288]{1,0:T(4,128)S(1)}, f32[4,288]{1,0:T(4,128)S(1)}, u32[]{:S(2)}, u32[]{:S(2)}) %collective-permute-start.78) | collective-permute-done | bytes 4640 | tf_op jit(solution)/shard_map/ppermute | solution.py:725
  (535 shorter events, 412.4 us)
Async XLA Ops:
  109.8 58.7 %collective-permute-start.11 = (bf16[288,2304]{1,0:T(8,128)(2,1)}, bf16[288,2304]{1,0:T(8,128)(2,1)}, u32[]{:S(2)}, u32[]{:S(2)}) collective-permute-start(bf16[288,2304]{1,0:T(8,128)(2,1)} %get-tuple-element.571), channel_id=1, source_target_pairs={{0,4},{4,0},{8,12},{12,8},{16,20},{20,16},{24,28},{28,24},{1,5},{5... | collective-permute-start | bytes 3981320 | tf_op jit(solution)/shard_map/ppermute | solution.py:278
  111.0 57.5 %collective-permute-start.9 = (bf16[288,2304]{1,0:T(8,128)(2,1)}, bf16[288,2304]{1,0:T(8,128)(2,1)}, u32[]{:S(2)}, u32[]{:S(2)}) collective-permute-start(bf16[288,2304]{1,0:T(8,128)(2,1)} %get-tuple-element.571), channel_id=1, source_target_pairs={{0,8},{4,12},{8,16},{12,20},{16,24},{20,28},{24,0},{28,4},{1,9},{5... | collective-permute-start | bytes 3981320 | tf_op jit(solution)/shard_map/ppermute | solution.py:275
  111.0 57.4 %collective-permute-start.12 = (bf16[288,2304]{1,0:T(8,128)(2,1)}, bf16[288,2304]{1,0:T(8,128)(2,1)}, u32[]{:S(2)}, u32[]{:S(2)}) collective-permute-start(bf16[288,2304]{1,0:T(8,128)(2,1)} %get-tuple-element.573), channel_id=1, source_target_pairs={{0,4},{4,0},{8,12},{12,8},{16,20},{20,16},{24,28},{28,24},{1,5},{5... | collective-permute-start | bytes 3981320 | tf_op jit(solution)/shard_map/ppermute | solution.py:278
  111.8 56.7 %collective-permute-start.10 = (bf16[288,2304]{1,0:T(8,128)(2,1)}, bf16[288,2304]{1,0:T(8,128)(2,1)}, u32[]{:S(2)}, u32[]{:S(2)}) collective-permute-start(bf16[288,2304]{1,0:T(8,128)(2,1)} %collective-permute-done.7), channel_id=1, source_target_pairs={{0,8},{4,12},{8,16},{12,20},{16,24},{20,28},{24,0},{28,4},{1,9},{5... | collective-permute-start | bytes 3981320 | tf_op jit(solution)/shard_map/ppermute | solution.py:275
  173.3 66.4 %collective-permute-start.18 = (bf16[448,2304]{1,0:T(8,128)(2,1)S(1)}, bf16[448,2304]{1,0:T(8,128)(2,1)S(1)}, u32[]{:S(2)}, u32[]{:S(2)}) collective-permute-start(bf16[448,2304]{1,0:T(8,128)(2,1)S(1)} %add_convert_fusion.9), channel_id=1, source_target_pairs={{0,2},{1,3},{2,0},{3,1},{4,6},{5,7},{6,4},{7,5},{8,10},{9,11},{10,... | collective-permute-start | bytes 6193160 | tf_op jit(solution)/shard_map/ppermute | solution.py:284
  175.0 61.7 %collective-permute-start.16 = (bf16[288,2304]{1,0:T(8,128)(2,1)}, bf16[288,2304]{1,0:T(8,128)(2,1)S(1)}, u32[]{:S(2)}, u32[]{:S(2)}) collective-permute-start(bf16[288,2304]{1,0:T(8,128)(2,1)} %collective-permute-done.9), channel_id=1, source_target_pairs={{0,4},{4,0},{8,12},{12,8},{16,20},{20,16},{24,28},{28,24},{1,5},{5... | collective-permute-start | bytes 3981320 | tf_op jit(solution)/shard_map/ppermute | solution.py:278
  175.3 61.3 %collective-permute-start.13 = (bf16[288,2304]{1,0:T(8,128)(2,1)}, bf16[288,2304]{1,0:T(8,128)(2,1)S(1)}, u32[]{:S(2)}, u32[]{:S(2)}) collective-permute-start(bf16[288,2304]{1,0:T(8,128)(2,1)} %collective-permute-done.9), channel_id=1, source_target_pairs={{0,8},{4,12},{8,16},{12,20},{16,24},{20,28},{24,0},{28,4},{1,9},{5... | collective-permute-start | bytes 3981320 | tf_op jit(solution)/shard_map/ppermute | solution.py:275
  176.0 60.7 %collective-permute-start.15 = (bf16[288,2304]{1,0:T(8,128)(2,1)}, bf16[288,2304]{1,0:T(8,128)(2,1)S(1)}, u32[]{:S(2)}, u32[]{:S(2)}) collective-permute-start(bf16[288,2304]{1,0:T(8,128)(2,1)} %collective-permute-done.7), channel_id=1, source_target_pairs={{0,4},{4,0},{8,12},{12,8},{16,20},{20,16},{24,28},{28,24},{1,5},{5... | collective-permute-start | bytes 3981320 | tf_op jit(solution)/shard_map/ppermute | solution.py:278
  177.9 58.7 %collective-permute-start.14 = (bf16[288,2304]{1,0:T(8,128)(2,1)}, bf16[288,2304]{1,0:T(8,128)(2,1)S(1)}, u32[]{:S(2)}, u32[]{:S(2)}) collective-permute-start(bf16[288,2304]{1,0:T(8,128)(2,1)} %collective-permute-done.10), channel_id=1, source_target_pairs={{0,8},{4,12},{8,16},{12,20},{16,24},{20,28},{24,0},{28,4},{1,9},{5... | collective-permute-start | bytes 3981320 | tf_op jit(solution)/shard_map/ppermute | solution.py:275
  240.2 60.3 %collective-permute-start.22 = (bf16[288,2304]{1,0:T(8,128)(2,1)}, bf16[288,2304]{1,0:T(8,128)(2,1)}, u32[]{:S(2)}, u32[]{:S(2)}) collective-permute-start(bf16[288,2304]{1,0:T(8,128)(2,1)} %copy-done.60), channel_id=1, source_target_pairs={{0,4},{4,0},{8,12},{12,8},{16,20},{20,16},{24,28},{28,24},{1,5},{5... | collective-permute-start | bytes 3981320 | tf_op jit(solution)/shard_map/ppermute | solution.py:278
  242.0 58.5 %collective-permute-start.19 = (bf16[288,2304]{1,0:T(8,128)(2,1)}, bf16[288,2304]{1,0:T(8,128)(2,1)}, u32[]{:S(2)}, u32[]{:S(2)}) collective-permute-start(bf16[288,2304]{1,0:T(8,128)(2,1)} %copy-done.60), channel_id=1, source_target_pairs={{0,8},{4,12},{8,16},{12,20},{16,24},{20,28},{24,0},{28,4},{1,9},{5... | collective-permute-start | bytes 3981320 | tf_op jit(solution)/shard_map/ppermute | solution.py:275
  242.4 58.1 %collective-permute-start.21 = (bf16[288,2304]{1,0:T(8,128)(2,1)}, bf16[288,2304]{1,0:T(8,128)(2,1)}, u32[]{:S(2)}, u32[]{:S(2)}) collective-permute-start(bf16[288,2304]{1,0:T(8,128)(2,1)} %collective-permute-done.10), channel_id=1, source_target_pairs={{0,4},{4,0},{8,12},{12,8},{16,20},{20,16},{24,28},{28,24},{1,5},{5... | collective-permute-start | bytes 3981320 | tf_op jit(solution)/shard_map/ppermute | solution.py:278
  242.8 60.9 %collective-permute-start.20 = (bf16[288,2304]{1,0:T(8,128)(2,1)S(1)}, bf16[288,2304]{1,0:T(8,128)(2,1)}, u32[]{:S(2)}, u32[]{:S(2)}) collective-permute-start(bf16[288,2304]{1,0:T(8,128)(2,1)S(1)} %copy-done.15), channel_id=1, source_target_pairs={{0,8},{4,12},{8,16},{12,20},{16,24},{20,28},{24,0},{28,4},{1,9},{5... | collective-permute-start | bytes 3981320 | tf_op jit(solution)/shard_map/ppermute | solution.py:275
  307.5 39.3 %collective-permute-start.26 = (bf16[288,2304]{1,0:T(8,128)(2,1)S(1)}, bf16[288,2304]{1,0:T(8,128)(2,1)S(1)}, u32[]{:S(2)}, u32[]{:S(2)}) collective-permute-start(bf16[288,2304]{1,0:T(8,128)(2,1)S(1)} %copy-done.59), channel_id=1, source_target_pairs={{0,4},{4,0},{8,12},{12,8},{16,20},{20,16},{24,28},{28,24},{1,5},{5... | collective-permute-start | bytes 3981320 | tf_op jit(solution)/shard_map/ppermute | solution.py:278
  307.8 58.5 %collective-permute-start.27 = (bf16[288,2304]{1,0:T(8,128)(2,1)}, bf16[288,2304]{1,0:T(8,128)(2,1)S(1)}, u32[]{:S(2)}, u32[]{:S(2)}) collective-permute-start(bf16[288,2304]{1,0:T(8,128)(2,1)} %collective-permute-done.19), channel_id=1, source_target_pairs={{0,4},{4,0},{8,12},{12,8},{16,20},{20,16},{24,28},{28,24},{1,5},{5... | collective-permute-start | bytes 3981320 | tf_op jit(solution)/shard_map/ppermute | solution.py:278
  367.3 37.1 %collective-permute-start.28 = (bf16[96,2304]{1,0:T(8,128)(2,1)S(1)}, bf16[96,2304]{1,0:T(8,128)(2,1)S(1)}, u32[]{:S(2)}, u32[]{:S(2)}) collective-permute-start(bf16[96,2304]{1,0:T(8,128)(2,1)S(1)} %copy-done.83), channel_id=1, source_target_pairs={{0,8},{4,12},{8,16},{12,20},{16,24},{20,28},{24,0},{28,4},{1,9},{5... | collective-permute-start | bytes 1327112 | tf_op jit(solution)/shard_map/ppermute | solution.py:275
  367.3 37.2 %collective-permute-start.29 = (bf16[192,2304]{1,0:T(8,128)(2,1)}, bf16[192,2304]{1,0:T(8,128)(2,1)S(1)}, u32[]{:S(2)}, u32[]{:S(2)}) collective-permute-start(bf16[192,2304]{1,0:T(8,128)(2,1)} %slice.212), channel_id=1, source_target_pairs={{0,4},{4,0},{8,12},{12,8},{16,20},{20,16},{24,28},{28,24},{1,5},{5... | collective-permute-start | bytes 2654216 | tf_op jit(solution)/shard_map/ppermute | solution.py:278
  367.7 38.0 %collective-permute-start.30 = (bf16[192,2304]{1,0:T(8,128)(2,1)}, bf16[192,2304]{1,0:T(8,128)(2,1)}, u32[]{:S(2)}, u32[]{:S(2)}) collective-permute-start(bf16[192,2304]{1,0:T(8,128)(2,1)} %slice.213), channel_id=1, source_target_pairs={{0,4},{4,0},{8,12},{12,8},{16,20},{20,16},{24,28},{28,24},{1,5},{5... | collective-permute-start | bytes 2654216 | tf_op jit(solution)/shard_map/ppermute | solution.py:278
  416.3 40.5 %collective-permute-start.34 = (bf16[192,2304]{1,0:T(8,128)(2,1)}, bf16[192,2304]{1,0:T(8,128)(2,1)S(1)}, u32[]{:S(2)}, u32[]{:S(2)}) collective-permute-start(bf16[192,2304]{1,0:T(8,128)(2,1)} %slice.215), channel_id=1, source_target_pairs={{0,4},{4,0},{8,12},{12,8},{16,20},{20,16},{24,28},{28,24},{1,5},{5... | collective-permute-start | bytes 2654216 | tf_op jit(solution)/shard_map/ppermute | solution.py:278
  520.5 40.8 %collective-permute-start.41 = (bf16[192,2304]{1,0:T(8,128)(2,1)}, bf16[192,2304]{1,0:T(8,128)(2,1)}, u32[]{:S(2)}, u32[]{:S(2)}) collective-permute-start(bf16[192,2304]{1,0:T(8,128)(2,1)} %get-tuple-element.666), channel_id=1, source_target_pairs={{0,4},{4,0},{8,12},{12,8},{16,20},{20,16},{24,28},{28,24},{1,5},{5... | collective-permute-start | bytes 2654216 | tf_op jit(solution)/shard_map/ppermute | solution.py:278
  520.8 41.0 %collective-permute-start.42 = (bf16[192,2304]{1,0:T(8,128)(2,1)}, bf16[192,2304]{1,0:T(8,128)(2,1)}, u32[]{:S(2)}, u32[]{:S(2)}) collective-permute-start(bf16[192,2304]{1,0:T(8,128)(2,1)} %get-tuple-element.667), channel_id=1, source_target_pairs={{0,4},{4,0},{8,12},{12,8},{16,20},{20,16},{24,28},{28,24},{1,5},{5... | collective-permute-start | bytes 2654216 | tf_op jit(solution)/shard_map/ppermute | solution.py:278
  522.5 38.8 %collective-permute-start.43 = (bf16[96,2304]{1,0:T(8,128)(2,1)}, bf16[96,2304]{1,0:T(8,128)(2,1)}, u32[]{:S(2)}, u32[]{:S(2)}) collective-permute-start(bf16[96,2304]{1,0:T(8,128)(2,1)} %get-tuple-element.668), channel_id=1, source_target_pairs={{0,8},{4,12},{8,16},{12,20},{16,24},{20,28},{24,0},{28,4},{1,9},{5... | collective-permute-start | bytes 1327112 | tf_op jit(solution)/shard_map/ppermute | solution.py:275
  564.9 53.2 %collective-permute-start.47 = (bf16[288,2304]{1,0:T(8,128)(2,1)}, bf16[288,2304]{1,0:T(8,128)(2,1)}, u32[]{:S(2)}, u32[]{:S(2)}) collective-permute-start(bf16[288,2304]{1,0:T(8,128)(2,1)} %add_convert_fusion.18), channel_id=1, source_target_pairs={{0,8},{4,12},{8,16},{12,20},{16,24},{20,28},{24,0},{28,4},{1,9},{5... | collective-permute-start | bytes 3981320 | tf_op jit(solution)/shard_map/ppermute | solution.py:275
  566.8 51.3 %collective-permute-start.44 = (bf16[192,2304]{1,0:T(8,128)(2,1)}, bf16[192,2304]{1,0:T(8,128)(2,1)}, u32[]{:S(2)}, u32[]{:S(2)}) collective-permute-start(bf16[192,2304]{1,0:T(8,128)(2,1)} %get-tuple-element.679), channel_id=1, source_target_pairs={{0,4},{4,0},{8,12},{12,8},{16,20},{20,16},{24,28},{28,24},{1,5},{5... | collective-permute-start | bytes 2654216 | tf_op jit(solution)/shard_map/ppermute | solution.py:278
  567.1 51.0 %collective-permute-start.45 = (bf16[192,2304]{1,0:T(8,128)(2,1)}, bf16[192,2304]{1,0:T(8,128)(2,1)}, u32[]{:S(2)}, u32[]{:S(2)}) collective-permute-start(bf16[192,2304]{1,0:T(8,128)(2,1)} %get-tuple-element.680), channel_id=1, source_target_pairs={{0,4},{4,0},{8,12},{12,8},{16,20},{20,16},{24,28},{28,24},{1,5},{5... | collective-permute-start | bytes 2654216 | tf_op jit(solution)/shard_map/ppermute | solution.py:278
  570.7 47.4 %collective-permute-start.46 = (bf16[96,2304]{1,0:T(8,128)(2,1)}, bf16[96,2304]{1,0:T(8,128)(2,1)}, u32[]{:S(2)}, u32[]{:S(2)}) collective-permute-start(bf16[96,2304]{1,0:T(8,128)(2,1)} %add_convert_fusion.28), channel_id=1, source_target_pairs={{0,8},{4,12},{8,16},{12,20},{16,24},{20,28},{24,0},{28,4},{1,9},{5... | collective-permute-start | bytes 1327112 | tf_op jit(solution)/shard_map/ppermute | solution.py:275
  618.2 37.5 %collective-permute-start.49 = (bf16[448,2304]{1,0:T(8,128)(2,1)}, bf16[448,2304]{1,0:T(8,128)(2,1)}, u32[]{:S(2)}, u32[]{:S(2)}) collective-permute-start(bf16[448,2304]{1,0:T(8,128)(2,1)} %get-tuple-element.694), channel_id=1, source_target_pairs={{0,1},{1,0},{2,3},{3,2},{4,5},{5,4},{6,7},{7,6},{8,9},{9,8},{10,11... | collective-permute-start | bytes 6193160 | tf_op jit(solution)/shard_map/ppermute | solution.py:281
  657.7 33.9 %collective-permute-start.55 = (bf16[288,2304]{1,0:T(8,128)(2,1)S(1)}, bf16[288,2304]{1,0:T(8,128)(2,1)S(1)}, u32[]{:S(2)}, u32[]{:S(2)}) collective-permute-start(bf16[288,2304]{1,0:T(8,128)(2,1)S(1)} %add_convert_fusion.15), channel_id=1, source_target_pairs={{0,8},{4,12},{8,16},{12,20},{16,24},{20,28},{24,0},{28,4},{1,9},{5... | collective-permute-start | bytes 3981320 | tf_op jit(solution)/shard_map/ppermute | solution.py:275
  660.0 62.9 %collective-permute-start.51 = (bf16[448,2304]{1,0:T(8,128)(2,1)S(1)}, bf16[448,2304]{1,0:T(8,128)(2,1)S(1)}, u32[]{:S(2)}, u32[]{:S(2)}) collective-permute-start(bf16[448,2304]{1,0:T(8,128)(2,1)S(1)} %add_convert_fusion.7), channel_id=1, source_target_pairs={{0,2},{1,3},{2,0},{3,1},{4,6},{5,7},{6,4},{7,5},{8,10},{9,11},{10,... | collective-permute-start | bytes 6193160 | tf_op jit(solution)/shard_map/ppermute | solution.py:284
  663.4 54.2 %collective-permute-start.54 = (bf16[288,2304]{1,0:T(8,128)(2,1)S(1)}, bf16[288,2304]{1,0:T(8,128)(2,1)S(1)}, u32[]{:S(2)}, u32[]{:S(2)}) collective-permute-start(bf16[288,2304]{1,0:T(8,128)(2,1)S(1)} %add_convert_fusion.16), channel_id=1, source_target_pairs={{0,8},{4,12},{8,16},{12,20},{16,24},{20,28},{24,0},{28,4},{1,9},{5... | collective-permute-start | bytes 3981320 | tf_op jit(solution)/shard_map/ppermute | solution.py:275
  665.3 52.3 %collective-permute-start.52 = (bf16[288,2304]{1,0:T(8,128)(2,1)S(1)}, bf16[288,2304]{1,0:T(8,128)(2,1)S(1)}, u32[]{:S(2)}, u32[]{:S(2)}) collective-permute-start(bf16[288,2304]{1,0:T(8,128)(2,1)S(1)} %copy-done.57), channel_id=1, source_target_pairs={{0,4},{4,0},{8,12},{12,8},{16,20},{20,16},{24,28},{28,24},{1,5},{5... | collective-permute-start | bytes 3981320 | tf_op jit(solution)/shard_map/ppermute | solution.py:278
  666.1 56.8 %collective-permute-start.53 = (bf16[288,2304]{1,0:T(8,128)(2,1)}, bf16[288,2304]{1,0:T(8,128)(2,1)S(1)}, u32[]{:S(2)}, u32[]{:S(2)}) collective-permute-start(bf16[288,2304]{1,0:T(8,128)(2,1)} %get-tuple-element.712), channel_id=1, source_target_pairs={{0,4},{4,0},{8,12},{12,8},{16,20},{20,16},{24,28},{28,24},{1,5},{5... | collective-permute-start | bytes 3981320 | tf_op jit(solution)/shard_map/ppermute | solution.py:278
  725.8 68.2 %collective-permute-start.58 = (bf16[288,2304]{1,0:T(8,128)(2,1)}, bf16[288,2304]{1,0:T(8,128)(2,1)}, u32[]{:S(2)}, u32[]{:S(2)}) collective-permute-start(bf16[288,2304]{1,0:T(8,128)(2,1)} %add_convert_fusion.14), channel_id=1, source_target_pairs={{0,8},{4,12},{8,16},{12,20},{16,24},{20,28},{24,0},{28,4},{1,9},{5... | collective-permute-start | bytes 3981320 | tf_op jit(solution)/shard_map/ppermute | solution.py:275
  731.7 62.3 %collective-permute-start.59 = (bf16[288,2304]{1,0:T(8,128)(2,1)}, bf16[288,2304]{1,0:T(8,128)(2,1)}, u32[]{:S(2)}, u32[]{:S(2)}) collective-permute-start(bf16[288,2304]{1,0:T(8,128)(2,1)} %add_convert_fusion.13), channel_id=1, source_target_pairs={{0,8},{4,12},{8,16},{12,20},{16,24},{20,28},{24,0},{28,4},{1,9},{5... | collective-permute-start | bytes 3981320 | tf_op jit(solution)/shard_map/ppermute | solution.py:275
  732.7 61.3 %collective-permute-start.56 = (bf16[288,2304]{1,0:T(8,128)(2,1)}, bf16[288,2304]{1,0:T(8,128)(2,1)}, u32[]{:S(2)}, u32[]{:S(2)}) collective-permute-start(bf16[288,2304]{1,0:T(8,128)(2,1)} %get-tuple-element.722), channel_id=1, source_target_pairs={{0,4},{4,0},{8,12},{12,8},{16,20},{20,16},{24,28},{28,24},{1,5},{5... | collective-permute-start | bytes 3981320 | tf_op jit(solution)/shard_map/ppermute | solution.py:278
  733.6 60.4 %collective-permute-start.57 = (bf16[288,2304]{1,0:T(8,128)(2,1)}, bf16[288,2304]{1,0:T(8,128)(2,1)}, u32[]{:S(2)}, u32[]{:S(2)}) collective-permute-start(bf16[288,2304]{1,0:T(8,128)(2,1)} %get-tuple-element.723), channel_id=1, source_target_pairs={{0,4},{4,0},{8,12},{12,8},{16,20},{20,16},{24,28},{28,24},{1,5},{5... | collective-permute-start | bytes 3981320 | tf_op jit(solution)/shard_map/ppermute | solution.py:278
  794.0 64.7 %collective-permute-start.64 = (bf16[448,2304]{1,0:T(8,128)(2,1)}, bf16[448,2304]{1,0:T(8,128)(2,1)}, u32[]{:S(2)}, u32[]{:S(2)}) collective-permute-start(bf16[448,2304]{1,0:T(8,128)(2,1)} %get-tuple-element.750), channel_id=1, source_target_pairs={{0,1},{1,0},{2,3},{3,2},{4,5},{5,4},{6,7},{7,6},{8,9},{9,8},{10,11... | collective-permute-start | bytes 6193160 | tf_op jit(solution)/shard_map/ppermute | solution.py:281
  797.8 43.1 %collective-permute-start.65 = (bf16[288,2304]{1,0:T(8,128)(2,1)}, bf16[288,2304]{1,0:T(8,128)(2,1)}, u32[]{:S(2)}, u32[]{:S(2)}) collective-permute-start(bf16[288,2304]{1,0:T(8,128)(2,1)} %add_convert_fusion.12), channel_id=1, source_target_pairs={{0,8},{4,12},{8,16},{12,20},{16,24},{20,28},{24,0},{28,4},{1,9},{5... | collective-permute-start | bytes 3981320 | tf_op jit(solution)/shard_map/ppermute | solution.py:275
  798.7 42.1 %collective-permute-start.61 = (bf16[288,2304]{1,0:T(8,128)(2,1)}, bf16[288,2304]{1,0:T(8,128)(2,1)}, u32[]{:S(2)}, u32[]{:S(2)}) collective-permute-start(bf16[288,2304]{1,0:T(8,128)(2,1)} %get-tuple-element.746), channel_id=1, source_target_pairs={{0,4},{4,0},{8,12},{12,8},{16,20},{20,16},{24,28},{28,24},{1,5},{5... | collective-permute-start | bytes 3981320 | tf_op jit(solution)/shard_map/ppermute | solution.py:278
  799.6 59.1 %collective-permute-start.62 = (bf16[288,2304]{1,0:T(8,128)(2,1)}, bf16[288,2304]{1,0:T(8,128)(2,1)}, u32[]{:S(2)}, u32[]{:S(2)}) collective-permute-start(bf16[288,2304]{1,0:T(8,128)(2,1)} %get-tuple-element.747), channel_id=1, source_target_pairs={{0,4},{4,0},{8,12},{12,8},{16,20},{20,16},{24,28},{28,24},{1,5},{5... | collective-permute-start | bytes 3981320 | tf_op jit(solution)/shard_map/ppermute | solution.py:278
  802.6 38.2 %collective-permute-start.63 = (bf16[96,2304]{1,0:T(8,128)(2,1)}, bf16[96,2304]{1,0:T(8,128)(2,1)}, u32[]{:S(2)}, u32[]{:S(2)}) collective-permute-start(bf16[96,2304]{1,0:T(8,128)(2,1)} %add_convert_fusion.27), channel_id=1, source_target_pairs={{0,8},{4,12},{8,16},{12,20},{16,24},{20,28},{24,0},{28,4},{1,9},{5... | collective-permute-start | bytes 1327112 | tf_op jit(solution)/shard_map/ppermute | solution.py:275
  863.2 35.3 %collective-permute-start.66 = (bf16[288,2304]{1,0:T(8,128)(2,1)}, bf16[288,2304]{1,0:T(8,128)(2,1)S(1)}, u32[]{:S(2)}, u32[]{:S(2)}) collective-permute-start(bf16[288,2304]{1,0:T(8,128)(2,1)} %get-tuple-element.765), channel_id=1, source_target_pairs={{0,4},{4,0},{8,12},{12,8},{16,20},{20,16},{24,28},{28,24},{1,5},{5... | collective-permute-start | bytes 3981320 | tf_op jit(solution)/shard_map/ppermute | solution.py:278
  864.1 67.4 %collective-permute-start.67 = (bf16[576,1536]{1,0:T(8,128)(2,1)}, bf16[576,1536]{1,0:T(8,128)(2,1)S(1)}, u32[]{:S(2)}, u32[]{:S(2)}) collective-permute-start(bf16[576,1536]{1,0:T(8,128)(2,1)} %get-tuple-element.766), channel_id=1, source_target_pairs={{0,4},{4,0},{8,12},{12,8},{16,20},{20,16},{24,28},{28,24},{1,5},{5... | collective-permute-start | bytes 5308424 | tf_op jit(solution)/shard_map/ppermute | solution.py:278
  867.9 63.5 %collective-permute-start.70 = (bf16[448,2304]{1,0:T(8,128)(2,1)S(1)}, bf16[448,2304]{1,0:T(8,128)(2,1)S(1)}, u32[]{:S(2)}, u32[]{:S(2)}) collective-permute-start(bf16[448,2304]{1,0:T(8,128)(2,1)S(1)} %add_convert_fusion.5), channel_id=1, source_target_pairs={{0,2},{1,3},{2,0},{3,1},{4,6},{5,7},{6,4},{7,5},{8,10},{9,11},{10,... | collective-permute-start | bytes 6193160 | tf_op jit(solution)/shard_map/ppermute | solution.py:284
  895.7 35.7 %collective-permute-start.69 = (bf16[288,2304]{1,0:T(8,128)(2,1)S(1)}, bf16[288,2304]{1,0:T(8,128)(2,1)S(1)}, u32[]{:S(2)}, u32[]{:S(2)}) collective-permute-start(bf16[288,2304]{1,0:T(8,128)(2,1)S(1)} %add_convert_fusion.10), channel_id=1, source_target_pairs={{0,8},{4,12},{8,16},{12,20},{16,24},{20,28},{24,0},{28,4},{1,9},{5... | collective-permute-start | bytes 3981320 | tf_op jit(solution)/shard_map/ppermute | solution.py:275
  933.0 51.3 %collective-permute-start.72 = (bf16[96,2304]{1,0:T(8,128)(2,1)S(1)}, bf16[96,2304]{1,0:T(8,128)(2,1)}, u32[]{:S(2)}, u32[]{:S(2)}) collective-permute-start(bf16[96,2304]{1,0:T(8,128)(2,1)S(1)} %add_convert_fusion.26), channel_id=1, source_target_pairs={{0,4},{4,0},{8,12},{12,8},{16,20},{20,16},{24,28},{28,24},{1,5},{5... | collective-permute-start | bytes 1327112 | tf_op jit(solution)/shard_map/ppermute | solution.py:278
  935.0 49.3 %collective-permute-start.73 = (bf16[288,1536]{1,0:T(8,128)(2,1)}, bf16[288,1536]{1,0:T(8,128)(2,1)}, u32[]{:S(2)}, u32[]{:S(2)}) collective-permute-start(bf16[288,1536]{1,0:T(8,128)(2,1)} %add_convert_fusion.25), channel_id=1, source_target_pairs={{0,8},{4,12},{8,16},{12,20},{16,24},{20,28},{24,0},{28,4},{1,9},{5... | collective-permute-start | bytes 2654216 | tf_op jit(solution)/shard_map/ppermute | solution.py:275
  936.3 48.0 %collective-permute-start.71 = (bf16[576,1536]{1,0:T(8,128)(2,1)}, bf16[576,1536]{1,0:T(8,128)(2,1)}, u32[]{:S(2)}, u32[]{:S(2)}) collective-permute-start(bf16[576,1536]{1,0:T(8,128)(2,1)} %get-tuple-element.774), channel_id=1, source_target_pairs={{0,4},{4,0},{8,12},{12,8},{16,20},{20,16},{24,28},{28,24},{1,5},{5... | collective-permute-start | bytes 5308424 | tf_op jit(solution)/shard_map/ppermute | solution.py:278
  (133 other events, 2310.1 us)

commit v3 on v2

--- a/solution.py
+++ b/solution.py
@@ -58,7 +58,7 @@
     return (first.astype(wide) + second.astype(wide)).astype(kind)
 
 
-BLOCK = 64
+BLOCK = 128
 
 
 def by_rows(body, side, rows, whole, outs, sums):
@@ -271,8 +271,8 @@
     def dot(pattern, first, second):
         return jnp.einsum(pattern, first, second, preferred_element_type=wide)
 
-    def around(tensor):
-        return lax.ppermute(tensor, "dp", ring_pairs(groups))
+    def around(tensor, hops=1):
+        return lax.ppermute(tensor, "dp", ring_pairs(groups, hops))
 
     def swap(tensor):
         return lax.ppermute(tensor, "dp", swap_pairs(groups, 1))
@@ -503,7 +503,7 @@
 
     if not paired:
         return simple()
-    cut = count // 3 * 2
+    cut = count // 2
 
     m1, n0 = around(mixer), swap(mixer)
     inputs, grad_out = start(tokens, cotangent)
@@ -511,7 +511,9 @@
     m2, n1 = around(m1), swap(m1)
     full = put(put(jnp.zeros((features, width_mixer), low), mixer[:count], 0), n0[:count], 0, half)
     wg, wu = jnp.zeros((features, width_ff), low), jnp.zeros((features, width_ff), low)
-    m2, n1, m1, full, gate, up, wg, wu = sync((m2, n1, m1, full, gate, up, wg, wu))
+    m2, n1, m1, full, gate, up, wg, wu, allowed, cosine, sine = sync(
+        (m2, n1, m1, full, gate, up, wg, wu, allowed, cosine, sine)
+    )
     m3, n2 = around(m2), swap(m2)
     full = put(put(full, m1[:count], 1), n1[:count], 1, half)
     m3, n2, m2, full, gate, up, down = sync((m3, n2, m2, full, gate, up, down))
@@ -546,34 +548,34 @@
     wg = put(put(wg, g2, 2), h1, 1, half)
     wu = put(put(wu, u2, 2), v1, 1, half)
     u3, g3, d1, h2, v2, hidden_in, wg, wu = sync((u3, g3, d1, h2, v2, hidden_in, wg, wu))
-    d2, h3, v3 = around(d1), swap(g3), swap(u3)
+    d2, h3 = around(d1), swap(g3)
+    v3 = swap(tie(u3, h3))
     wg, wu, h2, v2, u3, g3 = behind(wg, wu, h2, v2, u3, g3)
     wg = put(put(wg, g3, 3), h2, 2, half)
     wu = put(put(wu, u3, 3), v2, 2, half)
     wd_own = put(put(jnp.zeros((half, width_ff), low), down, 0), d1, 1)
     wd_peer = put(jnp.zeros((half, width_ff), low), down_far, 0, cut)
     d3 = around(d2)
+    wg = put(wg, h3, 3, half)
+    gate_out = dot("td,df->tf", hidden_in, wg)
     down_cut, d1_cut = down[:cut], d1[:cut]
-    d2, d3, h3, v3, wg, wu, wd_own, wd_peer, down_cut, d1_cut, down_far = sync(
-        (d2, d3, h3, v3, wg, wu, wd_own, wd_peer, down_cut, d1_cut, down_far)
+    d2, d3, v3, wg, gate_out, wu, wd_own, wd_peer, down_cut, d1_cut, down_far = sync(
+        (d2, d3, v3, wg, gate_out, wu, wd_own, wd_peer, down_cut, d1_cut, down_far)
     )
     f1, e0, e1 = around(down_far), swap(down_cut), swap(d1_cut)
-    wg, wu, h3, v3 = behind(wg, wu, h3, v3)
-    wg = put(wg, h3, 3, half)
+    wu, v3 = behind(wu, v3)
     wu = put(wu, v3, 3, half)
-    gate_out = dot("td,df->tf", hidden_in, wg)
     up_out = dot("td,df->tf", hidden_in, wu)
     act_low = gated(gate_out, up_out).astype(low)
     wd_own = put(put(wd_own, d2, 2), d3, 3)
     d2_cut, d3_cut = d2[:cut], d3[:cut]
-    f1, e0, e1, act_low, wd_own, d2_cut, d3_cut = sync((f1, e0, e1, act_low, wd_own, d2_cut, d3_cut))
+    given, kept = apart(down_part(act_low, wd_own))
+    f1, e0, e1, act_low, given, kept, d2_cut, d3_cut = sync((f1, e0, e1, act_low, given, kept, d2_cut, d3_cut))
     f2, e2, e3 = around(f1), swap(d2_cut), swap(d3_cut)
-
-    given, kept = apart(whole(down_part, act_low, wd_own))
     kept = add(kept, near(given))
     across = far(kept)
-    wd_peer, f1, e0, e1, f2 = behind(wd_peer, f1, e0, e1, f2)
-    f3 = around(f2)
+    wd_peer, f1, e0, e1 = behind(wd_peer, f1, e0, e1)
+    f3 = around(tie(f2, kept))
     wd_peer = put(put(put(put(wd_peer, f1, 1, cut), f2, 2, cut), e0, 0), e1, 1)
     f3, e2, e3, across, kept, wd_peer = sync((f3, e2, e3, across, kept, wd_peer))
     wd_peer = put(put(put(wd_peer, f3, 3, cut), e2, 2), e3, 3)
@@ -597,62 +599,73 @@
     def pieces(tensor):
         return [piece(tensor, hops) for hops in (3, 2, 1, 0)]
 
+    def rows_of(tensor, offset, rows):
+        starts = [lax.rem(place + hops, outer) * count + offset for hops in (3, 2, 1, 0)]
+        return [lax.dynamic_slice_in_dim(tensor, first, rows, 0) for first in starts]
+
     def both(hops, offset, tensors):
         target = lax.rem(place + hops, outer) * count + offset
         cuts = [lax.dynamic_slice_in_dim(t, target, count, 0) for t in tensors]
         return plain(jnp.concatenate(cuts, axis=1))
 
     grad_ffn_own, grad_ffn_peer, grad_gain3 = ffn_back(ffn_own, ffn_peer, grad_out, gains)
-    sent = pieces(weight_grad(grad_ffn_peer, act_low))
-    far_parts = [given[cut:] for given in sent]
-    sent = [given[:cut] for given in sent]
+    wd_grad = weight_grad(grad_ffn_peer, act_low)
+    cut = count * 7 // 18 // 16 * 16
+    sent, far_parts = jnp.concatenate(rows_of(wd_grad, 0, cut), axis=0), rows_of(wd_grad, cut, count - cut)
     sent, far_parts, grad_ffn_own, grad_ffn_peer = sync((sent, far_parts, grad_ffn_own, grad_ffn_peer))
-    def grown(arrived):
-        return jnp.pad(arrived, ((0, count - cut), (0, 0)))
-
-    d3, d2, f3 = swap(sent[0]), swap(sent[1]), around(far_parts[0])
-
-    def act_step(grad_own, grad_peer, gate_out, up_out, act_low, wd_own, wd_peer):
-        back_of_act = act_back(grad_own, grad_peer, gate_out, up_out, wd_own, wd_peer)
-        return back_of_act + (weight_grad(grad_own, act_low),)
-
-    grad_gate, grad_up, wd_grad = whole(
-        act_step, grad_ffn_own, grad_ffn_peer, gate_out, up_out, act_low, wd_own, wd_peer
-    )
-    d3, d2, f3, grad_gate, grad_up, wd_grad, sent[2:], far_parts[1:] = sync(
-        (d3, d2, f3, grad_gate, grad_up, wd_grad, sent[2:], far_parts[1:])
-    )
-    d1, d0, f2 = swap(sent[2]), swap(sent[3]), around(add(far_parts[1], f3))
-    came = around(plus(piece(wd_grad, 3), grown(d3)))
-
-    def hidden_step(grad_gate, grad_up, hidden_in, wg, wu):
-        given_kept = apart(hidden_back(grad_gate, grad_up, wg, wu))
-        return given_kept + (pieces(weight_grad(hidden_in[:, half:], grad_gate)),)
-
-    given, kept, gate_sent = whole(hidden_step, grad_gate, grad_up, hidden_in, wg, wu)
-    d1, d0, f2, came, given, kept, gate_sent, grad_gate, grad_up = sync(
-        (d1, d0, f2, came, given, kept, gate_sent, grad_gate, grad_up)
-    )
-    h3, theirs = swap(gate_sent[0]), near(given)
-    came = around(plus(piece(wd_grad, 2), grown(d2), came))
-
-    def rest_of_grads(grad_gate, grad_up, hidden_in):
+
+    arrived, f3 = swap(sent), around(far_parts[0])
+
+    def act_step(grad_own, grad_peer, gate_out, up_out, act_low, hidden_in, wd_own, wd_peer):
+        grad_gate, grad_up = act_back(grad_own, grad_peer, gate_out, up_out, wd_own, wd_peer)
+        gate_sent = pieces(weight_grad(hidden_in[:, half:], grad_gate))
+        return grad_gate, grad_up, weight_grad(grad_own, act_low), gate_sent
+
+    grad_gate, grad_up, wd_grad, gate_sent = whole(
+        act_step, grad_ffn_own, grad_ffn_peer, gate_out, up_out, act_low, hidden_in, wd_own, wd_peer
+    )
+    arrived, f3, grad_gate, grad_up, wd_grad, gate_sent, far_parts = sync(
+        (arrived, f3, grad_gate, grad_up, wd_grad, gate_sent, far_parts)
+    )
+
+    def grown(at):
+        return jnp.pad(arrived[at * cut : (at + 1) * cut], ((0, count - cut), (0, 0)))
+
+    h3 = swap(gate_sent[0])
+    came = around(plus(piece(wd_grad, 3), grown(0)))
+    f2 = around(add(far_parts[1], f3))
+
+    def hidden_step(grad_gate, grad_up, wg, wu):
+        return apart(hidden_back(grad_gate, grad_up, wg, wu))
+
+    given, kept = whole(hidden_step, grad_gate, grad_up, wg, wu)
+    h3, came, f2, given, kept, gate_sent, grad_gate, grad_up = sync(
+        (h3, came, f2, given, kept, gate_sent, grad_gate, grad_up)
+    )
+    h2, theirs = swap(gate_sent[1]), near(given)
+    came = around(plus(piece(wd_grad, 2), grown(1), came))
+    f1 = around(add(far_parts[2], f2))
+
+    def rest_of_grads(grad_gate, grad_up, hidden_in, gate_sent):
         up_sent = pieces(weight_grad(hidden_in[:, half:], grad_up))
         wg_grad = weight_grad(hidden_in[:, :half], grad_gate)
-        return up_sent, wg_grad, weight_grad(hidden_in[:, :half], grad_up)
-
-    up_sent, wg_grad, wu_grad = whole(rest_of_grads, grad_gate, grad_up, hidden_in)
-    h3, theirs, came, up_sent, wg_grad, wu_grad, gate_sent[1:], kept = sync(
-        (h3, theirs, came, up_sent, wg_grad, wu_grad, gate_sent[1:], kept)
-    )
+        mixed_sent = [jnp.concatenate(pair, axis=0) for pair in zip(gate_sent[2:], up_sent[:2])]
+        return mixed_sent, up_sent[2:], wg_grad, weight_grad(hidden_in[:, :half], grad_up)
+
+    mixed_sent, up_sent, wg_grad, wu_grad = whole(rest_of_grads, grad_gate, grad_up, hidden_in, gate_sent)
+    h2, theirs, came, f1, mixed_sent, up_sent, wg_grad, wu_grad, kept = sync(
+        (h2, theirs, came, f1, mixed_sent, up_sent, wg_grad, wu_grad, kept)
+    )
+    pair = swap(mixed_sent[0])
     kept = add(kept, theirs)
-    across, h2, v3 = far(kept), swap(gate_sent[1]), swap(up_sent[0])
-    came = around(plus(piece(wd_grad, 1), grown(d1), came))
+    across = far(kept)
+    came = around(plus(piece(wd_grad, 1), grown(2), came))
     gate_came = around(plus(piece(wg_grad, 3), h3))
-    across, h2, v3, came, gate_came, kept, gate_sent[2:], up_sent[1:] = sync(
-        (across, h2, v3, came, gate_came, kept, gate_sent[2:], up_sent[1:])
-    )
-    h1, h0 = swap(gate_sent[2]), swap(gate_sent[3])
+    across, pair, came, gate_came, kept, mixed_sent[1], up_sent = sync(
+        (across, pair, came, gate_came, kept, mixed_sent[1], up_sent)
+    )
+    h1, v3 = pair[:count], pair[count:]
+    pair = swap(mixed_sent[1])
     mine = add(kept, across)
     theirs = near(mine)
     gate_came = around(plus(piece(wg_grad, 2), h2, gate_came))
@@ -668,12 +681,12 @@
     given, kept, grad_resid, grad_attn, grad_gain1, grad_gain2, grad_raw = whole(
         mixer_back, inputs, attn_sum, mine, theirs, grad_out, gains, full, saved
     )
-    h1, h0, gate_came, up_came, given, kept, grad_resid, grad_attn, grad_raw, up_sent[1:], f2 = sync(
-        (h1, h0, gate_came, up_came, given, kept, grad_resid, grad_attn, grad_raw, up_sent[1:], f2)
-    )
-    v2, v1, theirs = swap(up_sent[1]), swap(up_sent[2]), near(given)
+    pair, gate_came, up_came, given, kept, grad_resid, grad_attn, grad_raw, up_sent = sync(
+        (pair, gate_came, up_came, given, kept, grad_resid, grad_attn, grad_raw, up_sent)
+    )
+    h0, v2 = pair[:count], pair[count:]
+    v1, theirs = swap(up_sent[0]), near(given)
     gate_came = around(plus(piece(wg_grad, 1), h1, gate_came))
-    f1 = around(add(far_parts[2], f2))
 
     def mixer_grads(normed_low, mixed_low, grad_raw, grad_attn):
         grads = weight_grad(normed_low, grad_raw), weight_grad(grad_attn, mixed_low)
@@ -682,20 +695,24 @@
         return mixer_sent, [both(hops, 0, grads) for hops in (3, 2, 1, 0)]
 
     mixer_sent, mixer_own = whole(mixer_grads, saved[0], saved[-1], grad_raw, grad_attn)
-    v2, v1, f1, theirs, gate_came, mixer_sent, mixer_own, kept, up_sent[3] = sync(
-        (v2, v1, f1, theirs, gate_came, mixer_sent, mixer_own, kept, up_sent[3])
-    )
+    v1, theirs, gate_came, mixer_sent, mixer_own, kept, up_sent = sync(
+        (v1, theirs, gate_came, mixer_sent, mixer_own, kept, up_sent)
+    )
+    v0, x32 = swap(up_sent[1]), swap(mixer_sent[0])
     kept = add(kept, theirs)
-    across, v0, x32 = far(kept), swap(up_sent[3]), swap(mixer_sent[0])
+    across = far(kept)
     up_came = around(plus(piece(wu_grad, 2), v2, up_came))
+    gate_late = tie(gate_came, up_came)
+    sum_gate = plus(piece(wg_grad, 0), h0, gate_late, wide)
     up_came = around(plus(piece(wu_grad, 1), v1, up_came))
-    v0, x32, up_came, across, kept, mixer_sent[1], inputs, f1 = sync(
-        (v0, x32, up_came, across, kept, mixer_sent[1], inputs, f1)
+    v0, x32, up_came, across, kept, mixer_sent[1], inputs, f1, sum_gate = sync(
+        (v0, x32, up_came, across, kept, mixer_sent[1], inputs, f1, sum_gate)
     )
     x10, b_far = swap(mixer_sent[1]), swap(add(far_parts[3], f1))
+    m3 = around(plus(mixer_own[0], x32[:count]), 3)
+    m2 = around(plus(mixer_own[1], x32[count:]), 2)
     mine = add(kept, across)
     theirs = near(mine)
-    passed = around(plus(mixer_own[0], x32[:count]))
 
     def finish(inputs, mine, theirs, grad_resid, attn_sum, ffn_own, ffn_peer, gains):
         block_out = layer_out(inputs, attn_sum, ffn_own, ffn_peer, gains)
@@ -705,26 +722,24 @@
     block_out, input_grad, grad_gain0 = whole(
         finish, inputs, mine, theirs, grad_resid, attn_sum, ffn_own, ffn_peer, gains
     )
-    x10, b_far, passed, block_out, input_grad, grad_gain0, x32 = sync(
-        (x10, b_far, passed, block_out, input_grad, grad_gain0, x32)
-    )
-    passed = around(plus(mixer_own[1], x32[count:], passed))
+    x10, b_far, m3, m2, block_out, input_grad, grad_gain0 = sync(
+        (x10, b_far, m3, m2, block_out, input_grad, grad_gain0)
+    )
+    m1 = around(plus(mixer_own[2], x10[:count]))
     grad_gains = jnp.concatenate([grad_gain0, grad_gain1, grad_gain2, grad_gain3], axis=0)
     gain_sum = grad_gains[:, :half] + swap(grad_gains[:, half:])
     gain_sum = gain_sum.reshape(4, outer, count)
-    down_total = plus(piece(wd_grad, 0), jnp.concatenate([d0, b_far], axis=0), came, wide)
+    down_total = plus(piece(wd_grad, 0), jnp.concatenate([arrived[3 * cut :], b_far], axis=0), came, wide)
     new_down = update_down(behind(down_total)[0])
-    sum_gate = plus(piece(wg_grad, 0), h0, gate_came, wide)
     sum_up = plus(piece(wu_grad, 0), v0, up_came, wide)
     new_gate_up = update_gate_up([sum_gate, sum_up])
-    passed, gain_sum, new_down, new_gate_up = sync((passed, gain_sum, new_down, new_gate_up))
-    passed = around(plus(mixer_own[2], x10[:count], passed))
     sum_gains = lax.dynamic_index_in_dim(gain_sum, place, 1, False)
     for hops in (1, 2, 3):
         given = lax.dynamic_index_in_dim(gain_sum, lax.rem(place + hops, outer), 1, False)
-        sum_gains = sum_gains + lax.ppermute(given, "dp", ring_pairs(groups, hops))
-    new_mixer = update_mixer(plus(mixer_own[3], x10[count:], passed, wide))
-    return results(block_out, input_grad, new_mixer, new_gate_up, new_down, sum_gains)
+        sum_gains = sum_gains + around(given, hops)
+    m1, sum_gains, new_down, new_gate_up = sync((m1, sum_gains, new_down, new_gate_up))
+    sum_mixer = plus(mixer_own[3], x10[count:], m1, wide) + m2.astype(wide) + m3.astype(wide)
+    return results(block_out, input_grad, update_mixer(sum_mixer), new_gate_up, new_down, sum_gains)
 
 
 def solution(mesh):

time: 1060 us -> 1020 us (0.962)
  waiting for transfers between devices: 422 us -> 377 us
  other arithmetic: 131 us -> 152 us
  Pallas kernels: 75.7 us -> 60.3 us
  matrix products: 210 us -> 222 us
    ppermute x33 -> x28, waiting for transfers between devices: 162 us -> 126 us  [swap(): return lax.ppermute(tensor, 'dp', swap_pairs(groups, 1))]
    pallas_call x7, Pallas kernels: 75.7 us -> 60.3 us  [by_rows(): pl.pallas_call(body, grid=(length // BLOCK,), in_specs=[pl.BlockSpec(memo...]
    unnamed x142 -> x134, local copies, waits for them, and re-layouts: 24.2 us -> 19.3 us
    ppermute x33 -> x28, starting transfers between devices: 34.8 us -> 30 us  [swap(): return lax.ppermute(tensor, 'dp', swap_pairs(groups, 1))]
    convert_element_type x12 -> x11, other arithmetic: 31.6 us -> 35.2 us  [plus(): return both.astype(kind)]
  transfers between devices with their start and end apart: 81 -> 76, of which waited for: 35 -> 34; matrix products, arithmetic and copies ran while one was open for 37% -> 43% of each run, Pallas kernels for 6% -> 5%
where the time goes in v3:
time: 1020 us; the launch traced here: 1010 us
  waiting for transfers between devices  377 us (37%)
  matrix products  222 us (22%)
  other arithmetic  152 us (15%)
  local copies, waits for them, and re-layouts  129 us (13%)
  starting transfers between devices  67.2 us (7%)
  Pallas kernels  60.3 us (6%)
    ppermute x33, waiting for transfers between devices, around(): return lax.ppermute(tensor, 'dp', ring_pairs(groups, hops))  219 us
    dot_general x25, matrix products, dot(): return jnp.einsum(pattern, first, second, preferred_element_type=wide)  217 us
    ppermute x28, waiting for transfers between devices, swap(): return lax.ppermute(tensor, 'dp', swap_pairs(groups, 1))  126 us
    pallas_call x7, Pallas kernels, by_rows(): pl.pallas_call(body, grid=(length // BLOCK,), in_specs=[pl.BlockSpec(memo...  60.3 us
    dynamic_update_slice x35, local copies, waits for them, and re-layouts, put(): lax.dynamic_update_slice_in_dim(full, piece, source(step) * count + offse...  53.5 us
    convert_element_type x11, other arithmetic, plus(): return both.astype(kind)  35.2 us
    ppermute x33, starting transfers between devices, around(): return lax.ppermute(tensor, 'dp', ring_pairs(groups, hops))  30.5 us
    ppermute x28, starting transfers between devices, swap(): return lax.ppermute(tensor, 'dp', swap_pairs(groups, 1))  30 us
  transfers between devices with their start and end apart: 76, of which 34 were waited for; matrix products, arithmetic and copies ran while one was open for 43% of the time, Pallas kernels for 5%

profile of v3, /device:TPU:0, one launch (start us, length us, event | category | flops | bytes accessed | tf_op | source)
XLA Modules:
  0.0 1009.7 jit_solution(10644095711924480561)
XLA Ops:
  19.7 8.7 shard_map.404
  41.7 13.0 %collective-permute-done.3 = bf16[304,1536]{1,0:T(8,128)(2,1)S(1)} collective-permute-done((bf16[304,1536]{1,0:T(8,128)(2,1)}, bf16[304,1536]{1,0:T(8,128)(2,1)S(1)}, u32[]{:S(2)}, u32[]{:S(2)}) %collective-permute-start.3) | collective-permute-done | bytes 933920 | tf_op jit(solution)/shard_map/ppermute | solution.py:278
  63.0 9.9 copy.134
  87.5 10.4 %collective-permute-done.8 = bf16[144,2304]{1,0:T(8,128)(2,1)S(1)} collective-permute-done((bf16[144,2304]{1,0:T(8,128)(2,1)S(1)}, bf16[144,2304]{1,0:T(8,128)(2,1)S(1)}, u32[]{:S(2)}, u32[]{:S(2)}) %collective-permute-start.8) | collective-permute-done | bytes 663584 | tf_op jit(solution)/shard_map/ppermute | solution.py:278
  97.9 16.0 %collective-permute-done.6 = bf16[304,1536]{1,0:T(8,128)(2,1)S(1)} collective-permute-done((bf16[304,1536]{1,0:T(8,128)(2,1)S(1)}, bf16[304,1536]{1,0:T(8,128)(2,1)S(1)}, u32[]{:S(2)}, u32[]{:S(2)}) %collective-permute-start.6) | collective-permute-done | bytes 933920 | tf_op jit(solution)/shard_map/ppermute | solution.py:278
  122.0 50.4 %conditional.7 = (bf16[448,2304]{1,0:T(8,128)(2,1)S(1)}, bf16[448,2304]{1,0:T(8,128)(2,1)S(1)}, bf16[896,2304]{1,0:T(8,128)(2,1)}, bf16[896,1,2,256]{3,0,2,1:T(8...) conditional(s32[]{:T(128)} %convert_element_type.461, ...), branch_computations={%region_1.2_spmd, %region_2.5_spmd} | conditional | flops 8014624768 | bytes 136611424 | solution.py:431
  155.6 7.9 fusion.84
  197.0 44.8 %collective-permute-done.14 = bf16[288,2304]{1,0:T(8,128)(2,1)S(1)} collective-permute-done((bf16[288,2304]{1,0:T(8,128)(2,1)}, bf16[288,2304]{1,0:T(8,128)(2,1)S(1)}, u32[]{:S(2)}, u32[]{:S(2)}) %collective-permute-start.14) | collective-permute-done | bytes 1327136 | tf_op jit(solution)/shard_map/ppermute | solution.py:275
  269.1 37.3 %collective-permute-done.21 = bf16[288,2304]{1,0:T(8,128)(2,1)} collective-permute-done((bf16[288,2304]{1,0:T(8,128)(2,1)}, bf16[288,2304]{1,0:T(8,128)(2,1)}, u32[]{:S(2)}, u32[]{:S(2)}) %collective-permute-start.21) | collective-permute-done | bytes 1327136 | tf_op jit(solution)/shard_map/ppermute | solution.py:278
  319.7 19.5 %collective-permute-done.26 = bf16[288,2304]{1,0:T(8,128)(2,1)S(1)} collective-permute-done((bf16[288,2304]{1,0:T(8,128)(2,1)}, bf16[288,2304]{1,0:T(8,128)(2,1)S(1)}, u32[]{:S(2)}, u32[]{:S(2)}) %collective-permute-start.26) | collective-permute-done | bytes 1327136 | tf_op jit(solution)/shard_map/ppermute | solution.py:278
  342.3 13.7 %fusion.94 = f32[896,2304]{1,0:T(8,128)} fusion(bf16[896,2304]{1,0:T(8,128)(2,1)S(1)} %copy-done.27, bf16[2304,2304]{1,0:T(8,128)(2,1)} %constant_dynamic-update-slice_fusion.15), kind=kOutput, calls=%fused_computation.310 | convolution fusion | flops 9512681472 | bytes 23003136 | tf_op jit(solution)/shard_map/td,df->tf/dot_general | solution.py:272
  356.0 12.3 %collective-permute-done.27 = bf16[288,2304]{1,0:T(8,128)(2,1)S(1)} collective-permute-done((bf16[288,2304]{1,0:T(8,128)(2,1)}, bf16[288,2304]{1,0:T(8,128)(2,1)S(1)}, u32[]{:S(2)}, u32[]{:S(2)}) %collective-permute-start.27) | collective-permute-done | bytes 1327136 | tf_op jit(solution)/shard_map/ppermute | solution.py:278
  374.6 16.9 %fusion.67 = (bf16[896,2304]{1,0:T(8,128)(2,1)}, f32[896,2304]{1,0:T(8,128)}) fusion(f32[896,2304]{1,0:T(8,128)} %fusion.94, bf16[896,2304]{1,0:T(8,128)(2,1)S(1)} %copy-done.27, bf16[2304,2304]{1,0:T(8,128)(2,1)} %constant_dynamic-update-slice_fusion.9), kind=kOutput, calls=%fused_computation.144 | convolution fusion | flops 9533325312 | bytes 35389440 | tf_op jit(solution)/shard_map/td,df->tf/dot_general | solution.py:272
  391.7 8.9 convolution_convert_fusion.11
  409.1 14.0 %collective-permute-done.31 = bf16[144,2304]{1,0:T(8,128)(2,1)S(1)} collective-permute-done((bf16[144,2304]{1,0:T(8,128)(2,1)}, bf16[144,2304]{1,0:T(8,128)(2,1)S(1)}, u32[]{:S(2)}, u32[]{:S(2)}) %collective-permute-start.31) | collective-permute-done | bytes 663584 | tf_op jit(solution)/shard_map/ppermute | solution.py:275
  427.1 8.1 collective-permute-done.35
  435.2 7.6 collective-permute-done.33
  445.4 8.9 convolution_convert_fusion.10
  459.1 23.2 %collective-permute-done.39 = bf16[448,1152]{1,0:T(8,128)(2,1)S(1)} collective-permute-done((bf16[448,1152]{1,0:T(8,128)(2,1)S(1)}, bf16[448,1152]{1,0:T(8,128)(2,1)S(1)}, u32[]{:S(2)}, u32[]{:S(2)}) %collective-permute-start.39) | collective-permute-done | bytes 1032224 | tf_op jit(solution)/shard_map/ppermute | solution.py:284
  493.8 8.6 convolution_convert_fusion.9
  507.8 48.8 %conditional.8 = (bf16[896,2304]{1,0:T(8,128)(2,1)}, bf16[896,2304]{1,0:T(8,128)(2,1)}, bf16[1152,2304]{1,0:T(8,128)(2,1)}, bf16[288,2304]{1,0:T(8,128)(2,1)}, b...) conditional(s32[]{:T(128)} %convert_element_type.461, () %tuple.124, ...), branch_computations={%region_5.6_spmd, %region_6.7_spmd} | conditional | flops 19082280960 | bytes 135660160 | solution.py:431
  507.8 10.6 %fusion.92 = f32[896,2304]{1,0:T(8,128)} fusion(bf16[896,1152]{1,0:T(8,128)(2,1)} %get-tuple-element.137, bf16[1152,2304]{1,0:T(8,128)(2,1)} %get-tuple-element.138), kind=kOutput, calls=%fused_computation.308 | convolution fusion | flops 4756340736 | bytes 15630336 | tf_op jit(solution)/shard_map/cond/branch_1_fun/td,df->tf/dot_general | solution.py:272
  518.4 18.2 %multiply_convert_fusion = (bf16[896,2304]{1,0:T(8,128)(2,1)}, bf16[896,2304]{1,0:T(8,128)(2,1)}) fusion(f32[896,2304]{1,0:T(8,128)} %get-tuple-element.142, f32[896,2304]{1,0:T(8,128)} %get-tuple-element.141, f32[896,2304]{1,0:T(8,128)} %fusion.92, bf16[896,1152]{1,0:T(8,128)(2,1)} %get-tuple-element.139, bf16[1152,2304]{1,0:T(8,128)(2,1)S(1)} %copy-done.22), kind=kOutput, calls=%fused_computation.49 | convolution fusion | flops 4807950336 | bytes 40402944 | tf_op jit(solution)/shard_map/cond/branch_1_fun/td,df->tf/dot_general | solution.py:272
  536.6 9.7 convolution_convert_fusion.2
  546.4 8.3 fusion.20
  564.2 35.9 %conditional.9 = (bf16[448,2304]{1,0:T(8,128)(2,1)}, bf16[448,2304]{1,0:T(8,128)(2,1)S(1)}) conditional(s32[]{:T(128)} %convert_element_type.461, () %tuple.127, (bf16[896,2304]{1,0:T(8,128)(2,1)}, bf16[2304,2304]{1,0:T(8,128)(2,1)}, bf16[896,2304]{1,0:T(8,128)(2,1)}, bf16[2304,2304]{1,0:T(8,128)(2,1)}, s32[]{:T(128)}) %tuple.128), branch_computations={%region_7.8_spmd, %region_8.9_spmd} | conditional | flops 19029491712 | bytes 58392700 | solution.py:431
  564.2 15.0 %fusion.93 = f32[896,2304]{1,0:T(8,128)} fusion(bf16[896,2304]{1,0:T(8,128)(2,1)} %get-tuple-element.146, bf16[2304,2304]{1,0:T(8,128)(2,1)} %get-tuple-element.147), kind=kOutput, calls=%fused_computation.309 | convolution fusion | flops 9512681472 | bytes 23003136 | tf_op jit(solution)/shard_map/cond/branch_1_fun/tf,df->td/dot_general | solution.py:272
  579.2 17.2 %add_convert_fusion.1 = bf16[896,2304]{1,0:T(8,128)(2,1)} fusion(f32[896,2304]{1,0:T(8,128)} %fusion.93, bf16[896,2304]{1,0:T(8,128)(2,1)} %get-tuple-element.148, bf16[2304,2304]{1,0:T(8,128)(2,1)} %get-tuple-element.149), kind=kOutput, calls=%fused_computation.56 | convolution fusion | flops 9516810240 | bytes 27131904 | tf_op jit(solution)/shard_map/cond/branch_1_fun/tf,df->td/dot_general | solution.py:272
  602.6 8.6 collective-permute-done.45
  617.7 31.7 %conditional.10 = (bf16[576,2304]{1,0:T(8,128)(2,1)S(1)}, bf16[576,2304]{1,0:T(8,128)(2,1)}, bf16[288,2304]{1,0:T(8,128)(2,1)}, bf16[288,2304]{1,0:T(8,128)(2,1)...) conditional(s32[]{:T(128)} %convert_element_type.461, () %tuple.130, (bf16[896,2304]{1,0:T(8,128)(2,1)}, ...), branch_computations={%region_9.10_spmd, %region_10.11_spmd} | conditional | flops 14287601664 | bytes 77562432 | solution.py:431
  617.7 10.3 %convolution_convert_fusion.4 = bf16[1152,2304]{1,0:T(8,128)(2,1)} fusion(bf16[896,2304]{1,0:T(8,128)(2,1)} %get-tuple-element.156, bf16[896,2304]{1,0:T(8,128)(2,1)} %get-tuple-element.152), kind=kOutput, calls=%fused_computation.60 | convolution fusion | flops 4758994944 | bytes 11501568 | tf_op jit(solution)/shard_map/cond/branch_1_fun/td,te->de/dot_general | solution.py:272
  627.9 9.5 convolution_convert_fusion.3
  637.5 8.3 convolution_convert_fusion.5
  649.3 16.1 %collective-permute-done.49 = bf16[176,2304]{1,0:T(8,128)(2,1)} collective-permute-done((bf16[176,2304]{1,0:T(8,128)(2,1)}, bf16[176,2304]{1,0:T(8,128)(2,1)}, u32[]{:S(2)}, u32[]{:S(2)}) %collective-permute-start.49) | collective-permute-done | bytes 811040 | tf_op jit(solution)/shard_map/ppermute | solution.py:275
  673.9 27.7 %collective-permute-done.52 = bf16[288,2304]{1,0:T(8,128)(2,1)S(1)} collective-permute-done((bf16[288,2304]{1,0:T(8,128)(2,1)S(1)}, bf16[288,2304]{1,0:T(8,128)(2,1)S(1)}, u32[]{:S(2)}, u32[]{:S(2)}) %collective-permute-start.52) | collective-permute-done | bytes 1327136 | tf_op jit(solution)/shard_map/ppermute | solution.py:275
  701.6 27.2 %collective-permute-done.53 = bf16[288,2304]{1,0:T(8,128)(2,1)S(1)} collective-permute-done((bf16[288,2304]{1,0:T(8,128)(2,1)S(1)}, bf16[288,2304]{1,0:T(8,128)(2,1)S(1)}, u32[]{:S(2)}, u32[]{:S(2)}) %collective-permute-start.53) | collective-permute-done | bytes 1327136 | tf_op jit(solution)/shard_map/ppermute | solution.py:275
  739.5 61.7 %conditional.11 = (bf16[448,2304]{1,0:T(8,128)(2,1)}, bf16[448,2304]{1,0:T(8,128)(2,1)}, f32[896,2304]{1,0:T(8,128)}, bf16[896,2304]{1,0:T(8,128)(2,1)}, f32[1,2...) conditional(s32[]{:T(128)} %convert_element_type.461, () %tuple.134, (s32[]{:T(128)}, ...), branch_computations={%region_11.12_spmd, %region_12.14_spmd} | conditional | flops 9665787904 | bytes 177748544 | solution.py:431
  747.8 13.5 %branch_1_fun.5 = (f32[896,2304]{1,0:T(8,128)}, bf16[896,2304]{1,0:T(8,128)(2,1)}, f32[1,2304]{1,0:T(1,128)}, f32[1,2304]{1,0:T(1,128)}) custom-call(s32[1]{0:T(128)} %get-tuple-element.158.side, bf16[896,2304]{1,0:T(8,128)(2,1)S(1)} %copy-done.2, bf16[896,2304]{1,0:T(8,128)(2,1)S(1)} %copy-done.5, bf16[896,2304]{1,0:T(8,128)(2,1)S(1)} %pad_maximum_fusion.3.grad_hidden, ...), custom_call_target="tpu_custom_call" | custom-call | tf_op jit(solution)/shard_map/cond/branch_1_fun/pallas_call | solution.py:73
  776.5 7.7 fusion.37
  791.6 7.4 convolution_convert_fusion.6
  814.5 22.7 %conditional.12 = (bf16[576,1536]{1,0:T(8,128)(2,1)}, bf16[576,1536]{1,0:T(8,128)(2,1)}, bf16[288,1536]{1,0:T(8,128)(2,1)S(1)}, bf16[288,1536]{1,0:T(8,128)(2,1)...) conditional(s32[]{:T(128)} %convert_element_type.461, () %tuple.137, ...), branch_computations={%region_14.15_spmd, %region_15.16_spmd} | conditional | flops 6366560256 | bytes 62915356 | solution.py:431
  844.2 23.2 %collective-permute-done.63 = bf16[288,2304]{1,0:T(8,128)(2,1)} collective-permute-done((bf16[288,2304]{1,0:T(8,128)(2,1)}, bf16[288,2304]{1,0:T(8,128)(2,1)}, u32[]{:S(2)}, u32[]{:S(2)}) %collective-permute-start.63) | collective-permute-done | bytes 1327136 | tf_op jit(solution)/shard_map/ppermute | solution.py:275
  875.3 28.7 %collective-permute-done.64 = bf16[288,2304]{1,0:T(8,128)(2,1)} collective-permute-done((bf16[288,2304]{1,0:T(8,128)(2,1)}, bf16[288,2304]{1,0:T(8,128)(2,1)}, u32[]{:S(2)}, u32[]{:S(2)}) %collective-permute-start.64) | collective-permute-done | bytes 1327136 | tf_op jit(solution)/shard_map/ppermute | solution.py:275
  925.4 12.2 %add_multiply_fusion = (f32[2,288,2304]{2,1,0:T(8,128)}, f32[2,288,2304]{2,1,0:T(8,128)}, f32[2,288,2304]{2,1,0:T(8,128)}, f32[2,288,2304]{2,1,0:T(8,128)}) fusion(f32[2,288,2304]{2,1,0:T(8,128)S(1)} %bitcast.227, f32[1,288,2304]{2,1,0:T(8,128)S(1)} %add_bitcast_fusion, f32[1,288,2304]{2,1,0:T(8,128)S(1)} %bitcast.233, f32[2,288,2304]{2,1,0:T(8,128)} %param.47, ...), kind=kLoop, calls=%fused_computation.148 | loop fusion | flops 19906560 | bytes 42467328 | tf_op jit(solution)/shard_map/mul | solution.py:226
  937.6 25.3 %conditional.13 = (bf16[896,2304]{1,0:T(8,128)(2,1)}, f32[896,2304]{1,0:T(8,128)}, f32[1,2304]{1,0:T(1,128)S(1)}) conditional(s32[]{:T(128)} %convert_element_type.461, () %tuple.142, (s32[1]{0:T(128)}, bf16[896,2304]{1,0:T(8,128)(2,1)}, bf16[896,2304]{1,0:T(8,128)(2,1)}, bf16[896,1152]{1,0:T(8,128)(2,1)S(1)}, bf16[896,1152]{1,0:T(8,128)(2,1)}, ...), branch_computations={%region_16.17_spmd, %region_17.18_spmd} | conditional | flops 10321921 | bytes 33030206 | solution.py:431
  937.6 9.7 branch_1_fun.6
  952.0 10.9 %branch_1_fun.7 = (f32[896,2304]{1,0:T(8,128)}, f32[1,2304]{1,0:T(1,128)S(1)}) custom-call(s32[1]{0:T(128)} %get-tuple-element.183.side, bf16[896,2304]{1,0:T(8,128)(2,1)S(1)} %copy-done.3, bf16[896,2304]{1,0:T(8,128)(2,1)S(1)} %pad_maximum_fusion.9.grad_normed, f32[896,2304]{1,0:T(8,128)} %get-tuple-element.192.grad_resid, ...), custom_call_target="tpu_custom_call" | custom-call | tf_op jit(solution)/shard_map/cond/branch_1_fun/pallas_call | solution.py:73
  989.0 7.8 fusion.71
  (505 shorter events, 409.6 us)
Async XLA Ops:
  81.0 32.9 %collective-permute-start.6 = (bf16[304,1536]{1,0:T(8,128)(2,1)S(1)}, bf16[304,1536]{1,0:T(8,128)(2,1)S(1)}, u32[]{:S(2)}, u32[]{:S(2)}) collective-permute-start(bf16[304,1536]{1,0:T(8,128)(2,1)S(1)} %collective-permute-done.4), channel_id=1, source_target_pairs={{0,4},{4,0},{8,12},{12,8},{16,20},{20,16},{24,28},{28,24},{1,5},{5... | collective-permute-start | bytes 2801672 | tf_op jit(solution)/shard_map/ppermute | solution.py:278
  82.1 32.7 %collective-permute-start.7 = (bf16[288,2304]{1,0:T(8,128)(2,1)}, bf16[288,2304]{1,0:T(8,128)(2,1)}, u32[]{:S(2)}, u32[]{:S(2)}) collective-permute-start(bf16[288,2304]{1,0:T(8,128)(2,1)} %get-tuple-element.519), channel_id=1, source_target_pairs={{0,8},{4,12},{8,16},{12,20},{16,24},{20,28},{24,0},{28,4},{1,9},{5... | collective-permute-start | bytes 3981320 | tf_op jit(solution)/shard_map/ppermute | solution.py:275
  114.8 57.6 %collective-permute-start.12 = (bf16[288,2304]{1,0:T(8,128)(2,1)}, bf16[288,2304]{1,0:T(8,128)(2,1)}, u32[]{:S(2)}, u32[]{:S(2)}) collective-permute-start(bf16[288,2304]{1,0:T(8,128)(2,1)} %get-tuple-element.519), channel_id=1, source_target_pairs={{0,4},{4,0},{8,12},{12,8},{16,20},{20,16},{24,28},{28,24},{1,5},{5... | collective-permute-start | bytes 3981320 | tf_op jit(solution)/shard_map/ppermute | solution.py:278
  115.8 56.6 %collective-permute-start.11 = (bf16[288,2304]{1,0:T(8,128)(2,1)}, bf16[288,2304]{1,0:T(8,128)(2,1)}, u32[]{:S(2)}, u32[]{:S(2)}) collective-permute-start(bf16[288,2304]{1,0:T(8,128)(2,1)} %get-tuple-element.517), channel_id=1, source_target_pairs={{0,4},{4,0},{8,12},{12,8},{16,20},{20,16},{24,28},{28,24},{1,5},{5... | collective-permute-start | bytes 3981320 | tf_op jit(solution)/shard_map/ppermute | solution.py:278
  116.8 55.6 %collective-permute-start.9 = (bf16[288,2304]{1,0:T(8,128)(2,1)}, bf16[288,2304]{1,0:T(8,128)(2,1)}, u32[]{:S(2)}, u32[]{:S(2)}) collective-permute-start(bf16[288,2304]{1,0:T(8,128)(2,1)} %get-tuple-element.517), channel_id=1, source_target_pairs={{0,8},{4,12},{8,16},{12,20},{16,24},{20,28},{24,0},{28,4},{1,9},{5... | collective-permute-start | bytes 3981320 | tf_op jit(solution)/shard_map/ppermute | solution.py:275
  116.8 55.9 %collective-permute-start.10 = (bf16[288,2304]{1,0:T(8,128)(2,1)}, bf16[288,2304]{1,0:T(8,128)(2,1)}, u32[]{:S(2)}, u32[]{:S(2)}) collective-permute-start(bf16[288,2304]{1,0:T(8,128)(2,1)} %collective-permute-done.7), channel_id=1, source_target_pairs={{0,8},{4,12},{8,16},{12,20},{16,24},{20,28},{24,0},{28,4},{1,9},{5... | collective-permute-start | bytes 3981320 | tf_op jit(solution)/shard_map/ppermute | solution.py:275
  178.7 64.2 %collective-permute-start.18 = (bf16[448,2304]{1,0:T(8,128)(2,1)}, bf16[448,2304]{1,0:T(8,128)(2,1)}, u32[]{:S(2)}, u32[]{:S(2)}) collective-permute-start(bf16[448,2304]{1,0:T(8,128)(2,1)} %add_convert_fusion.9), channel_id=1, source_target_pairs={{0,2},{1,3},{2,0},{3,1},{4,6},{5,7},{6,4},{7,5},{8,10},{9,11},{10,... | collective-permute-start | bytes 6193160 | tf_op jit(solution)/shard_map/ppermute | solution.py:284
  180.2 61.6 %collective-permute-start.16 = (bf16[288,2304]{1,0:T(8,128)(2,1)}, bf16[288,2304]{1,0:T(8,128)(2,1)S(1)}, u32[]{:S(2)}, u32[]{:S(2)}) collective-permute-start(bf16[288,2304]{1,0:T(8,128)(2,1)} %collective-permute-done.9), channel_id=1, source_target_pairs={{0,4},{4,0},{8,12},{12,8},{16,20},{20,16},{24,28},{28,24},{1,5},{5... | collective-permute-start | bytes 3981320 | tf_op jit(solution)/shard_map/ppermute | solution.py:278
  180.7 61.1 %collective-permute-start.13 = (bf16[288,2304]{1,0:T(8,128)(2,1)}, bf16[288,2304]{1,0:T(8,128)(2,1)}, u32[]{:S(2)}, u32[]{:S(2)}) collective-permute-start(bf16[288,2304]{1,0:T(8,128)(2,1)} %collective-permute-done.9), channel_id=1, source_target_pairs={{0,8},{4,12},{8,16},{12,20},{16,24},{20,28},{24,0},{28,4},{1,9},{5... | collective-permute-start | bytes 3981320 | tf_op jit(solution)/shard_map/ppermute | solution.py:275
  181.5 60.3 %collective-permute-start.15 = (bf16[288,2304]{1,0:T(8,128)(2,1)}, bf16[288,2304]{1,0:T(8,128)(2,1)S(1)}, u32[]{:S(2)}, u32[]{:S(2)}) collective-permute-start(bf16[288,2304]{1,0:T(8,128)(2,1)} %collective-permute-done.7), channel_id=1, source_target_pairs={{0,4},{4,0},{8,12},{12,8},{16,20},{20,16},{24,28},{28,24},{1,5},{5... | collective-permute-start | bytes 3981320 | tf_op jit(solution)/shard_map/ppermute | solution.py:278
  183.0 58.8 %collective-permute-start.14 = (bf16[288,2304]{1,0:T(8,128)(2,1)}, bf16[288,2304]{1,0:T(8,128)(2,1)S(1)}, u32[]{:S(2)}, u32[]{:S(2)}) collective-permute-start(bf16[288,2304]{1,0:T(8,128)(2,1)} %collective-permute-done.10), channel_id=1, source_target_pairs={{0,8},{4,12},{8,16},{12,20},{16,24},{20,28},{24,0},{28,4},{1,9},{5... | collective-permute-start | bytes 3981320 | tf_op jit(solution)/shard_map/ppermute | solution.py:275
  246.7 59.7 %collective-permute-start.22 = (bf16[288,2304]{1,0:T(8,128)(2,1)}, bf16[288,2304]{1,0:T(8,128)(2,1)}, u32[]{:S(2)}, u32[]{:S(2)}) collective-permute-start(bf16[288,2304]{1,0:T(8,128)(2,1)} %collective-permute-done.13), channel_id=1, source_target_pairs={{0,4},{4,0},{8,12},{12,8},{16,20},{20,16},{24,28},{28,24},{1,5},{5... | collective-permute-start | bytes 3981320 | tf_op jit(solution)/shard_map/ppermute | solution.py:278
  248.3 58.1 %collective-permute-start.19 = (bf16[288,2304]{1,0:T(8,128)(2,1)}, bf16[288,2304]{1,0:T(8,128)(2,1)}, u32[]{:S(2)}, u32[]{:S(2)}) collective-permute-start(bf16[288,2304]{1,0:T(8,128)(2,1)} %collective-permute-done.13), channel_id=1, source_target_pairs={{0,8},{4,12},{8,16},{12,20},{16,24},{20,28},{24,0},{28,4},{1,9},{5... | collective-permute-start | bytes 3981320 | tf_op jit(solution)/shard_map/ppermute | solution.py:275
  249.7 59.7 %collective-permute-start.20 = (bf16[288,2304]{1,0:T(8,128)(2,1)S(1)}, bf16[288,2304]{1,0:T(8,128)(2,1)S(1)}, u32[]{:S(2)}, u32[]{:S(2)}) collective-permute-start(bf16[288,2304]{1,0:T(8,128)(2,1)S(1)} %convert_bitcast_fusion), channel_id=1, source_target_pairs={{0,8},{4,12},{8,16},{12,20},{16,24},{20,28},{24,0},{28,4},{1,9},{5... | collective-permute-start | bytes 3981320 | tf_op jit(solution)/shard_map/ppermute | solution.py:275
  252.2 54.2 %collective-permute-start.21 = (bf16[288,2304]{1,0:T(8,128)(2,1)}, bf16[288,2304]{1,0:T(8,128)(2,1)}, u32[]{:S(2)}, u32[]{:S(2)}) collective-permute-start(bf16[288,2304]{1,0:T(8,128)(2,1)} %collective-permute-done.10), channel_id=1, source_target_pairs={{0,4},{4,0},{8,12},{12,8},{16,20},{20,16},{24,28},{28,24},{1,5},{5... | collective-permute-start | bytes 3981320 | tf_op jit(solution)/shard_map/ppermute | solution.py:278
  309.9 31.2 %collective-permute-start.24 = (bf16[288,2304]{1,0:T(8,128)(2,1)S(1)}, bf16[288,2304]{1,0:T(8,128)(2,1)S(1)}, u32[]{:S(2)}, u32[]{:S(2)}) collective-permute-start(bf16[288,2304]{1,0:T(8,128)(2,1)S(1)} %collective-permute-done.20), channel_id=1, source_target_pairs={{0,8},{4,12},{8,16},{12,20},{16,24},{20,28},{24,0},{28,4},{1,9},{5... | collective-permute-start | bytes 3981320 | tf_op jit(solution)/shard_map/ppermute | solution.py:275
  341.1 30.3 %collective-permute-start.25 = (bf16[288,2304]{1,0:T(8,128)(2,1)S(1)}, bf16[288,2304]{1,0:T(8,128)(2,1)S(1)}, u32[]{:S(2)}, u32[]{:S(2)}) collective-permute-start(bf16[288,2304]{1,0:T(8,128)(2,1)S(1)} %collective-permute-done.24), channel_id=1, source_target_pairs={{0,8},{4,12},{8,16},{12,20},{16,24},{20,28},{24,0},{28,4},{1,9},{5... | collective-permute-start | bytes 3981320 | tf_op jit(solution)/shard_map/ppermute | solution.py:275
  371.4 31.2 %collective-permute-start.28 = (bf16[144,2304]{1,0:T(8,128)(2,1)S(1)}, bf16[144,2304]{1,0:T(8,128)(2,1)}, u32[]{:S(2)}, u32[]{:S(2)}) collective-permute-start(bf16[144,2304]{1,0:T(8,128)(2,1)S(1)} %copy-done.69), channel_id=1, source_target_pairs={{0,8},{4,12},{8,16},{12,20},{16,24},{20,28},{24,0},{28,4},{1,9},{5... | collective-permute-start | bytes 1990664 | tf_op jit(solution)/shard_map/ppermute | solution.py:275
  371.4 31.2 %collective-permute-start.29 = (bf16[144,2304]{1,0:T(8,128)(2,1)}, bf16[144,2304]{1,0:T(8,128)(2,1)S(1)}, u32[]{:S(2)}, u32[]{:S(2)}) collective-permute-start(bf16[144,2304]{1,0:T(8,128)(2,1)} %slice.202), channel_id=1, source_target_pairs={{0,4},{4,0},{8,12},{12,8},{16,20},{20,16},{24,28},{28,24},{1,5},{5... | collective-permute-start | bytes 1990664 | tf_op jit(solution)/shard_map/ppermute | solution.py:278
  407.8 35.0 %collective-permute-start.36 = (bf16[448,1152]{1,0:T(8,128)(2,1)S(1)}, bf16[448,1152]{1,0:T(8,128)(2,1)S(1)}, u32[]{:S(2)}, u32[]{:S(2)}) collective-permute-start(bf16[448,1152]{1,0:T(8,128)(2,1)S(1)} %add_convert_fusion.22), channel_id=1, source_target_pairs={{0,2},{1,3},{2,0},{3,1},{4,6},{5,7},{6,4},{7,5},{8,10},{9,11},{10,... | collective-permute-start | bytes 3096584 | tf_op jit(solution)/shard_map/ppermute | solution.py:284
  505.8 50.7 %collective-permute-start.41 = (bf16[448,2304]{1,0:T(8,128)(2,1)}, bf16[448,2304]{1,0:T(8,128)(2,1)}, u32[]{:S(2)}, u32[]{:S(2)}) collective-permute-start(bf16[448,2304]{1,0:T(8,128)(2,1)} %pad_maximum_fusion.14), channel_id=1, source_target_pairs={{0,4},{4,0},{8,12},{12,8},{16,20},{20,16},{24,28},{28,24},{1,5},{5... | collective-permute-start | bytes 6193160 | tf_op jit(solution)/shard_map/ppermute | solution.py:278
  507.4 49.2 %collective-permute-start.42 = (bf16[176,2304]{1,0:T(8,128)(2,1)}, bf16[176,2304]{1,0:T(8,128)(2,1)}, u32[]{:S(2)}, u32[]{:S(2)}) collective-permute-start(bf16[176,2304]{1,0:T(8,128)(2,1)} %get-tuple-element.612), channel_id=1, source_target_pairs={{0,8},{4,12},{8,16},{12,20},{16,24},{20,28},{24,0},{28,4},{1,9},{5... | collective-permute-start | bytes 2433032 | tf_op jit(solution)/shard_map/ppermute | solution.py:275
  560.5 50.7 %collective-permute-start.44 = (bf16[288,2304]{1,0:T(8,128)(2,1)}, bf16[288,2304]{1,0:T(8,128)(2,1)}, u32[]{:S(2)}, u32[]{:S(2)}) collective-permute-start(bf16[288,2304]{1,0:T(8,128)(2,1)} %add_convert_fusion.18), channel_id=1, source_target_pairs={{0,8},{4,12},{8,16},{12,20},{16,24},{20,28},{24,0},{28,4},{1,9},{5... | collective-permute-start | bytes 3981320 | tf_op jit(solution)/shard_map/ppermute | solution.py:275
  560.5 50.7 %collective-permute-start.43 = (bf16[288,2304]{1,0:T(8,128)(2,1)}, bf16[288,2304]{1,0:T(8,128)(2,1)}, u32[]{:S(2)}, u32[]{:S(2)}) collective-permute-start(bf16[288,2304]{1,0:T(8,128)(2,1)} %get-tuple-element.625), channel_id=1, source_target_pairs={{0,4},{4,0},{8,12},{12,8},{16,20},{20,16},{24,28},{28,24},{1,5},{5... | collective-permute-start | bytes 3981320 | tf_op jit(solution)/shard_map/ppermute | solution.py:278
  563.3 47.9 %collective-permute-start.45 = (bf16[176,2304]{1,0:T(8,128)(2,1)}, bf16[176,2304]{1,0:T(8,128)(2,1)}, u32[]{:S(2)}, u32[]{:S(2)}) collective-permute-start(bf16[176,2304]{1,0:T(8,128)(2,1)} %add_convert_fusion.28), channel_id=1, source_target_pairs={{0,8},{4,12},{8,16},{12,20},{16,24},{20,28},{24,0},{28,4},{1,9},{5... | collective-permute-start | bytes 2433032 | tf_op jit(solution)/shard_map/ppermute | solution.py:275
  611.2 54.2 %collective-permute-start.47 = (bf16[448,2304]{1,0:T(8,128)(2,1)}, bf16[448,2304]{1,0:T(8,128)(2,1)}, u32[]{:S(2)}, u32[]{:S(2)}) collective-permute-start(bf16[448,2304]{1,0:T(8,128)(2,1)} %get-tuple-element.639), channel_id=1, source_target_pairs={{0,1},{1,0},{2,3},{3,2},{4,5},{5,4},{6,7},{7,6},{8,9},{9,8},{10,11... | collective-permute-start | bytes 6193160 | tf_op jit(solution)/shard_map/ppermute | solution.py:281
  614.4 51.0 %collective-permute-start.48 = (bf16[288,2304]{1,0:T(8,128)(2,1)}, bf16[288,2304]{1,0:T(8,128)(2,1)}, u32[]{:S(2)}, u32[]{:S(2)}) collective-permute-start(bf16[288,2304]{1,0:T(8,128)(2,1)} %add_convert_fusion.17), channel_id=1, source_target_pairs={{0,8},{4,12},{8,16},{12,20},{16,24},{20,28},{24,0},{28,4},{1,9},{5... | collective-permute-start | bytes 3981320 | tf_op jit(solution)/shard_map/ppermute | solution.py:275
  614.4 51.0 %collective-permute-start.46 = (bf16[288,2304]{1,0:T(8,128)(2,1)}, bf16[288,2304]{1,0:T(8,128)(2,1)}, u32[]{:S(2)}, u32[]{:S(2)}) collective-permute-start(bf16[288,2304]{1,0:T(8,128)(2,1)} %get-tuple-element.638), channel_id=1, source_target_pairs={{0,4},{4,0},{8,12},{12,8},{16,20},{20,16},{24,28},{28,24},{1,5},{5... | collective-permute-start | bytes 3981320 | tf_op jit(solution)/shard_map/ppermute | solution.py:278
  617.2 48.2 %collective-permute-start.49 = (bf16[176,2304]{1,0:T(8,128)(2,1)}, bf16[176,2304]{1,0:T(8,128)(2,1)}, u32[]{:S(2)}, u32[]{:S(2)}) collective-permute-start(bf16[176,2304]{1,0:T(8,128)(2,1)} %add_convert_fusion.27), channel_id=1, source_target_pairs={{0,8},{4,12},{8,16},{12,20},{16,24},{20,28},{24,0},{28,4},{1,9},{5... | collective-permute-start | bytes 2433032 | tf_op jit(solution)/shard_map/ppermute | solution.py:275
  667.7 33.9 %collective-permute-start.52 = (bf16[288,2304]{1,0:T(8,128)(2,1)S(1)}, bf16[288,2304]{1,0:T(8,128)(2,1)S(1)}, u32[]{:S(2)}, u32[]{:S(2)}) collective-permute-start(bf16[288,2304]{1,0:T(8,128)(2,1)S(1)} %add_convert_fusion.16), channel_id=1, source_target_pairs={{0,8},{4,12},{8,16},{12,20},{16,24},{20,28},{24,0},{28,4},{1,9},{5... | collective-permute-start | bytes 3981320 | tf_op jit(solution)/shard_map/ppermute | solution.py:275
  667.8 61.0 %collective-permute-start.51 = (bf16[576,2304]{1,0:T(8,128)(2,1)S(1)}, bf16[576,2304]{1,0:T(8,128)(2,1)S(1)}, u32[]{:S(2)}, u32[]{:S(2)}) collective-permute-start(bf16[576,2304]{1,0:T(8,128)(2,1)S(1)} %get-tuple-element.656), channel_id=1, source_target_pairs={{0,4},{4,0},{8,12},{12,8},{16,20},{20,16},{24,28},{28,24},{1,5},{5... | collective-permute-start | bytes 7962632 | tf_op jit(solution)/shard_map/ppermute | solution.py:278
  670.4 58.3 %collective-permute-start.50 = (bf16[448,2304]{1,0:T(8,128)(2,1)S(1)}, bf16[448,2304]{1,0:T(8,128)(2,1)S(1)}, u32[]{:S(2)}, u32[]{:S(2)}) collective-permute-start(bf16[448,2304]{1,0:T(8,128)(2,1)S(1)} %add_convert_fusion.7), channel_id=1, source_target_pairs={{0,2},{1,3},{2,0},{3,1},{4,6},{5,7},{6,4},{7,5},{8,10},{9,11},{10,... | collective-permute-start | bytes 6193160 | tf_op jit(solution)/shard_map/ppermute | solution.py:284
  673.8 54.9 %collective-permute-start.53 = (bf16[288,2304]{1,0:T(8,128)(2,1)S(1)}, bf16[288,2304]{1,0:T(8,128)(2,1)S(1)}, u32[]{:S(2)}, u32[]{:S(2)}) collective-permute-start(bf16[288,2304]{1,0:T(8,128)(2,1)S(1)} %add_convert_fusion.15), channel_id=1, source_target_pairs={{0,8},{4,12},{8,16},{12,20},{16,24},{20,28},{24,0},{28,4},{1,9},{5... | collective-permute-start | bytes 3981320 | tf_op jit(solution)/shard_map/ppermute | solution.py:275
  732.6 68.7 %collective-permute-start.56 = (bf16[288,2304]{1,0:T(8,128)(2,1)}, bf16[288,2304]{1,0:T(8,128)(2,1)}, u32[]{:S(2)}, u32[]{:S(2)}) collective-permute-start(bf16[288,2304]{1,0:T(8,128)(2,1)} %add_convert_fusion.13), channel_id=1, source_target_pairs={{0,8},{4,12},{8,16},{12,20},{16,24},{20,28},{24,0},{28,4},{1,9},{5... | collective-permute-start | bytes 3981320 | tf_op jit(solution)/shard_map/ppermute | solution.py:275
  732.6 68.7 %collective-permute-start.54 = (bf16[576,2304]{1,0:T(8,128)(2,1)}, bf16[576,2304]{1,0:T(8,128)(2,1)}, u32[]{:S(2)}, u32[]{:S(2)}) collective-permute-start(bf16[576,2304]{1,0:T(8,128)(2,1)} %get-tuple-element.663), channel_id=1, source_target_pairs={{0,4},{4,0},{8,12},{12,8},{16,20},{20,16},{24,28},{28,24},{1,5},{5... | collective-permute-start | bytes 7962632 | tf_op jit(solution)/shard_map/ppermute | solution.py:278
  738.5 62.8 %collective-permute-start.55 = (bf16[288,2304]{1,0:T(8,128)(2,1)}, bf16[288,2304]{1,0:T(8,128)(2,1)}, u32[]{:S(2)}, u32[]{:S(2)}) collective-permute-start(bf16[288,2304]{1,0:T(8,128)(2,1)} %add_convert_fusion.14), channel_id=1, source_target_pairs={{0,8},{4,12},{8,16},{12,20},{16,24},{20,28},{24,0},{28,4},{1,9},{5... | collective-permute-start | bytes 3981320 | tf_op jit(solution)/shard_map/ppermute | solution.py:275
  801.3 38.0 %collective-permute-start.59 = (bf16[448,2304]{1,0:T(8,128)(2,1)}, bf16[448,2304]{1,0:T(8,128)(2,1)}, u32[]{:S(2)}, u32[]{:S(2)}) collective-permute-start(bf16[448,2304]{1,0:T(8,128)(2,1)} %get-tuple-element.685), channel_id=1, source_target_pairs={{0,1},{1,0},{2,3},{3,2},{4,5},{5,4},{6,7},{7,6},{8,9},{9,8},{10,11... | collective-permute-start | bytes 6193160 | tf_op jit(solution)/shard_map/ppermute | solution.py:281
  805.2 34.1 %collective-permute-start.60 = (bf16[288,2304]{1,0:T(8,128)(2,1)}, bf16[288,2304]{1,0:T(8,128)(2,1)}, u32[]{:S(2)}, u32[]{:S(2)}) collective-permute-start(bf16[288,2304]{1,0:T(8,128)(2,1)} %add_convert_fusion.12), channel_id=1, source_target_pairs={{0,8},{4,12},{8,16},{12,20},{16,24},{20,28},{24,0},{28,4},{1,9},{5... | collective-permute-start | bytes 3981320 | tf_op jit(solution)/shard_map/ppermute | solution.py:275
  807.2 32.1 %collective-permute-start.58 = (bf16[288,2304]{1,0:T(8,128)(2,1)}, bf16[288,2304]{1,0:T(8,128)(2,1)}, u32[]{:S(2)}, u32[]{:S(2)}) collective-permute-start(bf16[288,2304]{1,0:T(8,128)(2,1)} %get-tuple-element.684), channel_id=1, source_target_pairs={{0,4},{4,0},{8,12},{12,8},{16,20},{20,16},{24,28},{28,24},{1,5},{5... | collective-permute-start | bytes 3981320 | tf_op jit(solution)/shard_map/ppermute | solution.py:278
  812.4 55.0 %collective-permute-start.63 = (bf16[288,2304]{1,0:T(8,128)(2,1)}, bf16[288,2304]{1,0:T(8,128)(2,1)}, u32[]{:S(2)}, u32[]{:S(2)}) collective-permute-start(bf16[288,2304]{1,0:T(8,128)(2,1)} %add_convert_fusion.11), channel_id=1, source_target_pairs={{0,8},{4,12},{8,16},{12,20},{16,24},{20,28},{24,0},{28,4},{1,9},{5... | collective-permute-start | bytes 3981320 | tf_op jit(solution)/shard_map/ppermute | solution.py:275
  839.3 68.8 %collective-permute-start.62 = (bf16[576,1536]{1,0:T(8,128)(2,1)}, bf16[576,1536]{1,0:T(8,128)(2,1)}, u32[]{:S(2)}, u32[]{:S(2)}) collective-permute-start(bf16[576,1536]{1,0:T(8,128)(2,1)} %get-tuple-element.700), channel_id=1, source_target_pairs={{0,4},{4,0},{8,12},{12,8},{16,20},{20,16},{24,28},{28,24},{1,5},{5... | collective-permute-start | bytes 5308424 | tf_op jit(solution)/shard_map/ppermute | solution.py:278
  843.6 64.6 %collective-permute-start.65 = (bf16[448,2304]{1,0:T(8,128)(2,1)S(1)}, bf16[448,2304]{1,0:T(8,128)(2,1)}, u32[]{:S(2)}, u32[]{:S(2)}) collective-permute-start(bf16[448,2304]{1,0:T(8,128)(2,1)S(1)} %add_convert_fusion.5), channel_id=1, source_target_pairs={{0,2},{1,3},{2,0},{3,1},{4,6},{5,7},{6,4},{7,5},{8,10},{9,11},{10,... | collective-permute-start | bytes 6193160 | tf_op jit(solution)/shard_map/ppermute | solution.py:284
  871.1 32.9 %collective-permute-start.64 = (bf16[288,2304]{1,0:T(8,128)(2,1)}, bf16[288,2304]{1,0:T(8,128)(2,1)}, u32[]{:S(2)}, u32[]{:S(2)}) collective-permute-start(bf16[288,2304]{1,0:T(8,128)(2,1)} %add_convert_fusion.10), channel_id=1, source_target_pairs={{0,8},{4,12},{8,16},{12,20},{16,24},{20,28},{24,0},{28,4},{1,9},{5... | collective-permute-start | bytes 3981320 | tf_op jit(solution)/shard_map/ppermute | solution.py:275
  871.1 37.1 %collective-permute-start.61 = (bf16[288,2304]{1,0:T(8,128)(2,1)}, bf16[288,2304]{1,0:T(8,128)(2,1)}, u32[]{:S(2)}, u32[]{:S(2)}) collective-permute-start(bf16[288,2304]{1,0:T(8,128)(2,1)} %get-tuple-element.699), channel_id=1, source_target_pairs={{0,4},{4,0},{8,12},{12,8},{16,20},{20,16},{24,28},{28,24},{1,5},{5... | collective-permute-start | bytes 3981320 | tf_op jit(solution)/shard_map/ppermute | solution.py:278
  910.4 52.5 %collective-permute-start.67 = (bf16[176,2304]{1,0:T(8,128)(2,1)}, bf16[176,2304]{1,0:T(8,128)(2,1)}, u32[]{:S(2)}, u32[]{:S(2)}) collective-permute-start(bf16[176,2304]{1,0:T(8,128)(2,1)} %add_convert_fusion.26), channel_id=1, source_target_pairs={{0,4},{4,0},{8,12},{12,8},{16,20},{20,16},{24,28},{28,24},{1,5},{5... | collective-permute-start | bytes 2433032 | tf_op jit(solution)/shard_map/ppermute | solution.py:278
  915.3 47.6 %collective-permute-start.69 = (bf16[288,1536]{1,0:T(8,128)(2,1)}, bf16[288,1536]{1,0:T(8,128)(2,1)}, u32[]{:S(2)}, u32[]{:S(2)}) collective-permute-start(bf16[288,1536]{1,0:T(8,128)(2,1)} %get-tuple-element.902), channel_id=1, source_target_pairs={{0,16},{4,20},{8,24},{12,28},{16,0},{20,4},{24,8},{28,12},{1,17},{... | collective-permute-start | bytes 2654216 | tf_op jit(solution)/shard_map/ppermute | solution.py:275
  916.8 46.2 %collective-permute-start.68 = (bf16[288,1536]{1,0:T(8,128)(2,1)}, bf16[288,1536]{1,0:T(8,128)(2,1)}, u32[]{:S(2)}, u32[]{:S(2)}) collective-permute-start(bf16[288,1536]{1,0:T(8,128)(2,1)} %get-tuple-element.903), channel_id=1, source_target_pairs={{0,24},{4,28},{8,0},{12,4},{16,8},{20,12},{24,16},{28,20},{1,25},{... | collective-permute-start | bytes 2654216 | tf_op jit(solution)/shard_map/ppermute | solution.py:275
  918.9 48.3 %collective-permute-start.66 = (bf16[576,1536]{1,0:T(8,128)(2,1)}, bf16[576,1536]{1,0:T(8,128)(2,1)}, u32[]{:S(2)}, u32[]{:S(2)}) collective-permute-start(bf16[576,1536]{1,0:T(8,128)(2,1)} %get-tuple-element.710), channel_id=1, source_target_pairs={{0,4},{4,0},{8,12},{12,8},{16,20},{20,16},{24,28},{28,24},{1,5},{5... | collective-permute-start | bytes 5308424 | tf_op jit(solution)/shard_map/ppermute | solution.py:278
  (119 other events, 2212.5 us)

commit v4 on v3

--- a/solution.py
+++ b/solution.py
@@ -142,12 +142,23 @@
     hidden[...] = (residual * factor_of(residual) * (1.0 + gains[2:3])).astype(low)
 
 
-def ffn_of(own, peer):
-    return jnp.concatenate([own[...].astype(wide), peer[...].astype(wide)], axis=1)
-
-
-def ffn_back_body(side, own, peer, grad_out, gains, grad_own, grad_peer, grad_gain):
-    ffn = ffn_of(own, peer)
+def ffn_of(groups, ordered, place, own, first, last):
+    own, first, last = (part[...].astype(wide) for part in (own, first, last))
+    if ordered:
+        return jnp.concatenate([own, first, last], axis=1)
+    outer = groups // 2
+    by_step = pieces_of(first, outer // 2) + pieces_of(last, outer // 2)
+    peer = []
+    for at in range(outer):
+        block = by_step[(outer - 1 - at) % outer]
+        for spot in range(outer - 1):
+            block = jnp.where(place == spot, by_step[(spot - at) % outer], block)
+        peer.append(block)
+    return jnp.concatenate([own] + peer, axis=1)
+
+
+def ffn_back_body(groups, ordered, spot, own, first, last, grad_out, gains, grad_own, grad_peer, grad_gain):
+    ffn = ffn_of(groups, ordered, spot[1], own, first, last)
     grad, term = back_of(ffn, factor_of(ffn), gains[3:4], grad_out[...].astype(wide))
     half = ffn.shape[1] // 2
     grad_own[...] = grad[:, :half].astype(low)
@@ -155,10 +166,10 @@
     add_up(grad_gain, term)
 
 
-def out_body(groups, side, inputs, attn, own, peer, gains, out):
-    ffn = ffn_of(own, peer)
+def out_body(groups, ordered, spot, inputs, attn, own, first, last, gains, out):
+    ffn = ffn_of(groups, ordered, spot[1], own, first, last)
     value = residual_of(inputs, attn, gains)[0] + ffn * factor_of(ffn) * (1.0 + gains[3:4])
-    out[...] = straighten(value, side[0], groups).astype(low)
+    out[...] = straighten(value, spot[0], groups).astype(low)
 
 
 def attn_back_body(side, inputs, attn, grad_hidden, grad_out, gains, grad_resid, grad_attn, gain1, gain2):
@@ -253,7 +264,8 @@
     outer = groups // 2
     index = lax.axis_index("dp")
     place = index // 2
-    side = lax.rem(index, 2).astype(jnp.int32).reshape(1)
+    side = lax.rem(index, 2)
+    spot = jnp.stack([side, place]).astype(jnp.int32)
     length, features = tokens.shape
     half = features // 2
     count = features // groups
@@ -296,7 +308,7 @@
     valid = (segments >= 0).astype(wide)[:, None]
 
     def projections(inputs, weights, gains):
-        (normed_low,) = by_rows(normed_body, side, [inputs], [gains], [(features, low)], [])
+        (normed_low,) = by_rows(normed_body, spot, [inputs], [gains], [(features, low)], [])
         mixer_raw = dot("td,de->te", normed_low, weights[:, :width_qkv])
         qraw = mixer_raw[:, :width_q].reshape(length, heads_local, HEAD_DIM)
         kraw = mixer_raw[:, width_q : width_q + width_kv].reshape(length, kv_local, HEAD_DIM)
@@ -344,23 +356,22 @@
     def weight_grad(first, second):
         return plain(dot("td,te->de", first, second).astype(low))
 
-    def ffn_back(ffn_own, ffn_peer, grad_out, gains):
-        return by_rows(
-            ffn_back_body, side, [ffn_own, ffn_peer, grad_out], [gains], [(half, low)] * 2, [features]
-        )
-
-    def layer_out(inputs, attn_sum, ffn_own, ffn_peer, gains):
-        rows = [inputs, attn_sum, ffn_own, ffn_peer]
-        return by_rows(partial(out_body, groups), side, rows, [gains], [(features, low)], [])[0]
+    def ffn_back(ffn_parts, grad_out, gains, ordered):
+        body = partial(ffn_back_body, groups, ordered)
+        return by_rows(body, spot, [*ffn_parts, grad_out], [gains], [(half, low)] * 2, [features])
+
+    def layer_out(inputs, attn_sum, ffn_parts, gains, ordered):
+        rows = [inputs, attn_sum, *ffn_parts]
+        return by_rows(partial(out_body, groups, ordered), spot, rows, [gains], [(features, low)], [])[0]
 
     def attn_back(inputs, attn_sum, grad_hidden, grad_out, gains):
         rows = [inputs, attn_sum, grad_hidden, grad_out]
         outs = [(features, wide), (features, low)]
-        return by_rows(attn_back_body, side, rows, [gains], outs, [features] * 2)
+        return by_rows(attn_back_body, spot, rows, [gains], outs, [features] * 2)
 
     def in_back(inputs, grad_normed, grad_resid, gains):
         rows = [inputs, grad_normed, grad_resid]
-        return by_rows(partial(in_back_body, groups), side, rows, [gains], [(features, wide)], [features])
+        return by_rows(partial(in_back_body, groups), spot, rows, [gains], [(features, wide)], [features])
 
     steps_done = float(ADAM_STEP)
 
@@ -411,7 +422,7 @@
 
     def start(tokens_in, cotangent_in):
         return by_rows(
-            partial(start_body, groups), side, [tokens_in, cotangent_in, valid], [], [(features, low)] * 2, []
+            partial(start_body, groups), spot, [tokens_in, cotangent_in, valid], [], [(features, low)] * 2, []
         )
 
     clock = [jnp.broadcast_to(valid[:8], (8, 128))]
@@ -479,13 +490,13 @@
         inputs, grad_out = start(tokens, cotangent)
         attn_part, saved = attention(projections(inputs, full, gains), full)
         attn_sum = over_heads(attn_part)
-        (hidden_in,) = by_rows(hidden_body, side, [inputs, attn_sum], [gains], [(features, low)], [])
+        (hidden_in,) = by_rows(hidden_body, spot, [inputs, attn_sum], [gains], [(features, low)], [])
         gate_out, up_out = dot("td,df->tf", hidden_in, wg), dot("td,df->tf", hidden_in, wu)
         act_low = gated(gate_out, up_out).astype(low)
         ffn = over_heads(down_part(act_low, wd))
-        own, peer = ffn[:, :half], ffn[:, half:]
-        block_out = layer_out(inputs, attn_sum, own, peer, gains)
-        grad_own, grad_peer, gain3 = ffn_back(own, peer, grad_out, gains)
+        ffn_parts = ffn[:, :half], ffn[:, half : half + half // 2], ffn[:, half + half // 2 :]
+        block_out = layer_out(inputs, attn_sum, ffn_parts, gains, True)
+        grad_own, grad_peer, gain3 = ffn_back(ffn_parts, grad_out, gains, True)
         grad_gate, grad_up = act_back(grad_own, grad_peer, gate_out, up_out, wd[:half], wd[half:])
         sum_down = scattered(weight_grad(jnp.concatenate([grad_own, grad_peer], axis=1), act_low))
         sums = [scattered(weight_grad(hidden_in, grad)) for grad in (grad_gate, grad_up)]
@@ -544,7 +555,7 @@
     u3, d1, h2, v2 = around(u2), around(down), swap(g2), swap(u2)
     mine = add(kept, across)
     attn_sum = together(mine, near(mine))
-    (hidden_in,) = by_rows(hidden_body, side, [inputs, attn_sum], [gains], [(features, low)], [])
+    (hidden_in,) = by_rows(hidden_body, spot, [inputs, attn_sum], [gains], [(features, low)], [])
     wg = put(put(wg, g2, 2), h1, 1, half)
     wu = put(put(wu, u2, 2), v1, 1, half)
     u3, g3, d1, h2, v2, hidden_in, wg, wu = sync((u3, g3, d1, h2, v2, hidden_in, wg, wu))
@@ -554,7 +565,7 @@
     wg = put(put(wg, g3, 3), h2, 2, half)
     wu = put(put(wu, u3, 3), v2, 2, half)
     wd_own = put(put(jnp.zeros((half, width_ff), low), down, 0), d1, 1)
-    wd_peer = put(jnp.zeros((half, width_ff), low), down_far, 0, cut)
+    wd_peer = jnp.zeros((half, width_ff), low)
     d3 = around(d2)
     wg = put(wg, h3, 3, half)
     gate_out = dot("td,df->tf", hidden_in, wg)
@@ -570,22 +581,30 @@
     wd_own = put(put(wd_own, d2, 2), d3, 3)
     d2_cut, d3_cut = d2[:cut], d3[:cut]
     given, kept = apart(down_part(act_low, wd_own))
-    f1, e0, e1, act_low, given, kept, d2_cut, d3_cut = sync((f1, e0, e1, act_low, given, kept, d2_cut, d3_cut))
+    f1, e0, e1, act_low, given, kept, d2_cut, d3_cut, wd_peer = sync(
+        (f1, e0, e1, act_low, given, kept, d2_cut, d3_cut, wd_peer)
+    )
     f2, e2, e3 = around(f1), swap(d2_cut), swap(d3_cut)
     kept = add(kept, near(given))
     across = far(kept)
-    wd_peer, f1, e0, e1 = behind(wd_peer, f1, e0, e1)
     f3 = around(tie(f2, kept))
-    wd_peer = put(put(put(put(wd_peer, f1, 1, cut), f2, 2, cut), e0, 0), e1, 1)
-    f3, e2, e3, across, kept, wd_peer = sync((f3, e2, e3, across, kept, wd_peer))
-    wd_peer = put(put(put(wd_peer, f3, 3, cut), e2, 2), e3, 3)
-    given, kept_peer = apart(down_part(act_low, wd_peer))
-    mine = add(kept, across)
-    kept_peer = add(kept_peer, near(given))
-    ffn_own = together(mine, near(mine))
-    across = far(kept_peer)
-    mine = add(kept_peer, across)
-    ffn_peer = together(mine, near(mine))
+    first_rows = jnp.concatenate([e0, down_far, e1, f1], axis=0)
+    given, kept_first = apart(down_part(act_low, first_rows))
+    kept_first = add(kept_first, near(given))
+    across_first = far(tie(kept_first, kept))
+    wd_peer = put(put(put(put(wd_peer, e0, 0), down_far, 0, cut), e1, 1), f1, 1, cut)
+    f2, f3, e2, e3, across, kept, across_first, kept_first, wd_peer = sync(
+        (f2, f3, e2, e3, across, kept, across_first, kept_first, wd_peer)
+    )
+    last_rows = jnp.concatenate([e2, f2, e3, f3], axis=0)
+    given, kept_last = apart(down_part(act_low, last_rows))
+    kept_last = add(kept_last, near(given))
+    across_last = far(kept_last)
+    ffn_parts = []
+    for held, came in ((kept, across), (kept_first, across_first), (kept_last, across_last)):
+        mine = add(held, came)
+        ffn_parts.append(together(mine, near(mine)))
+    wd_peer = put(put(put(put(wd_peer, e2, 2), f2, 2, cut), e3, 3), f3, 3, cut)
 
     def piece(tensor, hops):
         return rows_at(tensor, lax.rem(place + hops, outer), count)
@@ -608,11 +627,13 @@
         cuts = [lax.dynamic_slice_in_dim(t, target, count, 0) for t in tensors]
         return plain(jnp.concatenate(cuts, axis=1))
 
-    grad_ffn_own, grad_ffn_peer, grad_gain3 = ffn_back(ffn_own, ffn_peer, grad_out, gains)
+    grad_ffn_own, grad_ffn_peer, grad_gain3 = ffn_back(ffn_parts, grad_out, gains, False)
     wd_grad = weight_grad(grad_ffn_peer, act_low)
     cut = count * 7 // 18 // 16 * 16
     sent, far_parts = jnp.concatenate(rows_of(wd_grad, 0, cut), axis=0), rows_of(wd_grad, cut, count - cut)
-    sent, far_parts, grad_ffn_own, grad_ffn_peer = sync((sent, far_parts, grad_ffn_own, grad_ffn_peer))
+    sent, far_parts, grad_ffn_own, grad_ffn_peer, wd_peer = sync(
+        (sent, far_parts, grad_ffn_own, grad_ffn_peer, wd_peer)
+    )
 
     arrived, f3 = swap(sent), around(far_parts[0])
 
@@ -644,25 +665,27 @@
     )
     h2, theirs = swap(gate_sent[1]), near(given)
     came = around(plus(piece(wd_grad, 2), grown(1), came))
-    f1 = around(add(far_parts[2], f2))
-
-    def rest_of_grads(grad_gate, grad_up, hidden_in, gate_sent):
+
+    def rest_of_grads(grad_gate, grad_up, hidden_in, gate_sent, h3):
         up_sent = pieces(weight_grad(hidden_in[:, half:], grad_up))
         wg_grad = weight_grad(hidden_in[:, :half], grad_gate)
         mixed_sent = [jnp.concatenate(pair, axis=0) for pair in zip(gate_sent[2:], up_sent[:2])]
-        return mixed_sent, up_sent[2:], wg_grad, weight_grad(hidden_in[:, :half], grad_up)
-
-    mixed_sent, up_sent, wg_grad, wu_grad = whole(rest_of_grads, grad_gate, grad_up, hidden_in, gate_sent)
-    h2, theirs, came, f1, mixed_sent, up_sent, wg_grad, wu_grad, kept = sync(
-        (h2, theirs, came, f1, mixed_sent, up_sent, wg_grad, wu_grad, kept)
+        gate_first = plus(piece(wg_grad, 3), h3)
+        return mixed_sent, up_sent[2:], wg_grad, weight_grad(hidden_in[:, :half], grad_up), gate_first
+
+    mixed_sent, up_sent, wg_grad, wu_grad, gate_first = whole(
+        rest_of_grads, grad_gate, grad_up, hidden_in, gate_sent, h3
+    )
+    h2, theirs, came, mixed_sent, up_sent, wg_grad, wu_grad, kept, gate_first = sync(
+        (h2, theirs, came, mixed_sent, up_sent, wg_grad, wu_grad, kept, gate_first)
     )
     pair = swap(mixed_sent[0])
     kept = add(kept, theirs)
     across = far(kept)
     came = around(plus(piece(wd_grad, 1), grown(2), came))
-    gate_came = around(plus(piece(wg_grad, 3), h3))
-    across, pair, came, gate_came, kept, mixed_sent[1], up_sent = sync(
-        (across, pair, came, gate_came, kept, mixed_sent[1], up_sent)
+    gate_came = around(gate_first)
+    across, pair, came, gate_came, kept, mixed_sent[1], up_sent, f2 = sync(
+        (across, pair, came, gate_came, kept, mixed_sent[1], up_sent, f2)
     )
     h1, v3 = pair[:count], pair[count:]
     pair = swap(mixed_sent[1])
@@ -670,6 +693,7 @@
     theirs = near(mine)
     gate_came = around(plus(piece(wg_grad, 2), h2, gate_came))
     up_came = around(plus(piece(wu_grad, 3), v3))
+    f1 = around(add(far_parts[2], f2))
 
     def mixer_back(inputs, attn_sum, mine, theirs, grad_out, gains, full, saved):
         grad_hidden = together(mine, theirs)
@@ -681,8 +705,8 @@
     given, kept, grad_resid, grad_attn, grad_gain1, grad_gain2, grad_raw = whole(
         mixer_back, inputs, attn_sum, mine, theirs, grad_out, gains, full, saved
     )
-    pair, gate_came, up_came, given, kept, grad_resid, grad_attn, grad_raw, up_sent = sync(
-        (pair, gate_came, up_came, given, kept, grad_resid, grad_attn, grad_raw, up_sent)
+    pair, gate_came, up_came, f1, given, kept, grad_resid, grad_attn, grad_raw, up_sent = sync(
+        (pair, gate_came, up_came, f1, given, kept, grad_resid, grad_attn, grad_raw, up_sent)
     )
     h0, v2 = pair[:count], pair[count:]
     v1, theirs = swap(up_sent[0]), near(given)
@@ -714,18 +738,20 @@
     mine = add(kept, across)
     theirs = near(mine)
 
-    def finish(inputs, mine, theirs, grad_resid, attn_sum, ffn_own, ffn_peer, gains):
-        block_out = layer_out(inputs, attn_sum, ffn_own, ffn_peer, gains)
+    def finish(inputs, mine, theirs, grad_resid, attn_sum, ffn_parts, gains):
+        block_out = layer_out(inputs, attn_sum, ffn_parts, gains, False)
         input_grad, gain0 = in_back(inputs, together(mine, theirs), grad_resid, gains)
         return block_out, input_grad, gain0
 
     block_out, input_grad, grad_gain0 = whole(
-        finish, inputs, mine, theirs, grad_resid, attn_sum, ffn_own, ffn_peer, gains
+        finish, inputs, mine, theirs, grad_resid, attn_sum, ffn_parts, gains
     )
     x10, b_far, m3, m2, block_out, input_grad, grad_gain0 = sync(
         (x10, b_far, m3, m2, block_out, input_grad, grad_gain0)
     )
-    m1 = around(plus(mixer_own[2], x10[:count]))
+    mixed = plus(mixer_own[2], x10[:count])
+    m1 = around(mixed)
+    came = tie(came, mixed)
     grad_gains = jnp.concatenate([grad_gain0, grad_gain1, grad_gain2, grad_gain3], axis=0)
     gain_sum = grad_gains[:, :half] + swap(grad_gains[:, half:])
     gain_sum = gain_sum.reshape(4, outer, count)

time: 1020 us -> 1010 us (level)
    ppermute x33, waiting for transfers between devices: 219 us -> 202 us  [around(): return lax.ppermute(tensor, 'dp', ring_pairs(groups, hops))]
    ppermute x5 -> x6, waiting for transfers between devices: 23.2 us -> 33 us  [far(): return lax.ppermute(tensor, 'mp', swap_pairs(parts, 2))]
    convert_element_type x13 -> x15, other arithmetic: 22.3 us -> 20.1 us  [add(): return (first.astype(wide) + second.astype(wide)).astype(kind)]
    dot_general x25 -> x26, matrix products: 217 us -> 215 us  [dot(): return jnp.einsum(pattern, first, second, preferred_element_type=wide)]
  transfers between devices with their start and end apart: 76 -> 79, of which waited for: 34 -> 34; matrix products, arithmetic and copies ran while one was open for 43% -> 43% of each run, Pallas kernels for 5% -> 6%
where the time goes in v4:
time: 1010 us; the launch traced here: 996 us
  waiting for transfers between devices  376 us (37%)
  matrix products  217 us (21%)
  other arithmetic  148 us (15%)
  local copies, waits for them, and re-layouts  121 us (12%)
  Pallas kernels  66.7 us (7%)
  starting transfers between devices  64.7 us (6%)
    dot_general x26, matrix products, dot(): return jnp.einsum(pattern, first, second, preferred_element_type=wide)  215 us
    ppermute x33, waiting for transfers between devices, around(): return lax.ppermute(tensor, 'dp', ring_pairs(groups, hops))  202 us
    ppermute x28, waiting for transfers between devices, swap(): return lax.ppermute(tensor, 'dp', swap_pairs(groups, 1))  133 us
    pallas_call x7, Pallas kernels, by_rows(): pl.pallas_call(body, grid=(length // BLOCK,), in_specs=[pl.BlockSpec(memo...  66.7 us
    dynamic_update_slice x35, local copies, waits for them, and re-layouts, put(): lax.dynamic_update_slice_in_dim(full, piece, source(step) * count + offse...  45.7 us
    convert_element_type x11, other arithmetic, plus(): return both.astype(kind)  37.2 us
    ppermute x6, waiting for transfers between devices, far(): return lax.ppermute(tensor, 'mp', swap_pairs(parts, 2))  33 us
    ppermute x28, starting transfers between devices, swap(): return lax.ppermute(tensor, 'dp', swap_pairs(groups, 1))  30.5 us
  transfers between devices with their start and end apart: 79, of which 34 were waited for; matrix products, arithmetic and copies ran while one was open for 43% of the time, Pallas kernels for 6%

profile of v4, /device:TPU:0, one launch (start us, length us, event | category | flops | bytes accessed | tf_op | source)
XLA Modules:
  0.0 995.9 jit_solution(1377611299799137633)
XLA Ops:
  19.8 8.8 shard_map.404
  41.9 12.8 %collective-permute-done.3 = bf16[304,1536]{1,0:T(8,128)(2,1)S(1)} collective-permute-done((bf16[304,1536]{1,0:T(8,128)(2,1)}, bf16[304,1536]{1,0:T(8,128)(2,1)S(1)}, u32[]{:S(2)}, u32[]{:S(2)}) %collective-permute-start.3) | collective-permute-done | bytes 933920 | tf_op jit(solution)/shard_map/ppermute | solution.py:290
  63.0 9.8 copy.140
  87.5 10.4 %collective-permute-done.8 = bf16[144,2304]{1,0:T(8,128)(2,1)S(1)} collective-permute-done((bf16[144,2304]{1,0:T(8,128)(2,1)S(1)}, bf16[144,2304]{1,0:T(8,128)(2,1)S(1)}, u32[]{:S(2)}, u32[]{:S(2)}) %collective-permute-start.8) | collective-permute-done | bytes 663584 | tf_op jit(solution)/shard_map/ppermute | solution.py:290
  97.9 16.0 %collective-permute-done.6 = bf16[304,1536]{1,0:T(8,128)(2,1)S(1)} collective-permute-done((bf16[304,1536]{1,0:T(8,128)(2,1)S(1)}, bf16[304,1536]{1,0:T(8,128)(2,1)S(1)}, u32[]{:S(2)}, u32[]{:S(2)}) %collective-permute-start.6) | collective-permute-done | bytes 933920 | tf_op jit(solution)/shard_map/ppermute | solution.py:290
  121.9 43.4 %conditional.7 = (bf16[448,2304]{1,0:T(8,128)(2,1)S(1)}, bf16[448,2304]{1,0:T(8,128)(2,1)S(1)}, bf16[896,2304]{1,0:T(8,128)(2,1)}, bf16[896,1,2,256]{3,0,2,1:T(8...) conditional(s32[]{:T(128)} %convert_element_type.482, ...), branch_computations={%region_1.2_spmd, %region_2.5_spmd} | conditional | flops 8014624768 | bytes 162301568 | solution.py:442
  191.1 49.4 %collective-permute-done.14 = bf16[288,2304]{1,0:T(8,128)(2,1)S(1)} collective-permute-done((bf16[288,2304]{1,0:T(8,128)(2,1)}, bf16[288,2304]{1,0:T(8,128)(2,1)S(1)}, u32[]{:S(2)}, u32[]{:S(2)}) %collective-permute-start.14) | collective-permute-done | bytes 1327136 | tf_op jit(solution)/shard_map/ppermute | solution.py:287
  267.4 37.3 %collective-permute-done.21 = bf16[288,2304]{1,0:T(8,128)(2,1)} collective-permute-done((bf16[288,2304]{1,0:T(8,128)(2,1)}, bf16[288,2304]{1,0:T(8,128)(2,1)}, u32[]{:S(2)}, u32[]{:S(2)}) %collective-permute-start.21) | collective-permute-done | bytes 1327136 | tf_op jit(solution)/shard_map/ppermute | solution.py:290
  318.1 20.2 %collective-permute-done.26 = bf16[288,2304]{1,0:T(8,128)(2,1)S(1)} collective-permute-done((bf16[288,2304]{1,0:T(8,128)(2,1)}, bf16[288,2304]{1,0:T(8,128)(2,1)S(1)}, u32[]{:S(2)}, u32[]{:S(2)}) %collective-permute-start.26) | collective-permute-done | bytes 1327136 | tf_op jit(solution)/shard_map/ppermute | solution.py:290
  341.3 13.8 %fusion.118 = f32[896,2304]{1,0:T(8,128)} fusion(bf16[896,2304]{1,0:T(8,128)(2,1)S(1)} %copy-done.31, bf16[2304,2304]{1,0:T(8,128)(2,1)} %constant_dynamic-update-slice_fusion.15), kind=kOutput, calls=%fused_computation.336 | convolution fusion | flops 9512681472 | bytes 23003136 | tf_op jit(solution)/shard_map/td,df->tf/dot_general | solution.py:284
  355.1 13.0 %collective-permute-done.27 = bf16[288,2304]{1,0:T(8,128)(2,1)S(1)} collective-permute-done((bf16[288,2304]{1,0:T(8,128)(2,1)}, bf16[288,2304]{1,0:T(8,128)(2,1)S(1)}, u32[]{:S(2)}, u32[]{:S(2)}) %collective-permute-start.27) | collective-permute-done | bytes 1327136 | tf_op jit(solution)/shard_map/ppermute | solution.py:290
  374.4 16.9 %fusion.67 = (bf16[896,2304]{1,0:T(8,128)(2,1)}, f32[896,2304]{1,0:T(8,128)}) fusion(f32[896,2304]{1,0:T(8,128)} %fusion.118, bf16[896,2304]{1,0:T(8,128)(2,1)S(1)} %copy-done.31, bf16[2304,2304]{1,0:T(8,128)(2,1)} %constant_dynamic-update-slice_fusion.10), kind=kOutput, calls=%fused_computation.145 | convolution fusion | flops 9533325312 | bytes 35389440 | tf_op jit(solution)/shard_map/td,df->tf/dot_general | solution.py:284
  391.5 8.9 convolution_convert_fusion.10
  419.7 8.9 collective-permute-done.35
  428.6 19.5 %collective-permute-done.38 = bf16[448,576]{1,0:T(8,128)(2,1)S(1)} collective-permute-done((bf16[448,576]{1,0:T(8,128)(2,1)S(1)}, bf16[448,576]{1,0:T(8,128)(2,1)S(1)}, u32[]{:S(2)}, u32[]{:S(2)}) %collective-permute-start.38) | collective-permute-done | bytes 516128 | tf_op jit(solution)/shard_map/ppermute | solution.py:296
  458.5 13.5 %collective-permute-done.42 = bf16[448,576]{1,0:T(8,128)(2,1)S(1)} collective-permute-done((bf16[448,576]{1,0:T(8,128)(2,1)S(1)}, bf16[448,576]{1,0:T(8,128)(2,1)S(1)}, u32[]{:S(2)}, u32[]{:S(2)}) %collective-permute-start.42) | collective-permute-done | bytes 516128 | tf_op jit(solution)/shard_map/ppermute | solution.py:296
  475.7 9.6 shard_map.406
  485.3 8.6 convolution_convert_fusion.9
  499.6 48.7 %conditional.8 = (bf16[896,2304]{1,0:T(8,128)(2,1)}, bf16[896,2304]{1,0:T(8,128)(2,1)}, bf16[1152,2304]{1,0:T(8,128)(2,1)}, bf16[288,2304]{1,0:T(8,128)(2,1)}, b...) conditional(s32[]{:T(128)} %convert_element_type.482, () %tuple.125, ...), branch_computations={%region_5.6_spmd, %region_6.7_spmd} | conditional | flops 19082280960 | bytes 135660160 | solution.py:442
  499.6 10.6 %fusion.116 = f32[896,2304]{1,0:T(8,128)} fusion(bf16[896,1152]{1,0:T(8,128)(2,1)} %get-tuple-element.141, bf16[1152,2304]{1,0:T(8,128)(2,1)} %get-tuple-element.142), kind=kOutput, calls=%fused_computation.334 | convolution fusion | flops 4756340736 | bytes 15630336 | tf_op jit(solution)/shard_map/cond/branch_1_fun/td,df->tf/dot_general | solution.py:284
  510.2 18.1 %multiply_convert_fusion = (bf16[896,2304]{1,0:T(8,128)(2,1)}, bf16[896,2304]{1,0:T(8,128)(2,1)}) fusion(f32[896,2304]{1,0:T(8,128)} %get-tuple-element.146, f32[896,2304]{1,0:T(8,128)} %get-tuple-element.145, f32[896,2304]{1,0:T(8,128)} %fusion.116, bf16[896,1152]{1,0:T(8,128)(2,1)} %get-tuple-element.143, bf16[1152,2304]{1,0:T(8,128)(2,1)S(1)} %copy-done.26), kind=kOutput, calls=%fused_computation.49 | convolution fusion | flops 4807950336 | bytes 40402944 | tf_op jit(solution)/shard_map/cond/branch_1_fun/td,df->tf/dot_general | solution.py:284
  528.4 9.7 convolution_convert_fusion.2
  538.1 8.3 fusion.20
  559.8 35.9 %conditional.9 = (bf16[448,2304]{1,0:T(8,128)(2,1)}, bf16[448,2304]{1,0:T(8,128)(2,1)S(1)}) conditional(s32[]{:T(128)} %convert_element_type.482, () %tuple.128, (bf16[896,2304]{1,0:T(8,128)(2,1)}, bf16[2304,2304]{1,0:T(8,128)(2,1)}, bf16[896,2304]{1,0:T(8,128)(2,1)}, bf16[2304,2304]{1,0:T(8,128)(2,1)}, s32[]{:T(128)}) %tuple.129), branch_computations={%region_7.8_spmd, %region_8.9_spmd} | conditional | flops 19029491712 | bytes 58392700 | solution.py:442
  559.8 15.0 %fusion.117 = f32[896,2304]{1,0:T(8,128)} fusion(bf16[896,2304]{1,0:T(8,128)(2,1)} %get-tuple-element.150, bf16[2304,2304]{1,0:T(8,128)(2,1)} %get-tuple-element.151), kind=kOutput, calls=%fused_computation.335 | convolution fusion | flops 9512681472 | bytes 23003136 | tf_op jit(solution)/shard_map/cond/branch_1_fun/tf,df->td/dot_general | solution.py:284
  574.7 17.2 %add_convert_fusion.1 = bf16[896,2304]{1,0:T(8,128)(2,1)} fusion(f32[896,2304]{1,0:T(8,128)} %fusion.117, bf16[896,2304]{1,0:T(8,128)(2,1)} %get-tuple-element.152, bf16[2304,2304]{1,0:T(8,128)(2,1)} %get-tuple-element.153), kind=kOutput, calls=%fused_computation.56 | convolution fusion | flops 9516810240 | bytes 27131904 | tf_op jit(solution)/shard_map/cond/branch_1_fun/tf,df->td/dot_general | solution.py:284
  609.3 34.0 %conditional.10 = (bf16[576,2304]{1,0:T(8,128)(2,1)S(1)}, bf16[576,2304]{1,0:T(8,128)(2,1)}, bf16[288,2304]{1,0:T(8,128)(2,1)}, bf16[288,2304]{1,0:T(8,128)(2,1)...) conditional(s32[]{:T(128)} %convert_element_type.482, () %tuple.131, ...), branch_computations={%region_9.10_spmd, %region_10.11_spmd} | conditional | flops 14290255872 | bytes 102777448 | solution.py:442
  609.3 8.8 convolution_convert_fusion.4
  621.8 9.5 convolution_convert_fusion.3
  631.3 8.3 convolution_convert_fusion.5
  650.2 33.2 %collective-permute-done.54 = bf16[288,2304]{1,0:T(8,128)(2,1)S(1)} collective-permute-done((bf16[288,2304]{1,0:T(8,128)(2,1)S(1)}, bf16[288,2304]{1,0:T(8,128)(2,1)S(1)}, u32[]{:S(2)}, u32[]{:S(2)}) %collective-permute-start.54) | collective-permute-done | bytes 1327136 | tf_op jit(solution)/shard_map/ppermute | solution.py:287
  683.4 26.8 %collective-permute-done.55 = bf16[288,2304]{1,0:T(8,128)(2,1)S(1)} collective-permute-done((bf16[288,2304]{1,0:T(8,128)(2,1)}, bf16[288,2304]{1,0:T(8,128)(2,1)S(1)}, u32[]{:S(2)}, u32[]{:S(2)}) %collective-permute-start.55) | collective-permute-done | bytes 1327136 | tf_op jit(solution)/shard_map/ppermute | solution.py:287
  724.0 59.7 %conditional.11 = (bf16[448,2304]{1,0:T(8,128)(2,1)}, bf16[448,2304]{1,0:T(8,128)(2,1)}, f32[896,2304]{1,0:T(8,128)}, bf16[896,2304]{1,0:T(8,128)(2,1)}, f32[1,2...) conditional(s32[]{:T(128)} %convert_element_type.482, () %tuple.135, (s32[]{:T(128)}, ...), branch_computations={%region_11.12_spmd, %region_12.14_spmd} | conditional | flops 9665787904 | bytes 197016160 | solution.py:442
  732.2 14.1 %branch_1_fun.5 = (f32[896,2304]{1,0:T(8,128)}, bf16[896,2304]{1,0:T(8,128)(2,1)}, f32[1,2304]{1,0:T(1,128)}, f32[1,2304]{1,0:T(1,128)}) custom-call(s32[2]{0:T(128)S(1)} %get-tuple-element.163.side, bf16[896,2304]{1,0:T(8,128)(2,1)S(1)} %copy-done.2, bf16[896,2304]{1,0:T(8,128)(2,1)S(1)} %copy-done.6, bf16[896,2304]{1,0:T(8,128)(2,1)S(1)} %pad_maximum_fusion.3.grad_hidden, ...), custom_call_target="tpu_custom_call" | custom-call | tf_op jit(solution)/shard_map/cond/branch_1_fun/pallas_call | solution.py:73
  758.9 7.7 fusion.37
  774.0 7.4 convolution_convert_fusion.6
  783.6 7.8 collective-permute-done.59
  800.1 23.3 %conditional.12 = (bf16[576,1536]{1,0:T(8,128)(2,1)}, bf16[576,1536]{1,0:T(8,128)(2,1)}, bf16[288,1536]{1,0:T(8,128)(2,1)}, bf16[288,1536]{1,0:T(8,128)(2,1)S(1)...) conditional(s32[]{:T(128)} %convert_element_type.482, () %tuple.138, ...), branch_computations={%region_14.15_spmd, %region_15.16_spmd} | conditional | flops 6366560256 | bytes 62915356 | solution.py:442
  807.3 7.0 convolution_convert_fusion.7
  816.2 7.2 maximum_maximum_fusion
  834.2 23.0 %collective-permute-done.66 = bf16[288,2304]{1,0:T(8,128)(2,1)} collective-permute-done((bf16[288,2304]{1,0:T(8,128)(2,1)}, bf16[288,2304]{1,0:T(8,128)(2,1)}, u32[]{:S(2)}, u32[]{:S(2)}) %collective-permute-start.66) | collective-permute-done | bytes 1327136 | tf_op jit(solution)/shard_map/ppermute | solution.py:287
  864.8 28.9 %collective-permute-done.67 = bf16[288,2304]{1,0:T(8,128)(2,1)} collective-permute-done((bf16[288,2304]{1,0:T(8,128)(2,1)}, bf16[288,2304]{1,0:T(8,128)(2,1)}, u32[]{:S(2)}, u32[]{:S(2)}) %collective-permute-start.67) | collective-permute-done | bytes 1327136 | tf_op jit(solution)/shard_map/ppermute | solution.py:287
  913.1 12.2 %add_multiply_fusion = (f32[2,288,2304]{2,1,0:T(8,128)}, f32[2,288,2304]{2,1,0:T(8,128)}, f32[2,288,2304]{2,1,0:T(8,128)}, f32[2,288,2304]{2,1,0:T(8,128)}) fusion(f32[2,288,2304]{2,1,0:T(8,128)S(1)} %bitcast.230, f32[1,288,2304]{2,1,0:T(8,128)S(1)} %add_bitcast_fusion, f32[1,288,2304]{2,1,0:T(8,128)S(1)} %bitcast.236, f32[2,288,2304]{2,1,0:T(8,128)} %param.47, ...), kind=kLoop, calls=%fused_computation.149 | loop fusion | flops 19906560 | bytes 42467328 | tf_op jit(solution)/shard_map/mul | solution.py:237
  925.4 27.5 %conditional.13 = (bf16[896,2304]{1,0:T(8,128)(2,1)}, f32[896,2304]{1,0:T(8,128)}, f32[1,2304]{1,0:T(1,128)}) conditional(s32[]{:T(128)} %convert_element_type.482, () %tuple.143, (s32[2]{0:T(128)S(1)}, bf16[896,2304]{1,0:T(8,128)(2,1)}, bf16[896,2304]{1,0:T(8,128)(2,1)}, bf16[896,1152]{1,0:T(8,128)(2,1)S(1)}, bf16[896,576]{1,0:T(8,128)(2,1)S(1)}, ...), branch_computations={%region_16.17_spmd, %region_17.18_spmd} | conditional | flops 10321921 | bytes 33030206 | solution.py:442
  925.4 11.8 %branch_1_fun.6 = bf16[896,2304]{1,0:T(8,128)(2,1)} custom-call(s32[2]{0:T(128)S(1)} %get-tuple-element.188.spot.side, bf16[896,2304]{1,0:T(8,128)(2,1)} %get-tuple-element.189.inputs, bf16[896,2304]{1,0:T(8,128)(2,1)} %get-tuple-element.190.attn, bf16[896,1152]{1,0:T(8,128)(2,1)S(1)} %get-tuple-element.191.own, ...), custom_call_target="tpu_custom_call" | custom-call | tf_op jit(solution)/shard_map/cond/branch_1_fun/pallas_call | solution.py:73
  941.8 11.0 %branch_1_fun.7 = (f32[896,2304]{1,0:T(8,128)}, f32[1,2304]{1,0:T(1,128)}) custom-call(s32[2]{0:T(128)S(1)} %get-tuple-element.188.spot.side, bf16[896,2304]{1,0:T(8,128)(2,1)S(1)} %copy-done.3, bf16[896,2304]{1,0:T(8,128)(2,1)S(1)} %pad_maximum_fusion.9.grad_normed, f32[896,2304]{1,0:T(8,128)} %get-tuple-element.198.grad_resid, ...), custom_call_target="tpu_custom_call" | custom-call | tf_op jit(solution)/shard_map/cond/branch_1_fun/pallas_call | solution.py:73
  959.3 6.5 collective-permute-start.74
  979.6 7.8 fusion.87
  (535 shorter events, 397.8 us)
Async XLA Ops:
  81.0 32.9 %collective-permute-start.6 = (bf16[304,1536]{1,0:T(8,128)(2,1)S(1)}, bf16[304,1536]{1,0:T(8,128)(2,1)S(1)}, u32[]{:S(2)}, u32[]{:S(2)}) collective-permute-start(bf16[304,1536]{1,0:T(8,128)(2,1)S(1)} %collective-permute-done.4), channel_id=1, source_target_pairs={{0,4},{4,0},{8,12},{12,8},{16,20},{20,16},{24,28},{28,24},{1,5},{5... | collective-permute-start | bytes 2801672 | tf_op jit(solution)/shard_map/ppermute | solution.py:290
  82.1 32.7 %collective-permute-start.7 = (bf16[288,2304]{1,0:T(8,128)(2,1)}, bf16[288,2304]{1,0:T(8,128)(2,1)}, u32[]{:S(2)}, u32[]{:S(2)}) collective-permute-start(bf16[288,2304]{1,0:T(8,128)(2,1)} %get-tuple-element.530), channel_id=1, source_target_pairs={{0,8},{4,12},{8,16},{12,20},{16,24},{20,28},{24,0},{28,4},{1,9},{5... | collective-permute-start | bytes 3981320 | tf_op jit(solution)/shard_map/ppermute | solution.py:287
  114.8 50.6 %collective-permute-start.12 = (bf16[288,2304]{1,0:T(8,128)(2,1)}, bf16[288,2304]{1,0:T(8,128)(2,1)}, u32[]{:S(2)}, u32[]{:S(2)}) collective-permute-start(bf16[288,2304]{1,0:T(8,128)(2,1)} %get-tuple-element.530), channel_id=1, source_target_pairs={{0,4},{4,0},{8,12},{12,8},{16,20},{20,16},{24,28},{28,24},{1,5},{5... | collective-permute-start | bytes 3981320 | tf_op jit(solution)/shard_map/ppermute | solution.py:290
  115.8 54.4 %collective-permute-start.11 = (bf16[288,2304]{1,0:T(8,128)(2,1)}, bf16[288,2304]{1,0:T(8,128)(2,1)}, u32[]{:S(2)}, u32[]{:S(2)}) collective-permute-start(bf16[288,2304]{1,0:T(8,128)(2,1)} %get-tuple-element.528), channel_id=1, source_target_pairs={{0,4},{4,0},{8,12},{12,8},{16,20},{20,16},{24,28},{28,24},{1,5},{5... | collective-permute-start | bytes 3981320 | tf_op jit(solution)/shard_map/ppermute | solution.py:290
  116.8 53.4 %collective-permute-start.9 = (bf16[288,2304]{1,0:T(8,128)(2,1)}, bf16[288,2304]{1,0:T(8,128)(2,1)}, u32[]{:S(2)}, u32[]{:S(2)}) collective-permute-start(bf16[288,2304]{1,0:T(8,128)(2,1)} %get-tuple-element.528), channel_id=1, source_target_pairs={{0,8},{4,12},{8,16},{12,20},{16,24},{20,28},{24,0},{28,4},{1,9},{5... | collective-permute-start | bytes 3981320 | tf_op jit(solution)/shard_map/ppermute | solution.py:287
  116.8 55.9 %collective-permute-start.10 = (bf16[288,2304]{1,0:T(8,128)(2,1)}, bf16[288,2304]{1,0:T(8,128)(2,1)}, u32[]{:S(2)}, u32[]{:S(2)}) collective-permute-start(bf16[288,2304]{1,0:T(8,128)(2,1)} %collective-permute-done.7), channel_id=1, source_target_pairs={{0,8},{4,12},{8,16},{12,20},{16,24},{20,28},{24,0},{28,4},{1,9},{5... | collective-permute-start | bytes 3981320 | tf_op jit(solution)/shard_map/ppermute | solution.py:287
  177.4 65.2 %collective-permute-start.18 = (bf16[448,2304]{1,0:T(8,128)(2,1)S(1)}, bf16[448,2304]{1,0:T(8,128)(2,1)S(1)}, u32[]{:S(2)}, u32[]{:S(2)}) collective-permute-start(bf16[448,2304]{1,0:T(8,128)(2,1)S(1)} %add_convert_fusion.10), channel_id=1, source_target_pairs={{0,2},{1,3},{2,0},{3,1},{4,6},{5,7},{6,4},{7,5},{8,10},{9,11},{10,... | collective-permute-start | bytes 6193160 | tf_op jit(solution)/shard_map/ppermute | solution.py:296
  179.0 61.6 %collective-permute-start.16 = (bf16[288,2304]{1,0:T(8,128)(2,1)}, bf16[288,2304]{1,0:T(8,128)(2,1)S(1)}, u32[]{:S(2)}, u32[]{:S(2)}) collective-permute-start(bf16[288,2304]{1,0:T(8,128)(2,1)} %collective-permute-done.9), channel_id=1, source_target_pairs={{0,4},{4,0},{8,12},{12,8},{16,20},{20,16},{24,28},{28,24},{1,5},{5... | collective-permute-start | bytes 3981320 | tf_op jit(solution)/shard_map/ppermute | solution.py:290
  179.5 62.1 %collective-permute-start.13 = (bf16[288,2304]{1,0:T(8,128)(2,1)}, bf16[288,2304]{1,0:T(8,128)(2,1)}, u32[]{:S(2)}, u32[]{:S(2)}) collective-permute-start(bf16[288,2304]{1,0:T(8,128)(2,1)} %collective-permute-done.9), channel_id=1, source_target_pairs={{0,8},{4,12},{8,16},{12,20},{16,24},{20,28},{24,0},{28,4},{1,9},{5... | collective-permute-start | bytes 3981320 | tf_op jit(solution)/shard_map/ppermute | solution.py:287
  179.5 61.1 %collective-permute-start.15 = (bf16[288,2304]{1,0:T(8,128)(2,1)}, bf16[288,2304]{1,0:T(8,128)(2,1)S(1)}, u32[]{:S(2)}, u32[]{:S(2)}) collective-permute-start(bf16[288,2304]{1,0:T(8,128)(2,1)} %collective-permute-done.7), channel_id=1, source_target_pairs={{0,4},{4,0},{8,12},{12,8},{16,20},{20,16},{24,28},{28,24},{1,5},{5... | collective-permute-start | bytes 3981320 | tf_op jit(solution)/shard_map/ppermute | solution.py:290
  181.0 59.5 %collective-permute-start.14 = (bf16[288,2304]{1,0:T(8,128)(2,1)}, bf16[288,2304]{1,0:T(8,128)(2,1)S(1)}, u32[]{:S(2)}, u32[]{:S(2)}) collective-permute-start(bf16[288,2304]{1,0:T(8,128)(2,1)} %collective-permute-done.10), channel_id=1, source_target_pairs={{0,8},{4,12},{8,16},{12,20},{16,24},{20,28},{24,0},{28,4},{1,9},{5... | collective-permute-start | bytes 3981320 | tf_op jit(solution)/shard_map/ppermute | solution.py:287
  244.4 60.3 %collective-permute-start.22 = (bf16[288,2304]{1,0:T(8,128)(2,1)}, bf16[288,2304]{1,0:T(8,128)(2,1)}, u32[]{:S(2)}, u32[]{:S(2)}) collective-permute-start(bf16[288,2304]{1,0:T(8,128)(2,1)} %collective-permute-done.13), channel_id=1, source_target_pairs={{0,4},{4,0},{8,12},{12,8},{16,20},{20,16},{24,28},{28,24},{1,5},{5... | collective-permute-start | bytes 3981320 | tf_op jit(solution)/shard_map/ppermute | solution.py:290
  246.0 58.8 %collective-permute-start.19 = (bf16[288,2304]{1,0:T(8,128)(2,1)}, bf16[288,2304]{1,0:T(8,128)(2,1)}, u32[]{:S(2)}, u32[]{:S(2)}) collective-permute-start(bf16[288,2304]{1,0:T(8,128)(2,1)} %collective-permute-done.13), channel_id=1, source_target_pairs={{0,8},{4,12},{8,16},{12,20},{16,24},{20,28},{24,0},{28,4},{1,9},{5... | collective-permute-start | bytes 3981320 | tf_op jit(solution)/shard_map/ppermute | solution.py:287
  246.8 60.8 %collective-permute-start.20 = (bf16[288,2304]{1,0:T(8,128)(2,1)S(1)}, bf16[288,2304]{1,0:T(8,128)(2,1)S(1)}, u32[]{:S(2)}, u32[]{:S(2)}) collective-permute-start(bf16[288,2304]{1,0:T(8,128)(2,1)S(1)} %convert_bitcast_fusion), channel_id=1, source_target_pairs={{0,8},{4,12},{8,16},{12,20},{16,24},{20,28},{24,0},{28,4},{1,9},{5... | collective-permute-start | bytes 3981320 | tf_op jit(solution)/shard_map/ppermute | solution.py:287
  247.0 57.7 %collective-permute-start.21 = (bf16[288,2304]{1,0:T(8,128)(2,1)}, bf16[288,2304]{1,0:T(8,128)(2,1)}, u32[]{:S(2)}, u32[]{:S(2)}) collective-permute-start(bf16[288,2304]{1,0:T(8,128)(2,1)} %collective-permute-done.10), channel_id=1, source_target_pairs={{0,4},{4,0},{8,12},{12,8},{16,20},{20,16},{24,28},{28,24},{1,5},{5... | collective-permute-start | bytes 3981320 | tf_op jit(solution)/shard_map/ppermute | solution.py:290
  307.7 30.7 %collective-permute-start.26 = (bf16[288,2304]{1,0:T(8,128)(2,1)}, bf16[288,2304]{1,0:T(8,128)(2,1)S(1)}, u32[]{:S(2)}, u32[]{:S(2)}) collective-permute-start(bf16[288,2304]{1,0:T(8,128)(2,1)} %copy-done.53), channel_id=1, source_target_pairs={{0,4},{4,0},{8,12},{12,8},{16,20},{20,16},{24,28},{28,24},{1,5},{5... | collective-permute-start | bytes 3981320 | tf_op jit(solution)/shard_map/ppermute | solution.py:290
  308.2 32.0 %collective-permute-start.24 = (bf16[288,2304]{1,0:T(8,128)(2,1)S(1)}, bf16[288,2304]{1,0:T(8,128)(2,1)S(1)}, u32[]{:S(2)}, u32[]{:S(2)}) collective-permute-start(bf16[288,2304]{1,0:T(8,128)(2,1)S(1)} %collective-permute-done.20), channel_id=1, source_target_pairs={{0,8},{4,12},{8,16},{12,20},{16,24},{20,28},{24,0},{28,4},{1,9},{5... | collective-permute-start | bytes 3981320 | tf_op jit(solution)/shard_map/ppermute | solution.py:287
  338.3 29.7 %collective-permute-start.27 = (bf16[288,2304]{1,0:T(8,128)(2,1)}, bf16[288,2304]{1,0:T(8,128)(2,1)S(1)}, u32[]{:S(2)}, u32[]{:S(2)}) collective-permute-start(bf16[288,2304]{1,0:T(8,128)(2,1)} %collective-permute-done.19), channel_id=1, source_target_pairs={{0,4},{4,0},{8,12},{12,8},{16,20},{20,16},{24,28},{28,24},{1,5},{5... | collective-permute-start | bytes 3981320 | tf_op jit(solution)/shard_map/ppermute | solution.py:290
  340.1 31.0 %collective-permute-start.25 = (bf16[288,2304]{1,0:T(8,128)(2,1)S(1)}, bf16[288,2304]{1,0:T(8,128)(2,1)S(1)}, u32[]{:S(2)}, u32[]{:S(2)}) collective-permute-start(bf16[288,2304]{1,0:T(8,128)(2,1)S(1)} %collective-permute-done.24), channel_id=1, source_target_pairs={{0,8},{4,12},{8,16},{12,20},{16,24},{20,28},{24,0},{28,4},{1,9},{5... | collective-permute-start | bytes 3981320 | tf_op jit(solution)/shard_map/ppermute | solution.py:287
  410.5 37.6 %collective-permute-start.36 = (bf16[448,1152]{1,0:T(8,128)(2,1)S(1)}, bf16[448,1152]{1,0:T(8,128)(2,1)S(1)}, u32[]{:S(2)}, u32[]{:S(2)}) collective-permute-start(bf16[448,1152]{1,0:T(8,128)(2,1)S(1)} %add_convert_fusion.20), channel_id=1, source_target_pairs={{0,2},{1,3},{2,0},{3,1},{4,6},{5,7},{6,4},{7,5},{8,10},{9,11},{10,... | collective-permute-start | bytes 3096584 | tf_op jit(solution)/shard_map/ppermute | solution.py:296
  497.3 51.0 %collective-permute-start.44 = (bf16[448,2304]{1,0:T(8,128)(2,1)}, bf16[448,2304]{1,0:T(8,128)(2,1)}, u32[]{:S(2)}, u32[]{:S(2)}) collective-permute-start(bf16[448,2304]{1,0:T(8,128)(2,1)} %pad_maximum_fusion.13), channel_id=1, source_target_pairs={{0,4},{4,0},{8,12},{12,8},{16,20},{20,16},{24,28},{28,24},{1,5},{5... | collective-permute-start | bytes 6193160 | tf_op jit(solution)/shard_map/ppermute | solution.py:290
  498.6 49.7 %collective-permute-start.45 = (bf16[176,2304]{1,0:T(8,128)(2,1)}, bf16[176,2304]{1,0:T(8,128)(2,1)}, u32[]{:S(2)}, u32[]{:S(2)}) collective-permute-start(bf16[176,2304]{1,0:T(8,128)(2,1)} %get-tuple-element.623), channel_id=1, source_target_pairs={{0,8},{4,12},{8,16},{12,20},{16,24},{20,28},{24,0},{28,4},{1,9},{5... | collective-permute-start | bytes 2433032 | tf_op jit(solution)/shard_map/ppermute | solution.py:287
  552.2 50.5 %collective-permute-start.47 = (bf16[288,2304]{1,0:T(8,128)(2,1)}, bf16[288,2304]{1,0:T(8,128)(2,1)}, u32[]{:S(2)}, u32[]{:S(2)}) collective-permute-start(bf16[288,2304]{1,0:T(8,128)(2,1)} %add_convert_fusion.18), channel_id=1, source_target_pairs={{0,8},{4,12},{8,16},{12,20},{16,24},{20,28},{24,0},{28,4},{1,9},{5... | collective-permute-start | bytes 3981320 | tf_op jit(solution)/shard_map/ppermute | solution.py:287
  556.5 46.3 %collective-permute-start.46 = (bf16[288,2304]{1,0:T(8,128)(2,1)}, bf16[288,2304]{1,0:T(8,128)(2,1)}, u32[]{:S(2)}, u32[]{:S(2)}) collective-permute-start(bf16[288,2304]{1,0:T(8,128)(2,1)} %get-tuple-element.637), channel_id=1, source_target_pairs={{0,4},{4,0},{8,12},{12,8},{16,20},{20,16},{24,28},{28,24},{1,5},{5... | collective-permute-start | bytes 3981320 | tf_op jit(solution)/shard_map/ppermute | solution.py:290
  559.5 43.3 %collective-permute-start.48 = (bf16[176,2304]{1,0:T(8,128)(2,1)}, bf16[176,2304]{1,0:T(8,128)(2,1)}, u32[]{:S(2)}, u32[]{:S(2)}) collective-permute-start(bf16[176,2304]{1,0:T(8,128)(2,1)} %add_convert_fusion.26), channel_id=1, source_target_pairs={{0,8},{4,12},{8,16},{12,20},{16,24},{20,28},{24,0},{28,4},{1,9},{5... | collective-permute-start | bytes 2433032 | tf_op jit(solution)/shard_map/ppermute | solution.py:287
  602.8 40.5 %collective-permute-start.50 = (bf16[448,2304]{1,0:T(8,128)(2,1)}, bf16[448,2304]{1,0:T(8,128)(2,1)}, u32[]{:S(2)}, u32[]{:S(2)}) collective-permute-start(bf16[448,2304]{1,0:T(8,128)(2,1)} %get-tuple-element.651), channel_id=1, source_target_pairs={{0,1},{1,0},{2,3},{3,2},{4,5},{5,4},{6,7},{7,6},{8,9},{9,8},{10,11... | collective-permute-start | bytes 6193160 | tf_op jit(solution)/shard_map/ppermute | solution.py:293
  606.0 37.3 %collective-permute-start.51 = (bf16[288,2304]{1,0:T(8,128)(2,1)}, bf16[288,2304]{1,0:T(8,128)(2,1)}, u32[]{:S(2)}, u32[]{:S(2)}) collective-permute-start(bf16[288,2304]{1,0:T(8,128)(2,1)} %add_convert_fusion.17), channel_id=1, source_target_pairs={{0,8},{4,12},{8,16},{12,20},{16,24},{20,28},{24,0},{28,4},{1,9},{5... | collective-permute-start | bytes 3981320 | tf_op jit(solution)/shard_map/ppermute | solution.py:287
  608.6 34.7 %collective-permute-start.49 = (bf16[288,2304]{1,0:T(8,128)(2,1)}, bf16[288,2304]{1,0:T(8,128)(2,1)}, u32[]{:S(2)}, u32[]{:S(2)}) collective-permute-start(bf16[288,2304]{1,0:T(8,128)(2,1)} %get-tuple-element.650), channel_id=1, source_target_pairs={{0,4},{4,0},{8,12},{12,8},{16,20},{20,16},{24,28},{28,24},{1,5},{5... | collective-permute-start | bytes 3981320 | tf_op jit(solution)/shard_map/ppermute | solution.py:290
  643.3 66.9 %collective-permute-start.53 = (bf16[576,2304]{1,0:T(8,128)(2,1)S(1)}, bf16[576,2304]{1,0:T(8,128)(2,1)S(1)}, u32[]{:S(2)}, u32[]{:S(2)}) collective-permute-start(bf16[576,2304]{1,0:T(8,128)(2,1)S(1)} %get-tuple-element.668), channel_id=1, source_target_pairs={{0,4},{4,0},{8,12},{12,8},{16,20},{20,16},{24,28},{28,24},{1,5},{5... | collective-permute-start | bytes 7962632 | tf_op jit(solution)/shard_map/ppermute | solution.py:290
  646.7 63.5 %collective-permute-start.52 = (bf16[448,2304]{1,0:T(8,128)(2,1)S(1)}, bf16[448,2304]{1,0:T(8,128)(2,1)S(1)}, u32[]{:S(2)}, u32[]{:S(2)}) collective-permute-start(bf16[448,2304]{1,0:T(8,128)(2,1)S(1)} %add_convert_fusion.8), channel_id=1, source_target_pairs={{0,2},{1,3},{2,0},{3,1},{4,6},{5,7},{6,4},{7,5},{8,10},{9,11},{10,... | collective-permute-start | bytes 6193160 | tf_op jit(solution)/shard_map/ppermute | solution.py:296
  649.5 33.9 %collective-permute-start.54 = (bf16[288,2304]{1,0:T(8,128)(2,1)S(1)}, bf16[288,2304]{1,0:T(8,128)(2,1)S(1)}, u32[]{:S(2)}, u32[]{:S(2)}) collective-permute-start(bf16[288,2304]{1,0:T(8,128)(2,1)S(1)} %add_convert_fusion.16), channel_id=1, source_target_pairs={{0,8},{4,12},{8,16},{12,20},{16,24},{20,28},{24,0},{28,4},{1,9},{5... | collective-permute-start | bytes 3981320 | tf_op jit(solution)/shard_map/ppermute | solution.py:287
  649.9 60.2 %collective-permute-start.55 = (bf16[288,2304]{1,0:T(8,128)(2,1)}, bf16[288,2304]{1,0:T(8,128)(2,1)S(1)}, u32[]{:S(2)}, u32[]{:S(2)}) collective-permute-start(bf16[288,2304]{1,0:T(8,128)(2,1)} %get-tuple-element.670), channel_id=1, source_target_pairs={{0,8},{4,12},{8,16},{12,20},{16,24},{20,28},{24,0},{28,4},{1,9},{5... | collective-permute-start | bytes 3981320 | tf_op jit(solution)/shard_map/ppermute | solution.py:287
  714.0 77.4 %collective-permute-start.58 = (bf16[288,2304]{1,0:T(8,128)(2,1)}, bf16[288,2304]{1,0:T(8,128)(2,1)}, u32[]{:S(2)}, u32[]{:S(2)}) collective-permute-start(bf16[288,2304]{1,0:T(8,128)(2,1)} %add_convert_fusion.14), channel_id=1, source_target_pairs={{0,8},{4,12},{8,16},{12,20},{16,24},{20,28},{24,0},{28,4},{1,9},{5... | collective-permute-start | bytes 3981320 | tf_op jit(solution)/shard_map/ppermute | solution.py:287
  714.0 77.4 %collective-permute-start.56 = (bf16[576,2304]{1,0:T(8,128)(2,1)}, bf16[576,2304]{1,0:T(8,128)(2,1)}, u32[]{:S(2)}, u32[]{:S(2)}) collective-permute-start(bf16[576,2304]{1,0:T(8,128)(2,1)} %get-tuple-element.675), channel_id=1, source_target_pairs={{0,4},{4,0},{8,12},{12,8},{16,20},{20,16},{24,28},{28,24},{1,5},{5... | collective-permute-start | bytes 7962632 | tf_op jit(solution)/shard_map/ppermute | solution.py:290
  720.7 70.7 %collective-permute-start.57 = (bf16[288,2304]{1,0:T(8,128)(2,1)}, bf16[288,2304]{1,0:T(8,128)(2,1)}, u32[]{:S(2)}, u32[]{:S(2)}) collective-permute-start(bf16[288,2304]{1,0:T(8,128)(2,1)} %add_convert_fusion.15), channel_id=1, source_target_pairs={{0,8},{4,12},{8,16},{12,20},{16,24},{20,28},{24,0},{28,4},{1,9},{5... | collective-permute-start | bytes 3981320 | tf_op jit(solution)/shard_map/ppermute | solution.py:287
  722.9 68.4 %collective-permute-start.59 = (bf16[176,2304]{1,0:T(8,128)(2,1)}, bf16[176,2304]{1,0:T(8,128)(2,1)}, u32[]{:S(2)}, u32[]{:S(2)}) collective-permute-start(bf16[176,2304]{1,0:T(8,128)(2,1)} %add_convert_fusion.25), channel_id=1, source_target_pairs={{0,8},{4,12},{8,16},{12,20},{16,24},{20,28},{24,0},{28,4},{1,9},{5... | collective-permute-start | bytes 2433032 | tf_op jit(solution)/shard_map/ppermute | solution.py:287
  791.4 37.8 %collective-permute-start.62 = (bf16[448,2304]{1,0:T(8,128)(2,1)}, bf16[448,2304]{1,0:T(8,128)(2,1)}, u32[]{:S(2)}, u32[]{:S(2)}) collective-permute-start(bf16[448,2304]{1,0:T(8,128)(2,1)} %get-tuple-element.700), channel_id=1, source_target_pairs={{0,1},{1,0},{2,3},{3,2},{4,5},{5,4},{6,7},{7,6},{8,9},{9,8},{10,11... | collective-permute-start | bytes 6193160 | tf_op jit(solution)/shard_map/ppermute | solution.py:293
  795.1 34.0 %collective-permute-start.63 = (bf16[288,2304]{1,0:T(8,128)(2,1)}, bf16[288,2304]{1,0:T(8,128)(2,1)}, u32[]{:S(2)}, u32[]{:S(2)}) collective-permute-start(bf16[288,2304]{1,0:T(8,128)(2,1)} %add_convert_fusion.13), channel_id=1, source_target_pairs={{0,8},{4,12},{8,16},{12,20},{16,24},{20,28},{24,0},{28,4},{1,9},{5... | collective-permute-start | bytes 3981320 | tf_op jit(solution)/shard_map/ppermute | solution.py:287
  795.1 34.0 %collective-permute-start.61 = (bf16[288,2304]{1,0:T(8,128)(2,1)}, bf16[288,2304]{1,0:T(8,128)(2,1)}, u32[]{:S(2)}, u32[]{:S(2)}) collective-permute-start(bf16[288,2304]{1,0:T(8,128)(2,1)} %get-tuple-element.699), channel_id=1, source_target_pairs={{0,4},{4,0},{8,12},{12,8},{16,20},{20,16},{24,28},{28,24},{1,5},{5... | collective-permute-start | bytes 3981320 | tf_op jit(solution)/shard_map/ppermute | solution.py:290
  800.1 57.1 %collective-permute-start.66 = (bf16[288,2304]{1,0:T(8,128)(2,1)}, bf16[288,2304]{1,0:T(8,128)(2,1)}, u32[]{:S(2)}, u32[]{:S(2)}) collective-permute-start(bf16[288,2304]{1,0:T(8,128)(2,1)} %add_convert_fusion.12), channel_id=1, source_target_pairs={{0,8},{4,12},{8,16},{12,20},{16,24},{20,28},{24,0},{28,4},{1,9},{5... | collective-permute-start | bytes 3981320 | tf_op jit(solution)/shard_map/ppermute | solution.py:287
  829.2 68.6 %collective-permute-start.65 = (bf16[576,1536]{1,0:T(8,128)(2,1)}, bf16[576,1536]{1,0:T(8,128)(2,1)}, u32[]{:S(2)}, u32[]{:S(2)}) collective-permute-start(bf16[576,1536]{1,0:T(8,128)(2,1)} %get-tuple-element.715), channel_id=1, source_target_pairs={{0,4},{4,0},{8,12},{12,8},{16,20},{20,16},{24,28},{28,24},{1,5},{5... | collective-permute-start | bytes 5308424 | tf_op jit(solution)/shard_map/ppermute | solution.py:290
  833.2 64.6 %collective-permute-start.68 = (bf16[448,2304]{1,0:T(8,128)(2,1)S(1)}, bf16[448,2304]{1,0:T(8,128)(2,1)}, u32[]{:S(2)}, u32[]{:S(2)}) collective-permute-start(bf16[448,2304]{1,0:T(8,128)(2,1)S(1)} %add_convert_fusion.6), channel_id=1, source_target_pairs={{0,2},{1,3},{2,0},{3,1},{4,6},{5,7},{6,4},{7,5},{8,10},{9,11},{10,... | collective-permute-start | bytes 6193160 | tf_op jit(solution)/shard_map/ppermute | solution.py:296
  860.8 32.9 %collective-permute-start.67 = (bf16[288,2304]{1,0:T(8,128)(2,1)}, bf16[288,2304]{1,0:T(8,128)(2,1)}, u32[]{:S(2)}, u32[]{:S(2)}) collective-permute-start(bf16[288,2304]{1,0:T(8,128)(2,1)} %add_convert_fusion.11), channel_id=1, source_target_pairs={{0,8},{4,12},{8,16},{12,20},{16,24},{20,28},{24,0},{28,4},{1,9},{5... | collective-permute-start | bytes 3981320 | tf_op jit(solution)/shard_map/ppermute | solution.py:287
  860.9 37.0 %collective-permute-start.64 = (bf16[288,2304]{1,0:T(8,128)(2,1)}, bf16[288,2304]{1,0:T(8,128)(2,1)}, u32[]{:S(2)}, u32[]{:S(2)}) collective-permute-start(bf16[288,2304]{1,0:T(8,128)(2,1)} %get-tuple-element.714), channel_id=1, source_target_pairs={{0,4},{4,0},{8,12},{12,8},{16,20},{20,16},{24,28},{28,24},{1,5},{5... | collective-permute-start | bytes 3981320 | tf_op jit(solution)/shard_map/ppermute | solution.py:290
  900.1 52.7 %collective-permute-start.70 = (bf16[176,2304]{1,0:T(8,128)(2,1)}, bf16[176,2304]{1,0:T(8,128)(2,1)}, u32[]{:S(2)}, u32[]{:S(2)}) collective-permute-start(bf16[176,2304]{1,0:T(8,128)(2,1)} %add_convert_fusion.24), channel_id=1, source_target_pairs={{0,4},{4,0},{8,12},{12,8},{16,20},{20,16},{24,28},{28,24},{1,5},{5... | collective-permute-start | bytes 2433032 | tf_op jit(solution)/shard_map/ppermute | solution.py:290
  905.0 47.9 %collective-permute-start.72 = (bf16[288,1536]{1,0:T(8,128)(2,1)}, bf16[288,1536]{1,0:T(8,128)(2,1)}, u32[]{:S(2)}, u32[]{:S(2)}) collective-permute-start(bf16[288,1536]{1,0:T(8,128)(2,1)} %get-tuple-element.916), channel_id=1, source_target_pairs={{0,16},{4,20},{8,24},{12,28},{16,0},{20,4},{24,8},{28,12},{1,17},{... | collective-permute-start | bytes 2654216 | tf_op jit(solution)/shard_map/ppermute | solution.py:287
  905.0 47.9 %collective-permute-start.71 = (bf16[288,1536]{1,0:T(8,128)(2,1)}, bf16[288,1536]{1,0:T(8,128)(2,1)}, u32[]{:S(2)}, u32[]{:S(2)}) collective-permute-start(bf16[288,1536]{1,0:T(8,128)(2,1)} %get-tuple-element.917), channel_id=1, source_target_pairs={{0,24},{4,28},{8,0},{12,4},{16,8},{20,12},{24,16},{28,20},{1,25},{... | collective-permute-start | bytes 2654216 | tf_op jit(solution)/shard_map/ppermute | solution.py:287
  906.4 50.3 %collective-permute-start.69 = (bf16[576,1536]{1,0:T(8,128)(2,1)}, bf16[576,1536]{1,0:T(8,128)(2,1)}, u32[]{:S(2)}, u32[]{:S(2)}) collective-permute-start(bf16[576,1536]{1,0:T(8,128)(2,1)} %get-tuple-element.725), channel_id=1, source_target_pairs={{0,4},{4,0},{8,12},{12,8},{16,20},{20,16},{24,28},{28,24},{1,5},{5... | collective-permute-start | bytes 5308424 | tf_op jit(solution)/shard_map/ppermute | solution.py:290
  (130 other events, 1825.7 us)

commit v5 on v4

--- a/solution.py
+++ b/solution.py
@@ -58,7 +58,7 @@
     return (first.astype(wide) + second.astype(wide)).astype(kind)
 
 
-BLOCK = 128
+BLOCK = 224
 
 
 def by_rows(body, side, rows, whole, outs, sums):
@@ -546,21 +546,22 @@
     given, kept, saved, full = whole(attend, inputs, full, m3, n3, gains)
     given, kept, u1, g1, g2, v0, h0, saved, gains = sync((given, kept, u1, g1, g2, v0, h0, saved, gains))
     u2, g3, h1, v1 = around(u1), around(g2), swap(g1), swap(u1)
-    kept = add(kept, near(given))
-    across = far(kept)
+    theirs = near(given)
     wg, wu, h0, v0, u1, g1 = behind(wg, wu, h0, v0, u1, g1)
     wg = put(put(wg, g1, 1), h0, 0, half)
     wu = put(put(wu, u1, 1), v0, 0, half)
-    u2, g2, g3, h1, v1, across, kept, wg, wu, down = sync((u2, g2, g3, h1, v1, across, kept, wg, wu, down))
+    u2, g2, g3, h1, v1, theirs, kept, wg, wu, down = sync((u2, g2, g3, h1, v1, theirs, kept, wg, wu, down))
     u3, d1, h2, v2 = around(u2), around(down), swap(g2), swap(u2)
+    kept = add(kept, theirs)
+    across = far(kept)
+    wg = put(put(wg, g2, 2), h1, 1, half)
+    wu = put(put(wu, u2, 2), v1, 1, half)
+    u3, g3, d1, h2, v2, across, kept, wg, wu = sync((u3, g3, d1, h2, v2, across, kept, wg, wu))
+    d2, h3 = around(d1), swap(g3)
+    v3 = swap(tie(u3, h3))
     mine = add(kept, across)
     attn_sum = together(mine, near(mine))
     (hidden_in,) = by_rows(hidden_body, spot, [inputs, attn_sum], [gains], [(features, low)], [])
-    wg = put(put(wg, g2, 2), h1, 1, half)
-    wu = put(put(wu, u2, 2), v1, 1, half)
-    u3, g3, d1, h2, v2, hidden_in, wg, wu = sync((u3, g3, d1, h2, v2, hidden_in, wg, wu))
-    d2, h3 = around(d1), swap(g3)
-    v3 = swap(tie(u3, h3))
     wg, wu, h2, v2, u3, g3 = behind(wg, wu, h2, v2, u3, g3)
     wg = put(put(wg, g3, 3), h2, 2, half)
     wu = put(put(wu, u3, 3), v2, 2, half)
@@ -666,15 +667,15 @@
     h2, theirs = swap(gate_sent[1]), near(given)
     came = around(plus(piece(wd_grad, 2), grown(1), came))
 
-    def rest_of_grads(grad_gate, grad_up, hidden_in, gate_sent, h3):
+    def rest_of_grads(grad_gate, grad_up, hidden_in, gate_sent, h3, far_part, f2):
         up_sent = pieces(weight_grad(hidden_in[:, half:], grad_up))
         wg_grad = weight_grad(hidden_in[:, :half], grad_gate)
         mixed_sent = [jnp.concatenate(pair, axis=0) for pair in zip(gate_sent[2:], up_sent[:2])]
-        gate_first = plus(piece(wg_grad, 3), h3)
-        return mixed_sent, up_sent[2:], wg_grad, weight_grad(hidden_in[:, :half], grad_up), gate_first
-
-    mixed_sent, up_sent, wg_grad, wu_grad, gate_first = whole(
-        rest_of_grads, grad_gate, grad_up, hidden_in, gate_sent, h3
+        firsts = plus(piece(wg_grad, 3), h3), add(far_part, f2)
+        return mixed_sent, up_sent[2:], wg_grad, weight_grad(hidden_in[:, :half], grad_up), firsts
+
+    mixed_sent, up_sent, wg_grad, wu_grad, (gate_first, down_first) = whole(
+        rest_of_grads, grad_gate, grad_up, hidden_in, gate_sent, h3, far_parts[2], f2
     )
     h2, theirs, came, mixed_sent, up_sent, wg_grad, wu_grad, kept, gate_first = sync(
         (h2, theirs, came, mixed_sent, up_sent, wg_grad, wu_grad, kept, gate_first)
@@ -684,8 +685,8 @@
     across = far(kept)
     came = around(plus(piece(wd_grad, 1), grown(2), came))
     gate_came = around(gate_first)
-    across, pair, came, gate_came, kept, mixed_sent[1], up_sent, f2 = sync(
-        (across, pair, came, gate_came, kept, mixed_sent[1], up_sent, f2)
+    across, pair, came, gate_came, kept, mixed_sent[1], up_sent, down_first = sync(
+        (across, pair, came, gate_came, kept, mixed_sent[1], up_sent, down_first)
     )
     h1, v3 = pair[:count], pair[count:]
     pair = swap(mixed_sent[1])
@@ -693,7 +694,7 @@
     theirs = near(mine)
     gate_came = around(plus(piece(wg_grad, 2), h2, gate_came))
     up_came = around(plus(piece(wu_grad, 3), v3))
-    f1 = around(add(far_parts[2], f2))
+    f1 = around(down_first)
 
     def mixer_back(inputs, attn_sum, mine, theirs, grad_out, gains, full, saved):
         grad_hidden = together(mine, theirs)

time: 1010 us -> 999 us (0.989)
  transfers between devices with their start and end apart: 79 -> 79, of which waited for: 34 -> 35; matrix products, arithmetic and copies ran while one was open for 43% -> 43% of each run, Pallas kernels for 6% -> 5%
where the time goes in v5:
time: 999 us; the launch traced here: 990 us
  waiting for transfers between devices  378 us (38%)
  matrix products  219 us (22%)
  other arithmetic  148 us (15%)
  local copies, waits for them, and re-layouts  118 us (12%)
  starting transfers between devices  64.2 us (6%)
  Pallas kernels  60.1 us (6%)
    dot_general x26, matrix products, dot(): return jnp.einsum(pattern, first, second, preferred_element_type=wide)  217 us
    ppermute x33, waiting for transfers between devices, around(): return lax.ppermute(tensor, 'dp', ring_pairs(groups, hops))  206 us
    ppermute x28, waiting for transfers between devices, swap(): return lax.ppermute(tensor, 'dp', swap_pairs(groups, 1))  135 us
    pallas_call x7, Pallas kernels, by_rows(): pl.pallas_call(body, grid=(length // BLOCK,), in_specs=[pl.BlockSpec(memo...  60.1 us
    dynamic_update_slice x35, local copies, waits for them, and re-layouts, put(): lax.dynamic_update_slice_in_dim(full, piece, source(step) * count + offse...  43.4 us
    convert_element_type x11, other arithmetic, plus(): return both.astype(kind)  37.2 us
    ppermute x6, waiting for transfers between devices, far(): return lax.ppermute(tensor, 'mp', swap_pairs(parts, 2))  33.2 us
    ppermute x28, starting transfers between devices, swap(): return lax.ppermute(tensor, 'dp', swap_pairs(groups, 1))  30.5 us
  transfers between devices with their start and end apart: 79, of which 35 were waited for; matrix products, arithmetic and copies ran while one was open for 43% of the time, Pallas kernels for 5%

profile of v5, /device:TPU:0, one launch (start us, length us, event | category | flops | bytes accessed | tf_op | source)
XLA Modules:
  0.0 989.8 jit_solution(13053184564117811107)
XLA Ops:
  19.8 7.3 shard_map.404
  41.3 13.4 %collective-permute-done.3 = bf16[304,1536]{1,0:T(8,128)(2,1)S(1)} collective-permute-done((bf16[304,1536]{1,0:T(8,128)(2,1)}, bf16[304,1536]{1,0:T(8,128)(2,1)S(1)}, u32[]{:S(2)}, u32[]{:S(2)}) %collective-permute-start.3) | collective-permute-done | bytes 933920 | tf_op jit(solution)/shard_map/ppermute | solution.py:290
  63.0 9.8 copy.140
  87.5 10.4 %collective-permute-done.8 = bf16[144,2304]{1,0:T(8,128)(2,1)S(1)} collective-permute-done((bf16[144,2304]{1,0:T(8,128)(2,1)S(1)}, bf16[144,2304]{1,0:T(8,128)(2,1)S(1)}, u32[]{:S(2)}, u32[]{:S(2)}) %collective-permute-start.8) | collective-permute-done | bytes 663584 | tf_op jit(solution)/shard_map/ppermute | solution.py:290
  97.9 16.0 %collective-permute-done.6 = bf16[304,1536]{1,0:T(8,128)(2,1)S(1)} collective-permute-done((bf16[304,1536]{1,0:T(8,128)(2,1)S(1)}, bf16[304,1536]{1,0:T(8,128)(2,1)S(1)}, u32[]{:S(2)}, u32[]{:S(2)}) %collective-permute-start.6) | collective-permute-done | bytes 933920 | tf_op jit(solution)/shard_map/ppermute | solution.py:290
  122.1 41.4 %conditional.7 = (bf16[448,2304]{1,0:T(8,128)(2,1)S(1)}, bf16[448,2304]{1,0:T(8,128)(2,1)S(1)}, bf16[896,2304]{1,0:T(8,128)(2,1)}, bf16[896,1,2,256]{3,0,2,1:T(8...) conditional(s32[]{:T(128)} %convert_element_type.482, ...), branch_computations={%region_1.2_spmd, %region_2.5_spmd} | conditional | flops 8014624768 | bytes 162301568 | solution.py:442
  163.5 6.7 collective-permute-done.11
  184.9 51.0 %collective-permute-done.14 = bf16[288,2304]{1,0:T(8,128)(2,1)S(1)} collective-permute-done((bf16[288,2304]{1,0:T(8,128)(2,1)}, bf16[288,2304]{1,0:T(8,128)(2,1)S(1)}, u32[]{:S(2)}, u32[]{:S(2)}) %collective-permute-start.14) | collective-permute-done | bytes 1327136 | tf_op jit(solution)/shard_map/ppermute | solution.py:287
  252.1 47.2 %collective-permute-done.20 = bf16[288,2304]{1,0:T(8,128)(2,1)S(1)} collective-permute-done((bf16[288,2304]{1,0:T(8,128)(2,1)}, bf16[288,2304]{1,0:T(8,128)(2,1)S(1)}, u32[]{:S(2)}, u32[]{:S(2)}) %collective-permute-start.20) | collective-permute-done | bytes 1327136 | tf_op jit(solution)/shard_map/ppermute | solution.py:290
  313.0 18.4 %collective-permute-done.25 = bf16[288,2304]{1,0:T(8,128)(2,1)S(1)} collective-permute-done((bf16[288,2304]{1,0:T(8,128)(2,1)S(1)}, bf16[288,2304]{1,0:T(8,128)(2,1)S(1)}, u32[]{:S(2)}, u32[]{:S(2)}) %collective-permute-start.25) | collective-permute-done | bytes 1327136 | tf_op jit(solution)/shard_map/ppermute | solution.py:290
  342.3 15.1 %fusion.118 = f32[896,2304]{1,0:T(8,128)} fusion(bf16[896,2304]{1,0:T(8,128)(2,1)} %shard_map.405, bf16[2304,2304]{1,0:T(8,128)(2,1)} %constant_dynamic-update-slice_fusion.15), kind=kOutput, calls=%fused_computation.336 | convolution fusion | flops 9512681472 | bytes 23003136 | tf_op jit(solution)/shard_map/td,df->tf/dot_general | solution.py:284
  367.7 17.1 %fusion.67 = (bf16[896,2304]{1,0:T(8,128)(2,1)}, f32[896,2304]{1,0:T(8,128)}) fusion(f32[896,2304]{1,0:T(8,128)} %fusion.118, bf16[896,2304]{1,0:T(8,128)(2,1)S(1)} %copy-done.30, bf16[2304,2304]{1,0:T(8,128)(2,1)} %constant_dynamic-update-slice_fusion.10), kind=kOutput, calls=%fused_computation.146 | convolution fusion | flops 9533325312 | bytes 35389440 | tf_op jit(solution)/shard_map/td,df->tf/dot_general | solution.py:284
  385.0 8.9 convolution_convert_fusion.10
  412.2 8.4 collective-permute-done.35
  420.6 19.9 %collective-permute-done.38 = bf16[448,576]{1,0:T(8,128)(2,1)S(1)} collective-permute-done((bf16[448,576]{1,0:T(8,128)(2,1)S(1)}, bf16[448,576]{1,0:T(8,128)(2,1)S(1)}, u32[]{:S(2)}, u32[]{:S(2)}) %collective-permute-start.38) | collective-permute-done | bytes 516128 | tf_op jit(solution)/shard_map/ppermute | solution.py:296
  451.2 13.3 %collective-permute-done.42 = bf16[448,576]{1,0:T(8,128)(2,1)S(1)} collective-permute-done((bf16[448,576]{1,0:T(8,128)(2,1)S(1)}, bf16[448,576]{1,0:T(8,128)(2,1)S(1)}, u32[]{:S(2)}, u32[]{:S(2)}) %collective-permute-start.42) | collective-permute-done | bytes 516128 | tf_op jit(solution)/shard_map/ppermute | solution.py:296
  468.2 8.5 shard_map.406
  476.7 8.6 convolution_convert_fusion.9
  491.1 48.7 %conditional.8 = (bf16[896,2304]{1,0:T(8,128)(2,1)}, bf16[896,2304]{1,0:T(8,128)(2,1)}, bf16[1152,2304]{1,0:T(8,128)(2,1)}, bf16[288,2304]{1,0:T(8,128)(2,1)}, b...) conditional(s32[]{:T(128)} %convert_element_type.482, () %tuple.125, ...), branch_computations={%region_5.6_spmd, %region_6.7_spmd} | conditional | flops 19082280960 | bytes 135660160 | solution.py:442
  491.1 10.6 %fusion.116 = f32[896,2304]{1,0:T(8,128)} fusion(bf16[896,1152]{1,0:T(8,128)(2,1)} %get-tuple-element.145, bf16[1152,2304]{1,0:T(8,128)(2,1)} %get-tuple-element.146), kind=kOutput, calls=%fused_computation.334 | convolution fusion | flops 4756340736 | bytes 15630336 | tf_op jit(solution)/shard_map/cond/branch_1_fun/td,df->tf/dot_general | solution.py:284
  501.6 18.2 %multiply_convert_fusion = (bf16[896,2304]{1,0:T(8,128)(2,1)}, bf16[896,2304]{1,0:T(8,128)(2,1)}) fusion(f32[896,2304]{1,0:T(8,128)} %get-tuple-element.150, f32[896,2304]{1,0:T(8,128)} %get-tuple-element.149, f32[896,2304]{1,0:T(8,128)} %fusion.116, bf16[896,1152]{1,0:T(8,128)(2,1)} %get-tuple-element.147, bf16[1152,2304]{1,0:T(8,128)(2,1)S(1)} %copy-done.26), kind=kOutput, calls=%fused_computation.49 | convolution fusion | flops 4807950336 | bytes 40402944 | tf_op jit(solution)/shard_map/cond/branch_1_fun/td,df->tf/dot_general | solution.py:284
  519.8 9.7 convolution_convert_fusion.2
  529.6 8.3 fusion.20
  551.2 35.9 %conditional.9 = (bf16[448,2304]{1,0:T(8,128)(2,1)}, bf16[448,2304]{1,0:T(8,128)(2,1)S(1)}) conditional(s32[]{:T(128)} %convert_element_type.482, () %tuple.128, (bf16[896,2304]{1,0:T(8,128)(2,1)}, bf16[2304,2304]{1,0:T(8,128)(2,1)}, bf16[896,2304]{1,0:T(8,128)(2,1)}, bf16[2304,2304]{1,0:T(8,128)(2,1)}, s32[]{:T(128)}) %tuple.129), branch_computations={%region_7.8_spmd, %region_8.9_spmd} | conditional | flops 19029491712 | bytes 58392700 | solution.py:442
  551.2 15.0 %fusion.117 = f32[896,2304]{1,0:T(8,128)} fusion(bf16[896,2304]{1,0:T(8,128)(2,1)} %get-tuple-element.154, bf16[2304,2304]{1,0:T(8,128)(2,1)} %get-tuple-element.155), kind=kOutput, calls=%fused_computation.335 | convolution fusion | flops 9512681472 | bytes 23003136 | tf_op jit(solution)/shard_map/cond/branch_1_fun/tf,df->td/dot_general | solution.py:284
  566.2 17.2 %add_convert_fusion.1 = bf16[896,2304]{1,0:T(8,128)(2,1)} fusion(f32[896,2304]{1,0:T(8,128)} %fusion.117, bf16[896,2304]{1,0:T(8,128)(2,1)} %get-tuple-element.156, bf16[2304,2304]{1,0:T(8,128)(2,1)} %get-tuple-element.157), kind=kOutput, calls=%fused_computation.56 | convolution fusion | flops 9516810240 | bytes 27131904 | tf_op jit(solution)/shard_map/cond/branch_1_fun/tf,df->td/dot_general | solution.py:284
  600.5 36.4 %conditional.10 = (bf16[576,2304]{1,0:T(8,128)(2,1)S(1)}, bf16[576,2304]{1,0:T(8,128)(2,1)}, bf16[288,2304]{1,0:T(8,128)(2,1)}, bf16[288,2304]{1,0:T(8,128)(2,1)...) conditional(s32[]{:T(128)} %convert_element_type.482, ...), branch_computations={%region_9.10_spmd, %region_10.11_spmd} | conditional | flops 14291877888 | bytes 105210480 | solution.py:442
  602.9 8.8 convolution_convert_fusion.4
  615.4 9.5 convolution_convert_fusion.3
  624.9 8.3 convolution_convert_fusion.5
  644.0 33.2 %collective-permute-done.54 = bf16[288,2304]{1,0:T(8,128)(2,1)S(1)} collective-permute-done((bf16[288,2304]{1,0:T(8,128)(2,1)S(1)}, bf16[288,2304]{1,0:T(8,128)(2,1)S(1)}, u32[]{:S(2)}, u32[]{:S(2)}) %collective-permute-start.54) | collective-permute-done | bytes 1327136 | tf_op jit(solution)/shard_map/ppermute | solution.py:287
  677.2 26.8 %collective-permute-done.55 = bf16[288,2304]{1,0:T(8,128)(2,1)S(1)} collective-permute-done((bf16[288,2304]{1,0:T(8,128)(2,1)}, bf16[288,2304]{1,0:T(8,128)(2,1)S(1)}, u32[]{:S(2)}, u32[]{:S(2)}) %collective-permute-start.55) | collective-permute-done | bytes 1327136 | tf_op jit(solution)/shard_map/ppermute | solution.py:287
  715.5 60.3 %conditional.11 = (bf16[448,2304]{1,0:T(8,128)(2,1)}, bf16[448,2304]{1,0:T(8,128)(2,1)}, f32[896,2304]{1,0:T(8,128)}, bf16[896,2304]{1,0:T(8,128)(2,1)}, f32[1,2...) conditional(s32[]{:T(128)} %convert_element_type.482, () %tuple.135, (s32[]{:T(128)}, ...), branch_computations={%region_11.12_spmd, %region_12.14_spmd} | conditional | flops 9665787904 | bytes 197016160 | solution.py:442
  723.7 14.8 %branch_1_fun.5 = (f32[896,2304]{1,0:T(8,128)}, bf16[896,2304]{1,0:T(8,128)(2,1)}, f32[1,2304]{1,0:T(1,128)}, f32[1,2304]{1,0:T(1,128)}) custom-call(s32[2]{0:T(128)S(1)} %get-tuple-element.169.side, bf16[896,2304]{1,0:T(8,128)(2,1)S(1)} %copy-done.2, bf16[896,2304]{1,0:T(8,128)(2,1)S(1)} %copy-done.6, bf16[896,2304]{1,0:T(8,128)(2,1)S(1)} %pad_maximum_fusion.3.grad_hidden, ...), custom_call_target="tpu_custom_call" | custom-call | tf_op jit(solution)/shard_map/cond/branch_1_fun/pallas_call | solution.py:73
  751.1 7.7 fusion.37
  766.2 7.4 convolution_convert_fusion.6
  775.8 9.3 collective-permute-done.59
  793.9 23.3 %conditional.12 = (bf16[576,1536]{1,0:T(8,128)(2,1)}, bf16[576,1536]{1,0:T(8,128)(2,1)}, bf16[288,1536]{1,0:T(8,128)(2,1)}, bf16[288,1536]{1,0:T(8,128)(2,1)S(1)...) conditional(s32[]{:T(128)} %convert_element_type.482, () %tuple.138, ...), branch_computations={%region_14.15_spmd, %region_15.16_spmd} | conditional | flops 6366560256 | bytes 62915356 | solution.py:442
  801.2 7.0 convolution_convert_fusion.7
  810.0 7.2 maximum_maximum_fusion
  827.7 23.2 %collective-permute-done.66 = bf16[288,2304]{1,0:T(8,128)(2,1)} collective-permute-done((bf16[288,2304]{1,0:T(8,128)(2,1)}, bf16[288,2304]{1,0:T(8,128)(2,1)}, u32[]{:S(2)}, u32[]{:S(2)}) %collective-permute-start.66) | collective-permute-done | bytes 1327136 | tf_op jit(solution)/shard_map/ppermute | solution.py:287
  858.6 28.9 %collective-permute-done.67 = bf16[288,2304]{1,0:T(8,128)(2,1)} collective-permute-done((bf16[288,2304]{1,0:T(8,128)(2,1)}, bf16[288,2304]{1,0:T(8,128)(2,1)}, u32[]{:S(2)}, u32[]{:S(2)}) %collective-permute-start.67) | collective-permute-done | bytes 1327136 | tf_op jit(solution)/shard_map/ppermute | solution.py:287
  906.9 12.2 %add_multiply_fusion = (f32[2,288,2304]{2,1,0:T(8,128)}, f32[2,288,2304]{2,1,0:T(8,128)}, f32[2,288,2304]{2,1,0:T(8,128)}, f32[2,288,2304]{2,1,0:T(8,128)}) fusion(f32[2,288,2304]{2,1,0:T(8,128)S(1)} %bitcast.230, f32[1,288,2304]{2,1,0:T(8,128)S(1)} %add_bitcast_fusion, f32[1,288,2304]{2,1,0:T(8,128)S(1)} %bitcast.236, f32[2,288,2304]{2,1,0:T(8,128)} %param.47, ...), kind=kLoop, calls=%fused_computation.150 | loop fusion | flops 19906560 | bytes 42467328 | tf_op jit(solution)/shard_map/mul | solution.py:237
  919.1 25.1 %conditional.13 = (bf16[896,2304]{1,0:T(8,128)(2,1)}, f32[896,2304]{1,0:T(8,128)}, f32[1,2304]{1,0:T(1,128)}) conditional(s32[]{:T(128)} %convert_element_type.482, () %tuple.143, (s32[2]{0:T(128)S(1)}, bf16[896,2304]{1,0:T(8,128)(2,1)}, bf16[896,2304]{1,0:T(8,128)(2,1)}, bf16[896,1152]{1,0:T(8,128)(2,1)S(1)}, bf16[896,576]{1,0:T(8,128)(2,1)S(1)}, ...), branch_computations={%region_16.17_spmd, %region_17.18_spmd} | conditional | flops 10321921 | bytes 33030206 | solution.py:442
  919.1 10.4 %branch_1_fun.6 = bf16[896,2304]{1,0:T(8,128)(2,1)} custom-call(s32[2]{0:T(128)S(1)} %get-tuple-element.194.spot.side, bf16[896,2304]{1,0:T(8,128)(2,1)} %get-tuple-element.195.inputs, bf16[896,2304]{1,0:T(8,128)(2,1)} %get-tuple-element.196.attn, bf16[896,1152]{1,0:T(8,128)(2,1)S(1)} %get-tuple-element.197.own, ...), custom_call_target="tpu_custom_call" | custom-call | tf_op jit(solution)/shard_map/cond/branch_1_fun/pallas_call | solution.py:73
  934.2 10.0 %branch_1_fun.7 = (f32[896,2304]{1,0:T(8,128)}, f32[1,2304]{1,0:T(1,128)}) custom-call(s32[2]{0:T(128)S(1)} %get-tuple-element.194.spot.side, bf16[896,2304]{1,0:T(8,128)(2,1)S(1)} %copy-done.3, bf16[896,2304]{1,0:T(8,128)(2,1)S(1)} %pad_maximum_fusion.9.grad_normed, f32[896,2304]{1,0:T(8,128)} %get-tuple-element.204.grad_resid, ...), custom_call_target="tpu_custom_call" | custom-call | tf_op jit(solution)/shard_map/cond/branch_1_fun/pallas_call | solution.py:73
  953.0 6.6 collective-permute-start.74
  973.7 7.8 fusion.87
  (520 shorter events, 389.1 us)
Async XLA Ops:
  81.0 32.9 %collective-permute-start.6 = (bf16[304,1536]{1,0:T(8,128)(2,1)S(1)}, bf16[304,1536]{1,0:T(8,128)(2,1)S(1)}, u32[]{:S(2)}, u32[]{:S(2)}) collective-permute-start(bf16[304,1536]{1,0:T(8,128)(2,1)S(1)} %collective-permute-done.4), channel_id=1, source_target_pairs={{0,4},{4,0},{8,12},{12,8},{16,20},{20,16},{24,28},{28,24},{1,5},{5... | collective-permute-start | bytes 2801672 | tf_op jit(solution)/shard_map/ppermute | solution.py:290
  82.1 32.7 %collective-permute-start.7 = (bf16[288,2304]{1,0:T(8,128)(2,1)}, bf16[288,2304]{1,0:T(8,128)(2,1)}, u32[]{:S(2)}, u32[]{:S(2)}) collective-permute-start(bf16[288,2304]{1,0:T(8,128)(2,1)} %get-tuple-element.538), channel_id=1, source_target_pairs={{0,8},{4,12},{8,16},{12,20},{16,24},{20,28},{24,0},{28,4},{1,9},{5... | collective-permute-start | bytes 3981320 | tf_op jit(solution)/shard_map/ppermute | solution.py:287
  114.8 48.7 %collective-permute-start.12 = (bf16[288,2304]{1,0:T(8,128)(2,1)}, bf16[288,2304]{1,0:T(8,128)(2,1)}, u32[]{:S(2)}, u32[]{:S(2)}) collective-permute-start(bf16[288,2304]{1,0:T(8,128)(2,1)} %get-tuple-element.538), channel_id=1, source_target_pairs={{0,4},{4,0},{8,12},{12,8},{16,20},{20,16},{24,28},{28,24},{1,5},{5... | collective-permute-start | bytes 3981320 | tf_op jit(solution)/shard_map/ppermute | solution.py:290
  115.8 54.4 %collective-permute-start.11 = (bf16[288,2304]{1,0:T(8,128)(2,1)}, bf16[288,2304]{1,0:T(8,128)(2,1)}, u32[]{:S(2)}, u32[]{:S(2)}) collective-permute-start(bf16[288,2304]{1,0:T(8,128)(2,1)} %get-tuple-element.536), channel_id=1, source_target_pairs={{0,4},{4,0},{8,12},{12,8},{16,20},{20,16},{24,28},{28,24},{1,5},{5... | collective-permute-start | bytes 3981320 | tf_op jit(solution)/shard_map/ppermute | solution.py:290
  116.8 53.4 %collective-permute-start.9 = (bf16[288,2304]{1,0:T(8,128)(2,1)}, bf16[288,2304]{1,0:T(8,128)(2,1)}, u32[]{:S(2)}, u32[]{:S(2)}) collective-permute-start(bf16[288,2304]{1,0:T(8,128)(2,1)} %get-tuple-element.536), channel_id=1, source_target_pairs={{0,8},{4,12},{8,16},{12,20},{16,24},{20,28},{24,0},{28,4},{1,9},{5... | collective-permute-start | bytes 3981320 | tf_op jit(solution)/shard_map/ppermute | solution.py:287
  116.8 55.9 %collective-permute-start.10 = (bf16[288,2304]{1,0:T(8,128)(2,1)}, bf16[288,2304]{1,0:T(8,128)(2,1)}, u32[]{:S(2)}, u32[]{:S(2)}) collective-permute-start(bf16[288,2304]{1,0:T(8,128)(2,1)} %collective-permute-done.7), channel_id=1, source_target_pairs={{0,8},{4,12},{8,16},{12,20},{16,24},{20,28},{24,0},{28,4},{1,9},{5... | collective-permute-start | bytes 3981320 | tf_op jit(solution)/shard_map/ppermute | solution.py:287
  172.7 65.2 %collective-permute-start.17 = (bf16[448,2304]{1,0:T(8,128)(2,1)S(1)}, bf16[448,2304]{1,0:T(8,128)(2,1)S(1)}, u32[]{:S(2)}, u32[]{:S(2)}) collective-permute-start(bf16[448,2304]{1,0:T(8,128)(2,1)S(1)} %get-tuple-element.551), channel_id=1, source_target_pairs={{0,1},{1,0},{2,3},{3,2},{4,5},{5,4},{6,7},{7,6},{8,9},{9,8},{10,11... | collective-permute-start | bytes 6193160 | tf_op jit(solution)/shard_map/ppermute | solution.py:293
  172.7 63.1 %collective-permute-start.16 = (bf16[288,2304]{1,0:T(8,128)(2,1)}, bf16[288,2304]{1,0:T(8,128)(2,1)S(1)}, u32[]{:S(2)}, u32[]{:S(2)}) collective-permute-start(bf16[288,2304]{1,0:T(8,128)(2,1)} %collective-permute-done.9), channel_id=1, source_target_pairs={{0,4},{4,0},{8,12},{12,8},{16,20},{20,16},{24,28},{28,24},{1,5},{5... | collective-permute-start | bytes 3981320 | tf_op jit(solution)/shard_map/ppermute | solution.py:290
  174.1 62.8 %collective-permute-start.13 = (bf16[288,2304]{1,0:T(8,128)(2,1)}, bf16[288,2304]{1,0:T(8,128)(2,1)}, u32[]{:S(2)}, u32[]{:S(2)}) collective-permute-start(bf16[288,2304]{1,0:T(8,128)(2,1)} %collective-permute-done.9), channel_id=1, source_target_pairs={{0,8},{4,12},{8,16},{12,20},{16,24},{20,28},{24,0},{28,4},{1,9},{5... | collective-permute-start | bytes 3981320 | tf_op jit(solution)/shard_map/ppermute | solution.py:287
  174.1 61.7 %collective-permute-start.15 = (bf16[288,2304]{1,0:T(8,128)(2,1)}, bf16[288,2304]{1,0:T(8,128)(2,1)S(1)}, u32[]{:S(2)}, u32[]{:S(2)}) collective-permute-start(bf16[288,2304]{1,0:T(8,128)(2,1)} %collective-permute-done.7), channel_id=1, source_target_pairs={{0,4},{4,0},{8,12},{12,8},{16,20},{20,16},{24,28},{28,24},{1,5},{5... | collective-permute-start | bytes 3981320 | tf_op jit(solution)/shard_map/ppermute | solution.py:290
  174.8 61.0 %collective-permute-start.14 = (bf16[288,2304]{1,0:T(8,128)(2,1)}, bf16[288,2304]{1,0:T(8,128)(2,1)S(1)}, u32[]{:S(2)}, u32[]{:S(2)}) collective-permute-start(bf16[288,2304]{1,0:T(8,128)(2,1)} %collective-permute-done.10), channel_id=1, source_target_pairs={{0,8},{4,12},{8,16},{12,20},{16,24},{20,28},{24,0},{28,4},{1,9},{5... | collective-permute-start | bytes 3981320 | tf_op jit(solution)/shard_map/ppermute | solution.py:287
  239.8 62.5 %collective-permute-start.22 = (bf16[448,2304]{1,0:T(8,128)(2,1)}, bf16[448,2304]{1,0:T(8,128)(2,1)}, u32[]{:S(2)}, u32[]{:S(2)}) collective-permute-start(bf16[448,2304]{1,0:T(8,128)(2,1)} %add_convert_fusion.11), channel_id=1, source_target_pairs={{0,2},{1,3},{2,0},{3,1},{4,6},{5,7},{6,4},{7,5},{8,10},{9,11},{10,... | collective-permute-start | bytes 6193160 | tf_op jit(solution)/shard_map/ppermute | solution.py:296
  240.4 58.8 %collective-permute-start.21 = (bf16[288,2304]{1,0:T(8,128)(2,1)}, bf16[288,2304]{1,0:T(8,128)(2,1)S(1)}, u32[]{:S(2)}, u32[]{:S(2)}) collective-permute-start(bf16[288,2304]{1,0:T(8,128)(2,1)} %collective-permute-done.13), channel_id=1, source_target_pairs={{0,4},{4,0},{8,12},{12,8},{16,20},{20,16},{24,28},{28,24},{1,5},{5... | collective-permute-start | bytes 3981320 | tf_op jit(solution)/shard_map/ppermute | solution.py:290
  241.9 57.3 %collective-permute-start.18 = (bf16[288,2304]{1,0:T(8,128)(2,1)}, bf16[288,2304]{1,0:T(8,128)(2,1)}, u32[]{:S(2)}, u32[]{:S(2)}) collective-permute-start(bf16[288,2304]{1,0:T(8,128)(2,1)} %collective-permute-done.13), channel_id=1, source_target_pairs={{0,8},{4,12},{8,16},{12,20},{16,24},{20,28},{24,0},{28,4},{1,9},{5... | collective-permute-start | bytes 3981320 | tf_op jit(solution)/shard_map/ppermute | solution.py:287
  242.0 57.3 %collective-permute-start.20 = (bf16[288,2304]{1,0:T(8,128)(2,1)}, bf16[288,2304]{1,0:T(8,128)(2,1)S(1)}, u32[]{:S(2)}, u32[]{:S(2)}) collective-permute-start(bf16[288,2304]{1,0:T(8,128)(2,1)} %collective-permute-done.10), channel_id=1, source_target_pairs={{0,4},{4,0},{8,12},{12,8},{16,20},{20,16},{24,28},{28,24},{1,5},{5... | collective-permute-start | bytes 3981320 | tf_op jit(solution)/shard_map/ppermute | solution.py:290
  242.5 59.8 %collective-permute-start.19 = (bf16[288,2304]{1,0:T(8,128)(2,1)S(1)}, bf16[288,2304]{1,0:T(8,128)(2,1)S(1)}, u32[]{:S(2)}, u32[]{:S(2)}) collective-permute-start(bf16[288,2304]{1,0:T(8,128)(2,1)S(1)} %convert_bitcast_fusion), channel_id=1, source_target_pairs={{0,8},{4,12},{8,16},{12,20},{16,24},{20,28},{24,0},{28,4},{1,9},{5... | collective-permute-start | bytes 3981320 | tf_op jit(solution)/shard_map/ppermute | solution.py:287
  302.8 30.8 %collective-permute-start.23 = (bf16[288,2304]{1,0:T(8,128)(2,1)S(1)}, bf16[288,2304]{1,0:T(8,128)(2,1)S(1)}, u32[]{:S(2)}, u32[]{:S(2)}) collective-permute-start(bf16[288,2304]{1,0:T(8,128)(2,1)S(1)} %collective-permute-done.19), channel_id=1, source_target_pairs={{0,8},{4,12},{8,16},{12,20},{16,24},{20,28},{24,0},{28,4},{1,9},{5... | collective-permute-start | bytes 3981320 | tf_op jit(solution)/shard_map/ppermute | solution.py:287
  363.2 31.0 %collective-permute-start.29 = (bf16[144,2304]{1,0:T(8,128)(2,1)}, bf16[144,2304]{1,0:T(8,128)(2,1)S(1)}, u32[]{:S(2)}, u32[]{:S(2)}) collective-permute-start(bf16[144,2304]{1,0:T(8,128)(2,1)} %slice.202), channel_id=1, source_target_pairs={{0,4},{4,0},{8,12},{12,8},{16,20},{20,16},{24,28},{28,24},{1,5},{5... | collective-permute-start | bytes 1990664 | tf_op jit(solution)/shard_map/ppermute | solution.py:290
  403.4 37.1 %collective-permute-start.36 = (bf16[448,1152]{1,0:T(8,128)(2,1)S(1)}, bf16[448,1152]{1,0:T(8,128)(2,1)S(1)}, u32[]{:S(2)}, u32[]{:S(2)}) collective-permute-start(bf16[448,1152]{1,0:T(8,128)(2,1)S(1)} %add_convert_fusion.21), channel_id=1, source_target_pairs={{0,2},{1,3},{2,0},{3,1},{4,6},{5,7},{6,4},{7,5},{8,10},{9,11},{10,... | collective-permute-start | bytes 3096584 | tf_op jit(solution)/shard_map/ppermute | solution.py:296
  409.9 30.6 %collective-permute-start.33 = (bf16[144,2304]{1,0:T(8,128)(2,1)S(1)}, bf16[144,2304]{1,0:T(8,128)(2,1)S(1)}, u32[]{:S(2)}, u32[]{:S(2)}) collective-permute-start(bf16[144,2304]{1,0:T(8,128)(2,1)S(1)} %collective-permute-done.31), channel_id=1, source_target_pairs={{0,8},{4,12},{8,16},{12,20},{16,24},{20,28},{24,0},{28,4},{1,9},{5... | collective-permute-start | bytes 1990664 | tf_op jit(solution)/shard_map/ppermute | solution.py:287
  488.6 51.1 %collective-permute-start.44 = (bf16[448,2304]{1,0:T(8,128)(2,1)}, bf16[448,2304]{1,0:T(8,128)(2,1)}, u32[]{:S(2)}, u32[]{:S(2)}) collective-permute-start(bf16[448,2304]{1,0:T(8,128)(2,1)} %pad_maximum_fusion.13), channel_id=1, source_target_pairs={{0,4},{4,0},{8,12},{12,8},{16,20},{20,16},{24,28},{28,24},{1,5},{5... | collective-permute-start | bytes 6193160 | tf_op jit(solution)/shard_map/ppermute | solution.py:290
  490.2 49.6 %collective-permute-start.45 = (bf16[176,2304]{1,0:T(8,128)(2,1)}, bf16[176,2304]{1,0:T(8,128)(2,1)}, u32[]{:S(2)}, u32[]{:S(2)}) collective-permute-start(bf16[176,2304]{1,0:T(8,128)(2,1)} %get-tuple-element.632), channel_id=1, source_target_pairs={{0,8},{4,12},{8,16},{12,20},{16,24},{20,28},{24,0},{28,4},{1,9},{5... | collective-permute-start | bytes 2433032 | tf_op jit(solution)/shard_map/ppermute | solution.py:287
  543.7 50.5 %collective-permute-start.47 = (bf16[288,2304]{1,0:T(8,128)(2,1)}, bf16[288,2304]{1,0:T(8,128)(2,1)}, u32[]{:S(2)}, u32[]{:S(2)}) collective-permute-start(bf16[288,2304]{1,0:T(8,128)(2,1)} %add_convert_fusion.19), channel_id=1, source_target_pairs={{0,8},{4,12},{8,16},{12,20},{16,24},{20,28},{24,0},{28,4},{1,9},{5... | collective-permute-start | bytes 3981320 | tf_op jit(solution)/shard_map/ppermute | solution.py:287
  548.0 46.3 %collective-permute-start.46 = (bf16[288,2304]{1,0:T(8,128)(2,1)}, bf16[288,2304]{1,0:T(8,128)(2,1)}, u32[]{:S(2)}, u32[]{:S(2)}) collective-permute-start(bf16[288,2304]{1,0:T(8,128)(2,1)} %get-tuple-element.646), channel_id=1, source_target_pairs={{0,4},{4,0},{8,12},{12,8},{16,20},{20,16},{24,28},{28,24},{1,5},{5... | collective-permute-start | bytes 3981320 | tf_op jit(solution)/shard_map/ppermute | solution.py:290
  550.7 43.5 %collective-permute-start.48 = (bf16[176,2304]{1,0:T(8,128)(2,1)}, bf16[176,2304]{1,0:T(8,128)(2,1)}, u32[]{:S(2)}, u32[]{:S(2)}) collective-permute-start(bf16[176,2304]{1,0:T(8,128)(2,1)} %add_convert_fusion.26), channel_id=1, source_target_pairs={{0,8},{4,12},{8,16},{12,20},{16,24},{20,28},{24,0},{28,4},{1,9},{5... | collective-permute-start | bytes 2433032 | tf_op jit(solution)/shard_map/ppermute | solution.py:287
  594.2 42.6 %collective-permute-start.50 = (bf16[448,2304]{1,0:T(8,128)(2,1)}, bf16[448,2304]{1,0:T(8,128)(2,1)}, u32[]{:S(2)}, u32[]{:S(2)}) collective-permute-start(bf16[448,2304]{1,0:T(8,128)(2,1)} %get-tuple-element.660), channel_id=1, source_target_pairs={{0,1},{1,0},{2,3},{3,2},{4,5},{5,4},{6,7},{7,6},{8,9},{9,8},{10,11... | collective-permute-start | bytes 6193160 | tf_op jit(solution)/shard_map/ppermute | solution.py:293
  597.4 39.4 %collective-permute-start.51 = (bf16[288,2304]{1,0:T(8,128)(2,1)}, bf16[288,2304]{1,0:T(8,128)(2,1)}, u32[]{:S(2)}, u32[]{:S(2)}) collective-permute-start(bf16[288,2304]{1,0:T(8,128)(2,1)} %add_convert_fusion.18), channel_id=1, source_target_pairs={{0,8},{4,12},{8,16},{12,20},{16,24},{20,28},{24,0},{28,4},{1,9},{5... | collective-permute-start | bytes 3981320 | tf_op jit(solution)/shard_map/ppermute | solution.py:287
  600.0 36.9 %collective-permute-start.49 = (bf16[288,2304]{1,0:T(8,128)(2,1)}, bf16[288,2304]{1,0:T(8,128)(2,1)}, u32[]{:S(2)}, u32[]{:S(2)}) collective-permute-start(bf16[288,2304]{1,0:T(8,128)(2,1)} %get-tuple-element.659), channel_id=1, source_target_pairs={{0,4},{4,0},{8,12},{12,8},{16,20},{20,16},{24,28},{28,24},{1,5},{5... | collective-permute-start | bytes 3981320 | tf_op jit(solution)/shard_map/ppermute | solution.py:290
  636.9 67.1 %collective-permute-start.53 = (bf16[576,2304]{1,0:T(8,128)(2,1)S(1)}, bf16[576,2304]{1,0:T(8,128)(2,1)S(1)}, u32[]{:S(2)}, u32[]{:S(2)}) collective-permute-start(bf16[576,2304]{1,0:T(8,128)(2,1)S(1)} %get-tuple-element.679), channel_id=1, source_target_pairs={{0,4},{4,0},{8,12},{12,8},{16,20},{20,16},{24,28},{28,24},{1,5},{5... | collective-permute-start | bytes 7962632 | tf_op jit(solution)/shard_map/ppermute | solution.py:290
  640.5 63.4 %collective-permute-start.52 = (bf16[448,2304]{1,0:T(8,128)(2,1)S(1)}, bf16[448,2304]{1,0:T(8,128)(2,1)S(1)}, u32[]{:S(2)}, u32[]{:S(2)}) collective-permute-start(bf16[448,2304]{1,0:T(8,128)(2,1)S(1)} %add_convert_fusion.9), channel_id=1, source_target_pairs={{0,2},{1,3},{2,0},{3,1},{4,6},{5,7},{6,4},{7,5},{8,10},{9,11},{10,... | collective-permute-start | bytes 6193160 | tf_op jit(solution)/shard_map/ppermute | solution.py:296
  643.3 33.9 %collective-permute-start.54 = (bf16[288,2304]{1,0:T(8,128)(2,1)S(1)}, bf16[288,2304]{1,0:T(8,128)(2,1)S(1)}, u32[]{:S(2)}, u32[]{:S(2)}) collective-permute-start(bf16[288,2304]{1,0:T(8,128)(2,1)S(1)} %add_convert_fusion.17), channel_id=1, source_target_pairs={{0,8},{4,12},{8,16},{12,20},{16,24},{20,28},{24,0},{28,4},{1,9},{5... | collective-permute-start | bytes 3981320 | tf_op jit(solution)/shard_map/ppermute | solution.py:287
  643.7 60.2 %collective-permute-start.55 = (bf16[288,2304]{1,0:T(8,128)(2,1)}, bf16[288,2304]{1,0:T(8,128)(2,1)S(1)}, u32[]{:S(2)}, u32[]{:S(2)}) collective-permute-start(bf16[288,2304]{1,0:T(8,128)(2,1)} %get-tuple-element.681), channel_id=1, source_target_pairs={{0,8},{4,12},{8,16},{12,20},{16,24},{20,28},{24,0},{28,4},{1,9},{5... | collective-permute-start | bytes 3981320 | tf_op jit(solution)/shard_map/ppermute | solution.py:287
  707.7 77.4 %collective-permute-start.58 = (bf16[288,2304]{1,0:T(8,128)(2,1)}, bf16[288,2304]{1,0:T(8,128)(2,1)}, u32[]{:S(2)}, u32[]{:S(2)}) collective-permute-start(bf16[288,2304]{1,0:T(8,128)(2,1)} %add_convert_fusion.15), channel_id=1, source_target_pairs={{0,8},{4,12},{8,16},{12,20},{16,24},{20,28},{24,0},{28,4},{1,9},{5... | collective-permute-start | bytes 3981320 | tf_op jit(solution)/shard_map/ppermute | solution.py:287
  707.7 77.4 %collective-permute-start.56 = (bf16[576,2304]{1,0:T(8,128)(2,1)}, bf16[576,2304]{1,0:T(8,128)(2,1)}, u32[]{:S(2)}, u32[]{:S(2)}) collective-permute-start(bf16[576,2304]{1,0:T(8,128)(2,1)} %get-tuple-element.686), channel_id=1, source_target_pairs={{0,4},{4,0},{8,12},{12,8},{16,20},{20,16},{24,28},{28,24},{1,5},{5... | collective-permute-start | bytes 7962632 | tf_op jit(solution)/shard_map/ppermute | solution.py:290
  714.5 70.7 %collective-permute-start.57 = (bf16[288,2304]{1,0:T(8,128)(2,1)}, bf16[288,2304]{1,0:T(8,128)(2,1)}, u32[]{:S(2)}, u32[]{:S(2)}) collective-permute-start(bf16[288,2304]{1,0:T(8,128)(2,1)} %add_convert_fusion.16), channel_id=1, source_target_pairs={{0,8},{4,12},{8,16},{12,20},{16,24},{20,28},{24,0},{28,4},{1,9},{5... | collective-permute-start | bytes 3981320 | tf_op jit(solution)/shard_map/ppermute | solution.py:287
  714.5 70.7 %collective-permute-start.59 = (bf16[176,2304]{1,0:T(8,128)(2,1)}, bf16[176,2304]{1,0:T(8,128)(2,1)}, u32[]{:S(2)}, u32[]{:S(2)}) collective-permute-start(bf16[176,2304]{1,0:T(8,128)(2,1)} %get-tuple-element.692), channel_id=1, source_target_pairs={{0,8},{4,12},{8,16},{12,20},{16,24},{20,28},{24,0},{28,4},{1,9},{5... | collective-permute-start | bytes 2433032 | tf_op jit(solution)/shard_map/ppermute | solution.py:287
  785.1 37.8 %collective-permute-start.62 = (bf16[448,2304]{1,0:T(8,128)(2,1)}, bf16[448,2304]{1,0:T(8,128)(2,1)}, u32[]{:S(2)}, u32[]{:S(2)}) collective-permute-start(bf16[448,2304]{1,0:T(8,128)(2,1)} %get-tuple-element.710), channel_id=1, source_target_pairs={{0,1},{1,0},{2,3},{3,2},{4,5},{5,4},{6,7},{7,6},{8,9},{9,8},{10,11... | collective-permute-start | bytes 6193160 | tf_op jit(solution)/shard_map/ppermute | solution.py:293
  788.9 34.0 %collective-permute-start.63 = (bf16[288,2304]{1,0:T(8,128)(2,1)}, bf16[288,2304]{1,0:T(8,128)(2,1)}, u32[]{:S(2)}, u32[]{:S(2)}) collective-permute-start(bf16[288,2304]{1,0:T(8,128)(2,1)} %add_convert_fusion.14), channel_id=1, source_target_pairs={{0,8},{4,12},{8,16},{12,20},{16,24},{20,28},{24,0},{28,4},{1,9},{5... | collective-permute-start | bytes 3981320 | tf_op jit(solution)/shard_map/ppermute | solution.py:287
  788.9 34.0 %collective-permute-start.61 = (bf16[288,2304]{1,0:T(8,128)(2,1)}, bf16[288,2304]{1,0:T(8,128)(2,1)}, u32[]{:S(2)}, u32[]{:S(2)}) collective-permute-start(bf16[288,2304]{1,0:T(8,128)(2,1)} %get-tuple-element.709), channel_id=1, source_target_pairs={{0,4},{4,0},{8,12},{12,8},{16,20},{20,16},{24,28},{28,24},{1,5},{5... | collective-permute-start | bytes 3981320 | tf_op jit(solution)/shard_map/ppermute | solution.py:290
  793.9 57.0 %collective-permute-start.66 = (bf16[288,2304]{1,0:T(8,128)(2,1)}, bf16[288,2304]{1,0:T(8,128)(2,1)}, u32[]{:S(2)}, u32[]{:S(2)}) collective-permute-start(bf16[288,2304]{1,0:T(8,128)(2,1)} %add_convert_fusion.13), channel_id=1, source_target_pairs={{0,8},{4,12},{8,16},{12,20},{16,24},{20,28},{24,0},{28,4},{1,9},{5... | collective-permute-start | bytes 3981320 | tf_op jit(solution)/shard_map/ppermute | solution.py:287
  823.0 68.6 %collective-permute-start.65 = (bf16[576,1536]{1,0:T(8,128)(2,1)}, bf16[576,1536]{1,0:T(8,128)(2,1)}, u32[]{:S(2)}, u32[]{:S(2)}) collective-permute-start(bf16[576,1536]{1,0:T(8,128)(2,1)} %get-tuple-element.725), channel_id=1, source_target_pairs={{0,4},{4,0},{8,12},{12,8},{16,20},{20,16},{24,28},{28,24},{1,5},{5... | collective-permute-start | bytes 5308424 | tf_op jit(solution)/shard_map/ppermute | solution.py:290
  827.1 64.5 %collective-permute-start.68 = (bf16[448,2304]{1,0:T(8,128)(2,1)S(1)}, bf16[448,2304]{1,0:T(8,128)(2,1)}, u32[]{:S(2)}, u32[]{:S(2)}) collective-permute-start(bf16[448,2304]{1,0:T(8,128)(2,1)S(1)} %add_convert_fusion.7), channel_id=1, source_target_pairs={{0,2},{1,3},{2,0},{3,1},{4,6},{5,7},{6,4},{7,5},{8,10},{9,11},{10,... | collective-permute-start | bytes 6193160 | tf_op jit(solution)/shard_map/ppermute | solution.py:296
  854.6 32.9 %collective-permute-start.67 = (bf16[288,2304]{1,0:T(8,128)(2,1)}, bf16[288,2304]{1,0:T(8,128)(2,1)}, u32[]{:S(2)}, u32[]{:S(2)}) collective-permute-start(bf16[288,2304]{1,0:T(8,128)(2,1)} %add_convert_fusion.12), channel_id=1, source_target_pairs={{0,8},{4,12},{8,16},{12,20},{16,24},{20,28},{24,0},{28,4},{1,9},{5... | collective-permute-start | bytes 3981320 | tf_op jit(solution)/shard_map/ppermute | solution.py:287
  854.6 37.0 %collective-permute-start.64 = (bf16[288,2304]{1,0:T(8,128)(2,1)}, bf16[288,2304]{1,0:T(8,128)(2,1)}, u32[]{:S(2)}, u32[]{:S(2)}) collective-permute-start(bf16[288,2304]{1,0:T(8,128)(2,1)} %get-tuple-element.724), channel_id=1, source_target_pairs={{0,4},{4,0},{8,12},{12,8},{16,20},{20,16},{24,28},{28,24},{1,5},{5... | collective-permute-start | bytes 3981320 | tf_op jit(solution)/shard_map/ppermute | solution.py:290
  893.9 50.3 %collective-permute-start.70 = (bf16[176,2304]{1,0:T(8,128)(2,1)}, bf16[176,2304]{1,0:T(8,128)(2,1)}, u32[]{:S(2)}, u32[]{:S(2)}) collective-permute-start(bf16[176,2304]{1,0:T(8,128)(2,1)} %add_convert_fusion.25), channel_id=1, source_target_pairs={{0,4},{4,0},{8,12},{12,8},{16,20},{20,16},{24,28},{28,24},{1,5},{5... | collective-permute-start | bytes 2433032 | tf_op jit(solution)/shard_map/ppermute | solution.py:290
  898.8 45.4 %collective-permute-start.72 = (bf16[288,1536]{1,0:T(8,128)(2,1)}, bf16[288,1536]{1,0:T(8,128)(2,1)}, u32[]{:S(2)}, u32[]{:S(2)}) collective-permute-start(bf16[288,1536]{1,0:T(8,128)(2,1)} %get-tuple-element.926), channel_id=1, source_target_pairs={{0,16},{4,20},{8,24},{12,28},{16,0},{20,4},{24,8},{28,12},{1,17},{... | collective-permute-start | bytes 2654216 | tf_op jit(solution)/shard_map/ppermute | solution.py:287
  898.8 45.4 %collective-permute-start.71 = (bf16[288,1536]{1,0:T(8,128)(2,1)}, bf16[288,1536]{1,0:T(8,128)(2,1)}, u32[]{:S(2)}, u32[]{:S(2)}) collective-permute-start(bf16[288,1536]{1,0:T(8,128)(2,1)} %get-tuple-element.927), channel_id=1, source_target_pairs={{0,24},{4,28},{8,0},{12,4},{16,8},{20,12},{24,16},{28,20},{1,25},{... | collective-permute-start | bytes 2654216 | tf_op jit(solution)/shard_map/ppermute | solution.py:287
  900.2 50.2 %collective-permute-start.69 = (bf16[576,1536]{1,0:T(8,128)(2,1)}, bf16[576,1536]{1,0:T(8,128)(2,1)}, u32[]{:S(2)}, u32[]{:S(2)}) collective-permute-start(bf16[576,1536]{1,0:T(8,128)(2,1)} %get-tuple-element.735), channel_id=1, source_target_pairs={{0,4},{4,0},{8,12},{12,8},{16,20},{20,16},{24,28},{28,24},{1,5},{5... | collective-permute-start | bytes 5308424 | tf_op jit(solution)/shard_map/ppermute | solution.py:290
  (123 other events, 1793.8 us)

commit v6 on v5

--- a/solution.py
+++ b/solution.py
@@ -61,18 +61,18 @@
 BLOCK = 224
 
 
-def by_rows(body, side, rows, whole, outs, sums):
+def by_rows(body, side, rows, whole, outs, sums, block=BLOCK):
     length = rows[0].shape[0]
 
     def blocked(width):
-        return pl.BlockSpec((BLOCK, width), lambda i: (i, 0))
+        return pl.BlockSpec((block, width), lambda i: (i, 0))
 
     def kept(shape):
         return pl.BlockSpec(shape, lambda i: (0, 0))
 
     return pl.pallas_call(
         body,
-        grid=(length // BLOCK,),
+        grid=(length // block,),
         in_specs=[pl.BlockSpec(memory_space=pltpu.SMEM)]
         + [blocked(t.shape[1]) for t in rows]
         + [kept(t.shape) for t in whole],
@@ -367,7 +367,7 @@
     def attn_back(inputs, attn_sum, grad_hidden, grad_out, gains):
         rows = [inputs, attn_sum, grad_hidden, grad_out]
         outs = [(features, wide), (features, low)]
-        return by_rows(attn_back_body, spot, rows, [gains], outs, [features] * 2)
+        return by_rows(attn_back_body, spot, rows, [gains], outs, [features] * 2, 128)
 
     def in_back(inputs, grad_normed, grad_resid, gains):
         rows = [inputs, grad_normed, grad_resid]
@@ -713,15 +713,17 @@
     v1, theirs = swap(up_sent[0]), near(given)
     gate_came = around(plus(piece(wg_grad, 1), h1, gate_came))
 
-    def mixer_grads(normed_low, mixed_low, grad_raw, grad_attn):
+    def mixer_grads(normed_low, mixed_low, grad_raw, grad_attn, far_part, f1):
         grads = weight_grad(normed_low, grad_raw), weight_grad(grad_attn, mixed_low)
         pairs = ((3, 2), (1, 0))
         mixer_sent = [jnp.concatenate([both(hops, half, grads) for hops in pair], axis=0) for pair in pairs]
-        return mixer_sent, [both(hops, 0, grads) for hops in (3, 2, 1, 0)]
-
-    mixer_sent, mixer_own = whole(mixer_grads, saved[0], saved[-1], grad_raw, grad_attn)
-    v1, theirs, gate_came, mixer_sent, mixer_own, kept, up_sent = sync(
-        (v1, theirs, gate_came, mixer_sent, mixer_own, kept, up_sent)
+        return mixer_sent, [both(hops, 0, grads) for hops in (3, 2, 1, 0)], add(far_part, f1)
+
+    mixer_sent, mixer_own, down_last = whole(
+        mixer_grads, saved[0], saved[-1], grad_raw, grad_attn, far_parts[3], f1
+    )
+    v1, theirs, gate_came, mixer_sent, mixer_own, kept, up_sent, down_last = sync(
+        (v1, theirs, gate_came, mixer_sent, mixer_own, kept, up_sent, down_last)
     )
     v0, x32 = swap(up_sent[1]), swap(mixer_sent[0])
     kept = add(kept, theirs)
@@ -730,10 +732,10 @@
     gate_late = tie(gate_came, up_came)
     sum_gate = plus(piece(wg_grad, 0), h0, gate_late, wide)
     up_came = around(plus(piece(wu_grad, 1), v1, up_came))
-    v0, x32, up_came, across, kept, mixer_sent[1], inputs, f1, sum_gate = sync(
-        (v0, x32, up_came, across, kept, mixer_sent[1], inputs, f1, sum_gate)
-    )
-    x10, b_far = swap(mixer_sent[1]), swap(add(far_parts[3], f1))
+    v0, x32, up_came, across, kept, mixer_sent[1], inputs, down_last, sum_gate = sync(
+        (v0, x32, up_came, across, kept, mixer_sent[1], inputs, down_last, sum_gate)
+    )
+    x10, b_far = swap(mixer_sent[1]), swap(down_last)
     m3 = around(plus(mixer_own[0], x32[:count]), 3)
     m2 = around(plus(mixer_own[1], x32[count:]), 2)
     mine = add(kept, across)

time: 999 us -> 998 us (level)
  transfers between devices with their start and end apart: 79 -> 79, of which waited for: 35 -> 33; matrix products, arithmetic and copies ran while one was open for 43% -> 43% of each run, Pallas kernels for 5% -> 5%
where the time goes in v6:
time: 998 us; the launch traced here: 989 us
  waiting for transfers between devices  375 us (38%)
  matrix products  219 us (22%)
  other arithmetic  148 us (15%)
  local copies, waits for them, and re-layouts  118 us (12%)
  starting transfers between devices  67.1 us (7%)
  Pallas kernels  59.4 us (6%)
    dot_general x26, matrix products, dot(): return jnp.einsum(pattern, first, second, preferred_element_type=wide)  217 us
    ppermute x33, waiting for transfers between devices, around(): return lax.ppermute(tensor, 'dp', ring_pairs(groups, hops))  204 us
    ppermute x28, waiting for transfers between devices, swap(): return lax.ppermute(tensor, 'dp', swap_pairs(groups, 1))  134 us
    pallas_call x7, Pallas kernels, by_rows(): pl.pallas_call(body, grid=(length // block,), in_specs=[pl.BlockSpec(memo...  59.4 us
    dynamic_update_slice x35, local copies, waits for them, and re-layouts, put(): lax.dynamic_update_slice_in_dim(full, piece, source(step) * count + offse...  43.4 us
    convert_element_type x11, other arithmetic, plus(): return both.astype(kind)  37.2 us
    ppermute x6, waiting for transfers between devices, far(): return lax.ppermute(tensor, 'mp', swap_pairs(parts, 2))  33.2 us
    ppermute x28, starting transfers between devices, swap(): return lax.ppermute(tensor, 'dp', swap_pairs(groups, 1))  32.1 us
  transfers between devices with their start and end apart: 79, of which 33 were waited for; matrix products, arithmetic and copies ran while one was open for 43% of the time, Pallas kernels for 5%

profile of v6, /device:TPU:0, one launch (start us, length us, event | category | flops | bytes accessed | tf_op | source)
XLA Modules:
  0.0 988.7 jit_solution(8827753416513802855)
XLA Ops:
  19.8 7.3 shard_map.404
  41.3 13.4 %collective-permute-done.3 = bf16[304,1536]{1,0:T(8,128)(2,1)S(1)} collective-permute-done((bf16[304,1536]{1,0:T(8,128)(2,1)}, bf16[304,1536]{1,0:T(8,128)(2,1)S(1)}, u32[]{:S(2)}, u32[]{:S(2)}) %collective-permute-start.3) | collective-permute-done | bytes 933920 | tf_op jit(solution)/shard_map/ppermute | solution.py:290
  63.0 9.8 copy.140
  87.5 10.4 %collective-permute-done.8 = bf16[144,2304]{1,0:T(8,128)(2,1)S(1)} collective-permute-done((bf16[144,2304]{1,0:T(8,128)(2,1)S(1)}, bf16[144,2304]{1,0:T(8,128)(2,1)S(1)}, u32[]{:S(2)}, u32[]{:S(2)}) %collective-permute-start.8) | collective-permute-done | bytes 663584 | tf_op jit(solution)/shard_map/ppermute | solution.py:290
  97.9 16.0 %collective-permute-done.6 = bf16[304,1536]{1,0:T(8,128)(2,1)S(1)} collective-permute-done((bf16[304,1536]{1,0:T(8,128)(2,1)S(1)}, bf16[304,1536]{1,0:T(8,128)(2,1)S(1)}, u32[]{:S(2)}, u32[]{:S(2)}) %collective-permute-start.6) | collective-permute-done | bytes 933920 | tf_op jit(solution)/shard_map/ppermute | solution.py:290
  122.1 41.4 %conditional.7 = (bf16[448,2304]{1,0:T(8,128)(2,1)S(1)}, bf16[448,2304]{1,0:T(8,128)(2,1)S(1)}, bf16[896,2304]{1,0:T(8,128)(2,1)}, bf16[896,1,2,256]{3,0,2,1:T(8...) conditional(s32[]{:T(128)} %convert_element_type.482, ...), branch_computations={%region_1.2_spmd, %region_2.5_spmd} | conditional | flops 8014624768 | bytes 162301568 | solution.py:442
  163.5 6.7 collective-permute-done.11
  184.8 51.0 %collective-permute-done.14 = bf16[288,2304]{1,0:T(8,128)(2,1)S(1)} collective-permute-done((bf16[288,2304]{1,0:T(8,128)(2,1)}, bf16[288,2304]{1,0:T(8,128)(2,1)S(1)}, u32[]{:S(2)}, u32[]{:S(2)}) %collective-permute-start.14) | collective-permute-done | bytes 1327136 | tf_op jit(solution)/shard_map/ppermute | solution.py:287
  252.1 47.2 %collective-permute-done.20 = bf16[288,2304]{1,0:T(8,128)(2,1)S(1)} collective-permute-done((bf16[288,2304]{1,0:T(8,128)(2,1)}, bf16[288,2304]{1,0:T(8,128)(2,1)S(1)}, u32[]{:S(2)}, u32[]{:S(2)}) %collective-permute-start.20) | collective-permute-done | bytes 1327136 | tf_op jit(solution)/shard_map/ppermute | solution.py:290
  313.0 18.4 %collective-permute-done.25 = bf16[288,2304]{1,0:T(8,128)(2,1)S(1)} collective-permute-done((bf16[288,2304]{1,0:T(8,128)(2,1)S(1)}, bf16[288,2304]{1,0:T(8,128)(2,1)S(1)}, u32[]{:S(2)}, u32[]{:S(2)}) %collective-permute-start.25) | collective-permute-done | bytes 1327136 | tf_op jit(solution)/shard_map/ppermute | solution.py:290
  342.4 15.1 %fusion.118 = f32[896,2304]{1,0:T(8,128)} fusion(bf16[896,2304]{1,0:T(8,128)(2,1)} %shard_map.405, bf16[2304,2304]{1,0:T(8,128)(2,1)} %constant_dynamic-update-slice_fusion.15), kind=kOutput, calls=%fused_computation.336 | convolution fusion | flops 9512681472 | bytes 23003136 | tf_op jit(solution)/shard_map/td,df->tf/dot_general | solution.py:284
  367.7 17.1 %fusion.67 = (bf16[896,2304]{1,0:T(8,128)(2,1)}, f32[896,2304]{1,0:T(8,128)}) fusion(f32[896,2304]{1,0:T(8,128)} %fusion.118, bf16[896,2304]{1,0:T(8,128)(2,1)S(1)} %copy-done.30, bf16[2304,2304]{1,0:T(8,128)(2,1)} %constant_dynamic-update-slice_fusion.10), kind=kOutput, calls=%fused_computation.147 | convolution fusion | flops 9533325312 | bytes 35389440 | tf_op jit(solution)/shard_map/td,df->tf/dot_general | solution.py:284
  385.0 8.9 convolution_convert_fusion.10
  412.2 8.4 collective-permute-done.35
  420.6 19.9 %collective-permute-done.38 = bf16[448,576]{1,0:T(8,128)(2,1)S(1)} collective-permute-done((bf16[448,576]{1,0:T(8,128)(2,1)S(1)}, bf16[448,576]{1,0:T(8,128)(2,1)S(1)}, u32[]{:S(2)}, u32[]{:S(2)}) %collective-permute-start.38) | collective-permute-done | bytes 516128 | tf_op jit(solution)/shard_map/ppermute | solution.py:296
  451.2 13.3 %collective-permute-done.42 = bf16[448,576]{1,0:T(8,128)(2,1)S(1)} collective-permute-done((bf16[448,576]{1,0:T(8,128)(2,1)S(1)}, bf16[448,576]{1,0:T(8,128)(2,1)S(1)}, u32[]{:S(2)}, u32[]{:S(2)}) %collective-permute-start.42) | collective-permute-done | bytes 516128 | tf_op jit(solution)/shard_map/ppermute | solution.py:296
  468.2 8.5 shard_map.406
  476.7 8.6 convolution_convert_fusion.9
  491.1 48.6 %conditional.8 = (bf16[896,2304]{1,0:T(8,128)(2,1)}, bf16[896,2304]{1,0:T(8,128)(2,1)}, bf16[1152,2304]{1,0:T(8,128)(2,1)}, bf16[288,2304]{1,0:T(8,128)(2,1)}, b...) conditional(s32[]{:T(128)} %convert_element_type.482, () %tuple.125, ...), branch_computations={%region_5.6_spmd, %region_6.7_spmd} | conditional | flops 19082280960 | bytes 135660160 | solution.py:442
  491.1 10.6 %fusion.116 = f32[896,2304]{1,0:T(8,128)} fusion(bf16[896,1152]{1,0:T(8,128)(2,1)} %get-tuple-element.149, bf16[1152,2304]{1,0:T(8,128)(2,1)} %get-tuple-element.150), kind=kOutput, calls=%fused_computation.334 | convolution fusion | flops 4756340736 | bytes 15630336 | tf_op jit(solution)/shard_map/cond/branch_1_fun/td,df->tf/dot_general | solution.py:284
  501.6 18.1 %multiply_convert_fusion = (bf16[896,2304]{1,0:T(8,128)(2,1)}, bf16[896,2304]{1,0:T(8,128)(2,1)}) fusion(f32[896,2304]{1,0:T(8,128)} %get-tuple-element.154, f32[896,2304]{1,0:T(8,128)} %get-tuple-element.153, f32[896,2304]{1,0:T(8,128)} %fusion.116, bf16[896,1152]{1,0:T(8,128)(2,1)} %get-tuple-element.151, bf16[1152,2304]{1,0:T(8,128)(2,1)S(1)} %copy-done.26), kind=kOutput, calls=%fused_computation.49 | convolution fusion | flops 4807950336 | bytes 40402944 | tf_op jit(solution)/shard_map/cond/branch_1_fun/td,df->tf/dot_general | solution.py:284
  519.8 9.7 convolution_convert_fusion.2
  529.5 8.3 fusion.20
  551.1 35.9 %conditional.9 = (bf16[448,2304]{1,0:T(8,128)(2,1)}, bf16[448,2304]{1,0:T(8,128)(2,1)S(1)}) conditional(s32[]{:T(128)} %convert_element_type.482, () %tuple.128, (bf16[896,2304]{1,0:T(8,128)(2,1)}, bf16[2304,2304]{1,0:T(8,128)(2,1)}, bf16[896,2304]{1,0:T(8,128)(2,1)}, bf16[2304,2304]{1,0:T(8,128)(2,1)}, s32[]{:T(128)}) %tuple.129), branch_computations={%region_7.8_spmd, %region_8.9_spmd} | conditional | flops 19029491712 | bytes 58392700 | solution.py:442
  551.1 15.0 %fusion.117 = f32[896,2304]{1,0:T(8,128)} fusion(bf16[896,2304]{1,0:T(8,128)(2,1)} %get-tuple-element.158, bf16[2304,2304]{1,0:T(8,128)(2,1)} %get-tuple-element.159), kind=kOutput, calls=%fused_computation.335 | convolution fusion | flops 9512681472 | bytes 23003136 | tf_op jit(solution)/shard_map/cond/branch_1_fun/tf,df->td/dot_general | solution.py:284
  566.1 17.2 %add_convert_fusion.1 = bf16[896,2304]{1,0:T(8,128)(2,1)} fusion(f32[896,2304]{1,0:T(8,128)} %fusion.117, bf16[896,2304]{1,0:T(8,128)(2,1)} %get-tuple-element.160, bf16[2304,2304]{1,0:T(8,128)(2,1)} %get-tuple-element.161), kind=kOutput, calls=%fused_computation.56 | convolution fusion | flops 9516810240 | bytes 27131904 | tf_op jit(solution)/shard_map/cond/branch_1_fun/tf,df->td/dot_general | solution.py:284
  600.4 36.4 %conditional.10 = (bf16[576,2304]{1,0:T(8,128)(2,1)S(1)}, bf16[576,2304]{1,0:T(8,128)(2,1)}, bf16[288,2304]{1,0:T(8,128)(2,1)}, bf16[288,2304]{1,0:T(8,128)(2,1)...) conditional(s32[]{:T(128)} %convert_element_type.482, ...), branch_computations={%region_9.10_spmd, %region_10.11_spmd} | conditional | flops 14291877888 | bytes 105210480 | solution.py:442
  602.9 8.8 convolution_convert_fusion.4
  615.4 9.5 convolution_convert_fusion.3
  624.9 8.3 convolution_convert_fusion.5
  643.9 33.2 %collective-permute-done.54 = bf16[288,2304]{1,0:T(8,128)(2,1)S(1)} collective-permute-done((bf16[288,2304]{1,0:T(8,128)(2,1)S(1)}, bf16[288,2304]{1,0:T(8,128)(2,1)S(1)}, u32[]{:S(2)}, u32[]{:S(2)}) %collective-permute-start.54) | collective-permute-done | bytes 1327136 | tf_op jit(solution)/shard_map/ppermute | solution.py:287
  677.1 26.8 %collective-permute-done.55 = bf16[288,2304]{1,0:T(8,128)(2,1)S(1)} collective-permute-done((bf16[288,2304]{1,0:T(8,128)(2,1)}, bf16[288,2304]{1,0:T(8,128)(2,1)S(1)}, u32[]{:S(2)}, u32[]{:S(2)}) %collective-permute-start.55) | collective-permute-done | bytes 1327136 | tf_op jit(solution)/shard_map/ppermute | solution.py:287
  715.4 59.6 %conditional.11 = (bf16[448,2304]{1,0:T(8,128)(2,1)}, bf16[448,2304]{1,0:T(8,128)(2,1)}, f32[896,2304]{1,0:T(8,128)}, bf16[896,2304]{1,0:T(8,128)(2,1)}, f32[1,2...) conditional(s32[]{:T(128)} %convert_element_type.482, () %tuple.135, (s32[]{:T(128)}, ...), branch_computations={%region_11.12_spmd, %region_12.14_spmd} | conditional | flops 9665787904 | bytes 197016160 | solution.py:442
  723.7 14.1 %branch_1_fun.5 = (f32[896,2304]{1,0:T(8,128)}, bf16[896,2304]{1,0:T(8,128)(2,1)}, f32[1,2304]{1,0:T(1,128)}, f32[1,2304]{1,0:T(1,128)}) custom-call(s32[2]{0:T(128)S(1)} %get-tuple-element.173.side, bf16[896,2304]{1,0:T(8,128)(2,1)S(1)} %copy-done.2, bf16[896,2304]{1,0:T(8,128)(2,1)S(1)} %copy-done.6, bf16[896,2304]{1,0:T(8,128)(2,1)S(1)} %pad_maximum_fusion.3.grad_hidden, ...), custom_call_target="tpu_custom_call" | custom-call | tf_op jit(solution)/shard_map/cond/branch_1_fun/pallas_call | solution.py:73
  750.3 7.7 fusion.37
  765.4 7.4 convolution_convert_fusion.6
  775.1 10.0 %collective-permute-done.59 = bf16[176,2304]{1,0:T(8,128)(2,1)} collective-permute-done((bf16[176,2304]{1,0:T(8,128)(2,1)}, bf16[176,2304]{1,0:T(8,128)(2,1)}, u32[]{:S(2)}, u32[]{:S(2)}) %collective-permute-start.59) | collective-permute-done | bytes 811040 | tf_op jit(solution)/shard_map/ppermute | solution.py:287
  793.9 25.8 %conditional.12 = (bf16[576,1536]{1,0:T(8,128)(2,1)}, bf16[576,1536]{1,0:T(8,128)(2,1)}, bf16[288,1536]{1,0:T(8,128)(2,1)}, bf16[288,1536]{1,0:T(8,128)(2,1)S(1)...) conditional(s32[]{:T(128)} %convert_element_type.482, ...), branch_computations={%region_14.15_spmd, %region_15.16_spmd} | conditional | flops 6368182272 | bytes 65348388 | solution.py:442
  803.6 7.0 convolution_convert_fusion.7
  812.5 7.2 maximum_maximum_fusion
  827.7 23.3 %collective-permute-done.66 = bf16[288,2304]{1,0:T(8,128)(2,1)} collective-permute-done((bf16[288,2304]{1,0:T(8,128)(2,1)}, bf16[288,2304]{1,0:T(8,128)(2,1)}, u32[]{:S(2)}, u32[]{:S(2)}) %collective-permute-start.66) | collective-permute-done | bytes 1327136 | tf_op jit(solution)/shard_map/ppermute | solution.py:287
  858.5 28.9 %collective-permute-done.67 = bf16[288,2304]{1,0:T(8,128)(2,1)} collective-permute-done((bf16[288,2304]{1,0:T(8,128)(2,1)}, bf16[288,2304]{1,0:T(8,128)(2,1)}, u32[]{:S(2)}, u32[]{:S(2)}) %collective-permute-start.67) | collective-permute-done | bytes 1327136 | tf_op jit(solution)/shard_map/ppermute | solution.py:287
  905.8 12.2 %add_multiply_fusion = (f32[2,288,2304]{2,1,0:T(8,128)}, f32[2,288,2304]{2,1,0:T(8,128)}, f32[2,288,2304]{2,1,0:T(8,128)}, f32[2,288,2304]{2,1,0:T(8,128)}) fusion(f32[2,288,2304]{2,1,0:T(8,128)S(1)} %bitcast.230, f32[1,288,2304]{2,1,0:T(8,128)S(1)} %add_bitcast_fusion, f32[1,288,2304]{2,1,0:T(8,128)S(1)} %bitcast.236, f32[2,288,2304]{2,1,0:T(8,128)} %param.47, ...), kind=kLoop, calls=%fused_computation.151 | loop fusion | flops 19906560 | bytes 42467328 | tf_op jit(solution)/shard_map/mul | solution.py:237
  918.0 25.1 %conditional.13 = (bf16[896,2304]{1,0:T(8,128)(2,1)}, f32[896,2304]{1,0:T(8,128)}, f32[1,2304]{1,0:T(1,128)}) conditional(s32[]{:T(128)} %convert_element_type.482, () %tuple.143, (s32[2]{0:T(128)S(1)}, bf16[896,2304]{1,0:T(8,128)(2,1)}, bf16[896,2304]{1,0:T(8,128)(2,1)}, bf16[896,1152]{1,0:T(8,128)(2,1)S(1)}, bf16[896,576]{1,0:T(8,128)(2,1)S(1)}, ...), branch_computations={%region_16.17_spmd, %region_17.18_spmd} | conditional | flops 10321921 | bytes 33030206 | solution.py:442
  918.0 10.4 %branch_1_fun.6 = bf16[896,2304]{1,0:T(8,128)(2,1)} custom-call(s32[2]{0:T(128)S(1)} %get-tuple-element.200.spot.side, bf16[896,2304]{1,0:T(8,128)(2,1)} %get-tuple-element.201.inputs, bf16[896,2304]{1,0:T(8,128)(2,1)} %get-tuple-element.202.attn, bf16[896,1152]{1,0:T(8,128)(2,1)S(1)} %get-tuple-element.203.own, ...), custom_call_target="tpu_custom_call" | custom-call | tf_op jit(solution)/shard_map/cond/branch_1_fun/pallas_call | solution.py:73
  933.1 10.0 %branch_1_fun.7 = (f32[896,2304]{1,0:T(8,128)}, f32[1,2304]{1,0:T(1,128)}) custom-call(s32[2]{0:T(128)S(1)} %get-tuple-element.200.spot.side, bf16[896,2304]{1,0:T(8,128)(2,1)S(1)} %copy-done.3, bf16[896,2304]{1,0:T(8,128)(2,1)S(1)} %pad_maximum_fusion.9.grad_normed, f32[896,2304]{1,0:T(8,128)} %get-tuple-element.210.grad_resid, ...), custom_call_target="tpu_custom_call" | custom-call | tf_op jit(solution)/shard_map/cond/branch_1_fun/pallas_call | solution.py:73
  950.7 7.2 collective-permute-start.74
  973.0 7.8 fusion.87
  (518 shorter events, 387.3 us)
Async XLA Ops:
  81.0 32.9 %collective-permute-start.6 = (bf16[304,1536]{1,0:T(8,128)(2,1)S(1)}, bf16[304,1536]{1,0:T(8,128)(2,1)S(1)}, u32[]{:S(2)}, u32[]{:S(2)}) collective-permute-start(bf16[304,1536]{1,0:T(8,128)(2,1)S(1)} %collective-permute-done.4), channel_id=1, source_target_pairs={{0,4},{4,0},{8,12},{12,8},{16,20},{20,16},{24,28},{28,24},{1,5},{5... | collective-permute-start | bytes 2801672 | tf_op jit(solution)/shard_map/ppermute | solution.py:290
  82.1 32.7 %collective-permute-start.7 = (bf16[288,2304]{1,0:T(8,128)(2,1)}, bf16[288,2304]{1,0:T(8,128)(2,1)}, u32[]{:S(2)}, u32[]{:S(2)}) collective-permute-start(bf16[288,2304]{1,0:T(8,128)(2,1)} %get-tuple-element.546), channel_id=1, source_target_pairs={{0,8},{4,12},{8,16},{12,20},{16,24},{20,28},{24,0},{28,4},{1,9},{5... | collective-permute-start | bytes 3981320 | tf_op jit(solution)/shard_map/ppermute | solution.py:287
  114.8 48.7 %collective-permute-start.12 = (bf16[288,2304]{1,0:T(8,128)(2,1)}, bf16[288,2304]{1,0:T(8,128)(2,1)}, u32[]{:S(2)}, u32[]{:S(2)}) collective-permute-start(bf16[288,2304]{1,0:T(8,128)(2,1)} %get-tuple-element.546), channel_id=1, source_target_pairs={{0,4},{4,0},{8,12},{12,8},{16,20},{20,16},{24,28},{28,24},{1,5},{5... | collective-permute-start | bytes 3981320 | tf_op jit(solution)/shard_map/ppermute | solution.py:290
  115.8 54.4 %collective-permute-start.11 = (bf16[288,2304]{1,0:T(8,128)(2,1)}, bf16[288,2304]{1,0:T(8,128)(2,1)}, u32[]{:S(2)}, u32[]{:S(2)}) collective-permute-start(bf16[288,2304]{1,0:T(8,128)(2,1)} %get-tuple-element.544), channel_id=1, source_target_pairs={{0,4},{4,0},{8,12},{12,8},{16,20},{20,16},{24,28},{28,24},{1,5},{5... | collective-permute-start | bytes 3981320 | tf_op jit(solution)/shard_map/ppermute | solution.py:290
  116.8 53.4 %collective-permute-start.9 = (bf16[288,2304]{1,0:T(8,128)(2,1)}, bf16[288,2304]{1,0:T(8,128)(2,1)}, u32[]{:S(2)}, u32[]{:S(2)}) collective-permute-start(bf16[288,2304]{1,0:T(8,128)(2,1)} %get-tuple-element.544), channel_id=1, source_target_pairs={{0,8},{4,12},{8,16},{12,20},{16,24},{20,28},{24,0},{28,4},{1,9},{5... | collective-permute-start | bytes 3981320 | tf_op jit(solution)/shard_map/ppermute | solution.py:287
  116.8 55.9 %collective-permute-start.10 = (bf16[288,2304]{1,0:T(8,128)(2,1)}, bf16[288,2304]{1,0:T(8,128)(2,1)}, u32[]{:S(2)}, u32[]{:S(2)}) collective-permute-start(bf16[288,2304]{1,0:T(8,128)(2,1)} %collective-permute-done.7), channel_id=1, source_target_pairs={{0,8},{4,12},{8,16},{12,20},{16,24},{20,28},{24,0},{28,4},{1,9},{5... | collective-permute-start | bytes 3981320 | tf_op jit(solution)/shard_map/ppermute | solution.py:287
  172.7 65.2 %collective-permute-start.17 = (bf16[448,2304]{1,0:T(8,128)(2,1)S(1)}, bf16[448,2304]{1,0:T(8,128)(2,1)S(1)}, u32[]{:S(2)}, u32[]{:S(2)}) collective-permute-start(bf16[448,2304]{1,0:T(8,128)(2,1)S(1)} %get-tuple-element.559), channel_id=1, source_target_pairs={{0,1},{1,0},{2,3},{3,2},{4,5},{5,4},{6,7},{7,6},{8,9},{9,8},{10,11... | collective-permute-start | bytes 6193160 | tf_op jit(solution)/shard_map/ppermute | solution.py:293
  172.7 63.1 %collective-permute-start.16 = (bf16[288,2304]{1,0:T(8,128)(2,1)}, bf16[288,2304]{1,0:T(8,128)(2,1)S(1)}, u32[]{:S(2)}, u32[]{:S(2)}) collective-permute-start(bf16[288,2304]{1,0:T(8,128)(2,1)} %collective-permute-done.9), channel_id=1, source_target_pairs={{0,4},{4,0},{8,12},{12,8},{16,20},{20,16},{24,28},{28,24},{1,5},{5... | collective-permute-start | bytes 3981320 | tf_op jit(solution)/shard_map/ppermute | solution.py:290
  174.1 62.8 %collective-permute-start.13 = (bf16[288,2304]{1,0:T(8,128)(2,1)}, bf16[288,2304]{1,0:T(8,128)(2,1)}, u32[]{:S(2)}, u32[]{:S(2)}) collective-permute-start(bf16[288,2304]{1,0:T(8,128)(2,1)} %collective-permute-done.9), channel_id=1, source_target_pairs={{0,8},{4,12},{8,16},{12,20},{16,24},{20,28},{24,0},{28,4},{1,9},{5... | collective-permute-start | bytes 3981320 | tf_op jit(solution)/shard_map/ppermute | solution.py:287
  174.1 61.7 %collective-permute-start.15 = (bf16[288,2304]{1,0:T(8,128)(2,1)}, bf16[288,2304]{1,0:T(8,128)(2,1)S(1)}, u32[]{:S(2)}, u32[]{:S(2)}) collective-permute-start(bf16[288,2304]{1,0:T(8,128)(2,1)} %collective-permute-done.7), channel_id=1, source_target_pairs={{0,4},{4,0},{8,12},{12,8},{16,20},{20,16},{24,28},{28,24},{1,5},{5... | collective-permute-start | bytes 3981320 | tf_op jit(solution)/shard_map/ppermute | solution.py:290
  174.8 61.0 %collective-permute-start.14 = (bf16[288,2304]{1,0:T(8,128)(2,1)}, bf16[288,2304]{1,0:T(8,128)(2,1)S(1)}, u32[]{:S(2)}, u32[]{:S(2)}) collective-permute-start(bf16[288,2304]{1,0:T(8,128)(2,1)} %collective-permute-done.10), channel_id=1, source_target_pairs={{0,8},{4,12},{8,16},{12,20},{16,24},{20,28},{24,0},{28,4},{1,9},{5... | collective-permute-start | bytes 3981320 | tf_op jit(solution)/shard_map/ppermute | solution.py:287
  239.8 62.5 %collective-permute-start.22 = (bf16[448,2304]{1,0:T(8,128)(2,1)}, bf16[448,2304]{1,0:T(8,128)(2,1)}, u32[]{:S(2)}, u32[]{:S(2)}) collective-permute-start(bf16[448,2304]{1,0:T(8,128)(2,1)} %add_convert_fusion.12), channel_id=1, source_target_pairs={{0,2},{1,3},{2,0},{3,1},{4,6},{5,7},{6,4},{7,5},{8,10},{9,11},{10,... | collective-permute-start | bytes 6193160 | tf_op jit(solution)/shard_map/ppermute | solution.py:296
  240.4 58.8 %collective-permute-start.21 = (bf16[288,2304]{1,0:T(8,128)(2,1)}, bf16[288,2304]{1,0:T(8,128)(2,1)S(1)}, u32[]{:S(2)}, u32[]{:S(2)}) collective-permute-start(bf16[288,2304]{1,0:T(8,128)(2,1)} %collective-permute-done.13), channel_id=1, source_target_pairs={{0,4},{4,0},{8,12},{12,8},{16,20},{20,16},{24,28},{28,24},{1,5},{5... | collective-permute-start | bytes 3981320 | tf_op jit(solution)/shard_map/ppermute | solution.py:290
  241.9 57.3 %collective-permute-start.18 = (bf16[288,2304]{1,0:T(8,128)(2,1)}, bf16[288,2304]{1,0:T(8,128)(2,1)}, u32[]{:S(2)}, u32[]{:S(2)}) collective-permute-start(bf16[288,2304]{1,0:T(8,128)(2,1)} %collective-permute-done.13), channel_id=1, source_target_pairs={{0,8},{4,12},{8,16},{12,20},{16,24},{20,28},{24,0},{28,4},{1,9},{5... | collective-permute-start | bytes 3981320 | tf_op jit(solution)/shard_map/ppermute | solution.py:287
  242.0 57.3 %collective-permute-start.20 = (bf16[288,2304]{1,0:T(8,128)(2,1)}, bf16[288,2304]{1,0:T(8,128)(2,1)S(1)}, u32[]{:S(2)}, u32[]{:S(2)}) collective-permute-start(bf16[288,2304]{1,0:T(8,128)(2,1)} %collective-permute-done.10), channel_id=1, source_target_pairs={{0,4},{4,0},{8,12},{12,8},{16,20},{20,16},{24,28},{28,24},{1,5},{5... | collective-permute-start | bytes 3981320 | tf_op jit(solution)/shard_map/ppermute | solution.py:290
  242.5 59.8 %collective-permute-start.19 = (bf16[288,2304]{1,0:T(8,128)(2,1)S(1)}, bf16[288,2304]{1,0:T(8,128)(2,1)S(1)}, u32[]{:S(2)}, u32[]{:S(2)}) collective-permute-start(bf16[288,2304]{1,0:T(8,128)(2,1)S(1)} %convert_bitcast_fusion), channel_id=1, source_target_pairs={{0,8},{4,12},{8,16},{12,20},{16,24},{20,28},{24,0},{28,4},{1,9},{5... | collective-permute-start | bytes 3981320 | tf_op jit(solution)/shard_map/ppermute | solution.py:287
  302.8 30.8 %collective-permute-start.23 = (bf16[288,2304]{1,0:T(8,128)(2,1)S(1)}, bf16[288,2304]{1,0:T(8,128)(2,1)S(1)}, u32[]{:S(2)}, u32[]{:S(2)}) collective-permute-start(bf16[288,2304]{1,0:T(8,128)(2,1)S(1)} %collective-permute-done.19), channel_id=1, source_target_pairs={{0,8},{4,12},{8,16},{12,20},{16,24},{20,28},{24,0},{28,4},{1,9},{5... | collective-permute-start | bytes 3981320 | tf_op jit(solution)/shard_map/ppermute | solution.py:287
  363.2 31.0 %collective-permute-start.29 = (bf16[144,2304]{1,0:T(8,128)(2,1)}, bf16[144,2304]{1,0:T(8,128)(2,1)S(1)}, u32[]{:S(2)}, u32[]{:S(2)}) collective-permute-start(bf16[144,2304]{1,0:T(8,128)(2,1)} %slice.202), channel_id=1, source_target_pairs={{0,4},{4,0},{8,12},{12,8},{16,20},{20,16},{24,28},{28,24},{1,5},{5... | collective-permute-start | bytes 1990664 | tf_op jit(solution)/shard_map/ppermute | solution.py:290
  403.4 37.1 %collective-permute-start.36 = (bf16[448,1152]{1,0:T(8,128)(2,1)S(1)}, bf16[448,1152]{1,0:T(8,128)(2,1)S(1)}, u32[]{:S(2)}, u32[]{:S(2)}) collective-permute-start(bf16[448,1152]{1,0:T(8,128)(2,1)S(1)} %add_convert_fusion.22), channel_id=1, source_target_pairs={{0,2},{1,3},{2,0},{3,1},{4,6},{5,7},{6,4},{7,5},{8,10},{9,11},{10,... | collective-permute-start | bytes 3096584 | tf_op jit(solution)/shard_map/ppermute | solution.py:296
  409.9 30.6 %collective-permute-start.33 = (bf16[144,2304]{1,0:T(8,128)(2,1)S(1)}, bf16[144,2304]{1,0:T(8,128)(2,1)S(1)}, u32[]{:S(2)}, u32[]{:S(2)}) collective-permute-start(bf16[144,2304]{1,0:T(8,128)(2,1)S(1)} %collective-permute-done.31), channel_id=1, source_target_pairs={{0,8},{4,12},{8,16},{12,20},{16,24},{20,28},{24,0},{28,4},{1,9},{5... | collective-permute-start | bytes 1990664 | tf_op jit(solution)/shard_map/ppermute | solution.py:287
  488.6 51.1 %collective-permute-start.44 = (bf16[448,2304]{1,0:T(8,128)(2,1)}, bf16[448,2304]{1,0:T(8,128)(2,1)}, u32[]{:S(2)}, u32[]{:S(2)}) collective-permute-start(bf16[448,2304]{1,0:T(8,128)(2,1)} %pad_maximum_fusion.13), channel_id=1, source_target_pairs={{0,4},{4,0},{8,12},{12,8},{16,20},{20,16},{24,28},{28,24},{1,5},{5... | collective-permute-start | bytes 6193160 | tf_op jit(solution)/shard_map/ppermute | solution.py:290
  490.2 49.5 %collective-permute-start.45 = (bf16[176,2304]{1,0:T(8,128)(2,1)}, bf16[176,2304]{1,0:T(8,128)(2,1)}, u32[]{:S(2)}, u32[]{:S(2)}) collective-permute-start(bf16[176,2304]{1,0:T(8,128)(2,1)} %get-tuple-element.640), channel_id=1, source_target_pairs={{0,8},{4,12},{8,16},{12,20},{16,24},{20,28},{24,0},{28,4},{1,9},{5... | collective-permute-start | bytes 2433032 | tf_op jit(solution)/shard_map/ppermute | solution.py:287
  543.6 50.5 %collective-permute-start.47 = (bf16[288,2304]{1,0:T(8,128)(2,1)}, bf16[288,2304]{1,0:T(8,128)(2,1)}, u32[]{:S(2)}, u32[]{:S(2)}) collective-permute-start(bf16[288,2304]{1,0:T(8,128)(2,1)} %add_convert_fusion.20), channel_id=1, source_target_pairs={{0,8},{4,12},{8,16},{12,20},{16,24},{20,28},{24,0},{28,4},{1,9},{5... | collective-permute-start | bytes 3981320 | tf_op jit(solution)/shard_map/ppermute | solution.py:287
  547.9 46.3 %collective-permute-start.46 = (bf16[288,2304]{1,0:T(8,128)(2,1)}, bf16[288,2304]{1,0:T(8,128)(2,1)}, u32[]{:S(2)}, u32[]{:S(2)}) collective-permute-start(bf16[288,2304]{1,0:T(8,128)(2,1)} %get-tuple-element.654), channel_id=1, source_target_pairs={{0,4},{4,0},{8,12},{12,8},{16,20},{20,16},{24,28},{28,24},{1,5},{5... | collective-permute-start | bytes 3981320 | tf_op jit(solution)/shard_map/ppermute | solution.py:290
  550.6 43.5 %collective-permute-start.48 = (bf16[176,2304]{1,0:T(8,128)(2,1)}, bf16[176,2304]{1,0:T(8,128)(2,1)}, u32[]{:S(2)}, u32[]{:S(2)}) collective-permute-start(bf16[176,2304]{1,0:T(8,128)(2,1)} %add_convert_fusion.26), channel_id=1, source_target_pairs={{0,8},{4,12},{8,16},{12,20},{16,24},{20,28},{24,0},{28,4},{1,9},{5... | collective-permute-start | bytes 2433032 | tf_op jit(solution)/shard_map/ppermute | solution.py:287
  594.2 42.6 %collective-permute-start.50 = (bf16[448,2304]{1,0:T(8,128)(2,1)}, bf16[448,2304]{1,0:T(8,128)(2,1)}, u32[]{:S(2)}, u32[]{:S(2)}) collective-permute-start(bf16[448,2304]{1,0:T(8,128)(2,1)} %get-tuple-element.668), channel_id=1, source_target_pairs={{0,1},{1,0},{2,3},{3,2},{4,5},{5,4},{6,7},{7,6},{8,9},{9,8},{10,11... | collective-permute-start | bytes 6193160 | tf_op jit(solution)/shard_map/ppermute | solution.py:293
  597.4 39.4 %collective-permute-start.51 = (bf16[288,2304]{1,0:T(8,128)(2,1)}, bf16[288,2304]{1,0:T(8,128)(2,1)}, u32[]{:S(2)}, u32[]{:S(2)}) collective-permute-start(bf16[288,2304]{1,0:T(8,128)(2,1)} %add_convert_fusion.19), channel_id=1, source_target_pairs={{0,8},{4,12},{8,16},{12,20},{16,24},{20,28},{24,0},{28,4},{1,9},{5... | collective-permute-start | bytes 3981320 | tf_op jit(solution)/shard_map/ppermute | solution.py:287
  599.9 36.9 %collective-permute-start.49 = (bf16[288,2304]{1,0:T(8,128)(2,1)}, bf16[288,2304]{1,0:T(8,128)(2,1)}, u32[]{:S(2)}, u32[]{:S(2)}) collective-permute-start(bf16[288,2304]{1,0:T(8,128)(2,1)} %get-tuple-element.667), channel_id=1, source_target_pairs={{0,4},{4,0},{8,12},{12,8},{16,20},{20,16},{24,28},{28,24},{1,5},{5... | collective-permute-start | bytes 3981320 | tf_op jit(solution)/shard_map/ppermute | solution.py:290
  636.8 67.1 %collective-permute-start.53 = (bf16[576,2304]{1,0:T(8,128)(2,1)S(1)}, bf16[576,2304]{1,0:T(8,128)(2,1)S(1)}, u32[]{:S(2)}, u32[]{:S(2)}) collective-permute-start(bf16[576,2304]{1,0:T(8,128)(2,1)S(1)} %get-tuple-element.687), channel_id=1, source_target_pairs={{0,4},{4,0},{8,12},{12,8},{16,20},{20,16},{24,28},{28,24},{1,5},{5... | collective-permute-start | bytes 7962632 | tf_op jit(solution)/shard_map/ppermute | solution.py:290
  640.5 63.4 %collective-permute-start.52 = (bf16[448,2304]{1,0:T(8,128)(2,1)S(1)}, bf16[448,2304]{1,0:T(8,128)(2,1)S(1)}, u32[]{:S(2)}, u32[]{:S(2)}) collective-permute-start(bf16[448,2304]{1,0:T(8,128)(2,1)S(1)} %add_convert_fusion.10), channel_id=1, source_target_pairs={{0,2},{1,3},{2,0},{3,1},{4,6},{5,7},{6,4},{7,5},{8,10},{9,11},{10,... | collective-permute-start | bytes 6193160 | tf_op jit(solution)/shard_map/ppermute | solution.py:296
  643.2 33.9 %collective-permute-start.54 = (bf16[288,2304]{1,0:T(8,128)(2,1)S(1)}, bf16[288,2304]{1,0:T(8,128)(2,1)S(1)}, u32[]{:S(2)}, u32[]{:S(2)}) collective-permute-start(bf16[288,2304]{1,0:T(8,128)(2,1)S(1)} %add_convert_fusion.18), channel_id=1, source_target_pairs={{0,8},{4,12},{8,16},{12,20},{16,24},{20,28},{24,0},{28,4},{1,9},{5... | collective-permute-start | bytes 3981320 | tf_op jit(solution)/shard_map/ppermute | solution.py:287
  643.6 60.3 %collective-permute-start.55 = (bf16[288,2304]{1,0:T(8,128)(2,1)}, bf16[288,2304]{1,0:T(8,128)(2,1)S(1)}, u32[]{:S(2)}, u32[]{:S(2)}) collective-permute-start(bf16[288,2304]{1,0:T(8,128)(2,1)} %get-tuple-element.689), channel_id=1, source_target_pairs={{0,8},{4,12},{8,16},{12,20},{16,24},{20,28},{24,0},{28,4},{1,9},{5... | collective-permute-start | bytes 3981320 | tf_op jit(solution)/shard_map/ppermute | solution.py:287
  707.7 77.4 %collective-permute-start.58 = (bf16[288,2304]{1,0:T(8,128)(2,1)}, bf16[288,2304]{1,0:T(8,128)(2,1)}, u32[]{:S(2)}, u32[]{:S(2)}) collective-permute-start(bf16[288,2304]{1,0:T(8,128)(2,1)} %add_convert_fusion.16), channel_id=1, source_target_pairs={{0,8},{4,12},{8,16},{12,20},{16,24},{20,28},{24,0},{28,4},{1,9},{5... | collective-permute-start | bytes 3981320 | tf_op jit(solution)/shard_map/ppermute | solution.py:287
  707.7 77.4 %collective-permute-start.56 = (bf16[576,2304]{1,0:T(8,128)(2,1)}, bf16[576,2304]{1,0:T(8,128)(2,1)}, u32[]{:S(2)}, u32[]{:S(2)}) collective-permute-start(bf16[576,2304]{1,0:T(8,128)(2,1)} %get-tuple-element.694), channel_id=1, source_target_pairs={{0,4},{4,0},{8,12},{12,8},{16,20},{20,16},{24,28},{28,24},{1,5},{5... | collective-permute-start | bytes 7962632 | tf_op jit(solution)/shard_map/ppermute | solution.py:290
  714.4 70.7 %collective-permute-start.57 = (bf16[288,2304]{1,0:T(8,128)(2,1)}, bf16[288,2304]{1,0:T(8,128)(2,1)}, u32[]{:S(2)}, u32[]{:S(2)}) collective-permute-start(bf16[288,2304]{1,0:T(8,128)(2,1)} %add_convert_fusion.17), channel_id=1, source_target_pairs={{0,8},{4,12},{8,16},{12,20},{16,24},{20,28},{24,0},{28,4},{1,9},{5... | collective-permute-start | bytes 3981320 | tf_op jit(solution)/shard_map/ppermute | solution.py:287
  714.4 70.7 %collective-permute-start.59 = (bf16[176,2304]{1,0:T(8,128)(2,1)}, bf16[176,2304]{1,0:T(8,128)(2,1)}, u32[]{:S(2)}, u32[]{:S(2)}) collective-permute-start(bf16[176,2304]{1,0:T(8,128)(2,1)} %get-tuple-element.700), channel_id=1, source_target_pairs={{0,8},{4,12},{8,16},{12,20},{16,24},{20,28},{24,0},{28,4},{1,9},{5... | collective-permute-start | bytes 2433032 | tf_op jit(solution)/shard_map/ppermute | solution.py:287
  785.1 37.8 %collective-permute-start.62 = (bf16[448,2304]{1,0:T(8,128)(2,1)}, bf16[448,2304]{1,0:T(8,128)(2,1)}, u32[]{:S(2)}, u32[]{:S(2)}) collective-permute-start(bf16[448,2304]{1,0:T(8,128)(2,1)} %get-tuple-element.718), channel_id=1, source_target_pairs={{0,1},{1,0},{2,3},{3,2},{4,5},{5,4},{6,7},{7,6},{8,9},{9,8},{10,11... | collective-permute-start | bytes 6193160 | tf_op jit(solution)/shard_map/ppermute | solution.py:293
  788.9 34.0 %collective-permute-start.63 = (bf16[288,2304]{1,0:T(8,128)(2,1)}, bf16[288,2304]{1,0:T(8,128)(2,1)}, u32[]{:S(2)}, u32[]{:S(2)}) collective-permute-start(bf16[288,2304]{1,0:T(8,128)(2,1)} %add_convert_fusion.15), channel_id=1, source_target_pairs={{0,8},{4,12},{8,16},{12,20},{16,24},{20,28},{24,0},{28,4},{1,9},{5... | collective-permute-start | bytes 3981320 | tf_op jit(solution)/shard_map/ppermute | solution.py:287
  788.9 34.0 %collective-permute-start.61 = (bf16[288,2304]{1,0:T(8,128)(2,1)}, bf16[288,2304]{1,0:T(8,128)(2,1)}, u32[]{:S(2)}, u32[]{:S(2)}) collective-permute-start(bf16[288,2304]{1,0:T(8,128)(2,1)} %get-tuple-element.717), channel_id=1, source_target_pairs={{0,4},{4,0},{8,12},{12,8},{16,20},{20,16},{24,28},{28,24},{1,5},{5... | collective-permute-start | bytes 3981320 | tf_op jit(solution)/shard_map/ppermute | solution.py:290
  793.9 57.1 %collective-permute-start.66 = (bf16[288,2304]{1,0:T(8,128)(2,1)}, bf16[288,2304]{1,0:T(8,128)(2,1)}, u32[]{:S(2)}, u32[]{:S(2)}) collective-permute-start(bf16[288,2304]{1,0:T(8,128)(2,1)} %add_convert_fusion.14), channel_id=1, source_target_pairs={{0,8},{4,12},{8,16},{12,20},{16,24},{20,28},{24,0},{28,4},{1,9},{5... | collective-permute-start | bytes 3981320 | tf_op jit(solution)/shard_map/ppermute | solution.py:287
  822.9 68.6 %collective-permute-start.65 = (bf16[576,1536]{1,0:T(8,128)(2,1)}, bf16[576,1536]{1,0:T(8,128)(2,1)}, u32[]{:S(2)}, u32[]{:S(2)}) collective-permute-start(bf16[576,1536]{1,0:T(8,128)(2,1)} %get-tuple-element.736), channel_id=1, source_target_pairs={{0,4},{4,0},{8,12},{12,8},{16,20},{20,16},{24,28},{28,24},{1,5},{5... | collective-permute-start | bytes 5308424 | tf_op jit(solution)/shard_map/ppermute | solution.py:290
  827.0 64.5 %collective-permute-start.68 = (bf16[448,2304]{1,0:T(8,128)(2,1)S(1)}, bf16[448,2304]{1,0:T(8,128)(2,1)}, u32[]{:S(2)}, u32[]{:S(2)}) collective-permute-start(bf16[448,2304]{1,0:T(8,128)(2,1)S(1)} %add_convert_fusion.8), channel_id=1, source_target_pairs={{0,2},{1,3},{2,0},{3,1},{4,6},{5,7},{6,4},{7,5},{8,10},{9,11},{10,... | collective-permute-start | bytes 6193160 | tf_op jit(solution)/shard_map/ppermute | solution.py:296
  854.6 32.9 %collective-permute-start.67 = (bf16[288,2304]{1,0:T(8,128)(2,1)}, bf16[288,2304]{1,0:T(8,128)(2,1)}, u32[]{:S(2)}, u32[]{:S(2)}) collective-permute-start(bf16[288,2304]{1,0:T(8,128)(2,1)} %add_convert_fusion.13), channel_id=1, source_target_pairs={{0,8},{4,12},{8,16},{12,20},{16,24},{20,28},{24,0},{28,4},{1,9},{5... | collective-permute-start | bytes 3981320 | tf_op jit(solution)/shard_map/ppermute | solution.py:287
  854.6 37.0 %collective-permute-start.64 = (bf16[288,2304]{1,0:T(8,128)(2,1)}, bf16[288,2304]{1,0:T(8,128)(2,1)}, u32[]{:S(2)}, u32[]{:S(2)}) collective-permute-start(bf16[288,2304]{1,0:T(8,128)(2,1)} %get-tuple-element.735), channel_id=1, source_target_pairs={{0,4},{4,0},{8,12},{12,8},{16,20},{20,16},{24,28},{28,24},{1,5},{5... | collective-permute-start | bytes 3981320 | tf_op jit(solution)/shard_map/ppermute | solution.py:290
  891.6 51.6 %collective-permute-start.70 = (bf16[176,2304]{1,0:T(8,128)(2,1)}, bf16[176,2304]{1,0:T(8,128)(2,1)}, u32[]{:S(2)}, u32[]{:S(2)}) collective-permute-start(bf16[176,2304]{1,0:T(8,128)(2,1)} %get-tuple-element.747), channel_id=1, source_target_pairs={{0,4},{4,0},{8,12},{12,8},{16,20},{20,16},{24,28},{28,24},{1,5},{5... | collective-permute-start | bytes 2433032 | tf_op jit(solution)/shard_map/ppermute | solution.py:290
  896.5 46.7 %collective-permute-start.72 = (bf16[288,1536]{1,0:T(8,128)(2,1)}, bf16[288,1536]{1,0:T(8,128)(2,1)}, u32[]{:S(2)}, u32[]{:S(2)}) collective-permute-start(bf16[288,1536]{1,0:T(8,128)(2,1)} %get-tuple-element.940), channel_id=1, source_target_pairs={{0,16},{4,20},{8,24},{12,28},{16,0},{20,4},{24,8},{28,12},{1,17},{... | collective-permute-start | bytes 2654216 | tf_op jit(solution)/shard_map/ppermute | solution.py:287
  898.5 44.7 %collective-permute-start.71 = (bf16[288,1536]{1,0:T(8,128)(2,1)}, bf16[288,1536]{1,0:T(8,128)(2,1)}, u32[]{:S(2)}, u32[]{:S(2)}) collective-permute-start(bf16[288,1536]{1,0:T(8,128)(2,1)} %get-tuple-element.941), channel_id=1, source_target_pairs={{0,24},{4,28},{8,0},{12,4},{16,8},{20,12},{24,16},{28,20},{1,25},{... | collective-permute-start | bytes 2654216 | tf_op jit(solution)/shard_map/ppermute | solution.py:287
  898.5 49.7 %collective-permute-start.69 = (bf16[576,1536]{1,0:T(8,128)(2,1)}, bf16[576,1536]{1,0:T(8,128)(2,1)}, u32[]{:S(2)}, u32[]{:S(2)}) collective-permute-start(bf16[576,1536]{1,0:T(8,128)(2,1)} %get-tuple-element.746), channel_id=1, source_target_pairs={{0,4},{4,0},{8,12},{12,8},{16,20},{20,16},{24,28},{28,24},{1,5},{5... | collective-permute-start | bytes 5308424 | tf_op jit(solution)/shard_map/ppermute | solution.py:290
  (122 other events, 1754.8 us)
